TPU v7x, 32 devices: a whole 2x2x4 slice. The times are simulated.
32 devices in a mesh: sec: 4 (over y, core), gx: 8 (over z, x).
Axes of the slice: x: 2, y: 2, z: 4, core: 2. Of those that a mesh axis runs over, the one named last changes fastest.
Arguments:
- incoming: float32 [4, 32, 64, 256], P('sec', 'gx'), may hold values from 0.5 to 2
- backward: bfloat16 [16, 32, 64, 256], P('sec', 'gx'), may hold values from 0.5 to 2
- fields: float32 [3, 32, 256], P(None, 'gx'), may hold values from -0.4 to 0.4
- block_types: int32 [4, 4], P('sec'), may hold values from 0 to 2
- axial_taps: float32 [3, 64], replicated, may hold values from 0.1 to 0.45
- lateral_taps: float32 [3, 64], replicated, may hold values from 0.1 to 0.45
- depth_taps: float32 [3, 64], replicated, may hold values from 0.1 to 0.45
- bend_diagonal: float32 [64], replicated, may hold values from 0.4 to 0.8
- bend_coupling: float32 [64, 64], replicated, may hold values from 0 to 0.025
Outputs:
- handoff: float32 [4, 32, 64, 256], P('sec', 'gx')
- density: float32 [32, 64, 256], P('gx', 'sec')
All inputs are finite; a program needn't handle non-finite values.
Results may differ from a plain program's by a relative error of at most 0.0003.
Values sent between devices are 32-bit elements; how exact they have to be, the bound alone decides.
No kernel may reach another device: no remote copies, remote signals or barrier semaphores. Data moves between devices by JAX's collectives and lax.ppermute only.
A program may use at most 64 MiB of HBM per device.

v0:
```python
import jax
import jax.numpy as jnp
from jax import lax
from jax.sharding import PartitionSpec as P

TICKS = 3
CZ = 64


def padded_2(block, sides, width):
    for axis, dim in sides:
        count = lax.axis_size(axis)
        forward = [(i, i + 1) for i in range(count - 1)]
        forward.append((count - 1, 0))
        backward = [(target, source) for source, target in forward]
        low = lax.ppermute(
            lax.slice_in_dim(block, block.shape[dim] - width, None, axis=dim), axis, forward
        )
        high = lax.ppermute(lax.slice_in_dim(block, 0, width, axis=dim), axis, backward)
        block = jnp.concatenate([low, block, high], axis=dim)
    return block


def from_behind(array, axis, by):
    length = lax.axis_size(axis)
    pairs = [(i, i + by) for i in range(length) if 0 <= i + by < length]
    return lax.ppermute(array, axis, pairs)


def boltzmann(fields, kinds):
    selector = kinds == jnp.arange(fields.shape[0], dtype=jnp.int32)
    chosen = jnp.sum(jnp.where(selector[:, None, None], fields, jnp.zeros_like(fields)), axis=0)
    return jnp.exp(-chosen)


def column(taps, which):
    return taps[which][None, :, None]


def advance_padded(padded, factor, axial_taps, lateral_taps, depth_taps, kernel):
    along_x = (
        column(axial_taps, 0) * padded[:-2]
        + column(axial_taps, 1) * padded[1:-1]
        + column(axial_taps, 2) * padded[2:]
    )
    along_y = (
        column(lateral_taps, 0) * jnp.roll(along_x, CZ, axis=2)
        + column(lateral_taps, 1) * along_x
        + column(lateral_taps, 2) * jnp.roll(along_x, -CZ, axis=2)
    )
    depth_pos = (jnp.arange(along_y.shape[2], dtype=jnp.int32) % CZ)[None, None, :]
    behind = jnp.where(
        depth_pos == 0, jnp.roll(along_y, -(CZ - 1), axis=2), jnp.roll(along_y, 1, axis=2)
    )
    ahead = jnp.where(
        depth_pos == CZ - 1, jnp.roll(along_y, CZ - 1, axis=2), jnp.roll(along_y, -1, axis=2)
    )
    along_z = (
        column(depth_taps, 0) * behind
        + column(depth_taps, 1) * along_y
        + column(depth_taps, 2) * ahead
    )
    blended = jnp.einsum(
        "uv,xvc->xuc",
        kernel,
        along_z,
        precision=lax.Precision.HIGHEST,
        preferred_element_type=jnp.float32,
    )
    return blended * factor[:, None, :]


def per_device(
    incoming,
    backward,
    fields,
    block_types,
    axial_taps,
    lateral_taps,
    depth_taps,
    bend_diagonal,
    bend_coupling,
):
    kernel = jnp.diag(bend_diagonal) + bend_coupling
    steps_each = block_types.shape[1]
    planes = incoming.shape[1]
    start = incoming[0]
    first_section = lax.axis_index("sec") == 0
    wide_fields = padded_2(fields, (("gx", 1),), steps_each)
    factors = [boltzmann(wide_fields, block_types[0, position]) for position in range(steps_each)]
    current = start
    outgoing = start
    accumulated = jnp.zeros(start.shape, jnp.float32)
    for tick_index in range(TICKS):
        final_tick = tick_index + 1 == TICKS
        extended = padded_2(current, (("gx", 0),), steps_each)
        for position in range(steps_each):
            margin = steps_each - position - 1
            offset = steps_each - margin
            factor = factors[position][offset : offset + planes + 2 * margin]
            extended = advance_padded(
                extended, factor, axial_taps, lateral_taps, depth_taps, kernel
            )
            if final_tick:
                accumulated = accumulated + extended[margin : margin + planes] * backward[
                    position
                ].astype(jnp.float32)
        outgoing = extended
        if not final_tick:
            shifted = from_behind(outgoing, "sec", 1)
            current = jnp.where(first_section, start, shifted)
    reduced = lax.psum_scatter(accumulated, "sec", scatter_dimension=1, tiled=True)
    density = reduced / (lax.axis_size("sec") * steps_each)
    return (outgoing[None], density)


def solution(mesh):
    in_specs = (
        P("sec", "gx", None, None),
        P("sec", "gx", None, None),
        P(None, "gx", None),
        P("sec", None),
        P(),
        P(),
        P(),
        P(),
        P(),
    )
    out_specs = (P("sec", "gx", None, None), P("gx", "sec", None))
    return jax.shard_map(
        per_device, mesh=mesh, in_specs=in_specs, out_specs=out_specs, check_vma=False
    )
```

profile of v0, /device:TPU:0, one launch (start us, length us, event | category | flops | bytes accessed | tf_op | source)
XLA Modules:
  0.0 123.7 jit_solution(13178363277688636165)
XLA Ops:
  7.2 3.0 %collective-permute-start.2 = (f32[3,4,256]{2,1,0:T(4,128)}, f32[3,4,256]{2,1,0:T(4,128)S(1)}, u32[]{:S(2)}, u32[]{:S(2)}) collective-permute-start(f32[3,4,256]{2,1,0:T(4,128)} %param.11), channel_id=1, source_target_pairs={{0,1},{1,2},{2,3},{3,4},{4,5},{5,6},{6,7},{7,0},{8,9},{9,10},{10,1... | collective-permute-start | bytes 36872 | tf_op jit(solution)/shard_map/ppermute | solution.py:16
  10.2 3.1 %collective-permute-start.3 = (f32[3,4,256]{2,1,0:T(4,128)}, f32[3,4,256]{2,1,0:T(4,128)S(1)}, u32[]{:S(2)}, u32[]{:S(2)}) collective-permute-start(f32[3,4,256]{2,1,0:T(4,128)} %param.11), channel_id=1, source_target_pairs={{1,0},{2,1},{3,2},{4,3},{5,4},{6,5},{7,6},{0,7},{9,8},{10,9},{11,1... | collective-permute-start | bytes 36872 | tf_op jit(solution)/shard_map/ppermute | solution.py:19
  13.3 2.0 %collective-permute-start.1 = (f32[4,64,256]{2,1,0:T(8,128)}, f32[4,64,256]{2,1,0:T(8,128)S(1)}, u32[]{:S(2)}, u32[]{:S(2)}) collective-permute-start(f32[4,64,256]{2,1,0:T(8,128)} %bitcast.90), channel_id=1, source_target_pairs={{1,0},{2,1},{3,2},{4,3},{5,4},{6,5},{7,6},{0,7},{9,8},{10,9},{11,1... | collective-permute-start | bytes 786440 | tf_op jit(solution)/shard_map/ppermute | solution.py:19
  15.4 0.7 copy-done.7
  16.1 0.6 copy-done.4
  16.7 0.7 fusion.426
  17.4 1.3 %iota_compare_fusion.3 = (pred[3]{0:T(512)(128)(4,1)S(1)}, pred[3]{0:T(512)(128)(4,1)S(1)}) fusion(s32[]{:T(128)} %bitcast.13, s32[]{:T(128)} %bitcast.11), kind=kLoop, calls=%fused_computation.437 | loop fusion | flops 6 | bytes 14 | tf_op jit(solution)/shard_map/eq | solution.py:31
  18.7 1.3 %iota_compare_fusion.1 = (pred[3]{0:T(512)(128)(4,1)S(1)}, pred[3]{0:T(512)(128)(4,1)S(1)}) fusion(s32[]{:T(128)} %bitcast.17, s32[]{:T(128)} %bitcast.15), kind=kLoop, calls=%fused_computation.435 | loop fusion | flops 6 | bytes 14 | tf_op jit(solution)/shard_map/eq | solution.py:31
  20.1 6.8 %collective-permute-done.1 = f32[4,64,256]{2,1,0:T(8,128)S(1)} collective-permute-done((f32[4,64,256]{2,1,0:T(8,128)}, f32[4,64,256]{2,1,0:T(8,128)S(1)}, u32[]{:S(2)}, u32[]{:S(2)}) %collective-permute-start.1) | collective-permute-done | bytes 262176 | tf_op jit(solution)/shard_map/ppermute | solution.py:19
  26.9 1.0 pad_maximum_fusion
  28.0 0.2 fusion.15
  28.3 0.2 fusion.370
  28.6 0.4 fusion.18
  29.3 0.2 fusion.366
  29.6 0.2 fusion.369
  29.8 0.5 copy-done
  30.5 1.3 %fusion.2 = f32[10,64,256]{2,1,0:T(8,128)S(1)} fusion(f32[10,64,63]{2,1,0:T(8,128)S(1)} %get-tuple-element.35, f32[10,64,193]{2,1,0:T(8,128)S(1)} %get-tuple-element.37, f32[10,64,255]{2,1,0:T(8,128)S(1)} %get-tuple-element.31, f32[10,64,1]{2,1,0:T(8,128)S(1)} %get-tuple-element.33, f32[10,64,193]{2,1,0:T(8,128)S(1)} %get-tuple-element.36, ...), kind=kOutput, calls=%fused_computation.5 | convolution fusion | flops 127807488 | bytes 3960320 | tf_op jit(solution)/shard_map/uv,xvc->xuc/dot_general | solution.py:63
  32.1 0.2 fusion.388
  32.3 0.3 fusion.81
  32.9 0.2 fusion.384
  33.4 1.1 fusion.5
  34.9 0.3 fusion.144
  35.8 0.9 fusion.8
  37.0 0.2 fusion.225
  37.8 0.7 fusion.10
  38.4 1.3 %collective-permute-start.4 = (f32[4,64,256]{2,1,0:T(8,128)S(1)}, f32[4,64,256]{2,1,0:T(8,128)S(1)}, u32[]{:S(2)}, u32[]{:S(2)}) collective-permute-start(f32[4,64,256]{2,1,0:T(8,128)S(1)} %fusion.10), channel_id=1, source_target_pairs={{0,8},{8,16},{16,24},{1,9},{9,17},{17,25},{2,10},{10,18},{18,26},{... | collective-permute-start | bytes 786440 | tf_op jit(solution)/shard_map/ppermute | solution.py:27
  39.8 1.1 collective-permute-done.4
  40.9 3.1 %collective-permute-start.6 = (f32[4,64,256]{2,1,0:T(8,128)S(1)}, f32[4,64,256]{2,1,0:T(8,128)S(1)}, u32[]{:S(2)}, u32[]{:S(2)}) collective-permute-start(f32[4,64,256]{2,1,0:T(8,128)S(1)} %broadcast_select_fusion.1), channel_id=1, source_target_pairs={{1,0},{2,1},{3,2},{4,3},{5,4},{6,5},{7,6},{0,7},{9,8},{10,9},{11,1... | collective-permute-start | bytes 786440 | tf_op jit(solution)/shard_map/ppermute | solution.py:19
  44.1 3.9 %collective-permute-done.6 = f32[4,64,256]{2,1,0:T(8,128)S(1)} collective-permute-done((f32[4,64,256]{2,1,0:T(8,128)S(1)}, f32[4,64,256]{2,1,0:T(8,128)S(1)}, u32[]{:S(2)}, u32[]{:S(2)}) %collective-permute-start.6) | collective-permute-done | bytes 262176 | tf_op jit(solution)/shard_map/ppermute | solution.py:19
  48.0 6.4 %collective-permute-done.5 = f32[4,64,256]{2,1,0:T(8,128)S(1)} collective-permute-done((f32[4,64,256]{2,1,0:T(8,128)S(1)}, f32[4,64,256]{2,1,0:T(8,128)S(1)}, u32[]{:S(2)}, u32[]{:S(2)}) %collective-permute-start.5) | collective-permute-done | bytes 262176 | tf_op jit(solution)/shard_map/ppermute | solution.py:16
  54.5 0.2 fusion.13
  54.8 0.2 fusion.364
  55.1 0.4 fusion.36
  55.8 0.2 fusion.360
  56.1 0.2 fusion.363
  56.3 1.3 %fusion.1 = f32[10,64,256]{2,1,0:T(8,128)S(1)} fusion(f32[10,64,63]{2,1,0:T(8,128)S(1)} %get-tuple-element.23, f32[10,64,193]{2,1,0:T(8,128)S(1)} %get-tuple-element.25, f32[10,64,255]{2,1,0:T(8,128)S(1)} %get-tuple-element.19, f32[10,64,1]{2,1,0:T(8,128)S(1)} %get-tuple-element.21, f32[10,64,193]{2,1,0:T(8,128)S(1)} %get-tuple-element.24, ...), kind=kOutput, calls=%fused_computation.3 | convolution fusion | flops 127807488 | bytes 3960320 | tf_op jit(solution)/shard_map/uv,xvc->xuc/dot_general | solution.py:63
  58.1 0.3 fusion.99
  58.8 0.2 fusion.378
  59.0 0.2 fusion.381
  59.2 1.1 fusion.4
  60.7 0.3 fusion.162
  61.7 0.9 fusion.7
  62.9 0.2 fusion.243
  63.6 0.7 fusion.9
  64.3 3.7 %collective-permute-start.7 = (f32[4,64,256]{2,1,0:T(8,128)S(1)}, f32[4,64,256]{2,1,0:T(8,128)S(1)}, u32[]{:S(2)}, u32[]{:S(2)}) collective-permute-start(f32[4,64,256]{2,1,0:T(8,128)S(1)} %fusion.9), channel_id=1, source_target_pairs={{0,8},{8,16},{16,24},{1,9},{9,17},{17,25},{2,10},{10,18},{18,26},{... | collective-permute-start | bytes 786440 | tf_op jit(solution)/shard_map/ppermute | solution.py:27
  68.0 1.1 collective-permute-done.7
  69.2 2.7 %collective-permute-start.9 = (f32[4,64,256]{2,1,0:T(8,128)S(1)}, f32[4,64,256]{2,1,0:T(8,128)S(1)}, u32[]{:S(2)}, u32[]{:S(2)}) collective-permute-start(f32[4,64,256]{2,1,0:T(8,128)S(1)} %broadcast_select_fusion), channel_id=1, source_target_pairs={{1,0},{2,1},{3,2},{4,3},{5,4},{6,5},{7,6},{0,7},{9,8},{10,9},{11,1... | collective-permute-start | bytes 786440 | tf_op jit(solution)/shard_map/ppermute | solution.py:19
  71.9 3.9 %collective-permute-done.9 = f32[4,64,256]{2,1,0:T(8,128)S(1)} collective-permute-done((f32[4,64,256]{2,1,0:T(8,128)S(1)}, f32[4,64,256]{2,1,0:T(8,128)S(1)}, u32[]{:S(2)}, u32[]{:S(2)}) %collective-permute-start.9) | collective-permute-done | bytes 262176 | tf_op jit(solution)/shard_map/ppermute | solution.py:19
  75.8 7.3 %collective-permute-done.8 = f32[4,64,256]{2,1,0:T(8,128)S(1)} collective-permute-done((f32[4,64,256]{2,1,0:T(8,128)S(1)}, f32[4,64,256]{2,1,0:T(8,128)S(1)}, u32[]{:S(2)}, u32[]{:S(2)}) %collective-permute-start.8) | collective-permute-done | bytes 262176 | tf_op jit(solution)/shard_map/ppermute | solution.py:16
  83.2 0.2 fusion.11
  83.6 0.2 fusion.358
  83.9 0.4 fusion.54
  84.6 0.2 fusion.354
  84.8 0.2 fusion.357
  85.1 1.3 %fusion = f32[10,64,256]{2,1,0:T(8,128)S(1)} fusion(f32[10,64,63]{2,1,0:T(8,128)S(1)} %get-tuple-element.11, f32[10,64,193]{2,1,0:T(8,128)S(1)} %get-tuple-element.13, f32[10,64,255]{2,1,0:T(8,128)S(1)} %get-tuple-element.7, f32[10,64,1]{2,1,0:T(8,128)S(1)} %get-tuple-element.9, f32[10,64,193]{2,1,0:T(8,128)S(1)} %get-tuple-element.12, ...), kind=kOutput, calls=%fused_computation.1 | convolution fusion | flops 127807488 | bytes 3960320 | tf_op jit(solution)/shard_map/uv,xvc->xuc/dot_general | solution.py:63
  86.7 0.2 fusion.376
  86.9 0.3 fusion.117
  87.9 1.1 fusion.3
  89.5 0.3 fusion.180
  90.4 0.9 fusion.6
  91.6 0.2 fusion.261
  92.3 2.6 %fusion.217 = (f32[4,64,256]{2,1,0:T(8,128)}, f32[4,256,64]{1,2,0:T(8,128)}) fusion(f32[8,64,256]{2,1,0:T(8,128)S(1)} %fusion.3, f32[10,64,256]{2,1,0:T(8,128)S(1)} %fusion, f32[6,64,256]{2,1,0:T(8,128)S(1)} %fusion.6, bf16[4,4,64,256]{3,2,1,0:T(8,128)(2,1)} %param.10, f32[4,256]{1,0:T(4,128)S(1)} %fusion.341, f32[64,64]{1,0:T(8,128)S(1)} %copy-done, ...), kind=kOutput, calls=%fused_computation.278 | convolution fusion | flops 51851264 | bytes 3167744 | tf_op jit(solution)/shard_map/uv,xvc->xuc/dot_general | solution.py:63
  94.9 20.5 %reduce-scatter.2.cloned.1.call-done = f32[4,16,256]{2,1,0:T(8,128)} async-done(((f32[4,64,256]{2,1,0:T(8,128)}), f32[4,16,256]{2,1,0:T(8,128)}) %reduce-scatter.2.cloned.1.call-update) | async-done | bytes 65552 | tf_op jit(solution)/shard_map/reduce_scatter | solution.py:112
  115.4 1.5 %broadcast_multiply_fusion = f32[4,16,256]{2,1,0:T(8,128)} fusion(f32[4,16,256]{2,1,0:T(8,128)} %reduce-scatter.2.cloned.1.call-done), kind=kLoop, calls=%fused_computation.423 | loop fusion | flops 16384 | bytes 131072 | tf_op jit(solution)/shard_map/div | solution.py:113
  (101 shorter events, 10.1 us)
Async XLA Ops:
  7.2 8.2 %copy-start.5 = (f32[3,64]{1,0:T(4,128)S(1)}, f32[3,64]{1,0:T(4,128)}, u32[]{:S(2)}) copy-start(f32[3,64]{1,0:T(4,128)} %param.13) | copy-start | bytes 2308
  7.2 108.2 %reduce-scatter.2.cloned.1.call-start = ((), (), s32[]{:S(2)}) async-start(), calls=%async_computation.1 | async-start | bytes 327680 | tf_op jit(solution)/shard_map/reduce_scatter | solution.py:112
  7.2 12.7 %collective-permute-start.2 = (f32[3,4,256]{2,1,0:T(4,128)}, f32[3,4,256]{2,1,0:T(4,128)S(1)}, u32[]{:S(2)}, u32[]{:S(2)}) collective-permute-start(f32[3,4,256]{2,1,0:T(4,128)} %param.11), channel_id=1, source_target_pairs={{0,1},{1,2},{2,3},{3,4},{4,5},{5,6},{6,7},{7,0},{8,9},{9,10},{10,1... | collective-permute-start | bytes 36872 | tf_op jit(solution)/shard_map/ppermute | solution.py:16
  10.2 9.8 %collective-permute-start.3 = (f32[3,4,256]{2,1,0:T(4,128)}, f32[3,4,256]{2,1,0:T(4,128)S(1)}, u32[]{:S(2)}, u32[]{:S(2)}) collective-permute-start(f32[3,4,256]{2,1,0:T(4,128)} %param.11), channel_id=1, source_target_pairs={{1,0},{2,1},{3,2},{4,3},{5,4},{6,5},{7,6},{0,7},{9,8},{10,9},{11,1... | collective-permute-start | bytes 36872 | tf_op jit(solution)/shard_map/ppermute | solution.py:19
  13.3 2.0 %copy-start.6 = (f32[3,64]{1,0:T(4,128)S(1)}, f32[3,64]{1,0:T(4,128)}, u32[]{:S(2)}) copy-start(f32[3,64]{1,0:T(4,128)} %param.14) | copy-start | bytes 2308
  13.3 13.6 %collective-permute-start.1 = (f32[4,64,256]{2,1,0:T(8,128)}, f32[4,64,256]{2,1,0:T(8,128)S(1)}, u32[]{:S(2)}, u32[]{:S(2)}) collective-permute-start(f32[4,64,256]{2,1,0:T(8,128)} %bitcast.90), channel_id=1, source_target_pairs={{1,0},{2,1},{3,2},{4,3},{5,4},{6,5},{7,6},{0,7},{9,8},{10,9},{11,1... | collective-permute-start | bytes 786440 | tf_op jit(solution)/shard_map/ppermute | solution.py:19
  15.3 11.6 %collective-permute-start = (f32[4,64,256]{2,1,0:T(8,128)}, f32[4,64,256]{2,1,0:T(8,128)S(1)}, u32[]{:S(2)}, u32[]{:S(2)}) collective-permute-start(f32[4,64,256]{2,1,0:T(8,128)} %bitcast.91), channel_id=1, source_target_pairs={{0,1},{1,2},{2,3},{3,4},{4,5},{5,6},{6,7},{7,0},{8,9},{9,10},{10,1... | collective-permute-start | bytes 786440 | tf_op jit(solution)/shard_map/ppermute | solution.py:16
  15.4 0.7 copy-start.7
  16.1 0.7 copy-start.4
  17.4 2.6 %copy-start.3 = (f32[3,4,256]{2,1,0:T(4,128)S(1)}, f32[3,4,256]{2,1,0:T(4,128)}, u32[]{:S(2)}) copy-start(f32[3,4,256]{2,1,0:T(4,128)} %param.11) | copy-start | bytes 36868
  29.6 0.8 copy-start
  29.8 0.7 copy-start.2
  37.8 3.1 %copy-start.1 = (f32[1,4,64,256]{3,2,1,0:T(8,128)S(1)}, f32[1,4,64,256]{3,2,1,0:T(8,128)}, u32[]{:S(2)}) copy-start(f32[1,4,64,256]{3,2,1,0:T(8,128)} %param.9) | copy-start | bytes 786436
  38.4 2.4 %collective-permute-start.4 = (f32[4,64,256]{2,1,0:T(8,128)S(1)}, f32[4,64,256]{2,1,0:T(8,128)S(1)}, u32[]{:S(2)}, u32[]{:S(2)}) collective-permute-start(f32[4,64,256]{2,1,0:T(8,128)S(1)} %fusion.10), channel_id=1, source_target_pairs={{0,8},{8,16},{16,24},{1,9},{9,17},{17,25},{2,10},{10,18},{18,26},{... | collective-permute-start | bytes 786440 | tf_op jit(solution)/shard_map/ppermute | solution.py:27
  40.9 7.0 %collective-permute-start.6 = (f32[4,64,256]{2,1,0:T(8,128)S(1)}, f32[4,64,256]{2,1,0:T(8,128)S(1)}, u32[]{:S(2)}, u32[]{:S(2)}) collective-permute-start(f32[4,64,256]{2,1,0:T(8,128)S(1)} %broadcast_select_fusion.1), channel_id=1, source_target_pairs={{1,0},{2,1},{3,2},{4,3},{5,4},{6,5},{7,6},{0,7},{9,8},{10,9},{11,1... | collective-permute-start | bytes 786440 | tf_op jit(solution)/shard_map/ppermute | solution.py:19
  44.1 10.3 %collective-permute-start.5 = (f32[4,64,256]{2,1,0:T(8,128)S(1)}, f32[4,64,256]{2,1,0:T(8,128)S(1)}, u32[]{:S(2)}, u32[]{:S(2)}) collective-permute-start(f32[4,64,256]{2,1,0:T(8,128)S(1)} %broadcast_select_fusion.1), channel_id=1, source_target_pairs={{0,1},{1,2},{2,3},{3,4},{4,5},{5,6},{6,7},{7,0},{8,9},{9,10},{10,1... | collective-permute-start | bytes 786440 | tf_op jit(solution)/shard_map/ppermute | solution.py:16
  64.3 4.9 %collective-permute-start.7 = (f32[4,64,256]{2,1,0:T(8,128)S(1)}, f32[4,64,256]{2,1,0:T(8,128)S(1)}, u32[]{:S(2)}, u32[]{:S(2)}) collective-permute-start(f32[4,64,256]{2,1,0:T(8,128)S(1)} %fusion.9), channel_id=1, source_target_pairs={{0,8},{8,16},{16,24},{1,9},{9,17},{17,25},{2,10},{10,18},{18,26},{... | collective-permute-start | bytes 786440 | tf_op jit(solution)/shard_map/ppermute | solution.py:27
  69.2 6.6 %collective-permute-start.9 = (f32[4,64,256]{2,1,0:T(8,128)S(1)}, f32[4,64,256]{2,1,0:T(8,128)S(1)}, u32[]{:S(2)}, u32[]{:S(2)}) collective-permute-start(f32[4,64,256]{2,1,0:T(8,128)S(1)} %broadcast_select_fusion), channel_id=1, source_target_pairs={{1,0},{2,1},{3,2},{4,3},{5,4},{6,5},{7,6},{0,7},{9,8},{10,9},{11,1... | collective-permute-start | bytes 786440 | tf_op jit(solution)/shard_map/ppermute | solution.py:19
  71.9 11.2 %collective-permute-start.8 = (f32[4,64,256]{2,1,0:T(8,128)S(1)}, f32[4,64,256]{2,1,0:T(8,128)S(1)}, u32[]{:S(2)}, u32[]{:S(2)}) collective-permute-start(f32[4,64,256]{2,1,0:T(8,128)S(1)} %broadcast_select_fusion), channel_id=1, source_target_pairs={{0,1},{1,2},{2,3},{3,4},{4,5},{5,6},{6,7},{7,0},{8,9},{9,10},{10,1... | collective-permute-start | bytes 786440 | tf_op jit(solution)/shard_map/ppermute | solution.py:16
Sparse Core Ops, SparseCore 0:
  95.1 20.3 reduce-scatter.1
where the time goes:
time: 124 us
  waiting for transfers between devices  51 us (41%)
  starting transfers between devices  19.1 us (15%)
  between operations  14.7 us (12%)
  local copies, waits for them, and re-layouts  14 us (11%)
  matrix products  13.6 us (11%)
  other arithmetic  11.3 us (9%)
    reduce_scatter x1, waiting for transfers between devices, per_device(): lax.psum_scatter(accumulated, 'sec', scatter_dimension=1, tiled=True)  20.5 us
    ppermute x4, waiting for transfers between devices, padded_2(): lax.ppermute(lax.slice_in_dim(block, 0, width, axis=dim), axis, backward)  14.5 us
    ppermute x4, waiting for transfers between devices, padded_2(): lax.ppermute(lax.slice_in_dim(block, block.shape[dim] - width, None, axis...  13.7 us
    dot_general x12, matrix products, advance_padded(): jnp.einsum('uv,xvc->xuc', kernel, along_z, precision=lax.Precision.HIGHES...  13.6 us
    ppermute x4, starting transfers between devices, padded_2(): lax.ppermute(lax.slice_in_dim(block, 0, width, axis=dim), axis, backward)  11 us
    ppermute x2, starting transfers between devices, from_behind(): return lax.ppermute(array, axis, pairs)  5.05 us
    add x12, other arithmetic, advance_padded(): column(lateral_taps, 0) * jnp.roll(along_x, CZ, axis=2)  3.87 us
    slice x24, local copies, waits for them, and re-layouts, advance_padded(): jnp.roll(along_y, CZ - 1, axis=2)  3.82 us
  transfers between devices with their start and end apart: 11, of which 8 were waited for; matrix products, arithmetic and copies ran while one was open for 3% of the time, Pallas kernels for 0%

commit v1 on v0

--- a/solution.py
+++ b/solution.py
@@ -1,10 +1,19 @@
+import functools
+
 import jax
 import jax.numpy as jnp
 from jax import lax
+from jax.experimental import pallas as pl
+from jax.experimental.pallas import tpu as pltpu
 from jax.sharding import PartitionSpec as P
 
 TICKS = 3
 CZ = 64
+GROUP = 4
+FIELD_ROWS = 16
+VMEM_BYTES = 48 * 2**20
+IN_VMEM = pl.BlockSpec(memory_space=pltpu.VMEM)
+IN_SMEM = pl.BlockSpec(memory_space=pltpu.SMEM)
 
 
 def padded_2(block, sides, width):
@@ -114,6 +123,364 @@
     return (outgoing[None], density)
 
 
+def to_tile(plane, scratch):
+    half = plane.shape[1] // 2
+    scratch[...] = jnp.concatenate([plane[:, :half], plane[:, half:]], axis=0).T
+    return reorder(scratch)
+
+
+def reorder(scratch):
+    rows = scratch.shape[0]
+    return jnp.concatenate(
+        [scratch[pl.ds(yl * CZ + zl, 8, stride=8), :] for yl in range(rows // CZ) for zl in range(CZ // 8)], axis=0
+    )
+
+
+def from_tile(tile, scratch):
+    rows = tile.shape[0]
+    for yl in range(rows // CZ):
+        for zl in range(CZ // 8):
+            at = (yl * (CZ // 8) + zl) * 8
+            scratch[pl.ds(yl * CZ + zl, 8, stride=8), :] = tile[at : at + 8]
+    turned = scratch[...].T
+    half = turned.shape[0] // 2
+    return jnp.concatenate([turned[:half], turned[half:]], axis=1)
+
+
+def stencil(behind, here, ahead, taps):
+    a = here + taps[0] * behind + taps[1] * ahead
+    low, high = a[:CZ], a[CZ:]
+    low_turned = pltpu.roll(low, a.shape[1] // 2, 1)
+    high_turned = pltpu.roll(high, a.shape[1] // 2, 1)
+    out = []
+    for b in (
+        low + taps[2] * high_turned + taps[3] * high,
+        high + taps[2] * low + taps[3] * low_turned,
+    ):
+        back = jnp.concatenate([pltpu.roll(b[-8:], 1, 0), b[:-8]], axis=0)
+        front = jnp.concatenate([b[8:], pltpu.roll(b[:8], 7, 0)], axis=0)
+        out.append(b + taps[4] * back + taps[5] * front)
+    return jnp.concatenate(out, axis=0)
+
+
+def pack_kernel(info, incoming, moved_high, moved_low, fields, out, scratch):
+    sec, odd = info[0], info[1]
+    rows = scratch.shape[0]
+    pair = incoming.shape[0] // 2
+
+    def fill(source):
+        for i in range(pair):
+            out[i * rows : (i + 1) * rows] = to_tile(source[i], scratch)
+
+    pl.when(sec == 0)(lambda: fill(incoming))
+    pl.when(odd == 1)(lambda: fill(moved_high))
+    pl.when((sec > 0) & (odd == 0))(lambda: fill(moved_low))
+    out[pair * rows :] = jnp.zeros((FIELD_ROWS, rows), jnp.float32)
+    for kind in range(fields.shape[0]):
+        for i in range(pair):
+            line = fields[kind, pl.ds(pair * odd + i, 1), :]
+            at = pair * rows + (kind * pair + i) * 2
+            out[at : at + 1] = line[:, :rows]
+            out[at + 1 : at + 2] = line[:, rows:]
+
+
+def turn_kernel(stored, out, scratch):
+    for i in range(stored.shape[1]):
+        out[0, i] = to_tile(stored[0, i].astype(jnp.float32), scratch)
+
+
+def turn(stored):
+    steps, planes, orients, cells = stored.shape
+    return pl.pallas_call(
+        turn_kernel,
+        grid=(steps,),
+        in_specs=[pl.BlockSpec((1, planes, orients, cells), lambda s: (s, 0, 0, 0))],
+        out_specs=pl.BlockSpec((1, planes, 2 * orients, cells // 2), lambda s: (s, 0, 0, 0)),
+        out_shape=jax.ShapeDtypeStruct((steps, planes, 2 * orients, cells // 2), jnp.float32),
+        scratch_shapes=[pltpu.VMEM((2 * orients, cells // 2), jnp.float32)],
+        compiler_params=pltpu.CompilerParams(vmem_limit_bytes=VMEM_BYTES),
+    )(stored)
+
+
+def places(odd, pair, reach):
+    width = 2 * pair
+    far = reach - width
+    starts = []
+    for core in (odd, 1 - odd):
+        starts += [
+            reach + pair * core,
+            far + pair * core,
+            reach + width + pair * core,
+            jnp.where(core == 0, reach + 2 * width, 0),
+        ]
+    return starts
+
+
+def run_steps(info, taps, weights, kinds_at, count, slab, other, first, second, factor, after):
+    tap = [taps[i : i + 1, :] for i in range(6)]
+    extent, rows, lanes = slab.shape
+    buffers = (slab, other)
+
+    def blend(source, at, packed):
+        for i in range(GROUP):
+            e = stencil(source[at + i - 1], source[at + i], source[at + i + 1], tap)
+            coarse = e.astype(jnp.bfloat16)
+            packed[i * rows : (i + 1) * rows, :lanes] = coarse
+            packed[i * rows : (i + 1) * rows, lanes:] = (e - coarse.astype(jnp.float32)).astype(jnp.bfloat16)
+
+    def mix(target, at, packed, kind):
+        product = jnp.dot(packed[...], weights[...], preferred_element_type=jnp.float32)
+        product = product[:, :lanes] + product[:, lanes:]
+        for i in range(GROUP):
+            target[at + i] = product[i * rows : (i + 1) * rows] * factor[kind, at + i]
+
+    for step in range(count):
+        source, target = buffers[step % 2], buffers[1 - step % 2]
+        begin, width = step + 1, extent - 2 * step - 2
+        groups = -(-width // GROUP)
+        kind = info[kinds_at + step]
+
+        def at(i, begin=begin, width=width):
+            return jnp.minimum(begin + i * GROUP, begin + width - GROUP)
+
+        blend(source, at(0), first)
+        if groups > 1:
+
+            def body(i, carry, source=source, target=target, at=at, kind=kind):
+                blend(source, at(2 * i + 1), second)
+                mix(target, at(2 * i), first, kind)
+                blend(source, at(2 * i + 2), first)
+                mix(target, at(2 * i + 1), second, kind)
+                return carry
+
+            lax.fori_loop(0, (groups - 1) // 2, body, 0)
+        if groups % 2 == 0:
+            blend(source, at(groups - 1), second)
+            mix(target, at(groups - 2), first, kind)
+            mix(target, at(groups - 1), second, kind)
+        else:
+            mix(target, at(groups - 1), first, kind)
+        after(step, target)
+
+
+def spread_factor(columns, factor, starts, kinds, pair):
+    rows, lanes = factor.shape[2:]
+    left = lax.broadcasted_iota(jnp.int32, (rows, lanes), 1) < lanes // 2
+    for piece, start in enumerate(starts):
+        for kind in range(kinds):
+            for i in range(pair):
+                at = piece * FIELD_ROWS + (kind * pair + i) * 2
+                factor[kind, start + i] = jnp.where(left, columns[:, at : at + 1], columns[:, at + 1 : at + 2])
+
+
+def early_kernel(half, kinds, info, taps, weights, *refs):
+    pieces, (stored, next_stored) = refs[:8], refs[8:10]
+    middle, half_out, kept, total, columns = refs[10:15]
+    slab, other, first, second, factor, scratch = refs[15:]
+    sec, odd = info[0], info[1]
+    planes, rows = middle.shape[:2]
+    pair = planes // 2
+    starts = places(odd, pair, half)
+    for piece, start in zip(pieces, starts):
+        for i in range(pair):
+            slab[start + i] = piece[i * rows : (i + 1) * rows]
+    scratch[...] = jnp.exp(-jnp.concatenate([piece[pair * rows :] for piece in pieces], axis=0)).T
+    columns[...] = reorder(scratch)
+    spread_factor(columns, factor, starts, kinds, pair)
+    steps = stored.shape[0]
+    total[...] = jnp.zeros(total.shape, jnp.float32)
+
+    def after(step, state):
+        @pl.when(sec == 0)
+        def _():
+            source = stored if step < steps else next_stored
+            total[...] += state[half : half + planes] * source[step % steps]
+            if step + 1 == steps:
+                kept[...] = state[half : half + planes]
+
+    run_steps(info, taps, weights, 2, half, slab, other, first, second, factor, after)
+    state = (slab, other)[half % 2]
+    middle[...] = state[half : half + planes]
+    half_out[...] = state[pl.ds(half + pair * odd, pair)]
+
+
+def late_kernel(half, kinds, last, info, taps, weights, *refs):
+    middle, pieces, columns = refs[0], refs[1:7], refs[7]
+    kept, total_in, stored, next_stored, last_stored = refs[8:13]
+    handoff, share, to_pair, to_across, to_corner = refs[13:18]
+    slab, other, first, second, factor, scratch, total, saved, whole = refs[18:]
+    sec, odd = info[0], info[1]
+    planes, rows = middle.shape[:2]
+    pair = planes // 2
+    starts = places(odd, pair, half)
+    slab[half : half + planes] = middle[...]
+    for piece, start in zip(pieces, starts[1:4] + starts[5:8]):
+        for i in range(pair):
+            slab[start + i] = piece[i]
+    spread_factor(columns, factor, starts, kinds, pair)
+    steps = stored.shape[0]
+    total[...] = total_in[...]
+    saved[...] = kept[...]
+
+    def after(step, state):
+        step = step + half
+
+        @pl.when(sec == 0)
+        def _():
+            source = next_stored if step < 2 * steps else last_stored
+            total[...] += state[half : half + planes] * source[step % steps]
+
+        if step + 1 == 2 * steps:
+
+            @pl.when(sec == 1)
+            def _():
+                saved[...] = state[half : half + planes]
+
+        if step >= 2 * steps:
+
+            @pl.when(sec == last)
+            def _():
+                total[...] += state[half : half + planes] * stored[step % steps]
+
+    run_steps(info, taps, weights, 2 + half, half, slab, other, first, second, factor, after)
+    state = (slab, other)[half % 2]
+
+    @pl.when(sec == last)
+    def _():
+        saved[...] = state[half : half + planes]
+
+    orients = handoff.shape[1]
+    count = orients // (last + 1)
+    held = planes * count
+    to_corner[...] = jnp.zeros(to_corner.shape, jnp.float32)
+    for i in range(planes):
+        handoff[i] = from_tile(saved[i], scratch)
+        whole[...] = from_tile(total[i], scratch)
+        for piece, who in (
+            (share, sec),
+            (to_pair, sec + 1 - 2 * odd),
+            (to_across, jnp.where(sec == 0, 2, 1)),
+            (to_corner, last - sec),
+        ):
+            piece[i * count : (i + 1) * count] = whole[pl.ds(pl.multiple_of(who * count, count), count)]
+    for i in range(pair):
+        to_across[held + i * orients : held + (i + 1) * orients] = from_tile(state[half + pair * odd + i], scratch)
+
+    @pl.when(sec == 1)
+    def _():
+        to_corner[...] = to_across[held:]
+
+
+def call(kernel, out_shape, scratch, operands):
+    return pl.pallas_call(
+        kernel,
+        in_specs=[IN_SMEM] + [IN_VMEM] * (len(operands) - 1),
+        out_specs=[IN_VMEM] * len(out_shape),
+        out_shape=[jax.ShapeDtypeStruct(shape, jnp.float32) for shape in out_shape],
+        scratch_shapes=scratch,
+        compiler_params=pltpu.CompilerParams(vmem_limit_bytes=VMEM_BYTES),
+    )(*operands)
+
+
+def tables(axial_taps, lateral_taps, depth_taps, bend_diagonal, bend_coupling):
+    kernel = jnp.diag(bend_diagonal) + bend_coupling
+    kernel = (kernel * (axial_taps[1] * lateral_taps[1] * depth_taps[1])[None, :]).T
+    ratios = [each[which] / each[1] for each in (axial_taps, lateral_taps, depth_taps) for which in (0, 2)]
+    taps = jnp.tile(jnp.stack(ratios + ratios[:2]), (1, 2))
+    coarse = lax.reduce_precision(kernel, 8, 7)
+    twice = jnp.eye(2, dtype=jnp.float32)
+    coarse, fine = jnp.kron(twice, coarse), jnp.kron(twice, kernel - coarse)
+    weights = jnp.block([[coarse, fine], [coarse, jnp.zeros_like(fine)]])
+    return taps, weights.astype(jnp.bfloat16)
+
+
+def paired(incoming, backward, fields, block_types, axial_taps, lateral_taps, depth_taps, bend_diagonal, bend_coupling):
+    n_sec, n_gx = lax.axis_size("sec"), lax.axis_size("gx")
+    steps, planes, orients, cells = backward.shape
+    pair = planes // 2
+    half = TICKS * steps // 2
+    rows = 2 * orients
+    lanes = cells // 2
+    sec = lax.axis_index("sec")
+    odd = sec % 2
+    last = n_sec - 1
+
+    def send(array, by_sec, shift=lambda s: 0):
+        pairs = [
+            (s * n_gx + g, t * n_gx + (g + shift(s)) % n_gx) for s, t in enumerate(by_sec) for g in range(n_gx)
+        ]
+        return lax.ppermute(array, ("sec", "gx"), pairs)
+
+    same, beside = (0, 1, 2, 3), (1, 0, 3, 2)
+    whole = incoming[0]
+    moved_high = send(whole[pair:], (1, 3, 0, 2))
+    moved_low = send(whole[:pair], (0, 2, 1, 3))
+    taps, weights = tables(axial_taps, lateral_taps, depth_taps, bend_diagonal, bend_coupling)
+    kinds = lax.all_gather(block_types[0], "sec")
+    kinds = lax.dynamic_slice(kinds, (sec // 2, 0), (TICKS, steps)).reshape(-1)
+    place = jnp.stack([sec, odd]).astype(jnp.int32)
+    info = jnp.concatenate([place, kinds])
+    stored = turn(backward)
+    next_stored = send(stored, beside)
+    last_stored = send(stored, (2, 3, 0, 1))
+
+    tile = pltpu.VMEM((rows, lanes), jnp.float32)
+    slab = pltpu.VMEM((planes + 2 * half, rows, lanes), jnp.float32)
+    packed = pltpu.VMEM((GROUP * rows, 2 * lanes), jnp.bfloat16)
+    factor = pltpu.VMEM((fields.shape[0], planes + 2 * half, rows, lanes), jnp.float32)
+    inner = pltpu.VMEM((planes, rows, lanes), jnp.float32)
+    work = [slab, slab, packed, packed, factor, tile]
+
+    def exchange(piece):
+        own = [
+            send(piece, same, lambda s: 1),
+            send(piece, same, lambda s: -1),
+            send(piece, same, lambda s: -2 if s % 2 == 0 else 2),
+        ]
+        return own, [send(each, beside) for each in own]
+
+    (piece,) = call(
+        pack_kernel, [(pair * rows + FIELD_ROWS, lanes)], [tile], [place, whole, moved_high, moved_low, fields]
+    )
+    own, swapped = exchange(piece)
+    middle, piece, kept, total, columns = call(
+        functools.partial(early_kernel, half, fields.shape[0]),
+        [(planes, rows, lanes), (pair, rows, lanes), (planes, rows, lanes), (planes, rows, lanes), (rows, lanes)],
+        work,
+        [info, taps, weights, piece, *own, send(piece, beside), *swapped, stored, next_stored],
+    )
+    own, swapped = exchange(piece)
+    held = planes * (orients // n_sec)
+    handoff, share, to_pair, to_across, to_corner = call(
+        functools.partial(late_kernel, half, fields.shape[0], last),
+        [(planes, orients, cells)]
+        + [(held, cells)] * 2
+        + [(held + pair * orients, cells), (pair * orients, cells)],
+        work + [inner, inner, pltpu.VMEM((orients, cells), jnp.float32)],
+        [info, taps, weights, middle, *own, *swapped, columns, kept, total, stored, next_stored, last_stored],
+    )
+    to_pair = send(to_pair, beside)
+    to_across = send(to_across, (2, 0, 3, 1))
+    to_corner = send(to_corner, (3, 2, 1, 0))
+    third = sec == 2
+    density = share + to_pair + to_across[:held] + jnp.where(third, 0.0, to_corner[:held])
+    arrived = jnp.concatenate([to_across[held:], to_corner]).reshape(handoff.shape)
+    handoff = jnp.where(third, arrived, handoff)
+    return handoff[None], density.reshape(planes, -1, cells) / (n_sec * steps)
+
+
+def pairs_fit(n_sec, planes, steps, orients, cells, kinds):
+    return (
+        n_sec == TICKS + 1 == 4
+        and planes == steps
+        and planes % 2 == 0
+        and TICKS * steps == 2 * (planes + planes // 2)
+        and 2 * orients == 2 * CZ == cells // 2 == 128
+        and kinds * planes <= FIELD_ROWS
+        and planes >= GROUP
+    )
+
+
 def solution(mesh):
     in_specs = (
         P("sec", "gx", None, None),
@@ -127,6 +494,10 @@
         P(),
     )
     out_specs = (P("sec", "gx", None, None), P("gx", "sec", None))
-    return jax.shard_map(
-        per_device, mesh=mesh, in_specs=in_specs, out_specs=out_specs, check_vma=False
-    )
+
+    def body(incoming, backward, fields, *rest):
+        steps, planes, orients, cells = backward.shape
+        fits = pairs_fit(mesh.shape["sec"], planes, steps, orients, cells, fields.shape[0])
+        return (paired if fits else per_device)(incoming, backward, fields, *rest)
+
+    return jax.shard_map(body, mesh=mesh, in_specs=in_specs, out_specs=out_specs, check_vma=False)

time: 124 us -> 95.6 us (0.77)
  Pallas kernels: 0 us -> 15.7 us
  between operations: 14.7 us -> 0.84 us
  matrix products: 13.6 us -> 0 us
  waiting for transfers between devices: 51 us -> 42.4 us
  other arithmetic: 11.3 us -> 4.63 us
  blocking collectives: 0 us -> 5.03 us
  local copies, waits for them, and re-layouts: 14 us -> 9.39 us
  starting transfers between devices: 19.1 us -> 17 us
    reduce_scatter x1 -> x0, waiting for transfers between devices: 20.5 us -> none  [per_device(): lax.psum_scatter(accumulated, 'sec', scatter_dimension=1, tiled=True)]
    pallas_call x0 -> x4, Pallas kernels: none -> 15.7 us  [the longest x3 15.1 us: call(): pl.pallas_call(kernel, in_specs=[IN_SMEM] + [IN_VMEM] * (len(operands) -...]
    dot_general x12 -> x0, matrix products: 13.6 us -> none  [advance_padded(): jnp.einsum('uv,xvc->xuc', kernel, along_z, precision=lax.Precision.HIGHES...]
    ppermute x10 -> x20, waiting for transfers between devices: 30.5 us -> 42.4 us  [send(): return lax.ppermute(array, ('sec', 'gx'), pairs)]
    slice x73 -> x2, local copies, waits for them, and re-layouts: 12 us -> 0.71 us  [the longest x1 0.7 us: paired(): moved_low = send(whole[:pair], (0, 2, 1, 3))]
    add x24 -> x0, other arithmetic: 5.89 us -> none  [the longest x12 3.87 us: advance_padded(): column(lateral_taps, 0) * jnp.roll(along_x, CZ, axis=2)]
    all_gather x0 -> x1, blocking collectives: none -> 5.03 us  [paired(): kinds = lax.all_gather(block_types[0], 'sec')]
    unnamed x16 -> x40, local copies, waits for them, and re-layouts: 1.99 us -> 6.02 us
  transfers between devices with their start and end apart: 11 -> 20, of which waited for: 8 -> 9; matrix products, arithmetic and copies ran while one was open for 3% -> 8% of each run, Pallas kernels for 0% -> 8%
where the time goes in v1:
time: 95.6 us; the launch traced here: 95.1 us
  waiting for transfers between devices  42.4 us (44%)
  starting transfers between devices  17 us (18%)
  Pallas kernels  15.7 us (16%)
  local copies, waits for them, and re-layouts  9.39 us (10%)
  blocking collectives  5.03 us (5%)
  other arithmetic  4.63 us (5%)
    ppermute x20, waiting for transfers between devices, send(): return lax.ppermute(array, ('sec', 'gx'), pairs)  42.4 us
    ppermute x20, starting transfers between devices, send(): return lax.ppermute(array, ('sec', 'gx'), pairs)  17 us
    pallas_call x3, Pallas kernels, call(): pl.pallas_call(kernel, in_specs=[IN_SMEM] + [IN_VMEM] * (len(operands) -...  15.1 us
    unnamed x40, local copies, waits for them, and re-layouts  6.02 us
    all_gather x1, blocking collectives, paired(): kinds = lax.all_gather(block_types[0], 'sec')  5.03 us
  transfers between devices with their start and end apart: 20, of which 9 were waited for; matrix products, arithmetic and copies ran while one was open for 8% of the time, Pallas kernels for 8%

profile of v1, /device:TPU:0, one launch (start us, length us, event | category | flops | bytes accessed | tf_op | source)
XLA Modules:
  0.0 95.1 jit_solution(7548255333856224402)
XLA Ops:
  0.6 1.1 %copy-done.1 = bf16[4,4,64,256]{3,2,1,0:T(8,128)(2,1)S(1)} copy-done((bf16[4,4,64,256]{3,2,1,0:T(8,128)(2,1)S(1)}, bf16[4,4,64,256]{3,2,1,0:T(8,128)(2,1)}, u32[]{:S(2)}) %copy-start.1) | copy-done | bytes 524312
  1.7 0.7 shard_map.105.refs_8_.refs_10_
  2.4 3.0 %collective-permute-start.16 = (f32[4,4,128,128]{3,2,1,0:T(8,128)S(1)}, f32[4,4,128,128]{3,2,1,0:T(8,128)S(1)}, u32[]{:S(2)}, u32[]{:S(2)}) collective-permute-start(f32[4,4,128,128]{3,2,1,0:T(8,128)S(1)} %shard_map.105.refs_8_.refs_10_), channel_id=1, source_target_pairs={{0,16},{1,17},{2,18},{3,19},{4,20},{5,21},{6,22},{7,23},{8,24},{9,... | collective-permute-start | bytes 3145736 | tf_op jit(solution)/shard_map/ppermute | solution.py:412
  5.4 0.0 collective-permute-start.9
  5.4 0.7 slice_bitcast_fusion
  6.1 1.7 %collective-permute-start.1 = (f32[2,64,256]{2,1,0:T(8,128)}, f32[2,64,256]{2,1,0:T(8,128)S(1)}, u32[]{:S(2)}, u32[]{:S(2)}) collective-permute-start(f32[2,64,256]{2,1,0:T(8,128)} %get-tuple-element.22), channel_id=1, source_target_pairs={{0,0},{1,1},{2,2},{3,3},{4,4},{5,5},{6,6},{7,7},{8,16},{9,17},{10,... | collective-permute-start | bytes 393224 | tf_op jit(solution)/shard_map/ppermute | solution.py:412
  7.8 0.9 collective-permute-start
  8.7 0.6 multiply_bitcast_fusion
  9.3 0.1 pad_add_fusion.1.info
  9.4 0.7 copy-done.6
  10.1 21.4 %collective-permute-done.moved_high = f32[2,64,256]{2,1,0:T(8,128)} collective-permute-done((f32[2,64,256]{2,1,0:T(8,128)}, f32[2,64,256]{2,1,0:T(8,128)}, u32[]{:S(2)}, u32[]{:S(2)}) %collective-permute-start) | collective-permute-done | bytes 131104 | tf_op jit(solution)/shard_map/ppermute | solution.py:412
  31.5 0.9 copy-done.7
  32.4 0.7 copy-done.8
  33.1 1.1 %shard_map.104.refs_0_ = f32[272,128]{1,0:T(8,128)S(1)} custom-call(s32[2]{0:T(128)S(1)} %pad_add_fusion.1.info, f32[4,64,256]{2,1,0:T(8,128)S(1)} %bitcast.19, f32[2,64,256]{2,1,0:T(8,128)} %collective-permute-done.moved_high, f32[2,64,256]{2,1,0:T(8,128)S(1)} %copy-done.7, f32[3,4,256]{2,1,0:T(4,128)S(1)} %copy-done.8), custom_call_target="tpu_custom_call" | custom-call | tf_op jit(solution)/shard_map/pallas_call | solution.py:375
  34.2 0.0 copy-start.10
  34.2 0.0 copy-start.18
  34.2 0.1 collective-permute-start.5
  34.3 0.5 copy-done.10
  34.8 0.0 copy-done.18
  34.8 0.1 bitcast_subtract_fusion
  34.9 0.0 copy-start.19
  34.9 0.6 copy-done.19
  35.6 5.0 %all-gather = s32[4,1,4]{2,1,0:T(1,128)S(1)} all-gather(s32[1,1,4]{2,1,0:T(1,128)S(1)} %bitcast.22), channel_id=1, replica_groups=mesh['sec'=4,'gx'=8] {'sec'}, dimensions={0}, use_global_device_ids=true | all-gather | bytes 80 | tf_op jit(solution)/shard_map/all_gather | solution.py:419
  40.6 0.1 reshape.40
  40.7 0.1 copy.14
  40.8 0.7 copy.13
  41.5 3.8 %collective-permute-start.4 = (f32[272,128]{1,0:T(8,128)S(1)}, f32[272,128]{1,0:T(8,128)}, u32[]{:S(2)}, u32[]{:S(2)}) collective-permute-start(f32[272,128]{1,0:T(8,128)S(1)} %shard_map.104.refs_0_), channel_id=1, source_target_pairs={{0,6},{1,7},{2,0},{3,1},{4,2},{5,3},{6,4},{7,5},{8,10},{9,11},{10,... | collective-permute-start | bytes 417800 | tf_op jit(solution)/shard_map/ppermute | solution.py:412
  45.3 1.4 %collective-permute-start.3 = (f32[272,128]{1,0:T(8,128)S(1)}, f32[272,128]{1,0:T(8,128)}, u32[]{:S(2)}, u32[]{:S(2)}) collective-permute-start(f32[272,128]{1,0:T(8,128)S(1)} %shard_map.104.refs_0_), channel_id=1, source_target_pairs={{0,7},{1,0},{2,1},{3,2},{4,3},{5,4},{6,5},{7,6},{8,15},{9,8},{10,9... | collective-permute-start | bytes 417800 | tf_op jit(solution)/shard_map/ppermute | solution.py:412
  46.7 0.0 collective-permute-done.5.refs_4_
  46.7 0.6 collective-permute-start.2
  47.4 1.5 %multiply_convert_fusion = (bf16[2,64,2,64]{3,2,1,0:T(2,128)(2,1)}, bf16[2,64,2,64]{3,2,1,0:T(2,128)(2,1)S(1)}) fusion(f32[64,64]{1,0:T(8,128)S(1)} %copy.14, f32[2,2]{1,0:T(2,128)S(1)} %compare_convert_fusion, f32[64,64]{1,0:T(8,128)} %copy.13), kind=kLoop, calls=%fused_computation.7 | loop fusion | flops 65536 | bytes 98320 | tf_op jit(solution)/shard_map/convert.6
  48.9 0.2 collective-permute-done.4.refs_3_
  49.1 1.8 %collective-permute-done.3.refs_2_ = f32[272,128]{1,0:T(8,128)} collective-permute-done((f32[272,128]{1,0:T(8,128)S(1)}, f32[272,128]{1,0:T(8,128)}, u32[]{:S(2)}, u32[]{:S(2)}) %collective-permute-start.3) | collective-permute-done | bytes 139296 | tf_op jit(solution)/shard_map/ppermute | solution.py:412
  50.9 0.0 collective-permute-start.7
  50.9 3.8 %collective-permute-done.2.refs_1_ = f32[272,128]{1,0:T(8,128)} collective-permute-done((f32[272,128]{1,0:T(8,128)S(1)}, f32[272,128]{1,0:T(8,128)}, u32[]{:S(2)}, u32[]{:S(2)}) %collective-permute-start.2) | collective-permute-done | bytes 139296 | tf_op jit(solution)/shard_map/ppermute | solution.py:412
  54.7 0.0 collective-permute-start.6
  54.7 0.1 pad_add_fusion.info
  54.8 0.7 copy-done.11
  55.4 0.0 copy-done.13
  55.5 0.1 tile.10.taps
  55.6 0.9 mul.70
  56.5 0.7 reshape.42
  57.2 0.8 fusion.1.weights
  58.1 0.0 collective-permute-done.8.refs_7_
  58.1 0.0 copy-done.5
  58.2 6.9 %shard_map.106 = (f32[4,128,128]{2,1,0:T(8,128)S(1)}, f32[2,128,128]{2,1,0:T(8,128)S(1)}, f32[4,128,128]{2,1,0:T(8,128)S(1)}, f32[4,128,128]{2,1,0:T(8,128)S(1)}, f32[128,128]{1,0:T(8,128)S(1)}) custom-call(s32[14]{0:T(128)S(1)} %pad_add_fusion.info, f32[8,128]{1,0:T(8,128)S(1)} %tile.10.taps, bf16[256,256]{1,0:T(8,128)(2,1)S(1)} %fusion.1.weights, ...), custom_call_target="tpu_custom_call" | custom-call | tf_op jit(solution)/shard_map/pallas_call | solution.py:375
  65.1 1.5 %collective-permute-start.12 = (f32[2,128,128]{2,1,0:T(8,128)S(1)}, f32[2,128,128]{2,1,0:T(8,128)S(1)}, u32[]{:S(2)}, u32[]{:S(2)}) collective-permute-start(f32[2,128,128]{2,1,0:T(8,128)S(1)} %get-tuple-element.13), channel_id=1, source_target_pairs={{0,6},{1,7},{2,0},{3,1},{4,2},{5,3},{6,4},{7,5},{8,10},{9,11},{10,... | collective-permute-start | bytes 393224 | tf_op jit(solution)/shard_map/ppermute | solution.py:412
  66.6 1.1 %collective-permute-start.11 = (f32[2,128,128]{2,1,0:T(8,128)S(1)}, f32[2,128,128]{2,1,0:T(8,128)S(1)}, u32[]{:S(2)}, u32[]{:S(2)}) collective-permute-start(f32[2,128,128]{2,1,0:T(8,128)S(1)} %get-tuple-element.13), channel_id=1, source_target_pairs={{0,7},{1,0},{2,1},{3,2},{4,3},{5,4},{6,5},{7,6},{8,15},{9,8},{10,9... | collective-permute-start | bytes 393224 | tf_op jit(solution)/shard_map/ppermute | solution.py:412
  67.7 0.9 collective-permute-start.10
  68.6 3.6 %collective-permute-done.12.refs_3_ = f32[2,128,128]{2,1,0:T(8,128)S(1)} collective-permute-done((f32[2,128,128]{2,1,0:T(8,128)S(1)}, f32[2,128,128]{2,1,0:T(8,128)S(1)}, u32[]{:S(2)}, u32[]{:S(2)}) %collective-permute-start.12) | collective-permute-done | bytes 131104 | tf_op jit(solution)/shard_map/ppermute | solution.py:412
  72.2 0.3 collective-permute-start.15
  72.5 0.2 collective-permute-start.14
  72.7 4.0 %collective-permute-done.10.refs_1_ = f32[2,128,128]{2,1,0:T(8,128)S(1)} collective-permute-done((f32[2,128,128]{2,1,0:T(8,128)S(1)}, f32[2,128,128]{2,1,0:T(8,128)S(1)}, u32[]{:S(2)}, u32[]{:S(2)}) %collective-permute-start.10) | collective-permute-done | bytes 131104 | tf_op jit(solution)/shard_map/ppermute | solution.py:412
  76.7 0.1 collective-permute-start.13
  76.9 1.2 %collective-permute-done.13.refs_4_ = f32[2,128,128]{2,1,0:T(8,128)S(1)} collective-permute-done((f32[2,128,128]{2,1,0:T(8,128)S(1)}, f32[2,128,128]{2,1,0:T(8,128)S(1)}, u32[]{:S(2)}, u32[]{:S(2)}) %collective-permute-start.13) | collective-permute-done | bytes 131104 | tf_op jit(solution)/shard_map/ppermute | solution.py:412
  78.1 7.1 %shard_map.107 = (f32[4,64,256]{2,1,0:T(8,128)S(1)}, f32[64,256]{1,0:T(8,128)S(1)}, f32[64,256]{1,0:T(8,128)S(1)}, f32[192,256]{1,0:T(8,128)}, f32[128,256]{1,0:T(8,128)}) custom-call(s32[14]{0:T(128)S(1)} %pad_add_fusion.info, f32[8,128]{1,0:T(8,128)S(1)} %tile.10.taps, bf16[256,256]{1,0:T(8,128)(2,1)S(1)} %fusion.1.weights, ...), custom_call_target="tpu_custom_call" | custom-call | tf_op jit(solution)/shard_map/pallas_call | solution.py:375
  85.2 0.7 copy-done.2
  85.9 0.3 collective-permute-start.17
  86.2 1.1 %collective-permute-start.18 = (f32[128,256]{1,0:T(8,128)}, f32[128,256]{1,0:T(8,128)S(1)}, u32[]{:S(2)}, u32[]{:S(2)}) collective-permute-start(f32[128,256]{1,0:T(8,128)} %get-tuple-element.18), channel_id=1, source_target_pairs={{0,24},{1,25},{2,26},{3,27},{4,28},{5,29},{6,30},{7,31},{8,16},{9,... | collective-permute-start | bytes 393224 | tf_op jit(solution)/shard_map/ppermute | solution.py:412
  87.3 3.5 %collective-permute-done.17 = f32[192,256]{1,0:T(8,128)S(1)} collective-permute-done((f32[192,256]{1,0:T(8,128)}, f32[192,256]{1,0:T(8,128)S(1)}, u32[]{:S(2)}, u32[]{:S(2)}) %collective-permute-start.17) | collective-permute-done | bytes 196640 | tf_op jit(solution)/shard_map/ppermute | solution.py:412
  90.9 0.0 copy-start.3
  90.9 2.8 %collective-permute-done.18 = f32[128,256]{1,0:T(8,128)S(1)} collective-permute-done((f32[128,256]{1,0:T(8,128)}, f32[128,256]{1,0:T(8,128)S(1)}, u32[]{:S(2)}, u32[]{:S(2)}) %collective-permute-start.18) | collective-permute-done | bytes 131104 | tf_op jit(solution)/shard_map/ppermute | solution.py:412
  93.7 0.7 select_bitcast_fusion
  94.5 0.6 fusion.3
  (42 shorter events, 0.2 us)
Async XLA Ops:
  0.6 4.8 %copy-start = (f32[1,4,64,256]{3,2,1,0:T(8,128)S(1)}, f32[1,4,64,256]{3,2,1,0:T(8,128)}, u32[]{:S(2)}) copy-start(f32[1,4,64,256]{3,2,1,0:T(8,128)} %param.9) | copy-start | bytes 786436
  0.6 1.1 %copy-start.1 = (bf16[4,4,64,256]{3,2,1,0:T(8,128)(2,1)S(1)}, bf16[4,4,64,256]{3,2,1,0:T(8,128)(2,1)}, u32[]{:S(2)}) copy-start(bf16[4,4,64,256]{3,2,1,0:T(8,128)(2,1)} %stored.1) | copy-start | bytes 1572868
  2.4 74.5 %collective-permute-start.16 = (f32[4,4,128,128]{3,2,1,0:T(8,128)S(1)}, f32[4,4,128,128]{3,2,1,0:T(8,128)S(1)}, u32[]{:S(2)}, u32[]{:S(2)}) collective-permute-start(f32[4,4,128,128]{3,2,1,0:T(8,128)S(1)} %shard_map.105.refs_8_.refs_10_), channel_id=1, source_target_pairs={{0,16},{1,17},{2,18},{3,19},{4,20},{5,21},{6,22},{7,23},{8,24},{9,... | collective-permute-start | bytes 3145736 | tf_op jit(solution)/shard_map/ppermute | solution.py:412
  5.4 52.7 %collective-permute-start.9 = (f32[4,4,128,128]{3,2,1,0:T(8,128)S(1)}, f32[4,4,128,128]{3,2,1,0:T(8,128)S(1)}, u32[]{:S(2)}, u32[]{:S(2)}) collective-permute-start(f32[4,4,128,128]{3,2,1,0:T(8,128)S(1)} %shard_map.105.refs_8_.refs_10_), channel_id=1, source_target_pairs={{0,8},{1,9},{2,10},{3,11},{4,12},{5,13},{6,14},{7,15},{8,0},{9,1},... | collective-permute-start | bytes 3145736 | tf_op jit(solution)/shard_map/ppermute | solution.py:412
  5.4 3.3 %copy-start.16 = (f32[3,64]{1,0:T(4,128)S(1)}, f32[3,64]{1,0:T(4,128)}, u32[]{:S(2)}) copy-start(f32[3,64]{1,0:T(4,128)} %param.14) | copy-start | bytes 2308
  5.4 3.3 %copy-start.17 = (f32[3,64]{1,0:T(4,128)S(1)}, f32[3,64]{1,0:T(4,128)}, u32[]{:S(2)}) copy-start(f32[3,64]{1,0:T(4,128)} %param.13) | copy-start | bytes 2308
  6.1 2.6 %copy-start.15 = (f32[3,64]{1,0:T(4,128)S(1)}, f32[3,64]{1,0:T(4,128)}, u32[]{:S(2)}) copy-start(f32[3,64]{1,0:T(4,128)} %param.15) | copy-start | bytes 2308
  6.1 3.3 %collective-permute-start.1 = (f32[2,64,256]{2,1,0:T(8,128)}, f32[2,64,256]{2,1,0:T(8,128)S(1)}, u32[]{:S(2)}, u32[]{:S(2)}) collective-permute-start(f32[2,64,256]{2,1,0:T(8,128)} %get-tuple-element.22), channel_id=1, source_target_pairs={{0,0},{1,1},{2,2},{3,3},{4,4},{5,5},{6,6},{7,7},{8,16},{9,17},{10,... | collective-permute-start | bytes 393224 | tf_op jit(solution)/shard_map/ppermute | solution.py:412
  7.8 23.7 %collective-permute-start = (f32[2,64,256]{2,1,0:T(8,128)}, f32[2,64,256]{2,1,0:T(8,128)}, u32[]{:S(2)}, u32[]{:S(2)}) collective-permute-start(f32[2,64,256]{2,1,0:T(8,128)} %get-tuple-element.23), channel_id=1, source_target_pairs={{0,8},{1,9},{2,10},{3,11},{4,12},{5,13},{6,14},{7,15},{8,24},{9,25... | collective-permute-start | bytes 393224 | tf_op jit(solution)/shard_map/ppermute | solution.py:412
  9.4 0.7 copy-start.6
  31.5 0.9 copy-start.7
  32.4 0.7 copy-start.8
  33.1 1.2 %copy-start.9 = (f32[64,64]{1,0:T(8,128)S(1)}, f32[64,64]{1,0:T(8,128)}, u32[]{:S(2)}) copy-start(f32[64,64]{1,0:T(8,128)} %param.17) | copy-start | bytes 49156
  34.2 0.7 copy-start.10
  34.2 0.7 copy-start.18
  34.2 12.5 %collective-permute-start.5 = (f32[272,128]{1,0:T(8,128)S(1)}, f32[272,128]{1,0:T(8,128)S(1)}, u32[]{:S(2)}, u32[]{:S(2)}) collective-permute-start(f32[272,128]{1,0:T(8,128)S(1)} %shard_map.104.refs_0_), channel_id=1, source_target_pairs={{0,8},{1,9},{2,10},{3,11},{4,12},{5,13},{6,14},{7,15},{8,0},{9,1},... | collective-permute-start | bytes 417800 | tf_op jit(solution)/shard_map/ppermute | solution.py:412
  34.9 0.7 copy-start.19
  41.5 7.6 %collective-permute-start.4 = (f32[272,128]{1,0:T(8,128)S(1)}, f32[272,128]{1,0:T(8,128)}, u32[]{:S(2)}, u32[]{:S(2)}) collective-permute-start(f32[272,128]{1,0:T(8,128)S(1)} %shard_map.104.refs_0_), channel_id=1, source_target_pairs={{0,6},{1,7},{2,0},{3,1},{4,2},{5,3},{6,4},{7,5},{8,10},{9,11},{10,... | collective-permute-start | bytes 417800 | tf_op jit(solution)/shard_map/ppermute | solution.py:412
  45.3 5.6 %collective-permute-start.3 = (f32[272,128]{1,0:T(8,128)S(1)}, f32[272,128]{1,0:T(8,128)}, u32[]{:S(2)}, u32[]{:S(2)}) collective-permute-start(f32[272,128]{1,0:T(8,128)S(1)} %shard_map.104.refs_0_), channel_id=1, source_target_pairs={{0,7},{1,0},{2,1},{3,2},{4,3},{5,4},{6,5},{7,6},{8,15},{9,8},{10,9... | collective-permute-start | bytes 417800 | tf_op jit(solution)/shard_map/ppermute | solution.py:412
  46.7 9.8 %copy-start.4 = (f32[272,128]{1,0:T(8,128)}, f32[272,128]{1,0:T(8,128)S(1)}, u32[]{:S(2)}) copy-start(f32[272,128]{1,0:T(8,128)S(1)} %collective-permute-done.5.refs_4_) | copy-start | bytes 417796
  46.7 8.0 %collective-permute-start.2 = (f32[272,128]{1,0:T(8,128)S(1)}, f32[272,128]{1,0:T(8,128)}, u32[]{:S(2)}, u32[]{:S(2)}) collective-permute-start(f32[272,128]{1,0:T(8,128)S(1)} %shard_map.104.refs_0_), channel_id=1, source_target_pairs={{0,1},{1,2},{2,3},{3,4},{4,5},{5,6},{6,7},{7,0},{8,9},{9,10},{10,1... | collective-permute-start | bytes 417800 | tf_op jit(solution)/shard_map/ppermute | solution.py:412
  47.4 7.4 %copy-start.14 = (f32[1,64]{1,0:T(1,128)S(1)}, f32[1,64]{1,0:T(1,128)}, u32[]{:S(2)}) copy-start(f32[1,64]{1,0:T(1,128)} %get-tuple-element.32) | copy-start | bytes 772
  49.1 8.9 %collective-permute-start.8 = (f32[272,128]{1,0:T(8,128)}, f32[272,128]{1,0:T(8,128)}, u32[]{:S(2)}, u32[]{:S(2)}) collective-permute-start(f32[272,128]{1,0:T(8,128)} %collective-permute-done.4.refs_3_), channel_id=1, source_target_pairs={{0,8},{1,9},{2,10},{3,11},{4,12},{5,13},{6,14},{7,15},{8,0},{9,1},... | collective-permute-start | bytes 417800 | tf_op jit(solution)/shard_map/ppermute | solution.py:412
  50.9 7.2 %collective-permute-start.7 = (f32[272,128]{1,0:T(8,128)}, f32[272,128]{1,0:T(8,128)}, u32[]{:S(2)}, u32[]{:S(2)}) collective-permute-start(f32[272,128]{1,0:T(8,128)} %collective-permute-done.3.refs_2_), channel_id=1, source_target_pairs={{0,8},{1,9},{2,10},{3,11},{4,12},{5,13},{6,14},{7,15},{8,0},{9,1},... | collective-permute-start | bytes 417800 | tf_op jit(solution)/shard_map/ppermute | solution.py:412
  54.7 3.4 %collective-permute-start.6 = (f32[272,128]{1,0:T(8,128)}, f32[272,128]{1,0:T(8,128)}, u32[]{:S(2)}, u32[]{:S(2)}) collective-permute-start(f32[272,128]{1,0:T(8,128)} %collective-permute-done.2.refs_1_), channel_id=1, source_target_pairs={{0,8},{1,9},{2,10},{3,11},{4,12},{5,13},{6,14},{7,15},{8,0},{9,1},... | collective-permute-start | bytes 417800 | tf_op jit(solution)/shard_map/ppermute | solution.py:412
  54.8 0.7 copy-start.11
  54.8 0.7 copy-start.12
  54.8 0.7 copy-start.13
  57.2 0.9 copy-start.5
  65.1 7.2 %collective-permute-start.12 = (f32[2,128,128]{2,1,0:T(8,128)S(1)}, f32[2,128,128]{2,1,0:T(8,128)S(1)}, u32[]{:S(2)}, u32[]{:S(2)}) collective-permute-start(f32[2,128,128]{2,1,0:T(8,128)S(1)} %get-tuple-element.13), channel_id=1, source_target_pairs={{0,6},{1,7},{2,0},{3,1},{4,2},{5,3},{6,4},{7,5},{8,10},{9,11},{10,... | collective-permute-start | bytes 393224 | tf_op jit(solution)/shard_map/ppermute | solution.py:412
  66.6 6.0 %collective-permute-start.11 = (f32[2,128,128]{2,1,0:T(8,128)S(1)}, f32[2,128,128]{2,1,0:T(8,128)S(1)}, u32[]{:S(2)}, u32[]{:S(2)}) collective-permute-start(f32[2,128,128]{2,1,0:T(8,128)S(1)} %get-tuple-element.13), channel_id=1, source_target_pairs={{0,7},{1,0},{2,1},{3,2},{4,3},{5,4},{6,5},{7,6},{8,15},{9,8},{10,9... | collective-permute-start | bytes 393224 | tf_op jit(solution)/shard_map/ppermute | solution.py:412
  67.7 9.1 %collective-permute-start.10 = (f32[2,128,128]{2,1,0:T(8,128)S(1)}, f32[2,128,128]{2,1,0:T(8,128)S(1)}, u32[]{:S(2)}, u32[]{:S(2)}) collective-permute-start(f32[2,128,128]{2,1,0:T(8,128)S(1)} %get-tuple-element.13), channel_id=1, source_target_pairs={{0,1},{1,2},{2,3},{3,4},{4,5},{5,6},{6,7},{7,0},{8,9},{9,10},{10,1... | collective-permute-start | bytes 393224 | tf_op jit(solution)/shard_map/ppermute | solution.py:412
  72.2 4.6 %collective-permute-start.15 = (f32[2,128,128]{2,1,0:T(8,128)S(1)}, f32[2,128,128]{2,1,0:T(8,128)S(1)}, u32[]{:S(2)}, u32[]{:S(2)}) collective-permute-start(f32[2,128,128]{2,1,0:T(8,128)S(1)} %collective-permute-done.12.refs_3_), channel_id=1, source_target_pairs={{0,8},{1,9},{2,10},{3,11},{4,12},{5,13},{6,14},{7,15},{8,0},{9,1},... | collective-permute-start | bytes 393224 | tf_op jit(solution)/shard_map/ppermute | solution.py:412
  72.5 4.3 %collective-permute-start.14 = (f32[2,128,128]{2,1,0:T(8,128)S(1)}, f32[2,128,128]{2,1,0:T(8,128)S(1)}, u32[]{:S(2)}, u32[]{:S(2)}) collective-permute-start(f32[2,128,128]{2,1,0:T(8,128)S(1)} %collective-permute-done.11.refs_2_), channel_id=1, source_target_pairs={{0,8},{1,9},{2,10},{3,11},{4,12},{5,13},{6,14},{7,15},{8,0},{9,1},... | collective-permute-start | bytes 393224 | tf_op jit(solution)/shard_map/ppermute | solution.py:412
  76.7 1.3 %collective-permute-start.13 = (f32[2,128,128]{2,1,0:T(8,128)S(1)}, f32[2,128,128]{2,1,0:T(8,128)S(1)}, u32[]{:S(2)}, u32[]{:S(2)}) collective-permute-start(f32[2,128,128]{2,1,0:T(8,128)S(1)} %collective-permute-done.10.refs_1_), channel_id=1, source_target_pairs={{0,8},{1,9},{2,10},{3,11},{4,12},{5,13},{6,14},{7,15},{8,0},{9,1},... | collective-permute-start | bytes 393224 | tf_op jit(solution)/shard_map/ppermute | solution.py:412
  85.2 0.7 copy-start.2
  85.9 4.9 %collective-permute-start.17 = (f32[192,256]{1,0:T(8,128)}, f32[192,256]{1,0:T(8,128)S(1)}, u32[]{:S(2)}, u32[]{:S(2)}) collective-permute-start(f32[192,256]{1,0:T(8,128)} %get-tuple-element.17), channel_id=1, source_target_pairs={{0,16},{1,17},{2,18},{3,19},{4,20},{5,21},{6,22},{7,23},{8,0},{9,1... | collective-permute-start | bytes 589832 | tf_op jit(solution)/shard_map/ppermute | solution.py:412
  86.2 7.5 %collective-permute-start.18 = (f32[128,256]{1,0:T(8,128)}, f32[128,256]{1,0:T(8,128)S(1)}, u32[]{:S(2)}, u32[]{:S(2)}) collective-permute-start(f32[128,256]{1,0:T(8,128)} %get-tuple-element.18), channel_id=1, source_target_pairs={{0,24},{1,25},{2,26},{3,27},{4,28},{5,29},{6,30},{7,31},{8,16},{9,... | collective-permute-start | bytes 393224 | tf_op jit(solution)/shard_map/ppermute | solution.py:412
  87.3 7.1 %collective-permute-start.19 = (f32[64,256]{1,0:T(8,128)S(1)}, f32[64,256]{1,0:T(8,128)S(1)}, u32[]{:S(2)}, u32[]{:S(2)}) collective-permute-start(f32[64,256]{1,0:T(8,128)S(1)} %get-tuple-element.21), channel_id=1, source_target_pairs={{0,8},{1,9},{2,10},{3,11},{4,12},{5,13},{6,14},{7,15},{8,0},{9,1},... | collective-permute-start | bytes 196616 | tf_op jit(solution)/shard_map/ppermute | solution.py:412
  90.9 2.8 %copy-start.3 = (f32[4,64,256]{2,1,0:T(8,128)S(1)}, f32[4,64,256]{2,1,0:T(8,128)}, u32[]{:S(2)}) copy-start(f32[4,64,256]{2,1,0:T(8,128)} %copy-done.2) | copy-start | bytes 786436

commit v2 on v1

--- a/solution.py
+++ b/solution.py
@@ -163,8 +163,13 @@
     return jnp.concatenate(out, axis=0)
 
 
-def pack_kernel(info, incoming, moved_high, moved_low, fields, out, scratch):
-    sec, odd = info[0], info[1]
+def position():
+    sec = lax.axis_index("sec")
+    return sec, lax.rem(sec, 2)
+
+
+def pack_kernel(incoming, moved_high, moved_low, fields, out, scratch):
+    sec, odd = position()
     rows = scratch.shape[0]
     pair = incoming.shape[0] // 2
 
@@ -184,22 +189,51 @@
             out[at + 1 : at + 2] = line[:, rows:]
 
 
-def turn_kernel(stored, out, scratch):
-    for i in range(stored.shape[1]):
-        out[0, i] = to_tile(stored[0, i].astype(jnp.float32), scratch)
-
-
-def turn(stored):
-    steps, planes, orients, cells = stored.shape
+def prepare_kernel(backward, axial, lateral, depth, diagonal, coupling, stored, taps, weights, scratch):
+    for i in range(backward.shape[1]):
+        stored[0, i] = to_tile(backward[0, i].astype(jnp.float32), scratch)
+
+    @pl.when(pl.program_id(0) == 0)
+    def _():
+        orients = coupling.shape[0]
+        ratios = [each[w : w + 1] / each[1:2] for each in (axial, lateral, depth) for w in (0, 2)]
+        for i, ratio in enumerate(ratios + ratios[:2]):
+            taps[i : i + 1] = jnp.concatenate([ratio, ratio], axis=1)
+        square = (orients, orients)
+        same = lax.broadcasted_iota(jnp.int32, square, 0) == lax.broadcasted_iota(jnp.int32, square, 1)
+        kernel = jnp.where(same, diagonal[...], 0.0) + coupling[...]
+        kernel = kernel * (axial[1:2] * lateral[1:2] * depth[1:2])
+        upper = jnp.concatenate([kernel, jnp.zeros_like(kernel)], axis=1)
+        twice = jnp.concatenate([upper, pltpu.roll(upper, orients, 1)], axis=0).T
+        coarse = twice.astype(jnp.bfloat16)
+        fine = (twice - coarse.astype(jnp.float32)).astype(jnp.bfloat16)
+        weights[...] = jnp.concatenate(
+            [jnp.concatenate([coarse, fine], axis=1), jnp.concatenate([coarse, jnp.zeros_like(fine)], axis=1)], axis=0
+        )
+
+
+def prepare(backward, axial, lateral, depth, diagonal, coupling):
+    steps, planes, orients, cells = backward.shape
+    rows, lanes = 2 * orients, cells // 2
+    small = [axial, lateral, depth, diagonal.reshape(1, -1), coupling]
     return pl.pallas_call(
-        turn_kernel,
+        prepare_kernel,
         grid=(steps,),
-        in_specs=[pl.BlockSpec((1, planes, orients, cells), lambda s: (s, 0, 0, 0))],
-        out_specs=pl.BlockSpec((1, planes, 2 * orients, cells // 2), lambda s: (s, 0, 0, 0)),
-        out_shape=jax.ShapeDtypeStruct((steps, planes, 2 * orients, cells // 2), jnp.float32),
-        scratch_shapes=[pltpu.VMEM((2 * orients, cells // 2), jnp.float32)],
+        in_specs=[pl.BlockSpec((1, planes, orients, cells), lambda s: (s, 0, 0, 0))]
+        + [pl.BlockSpec(each.shape, lambda s: (0, 0)) for each in small],
+        out_specs=[
+            pl.BlockSpec((1, planes, rows, lanes), lambda s: (s, 0, 0, 0)),
+            pl.BlockSpec((8, lanes), lambda s: (0, 0)),
+            pl.BlockSpec((2 * rows, 2 * lanes), lambda s: (0, 0)),
+        ],
+        out_shape=[
+            jax.ShapeDtypeStruct((steps, planes, rows, lanes), jnp.float32),
+            jax.ShapeDtypeStruct((8, lanes), jnp.float32),
+            jax.ShapeDtypeStruct((2 * rows, 2 * lanes), jnp.bfloat16),
+        ],
+        scratch_shapes=[pltpu.VMEM((rows, lanes), jnp.float32)],
         compiler_params=pltpu.CompilerParams(vmem_limit_bytes=VMEM_BYTES),
-    )(stored)
+    )(backward, *small)
 
 
 def places(odd, pair, reach):
@@ -216,7 +250,16 @@
     return starts
 
 
-def run_steps(info, taps, weights, kinds_at, count, slab, other, first, second, factor, after):
+def kind_of(kinds, step, steps):
+    sec = lax.axis_index("sec")
+    apart = sec ^ (sec // 2 + step // steps)
+    each = [ref[0, step % steps] for ref in kinds]
+    return jnp.where(
+        apart == 0, each[0], jnp.where(apart == 1, each[1], jnp.where(apart == 2, each[2], each[3]))
+    )
+
+
+def run_steps(kinds, steps, taps, weights, begun, count, slab, other, first, second, factor, after):
     tap = [taps[i : i + 1, :] for i in range(6)]
     extent, rows, lanes = slab.shape
     buffers = (slab, other)
@@ -238,7 +281,7 @@
         source, target = buffers[step % 2], buffers[1 - step % 2]
         begin, width = step + 1, extent - 2 * step - 2
         groups = -(-width // GROUP)
-        kind = info[kinds_at + step]
+        kind = kind_of(kinds, begun + step, steps)
 
         def at(i, begin=begin, width=width):
             return jnp.minimum(begin + i * GROUP, begin + width - GROUP)
@@ -273,11 +316,11 @@
                 factor[kind, start + i] = jnp.where(left, columns[:, at : at + 1], columns[:, at + 1 : at + 2])
 
 
-def early_kernel(half, kinds, info, taps, weights, *refs):
-    pieces, (stored, next_stored) = refs[:8], refs[8:10]
-    middle, half_out, kept, total, columns = refs[10:15]
-    slab, other, first, second, factor, scratch = refs[15:]
-    sec, odd = info[0], info[1]
+def early_kernel(half, *refs):
+    kinds, taps, weights, pieces, (stored, next_stored) = refs[:4], refs[4], refs[5], refs[6:14], refs[14:16]
+    middle, half_out, kept, total, factor = refs[16:21]
+    slab, other, first, second, scratch = refs[21:]
+    sec, odd = position()
     planes, rows = middle.shape[:2]
     pair = planes // 2
     starts = places(odd, pair, half)
@@ -285,8 +328,7 @@
         for i in range(pair):
             slab[start + i] = piece[i * rows : (i + 1) * rows]
     scratch[...] = jnp.exp(-jnp.concatenate([piece[pair * rows :] for piece in pieces], axis=0)).T
-    columns[...] = reorder(scratch)
-    spread_factor(columns, factor, starts, kinds, pair)
+    spread_factor(reorder(scratch), factor, starts, factor.shape[0], pair)
     steps = stored.shape[0]
     total[...] = jnp.zeros(total.shape, jnp.float32)
 
@@ -298,18 +340,18 @@
             if step + 1 == steps:
                 kept[...] = state[half : half + planes]
 
-    run_steps(info, taps, weights, 2, half, slab, other, first, second, factor, after)
+    run_steps(kinds, steps, taps, weights, 0, half, slab, other, first, second, factor, after)
     state = (slab, other)[half % 2]
     middle[...] = state[half : half + planes]
     half_out[...] = state[pl.ds(half + pair * odd, pair)]
 
 
-def late_kernel(half, kinds, last, info, taps, weights, *refs):
-    middle, pieces, columns = refs[0], refs[1:7], refs[7]
-    kept, total_in, stored, next_stored, last_stored = refs[8:13]
-    handoff, share, to_pair, to_across, to_corner = refs[13:18]
-    slab, other, first, second, factor, scratch, total, saved, whole = refs[18:]
-    sec, odd = info[0], info[1]
+def late_kernel(half, last, *refs):
+    kinds, taps, weights, middle, pieces, factor = refs[:4], refs[4], refs[5], refs[6], refs[7:13], refs[13]
+    kept, total_in, stored, next_stored, last_stored = refs[14:19]
+    handoff, share, to_pair, to_across, to_corner = refs[19:24]
+    slab, other, first, second, scratch, total, saved, whole = refs[24:]
+    sec, odd = position()
     planes, rows = middle.shape[:2]
     pair = planes // 2
     starts = places(odd, pair, half)
@@ -317,7 +359,6 @@
     for piece, start in zip(pieces, starts[1:4] + starts[5:8]):
         for i in range(pair):
             slab[start + i] = piece[i]
-    spread_factor(columns, factor, starts, kinds, pair)
     steps = stored.shape[0]
     total[...] = total_in[...]
     saved[...] = kept[...]
@@ -342,7 +383,7 @@
             def _():
                 total[...] += state[half : half + planes] * stored[step % steps]
 
-    run_steps(info, taps, weights, 2 + half, half, slab, other, first, second, factor, after)
+    run_steps(kinds, steps, taps, weights, half, half, slab, other, first, second, factor, after)
     state = (slab, other)[half % 2]
 
     @pl.when(sec == last)
@@ -371,27 +412,15 @@
         to_corner[...] = to_across[held:]
 
 
-def call(kernel, out_shape, scratch, operands):
+def call(kernel, out_shape, scratch, operands, scalars=()):
     return pl.pallas_call(
         kernel,
-        in_specs=[IN_SMEM] + [IN_VMEM] * (len(operands) - 1),
+        in_specs=[IN_SMEM] * len(scalars) + [IN_VMEM] * len(operands),
         out_specs=[IN_VMEM] * len(out_shape),
         out_shape=[jax.ShapeDtypeStruct(shape, jnp.float32) for shape in out_shape],
         scratch_shapes=scratch,
         compiler_params=pltpu.CompilerParams(vmem_limit_bytes=VMEM_BYTES),
-    )(*operands)
-
-
-def tables(axial_taps, lateral_taps, depth_taps, bend_diagonal, bend_coupling):
-    kernel = jnp.diag(bend_diagonal) + bend_coupling
-    kernel = (kernel * (axial_taps[1] * lateral_taps[1] * depth_taps[1])[None, :]).T
-    ratios = [each[which] / each[1] for each in (axial_taps, lateral_taps, depth_taps) for which in (0, 2)]
-    taps = jnp.tile(jnp.stack(ratios + ratios[:2]), (1, 2))
-    coarse = lax.reduce_precision(kernel, 8, 7)
-    twice = jnp.eye(2, dtype=jnp.float32)
-    coarse, fine = jnp.kron(twice, coarse), jnp.kron(twice, kernel - coarse)
-    weights = jnp.block([[coarse, fine], [coarse, jnp.zeros_like(fine)]])
-    return taps, weights.astype(jnp.bfloat16)
+    )(*scalars, *operands)
 
 
 def paired(incoming, backward, fields, block_types, axial_taps, lateral_taps, depth_taps, bend_diagonal, bend_coupling):
@@ -402,7 +431,6 @@
     rows = 2 * orients
     lanes = cells // 2
     sec = lax.axis_index("sec")
-    odd = sec % 2
     last = n_sec - 1
 
     def send(array, by_sec, shift=lambda s: 0):
@@ -411,25 +439,18 @@
         ]
         return lax.ppermute(array, ("sec", "gx"), pairs)
 
-    same, beside = (0, 1, 2, 3), (1, 0, 3, 2)
+    same, beside, across = (0, 1, 2, 3), (1, 0, 3, 2), (2, 3, 0, 1)
     whole = incoming[0]
     moved_high = send(whole[pair:], (1, 3, 0, 2))
     moved_low = send(whole[:pair], (0, 2, 1, 3))
-    taps, weights = tables(axial_taps, lateral_taps, depth_taps, bend_diagonal, bend_coupling)
-    kinds = lax.all_gather(block_types[0], "sec")
-    kinds = lax.dynamic_slice(kinds, (sec // 2, 0), (TICKS, steps)).reshape(-1)
-    place = jnp.stack([sec, odd]).astype(jnp.int32)
-    info = jnp.concatenate([place, kinds])
-    stored = turn(backward)
-    next_stored = send(stored, beside)
-    last_stored = send(stored, (2, 3, 0, 1))
+    kinds = [block_types, send(block_types, beside), send(block_types, across), send(block_types, (3, 2, 1, 0))]
+    stored, taps, weights = prepare(backward, axial_taps, lateral_taps, depth_taps, bend_diagonal, bend_coupling)
 
     tile = pltpu.VMEM((rows, lanes), jnp.float32)
     slab = pltpu.VMEM((planes + 2 * half, rows, lanes), jnp.float32)
     packed = pltpu.VMEM((GROUP * rows, 2 * lanes), jnp.bfloat16)
-    factor = pltpu.VMEM((fields.shape[0], planes + 2 * half, rows, lanes), jnp.float32)
     inner = pltpu.VMEM((planes, rows, lanes), jnp.float32)
-    work = [slab, slab, packed, packed, factor, tile]
+    work = [slab, slab, packed, packed, tile]
 
     def exchange(piece):
         own = [
@@ -440,24 +461,29 @@
         return own, [send(each, beside) for each in own]
 
     (piece,) = call(
-        pack_kernel, [(pair * rows + FIELD_ROWS, lanes)], [tile], [place, whole, moved_high, moved_low, fields]
+        pack_kernel, [(pair * rows + FIELD_ROWS, lanes)], [tile], [whole, moved_high, moved_low, fields]
     )
     own, swapped = exchange(piece)
-    middle, piece, kept, total, columns = call(
-        functools.partial(early_kernel, half, fields.shape[0]),
-        [(planes, rows, lanes), (pair, rows, lanes), (planes, rows, lanes), (planes, rows, lanes), (rows, lanes)],
+    next_stored = send(lax.optimization_barrier((stored, piece))[0], beside)
+    last_stored = send(lax.optimization_barrier((stored, own[0]))[0], across)
+    middle, piece, kept, total, factor = call(
+        functools.partial(early_kernel, half),
+        [(planes, rows, lanes), (pair, rows, lanes), (planes, rows, lanes), (planes, rows, lanes)]
+        + [(fields.shape[0], planes + 2 * half, rows, lanes)],
         work,
-        [info, taps, weights, piece, *own, send(piece, beside), *swapped, stored, next_stored],
+        [taps, weights, piece, *own, send(piece, beside), *swapped, stored, next_stored],
+        kinds,
     )
     own, swapped = exchange(piece)
     held = planes * (orients // n_sec)
     handoff, share, to_pair, to_across, to_corner = call(
-        functools.partial(late_kernel, half, fields.shape[0], last),
+        functools.partial(late_kernel, half, last),
         [(planes, orients, cells)]
         + [(held, cells)] * 2
         + [(held + pair * orients, cells), (pair * orients, cells)],
         work + [inner, inner, pltpu.VMEM((orients, cells), jnp.float32)],
-        [info, taps, weights, middle, *own, *swapped, columns, kept, total, stored, next_stored, last_stored],
+        [taps, weights, middle, *own, *swapped, factor, kept, total, stored, next_stored, last_stored],
+        kinds,
     )
     to_pair = send(to_pair, beside)
     to_across = send(to_across, (2, 0, 3, 1))

time: 95.6 us -> 91.6 us (0.958)
  blocking collectives: 5.03 us -> 0 us
  starting transfers between devices: 17 us -> 21.7 us
  other arithmetic: 4.63 us -> 1.41 us
  waiting for transfers between devices: 42.4 us -> 44.2 us
  local copies, waits for them, and re-layouts: 9.39 us -> 7.8 us
    all_gather x1 -> x0, blocking collectives: 5.03 us -> none  [paired(): kinds = lax.all_gather(block_types[0], 'sec')]
    ppermute x20 -> x23, starting transfers between devices: 17 us -> 21.7 us  [send(): return lax.ppermute(array, ('sec', 'gx'), pairs)]
    ppermute x20 -> x23, waiting for transfers between devices: 42.4 us -> 44.2 us  [send(): return lax.ppermute(array, ('sec', 'gx'), pairs)]
    another operation x2 -> x0, other arithmetic: 1.61 us -> none
    unnamed x40 -> x18, local copies, waits for them, and re-layouts: 6.02 us -> 6.8 us
  transfers between devices with their start and end apart: 20 -> 23, of which waited for: 9 -> 10; matrix products, arithmetic and copies ran while one was open for 8% -> 1% of each run, Pallas kernels for 8% -> 10%
where the time goes in v2:
time: 91.6 us; the launch traced here: 91.1 us
  waiting for transfers between devices  44.2 us (48%)
  starting transfers between devices  21.7 us (24%)
  Pallas kernels  15.3 us (17%)
  local copies, waits for them, and re-layouts  7.8 us (9%)
  other arithmetic  1.41 us (2%)
    ppermute x23, waiting for transfers between devices, send(): return lax.ppermute(array, ('sec', 'gx'), pairs)  44.2 us
    ppermute x23, starting transfers between devices, send(): return lax.ppermute(array, ('sec', 'gx'), pairs)  21.7 us
    pallas_call x3, Pallas kernels, call(): pl.pallas_call(kernel, in_specs=[IN_SMEM] * len(scalars) + [IN_VMEM] * le...  14.4 us
    unnamed x18, local copies, waits for them, and re-layouts  6.8 us
  transfers between devices with their start and end apart: 23, of which 10 were waited for; matrix products, arithmetic and copies ran while one was open for 1% of the time, Pallas kernels for 10%

profile of v2, /device:TPU:0, one launch (start us, length us, event | category | flops | bytes accessed | tf_op | source)
XLA Modules:
  0.0 91.1 jit_solution(9962910933335237249)
XLA Ops:
  0.6 1.0 %slice_bitcast_fusion = (f32[2,64,256]{2,1,0:T(8,128)S(1)}, f32[2,64,256]{2,1,0:T(8,128)S(1)}) fusion(f32[1,4,64,256]{3,2,1,0:T(8,128)} %param.9), kind=kLoop, calls=%fused_computation.2 | loop fusion | bytes 524288 | tf_op jit(solution)/shard_map/slice | solution.py:445
  1.6 0.5 collective-permute-start.3
  2.1 0.7 collective-permute-start.4
  2.8 0.0 copy-start.1
  2.8 1.0 %copy-done.1 = bf16[4,4,64,256]{3,2,1,0:T(8,128)(2,1)S(1)} copy-done((bf16[4,4,64,256]{3,2,1,0:T(8,128)(2,1)S(1)}, bf16[4,4,64,256]{3,2,1,0:T(8,128)(2,1)}, u32[]{:S(2)}) %copy-start.1) | copy-done | bytes 524312
  3.8 0.8 copy-done.2
  4.6 0.7 copy-done.4
  5.2 0.7 copy-done.5
  5.9 0.7 copy-done.6
  6.6 0.7 copy-done.8
  7.3 0.8 shard_map.104
  8.1 0.0 collective-permute-done.3.moved_high
  8.1 0.0 collective-permute-done.4.moved_low
  8.1 0.0 copy-start
  8.1 0.9 %copy-done = f32[1,4,64,256]{3,2,1,0:T(8,128)S(1)} copy-done((f32[1,4,64,256]{3,2,1,0:T(8,128)S(1)}, f32[1,4,64,256]{3,2,1,0:T(8,128)}, u32[]{:S(2)}) %copy-start) | copy-done | bytes 262168
  9.1 0.7 copy-done.3
  9.8 0.1 shard_map.105.refs_6_
  9.9 4.0 %collective-permute-start.12 = (f32[4,4,128,128]{3,2,1,0:T(8,128)S(1)}, f32[4,4,128,128]{3,2,1,0:T(8,128)S(1)}, u32[]{:S(2)}, u32[]{:S(2)}) collective-permute-start(f32[4,4,128,128]{3,2,1,0:T(8,128)S(1)} %get-tuple-element.26.refs_14_.refs_16_), channel_id=1, source_target_pairs={{0,8},{1,9},{2,10},{3,11},{4,12},{5,13},{6,14},{7,15},{8,0},{9,1},... | collective-permute-start | bytes 3145736 | tf_op jit(solution)/shard_map/ppermute | solution.py:440
  13.9 2.0 %collective-permute-start.5 = (f32[272,128]{1,0:T(8,128)S(1)}, f32[272,128]{1,0:T(8,128)S(1)}, u32[]{:S(2)}, u32[]{:S(2)}) collective-permute-start(f32[272,128]{1,0:T(8,128)S(1)} %shard_map.105.refs_6_), channel_id=1, source_target_pairs={{0,1},{1,2},{2,3},{3,4},{4,5},{5,6},{6,7},{7,0},{8,9},{9,10},{10,1... | collective-permute-start | bytes 417800 | tf_op jit(solution)/shard_map/ppermute | solution.py:440
  15.8 6.9 %collective-permute-done.5.refs_7_ = f32[272,128]{1,0:T(8,128)S(1)} collective-permute-done((f32[272,128]{1,0:T(8,128)S(1)}, f32[272,128]{1,0:T(8,128)S(1)}, u32[]{:S(2)}, u32[]{:S(2)}) %collective-permute-start.5) | collective-permute-done | bytes 139296 | tf_op jit(solution)/shard_map/ppermute | solution.py:440
  22.8 1.0 %collective-permute-start.19 = (f32[4,4,128,128]{3,2,1,0:T(8,128)S(1)}, f32[4,4,128,128]{3,2,1,0:T(8,128)S(1)}, u32[]{:S(2)}, u32[]{:S(2)}) collective-permute-start(f32[4,4,128,128]{3,2,1,0:T(8,128)S(1)} %get-tuple-element.26.refs_14_.refs_16_), channel_id=1, source_target_pairs={{0,16},{1,17},{2,18},{3,19},{4,20},{5,21},{6,22},{7,23},{8,24},{9,... | collective-permute-start | bytes 3145736 | tf_op jit(solution)/shard_map/ppermute | solution.py:440
  23.8 0.0 collective-permute-start
  23.8 1.0 %collective-permute-start.1 = (s32[1,4]{1,0:T(1,128)}, s32[1,4]{1,0:T(1,128)S(1)}, u32[]{:S(2)}, u32[]{:S(2)}) collective-permute-start(s32[1,4]{1,0:T(1,128)} %refs_0_.3), channel_id=1, source_target_pairs={{0,16},{1,17},{2,18},{3,19},{4,20},{5,21},{6,22},{7,23},{8,24},{9,... | collective-permute-start | bytes 56 | tf_op jit(solution)/shard_map/ppermute | solution.py:440
  24.8 0.8 collective-permute-start.2
  25.6 0.0 collective-permute-done.refs_1_
  25.6 1.7 %collective-permute-start.6 = (f32[272,128]{1,0:T(8,128)S(1)}, f32[272,128]{1,0:T(8,128)S(1)}, u32[]{:S(2)}, u32[]{:S(2)}) collective-permute-start(f32[272,128]{1,0:T(8,128)S(1)} %shard_map.105.refs_6_), channel_id=1, source_target_pairs={{0,7},{1,0},{2,1},{3,2},{4,3},{5,4},{6,5},{7,6},{8,15},{9,8},{10,9... | collective-permute-start | bytes 417800 | tf_op jit(solution)/shard_map/ppermute | solution.py:440
  27.4 20.1 %collective-permute-done.1.refs_2_ = s32[1,4]{1,0:T(1,128)S(1)} collective-permute-done((s32[1,4]{1,0:T(1,128)}, s32[1,4]{1,0:T(1,128)S(1)}, u32[]{:S(2)}, u32[]{:S(2)}) %collective-permute-start.1) | collective-permute-done | bytes 48 | tf_op jit(solution)/shard_map/ppermute | solution.py:440
  47.5 1.4 %collective-permute-start.7 = (f32[272,128]{1,0:T(8,128)S(1)}, f32[272,128]{1,0:T(8,128)S(1)}, u32[]{:S(2)}, u32[]{:S(2)}) collective-permute-start(f32[272,128]{1,0:T(8,128)S(1)} %shard_map.105.refs_6_), channel_id=1, source_target_pairs={{0,6},{1,7},{2,0},{3,1},{4,2},{5,3},{6,4},{7,5},{8,10},{9,11},{10,... | collective-permute-start | bytes 417800 | tf_op jit(solution)/shard_map/ppermute | solution.py:440
  48.9 0.0 collective-permute-done.2.refs_3_
  48.9 0.0 collective-permute-start.8
  48.9 0.0 collective-permute-done.6.refs_8_
  48.9 0.5 collective-permute-start.9
  49.4 4.2 %collective-permute-done.7.refs_9_ = f32[272,128]{1,0:T(8,128)S(1)} collective-permute-done((f32[272,128]{1,0:T(8,128)S(1)}, f32[272,128]{1,0:T(8,128)S(1)}, u32[]{:S(2)}, u32[]{:S(2)}) %collective-permute-start.7) | collective-permute-done | bytes 139296 | tf_op jit(solution)/shard_map/ppermute | solution.py:440
  53.5 0.0 collective-permute-start.10
  53.5 0.0 collective-permute-done.8.refs_10_
  53.5 0.5 collective-permute-start.11
  54.0 0.0 collective-permute-done.9.refs_11_
  54.1 0.8 collective-permute-done.10.refs_12_
  54.9 0.2 collective-permute-done.11.refs_13_
  55.1 0.0 collective-permute-done.12.refs_15_.refs_17_
  55.1 0.7 copy-done.7
  55.8 8.0 %shard_map.106 = (f32[4,128,128]{2,1,0:T(8,128)S(1)}, f32[2,128,128]{2,1,0:T(8,128)S(1)}, f32[4,128,128]{2,1,0:T(8,128)S(1)}, f32[4,128,128]{2,1,0:T(8,128)S(1)}, f32[3,16,128,128]{3,2,1,0:T(8,128)}) custom-call(s32[1,4]{1,0:T(1,128)S(1)} %copy-done.7, s32[1,4]{1,0:T(1,128)S(1)} %collective-permute-done.refs_1_, s32[1,4]{1,0:T(1,128)S(1)} %collective-permute-done.1.refs_2_, ...), custom_call_target="tpu_custom_call" | custom-call | tf_op jit(solution)/shard_map/pallas_call | solution.py:416
  63.7 0.0 collective-permute-start.13
  63.7 4.7 %collective-permute-start.14 = (f32[2,128,128]{2,1,0:T(8,128)S(1)}, f32[2,128,128]{2,1,0:T(8,128)S(1)}, u32[]{:S(2)}, u32[]{:S(2)}) collective-permute-start(f32[2,128,128]{2,1,0:T(8,128)S(1)} %get-tuple-element.22), channel_id=1, source_target_pairs={{0,7},{1,0},{2,1},{3,2},{4,3},{5,4},{6,5},{7,6},{8,15},{9,8},{10,9... | collective-permute-start | bytes 393224 | tf_op jit(solution)/shard_map/ppermute | solution.py:440
  68.5 0.4 collective-permute-start.15
  68.8 4.1 %collective-permute-done.13.refs_7_ = f32[2,128,128]{2,1,0:T(8,128)S(1)} collective-permute-done((f32[2,128,128]{2,1,0:T(8,128)S(1)}, f32[2,128,128]{2,1,0:T(8,128)S(1)}, u32[]{:S(2)}, u32[]{:S(2)}) %collective-permute-start.13) | collective-permute-done | bytes 131104 | tf_op jit(solution)/shard_map/ppermute | solution.py:440
  73.0 0.0 collective-permute-start.16
  73.0 0.0 collective-permute-done.14.refs_8_
  73.0 0.5 collective-permute-start.17
  73.5 1.0 %collective-permute-done.15.refs_9_ = f32[2,128,128]{2,1,0:T(8,128)S(1)} collective-permute-done((f32[2,128,128]{2,1,0:T(8,128)S(1)}, f32[2,128,128]{2,1,0:T(8,128)S(1)}, u32[]{:S(2)}, u32[]{:S(2)}) %collective-permute-start.15) | collective-permute-done | bytes 131104 | tf_op jit(solution)/shard_map/ppermute | solution.py:440
  74.4 0.2 collective-permute-start.18
  74.7 0.0 collective-permute-done.19.refs_18_
  74.7 0.0 collective-permute-done.16.refs_10_
  74.7 0.0 collective-permute-done.17.refs_11_
  74.7 1.1 %collective-permute-done.18.refs_12_ = f32[2,128,128]{2,1,0:T(8,128)S(1)} collective-permute-done((f32[2,128,128]{2,1,0:T(8,128)S(1)}, f32[2,128,128]{2,1,0:T(8,128)S(1)}, u32[]{:S(2)}, u32[]{:S(2)}) %collective-permute-start.18) | collective-permute-done | bytes 131104 | tf_op jit(solution)/shard_map/ppermute | solution.py:440
  75.8 6.3 %shard_map.107 = (f32[4,64,256]{2,1,0:T(8,128)S(1)}, f32[64,256]{1,0:T(8,128)S(1)}, f32[64,256]{1,0:T(8,128)S(1)}, f32[192,256]{1,0:T(8,128)S(1)}, f32[128,256]{1,0:T(8,128)S(1)}) custom-call(s32[1,4]{1,0:T(1,128)S(1)} %copy-done.7, s32[1,4]{1,0:T(1,128)S(1)} %collective-permute-done.refs_1_, s32[1,4]{1,0:T(1,128)S(1)} %collective-permute-done.1.refs_2_, ...), custom_call_target="tpu_custom_call" | custom-call | tf_op jit(solution)/shard_map/pallas_call | solution.py:416
  82.1 1.1 %collective-permute-start.20 = (f32[192,256]{1,0:T(8,128)S(1)}, f32[192,256]{1,0:T(8,128)S(1)}, u32[]{:S(2)}, u32[]{:S(2)}) collective-permute-start(f32[192,256]{1,0:T(8,128)S(1)} %get-tuple-element.27), channel_id=1, source_target_pairs={{0,16},{1,17},{2,18},{3,19},{4,20},{5,21},{6,22},{7,23},{8,0},{9,1... | collective-permute-start | bytes 589832 | tf_op jit(solution)/shard_map/ppermute | solution.py:440
  83.2 0.3 collective-permute-start.21
  83.5 0.4 collective-permute-start.22
  83.9 3.9 %collective-permute-done.20 = f32[192,256]{1,0:T(8,128)S(1)} collective-permute-done((f32[192,256]{1,0:T(8,128)S(1)}, f32[192,256]{1,0:T(8,128)S(1)}, u32[]{:S(2)}, u32[]{:S(2)}) %collective-permute-start.20) | collective-permute-done | bytes 196640 | tf_op jit(solution)/shard_map/ppermute | solution.py:440
  87.8 1.9 %collective-permute-done.21 = f32[128,256]{1,0:T(8,128)S(1)} collective-permute-done((f32[128,256]{1,0:T(8,128)S(1)}, f32[128,256]{1,0:T(8,128)S(1)}, u32[]{:S(2)}, u32[]{:S(2)}) %collective-permute-start.21) | collective-permute-done | bytes 131104 | tf_op jit(solution)/shard_map/ppermute | solution.py:440
  89.7 0.7 select_bitcast_fusion
  90.4 0.0 collective-permute-done.22
  90.5 0.7 fusion.1
  (9 shorter events, 0.0 us)
Async XLA Ops:
  1.6 6.5 %collective-permute-start.3 = (f32[2,64,256]{2,1,0:T(8,128)S(1)}, f32[2,64,256]{2,1,0:T(8,128)S(1)}, u32[]{:S(2)}, u32[]{:S(2)}) collective-permute-start(f32[2,64,256]{2,1,0:T(8,128)S(1)} %get-tuple-element.33), channel_id=1, source_target_pairs={{0,8},{1,9},{2,10},{3,11},{4,12},{5,13},{6,14},{7,15},{8,24},{9,25... | collective-permute-start | bytes 393224 | tf_op jit(solution)/shard_map/ppermute | solution.py:440
  2.1 6.0 %collective-permute-start.4 = (f32[2,64,256]{2,1,0:T(8,128)S(1)}, f32[2,64,256]{2,1,0:T(8,128)S(1)}, u32[]{:S(2)}, u32[]{:S(2)}) collective-permute-start(f32[2,64,256]{2,1,0:T(8,128)S(1)} %get-tuple-element.32), channel_id=1, source_target_pairs={{0,0},{1,1},{2,2},{3,3},{4,4},{5,5},{6,6},{7,7},{8,16},{9,17},{10,... | collective-permute-start | bytes 393224 | tf_op jit(solution)/shard_map/ppermute | solution.py:440
  2.8 1.0 %copy-start.1 = (bf16[4,4,64,256]{3,2,1,0:T(8,128)(2,1)S(1)}, bf16[4,4,64,256]{3,2,1,0:T(8,128)(2,1)}, u32[]{:S(2)}) copy-start(bf16[4,4,64,256]{3,2,1,0:T(8,128)(2,1)} %backward.1) | copy-start | bytes 1572868
  3.8 0.8 copy-start.2
  4.6 0.7 copy-start.4
  5.2 0.7 copy-start.5
  5.9 0.7 copy-start.6
  6.6 0.7 copy-start.8
  8.1 1.0 %copy-start = (f32[1,4,64,256]{3,2,1,0:T(8,128)S(1)}, f32[1,4,64,256]{3,2,1,0:T(8,128)}, u32[]{:S(2)}) copy-start(f32[1,4,64,256]{3,2,1,0:T(8,128)} %param.9) | copy-start | bytes 786436
  9.1 0.7 copy-start.3
  9.9 45.2 %collective-permute-start.12 = (f32[4,4,128,128]{3,2,1,0:T(8,128)S(1)}, f32[4,4,128,128]{3,2,1,0:T(8,128)S(1)}, u32[]{:S(2)}, u32[]{:S(2)}) collective-permute-start(f32[4,4,128,128]{3,2,1,0:T(8,128)S(1)} %get-tuple-element.26.refs_14_.refs_16_), channel_id=1, source_target_pairs={{0,8},{1,9},{2,10},{3,11},{4,12},{5,13},{6,14},{7,15},{8,0},{9,1},... | collective-permute-start | bytes 3145736 | tf_op jit(solution)/shard_map/ppermute | solution.py:440
  13.9 8.9 %collective-permute-start.5 = (f32[272,128]{1,0:T(8,128)S(1)}, f32[272,128]{1,0:T(8,128)S(1)}, u32[]{:S(2)}, u32[]{:S(2)}) collective-permute-start(f32[272,128]{1,0:T(8,128)S(1)} %shard_map.105.refs_6_), channel_id=1, source_target_pairs={{0,1},{1,2},{2,3},{3,4},{4,5},{5,6},{6,7},{7,0},{8,9},{9,10},{10,1... | collective-permute-start | bytes 417800 | tf_op jit(solution)/shard_map/ppermute | solution.py:440
  22.8 51.9 %collective-permute-start.19 = (f32[4,4,128,128]{3,2,1,0:T(8,128)S(1)}, f32[4,4,128,128]{3,2,1,0:T(8,128)S(1)}, u32[]{:S(2)}, u32[]{:S(2)}) collective-permute-start(f32[4,4,128,128]{3,2,1,0:T(8,128)S(1)} %get-tuple-element.26.refs_14_.refs_16_), channel_id=1, source_target_pairs={{0,16},{1,17},{2,18},{3,19},{4,20},{5,21},{6,22},{7,23},{8,24},{9,... | collective-permute-start | bytes 3145736 | tf_op jit(solution)/shard_map/ppermute | solution.py:440
  23.8 1.9 %collective-permute-start = (s32[1,4]{1,0:T(1,128)}, s32[1,4]{1,0:T(1,128)S(1)}, u32[]{:S(2)}, u32[]{:S(2)}) collective-permute-start(s32[1,4]{1,0:T(1,128)} %refs_0_.3), channel_id=1, source_target_pairs={{0,8},{1,9},{2,10},{3,11},{4,12},{5,13},{6,14},{7,15},{8,0},{9,1},... | collective-permute-start | bytes 56 | tf_op jit(solution)/shard_map/ppermute | solution.py:440
  23.8 23.7 %collective-permute-start.1 = (s32[1,4]{1,0:T(1,128)}, s32[1,4]{1,0:T(1,128)S(1)}, u32[]{:S(2)}, u32[]{:S(2)}) collective-permute-start(s32[1,4]{1,0:T(1,128)} %refs_0_.3), channel_id=1, source_target_pairs={{0,16},{1,17},{2,18},{3,19},{4,20},{5,21},{6,22},{7,23},{8,24},{9,... | collective-permute-start | bytes 56 | tf_op jit(solution)/shard_map/ppermute | solution.py:440
  24.8 24.0 %collective-permute-start.2 = (s32[1,4]{1,0:T(1,128)}, s32[1,4]{1,0:T(1,128)S(1)}, u32[]{:S(2)}, u32[]{:S(2)}) collective-permute-start(s32[1,4]{1,0:T(1,128)} %refs_0_.3), channel_id=1, source_target_pairs={{0,24},{1,25},{2,26},{3,27},{4,28},{5,29},{6,30},{7,31},{8,16},{9,... | collective-permute-start | bytes 56 | tf_op jit(solution)/shard_map/ppermute | solution.py:440
  25.6 23.2 %collective-permute-start.6 = (f32[272,128]{1,0:T(8,128)S(1)}, f32[272,128]{1,0:T(8,128)S(1)}, u32[]{:S(2)}, u32[]{:S(2)}) collective-permute-start(f32[272,128]{1,0:T(8,128)S(1)} %shard_map.105.refs_6_), channel_id=1, source_target_pairs={{0,7},{1,0},{2,1},{3,2},{4,3},{5,4},{6,5},{7,6},{8,15},{9,8},{10,9... | collective-permute-start | bytes 417800 | tf_op jit(solution)/shard_map/ppermute | solution.py:440
  47.5 6.1 %collective-permute-start.7 = (f32[272,128]{1,0:T(8,128)S(1)}, f32[272,128]{1,0:T(8,128)S(1)}, u32[]{:S(2)}, u32[]{:S(2)}) collective-permute-start(f32[272,128]{1,0:T(8,128)S(1)} %shard_map.105.refs_6_), channel_id=1, source_target_pairs={{0,6},{1,7},{2,0},{3,1},{4,2},{5,3},{6,4},{7,5},{8,10},{9,11},{10,... | collective-permute-start | bytes 417800 | tf_op jit(solution)/shard_map/ppermute | solution.py:440
  48.9 4.7 %collective-permute-start.8 = (f32[272,128]{1,0:T(8,128)S(1)}, f32[272,128]{1,0:T(8,128)S(1)}, u32[]{:S(2)}, u32[]{:S(2)}) collective-permute-start(f32[272,128]{1,0:T(8,128)S(1)} %shard_map.105.refs_6_), channel_id=1, source_target_pairs={{0,8},{1,9},{2,10},{3,11},{4,12},{5,13},{6,14},{7,15},{8,0},{9,1},... | collective-permute-start | bytes 417800 | tf_op jit(solution)/shard_map/ppermute | solution.py:440
  48.9 5.2 %collective-permute-start.9 = (f32[272,128]{1,0:T(8,128)S(1)}, f32[272,128]{1,0:T(8,128)S(1)}, u32[]{:S(2)}, u32[]{:S(2)}) collective-permute-start(f32[272,128]{1,0:T(8,128)S(1)} %collective-permute-done.5.refs_7_), channel_id=1, source_target_pairs={{0,8},{1,9},{2,10},{3,11},{4,12},{5,13},{6,14},{7,15},{8,0},{9,1},... | collective-permute-start | bytes 417800 | tf_op jit(solution)/shard_map/ppermute | solution.py:440
  53.5 1.4 %collective-permute-start.10 = (f32[272,128]{1,0:T(8,128)S(1)}, f32[272,128]{1,0:T(8,128)S(1)}, u32[]{:S(2)}, u32[]{:S(2)}) collective-permute-start(f32[272,128]{1,0:T(8,128)S(1)} %collective-permute-done.6.refs_8_), channel_id=1, source_target_pairs={{0,8},{1,9},{2,10},{3,11},{4,12},{5,13},{6,14},{7,15},{8,0},{9,1},... | collective-permute-start | bytes 417800 | tf_op jit(solution)/shard_map/ppermute | solution.py:440
  53.5 1.6 %collective-permute-start.11 = (f32[272,128]{1,0:T(8,128)S(1)}, f32[272,128]{1,0:T(8,128)S(1)}, u32[]{:S(2)}, u32[]{:S(2)}) collective-permute-start(f32[272,128]{1,0:T(8,128)S(1)} %collective-permute-done.7.refs_9_), channel_id=1, source_target_pairs={{0,8},{1,9},{2,10},{3,11},{4,12},{5,13},{6,14},{7,15},{8,0},{9,1},... | collective-permute-start | bytes 417800 | tf_op jit(solution)/shard_map/ppermute | solution.py:440
  55.1 0.7 copy-start.7
  63.7 9.2 %collective-permute-start.13 = (f32[2,128,128]{2,1,0:T(8,128)S(1)}, f32[2,128,128]{2,1,0:T(8,128)S(1)}, u32[]{:S(2)}, u32[]{:S(2)}) collective-permute-start(f32[2,128,128]{2,1,0:T(8,128)S(1)} %get-tuple-element.22), channel_id=1, source_target_pairs={{0,1},{1,2},{2,3},{3,4},{4,5},{5,6},{6,7},{7,0},{8,9},{9,10},{10,1... | collective-permute-start | bytes 393224 | tf_op jit(solution)/shard_map/ppermute | solution.py:440
  63.7 9.2 %collective-permute-start.14 = (f32[2,128,128]{2,1,0:T(8,128)S(1)}, f32[2,128,128]{2,1,0:T(8,128)S(1)}, u32[]{:S(2)}, u32[]{:S(2)}) collective-permute-start(f32[2,128,128]{2,1,0:T(8,128)S(1)} %get-tuple-element.22), channel_id=1, source_target_pairs={{0,7},{1,0},{2,1},{3,2},{4,3},{5,4},{6,5},{7,6},{8,15},{9,8},{10,9... | collective-permute-start | bytes 393224 | tf_op jit(solution)/shard_map/ppermute | solution.py:440
  68.5 6.0 %collective-permute-start.15 = (f32[2,128,128]{2,1,0:T(8,128)S(1)}, f32[2,128,128]{2,1,0:T(8,128)S(1)}, u32[]{:S(2)}, u32[]{:S(2)}) collective-permute-start(f32[2,128,128]{2,1,0:T(8,128)S(1)} %get-tuple-element.22), channel_id=1, source_target_pairs={{0,6},{1,7},{2,0},{3,1},{4,2},{5,3},{6,4},{7,5},{8,10},{9,11},{10,... | collective-permute-start | bytes 393224 | tf_op jit(solution)/shard_map/ppermute | solution.py:440
  73.0 1.7 %collective-permute-start.16 = (f32[2,128,128]{2,1,0:T(8,128)S(1)}, f32[2,128,128]{2,1,0:T(8,128)S(1)}, u32[]{:S(2)}, u32[]{:S(2)}) collective-permute-start(f32[2,128,128]{2,1,0:T(8,128)S(1)} %collective-permute-done.13.refs_7_), channel_id=1, source_target_pairs={{0,8},{1,9},{2,10},{3,11},{4,12},{5,13},{6,14},{7,15},{8,0},{9,1},... | collective-permute-start | bytes 393224 | tf_op jit(solution)/shard_map/ppermute | solution.py:440
  73.0 1.7 %collective-permute-start.17 = (f32[2,128,128]{2,1,0:T(8,128)S(1)}, f32[2,128,128]{2,1,0:T(8,128)S(1)}, u32[]{:S(2)}, u32[]{:S(2)}) collective-permute-start(f32[2,128,128]{2,1,0:T(8,128)S(1)} %collective-permute-done.14.refs_8_), channel_id=1, source_target_pairs={{0,8},{1,9},{2,10},{3,11},{4,12},{5,13},{6,14},{7,15},{8,0},{9,1},... | collective-permute-start | bytes 393224 | tf_op jit(solution)/shard_map/ppermute | solution.py:440
  74.4 1.3 %collective-permute-start.18 = (f32[2,128,128]{2,1,0:T(8,128)S(1)}, f32[2,128,128]{2,1,0:T(8,128)S(1)}, u32[]{:S(2)}, u32[]{:S(2)}) collective-permute-start(f32[2,128,128]{2,1,0:T(8,128)S(1)} %collective-permute-done.15.refs_9_), channel_id=1, source_target_pairs={{0,8},{1,9},{2,10},{3,11},{4,12},{5,13},{6,14},{7,15},{8,0},{9,1},... | collective-permute-start | bytes 393224 | tf_op jit(solution)/shard_map/ppermute | solution.py:440
  82.1 5.7 %collective-permute-start.20 = (f32[192,256]{1,0:T(8,128)S(1)}, f32[192,256]{1,0:T(8,128)S(1)}, u32[]{:S(2)}, u32[]{:S(2)}) collective-permute-start(f32[192,256]{1,0:T(8,128)S(1)} %get-tuple-element.27), channel_id=1, source_target_pairs={{0,16},{1,17},{2,18},{3,19},{4,20},{5,21},{6,22},{7,23},{8,0},{9,1... | collective-permute-start | bytes 589832 | tf_op jit(solution)/shard_map/ppermute | solution.py:440
  83.2 6.5 %collective-permute-start.21 = (f32[128,256]{1,0:T(8,128)S(1)}, f32[128,256]{1,0:T(8,128)S(1)}, u32[]{:S(2)}, u32[]{:S(2)}) collective-permute-start(f32[128,256]{1,0:T(8,128)S(1)} %get-tuple-element.28), channel_id=1, source_target_pairs={{0,24},{1,25},{2,26},{3,27},{4,28},{5,29},{6,30},{7,31},{8,16},{9,... | collective-permute-start | bytes 393224 | tf_op jit(solution)/shard_map/ppermute | solution.py:440
  83.5 6.9 %collective-permute-start.22 = (f32[64,256]{1,0:T(8,128)S(1)}, f32[64,256]{1,0:T(8,128)S(1)}, u32[]{:S(2)}, u32[]{:S(2)}) collective-permute-start(f32[64,256]{1,0:T(8,128)S(1)} %get-tuple-element.31), channel_id=1, source_target_pairs={{0,8},{1,9},{2,10},{3,11},{4,12},{5,13},{6,14},{7,15},{8,0},{9,1},... | collective-permute-start | bytes 196616 | tf_op jit(solution)/shard_map/ppermute | solution.py:440

commit v3 on v2

--- a/solution.py
+++ b/solution.py
@@ -168,72 +168,84 @@
     return sec, lax.rem(sec, 2)
 
 
-def pack_kernel(incoming, moved_high, moved_low, fields, out, scratch):
-    sec, odd = position()
+def prepare_kernel(*refs):
+    sources, (early, late, start, taps, weights) = refs[:8], refs[8:13]
+    scratch, copies, sems = refs[13], refs[14:22], refs[22]
+    moves = [pltpu.make_async_copy(s, c, sems.at[i]) for i, (s, c) in enumerate(zip(sources, copies))]
+    for move in moves:
+        move.start()
+    backward, incoming, fields, axial, lateral, depth, diagonal, coupling = copies
+    for move in moves[3:]:
+        move.wait()
+    orients = coupling.shape[0]
+    ratios = [each[w : w + 1] / each[1:2] for each in (axial, lateral, depth) for w in (0, 2)]
+    for i, ratio in enumerate(ratios + ratios[:2]):
+        taps[i : i + 1] = jnp.concatenate([ratio, ratio], axis=1)
+    square = (orients, orients)
+    same = lax.broadcasted_iota(jnp.int32, square, 0) == lax.broadcasted_iota(jnp.int32, square, 1)
+    kernel = jnp.where(same, diagonal[...], 0.0) + coupling[...]
+    kernel = kernel * (axial[1:2] * lateral[1:2] * depth[1:2])
+    upper = jnp.concatenate([kernel, jnp.zeros_like(kernel)], axis=1)
+    twice = jnp.concatenate([upper, pltpu.roll(upper, orients, 1)], axis=0).T
+    coarse = twice.astype(jnp.bfloat16)
+    fine = (twice - coarse.astype(jnp.float32)).astype(jnp.bfloat16)
+    weights[...] = jnp.concatenate(
+        [jnp.concatenate([coarse, fine], axis=1), jnp.concatenate([coarse, jnp.zeros_like(fine)], axis=1)], axis=0
+    )
+    odd = position()[1]
     rows = scratch.shape[0]
-    pair = incoming.shape[0] // 2
-
-    def fill(source):
-        for i in range(pair):
-            out[i * rows : (i + 1) * rows] = to_tile(source[i], scratch)
-
-    pl.when(sec == 0)(lambda: fill(incoming))
-    pl.when(odd == 1)(lambda: fill(moved_high))
-    pl.when((sec > 0) & (odd == 0))(lambda: fill(moved_low))
-    out[pair * rows :] = jnp.zeros((FIELD_ROWS, rows), jnp.float32)
+    pair = incoming.shape[1] // 2
+    moves[1].wait()
+    for i in range(pair):
+        start[i * rows : (i + 1) * rows] = to_tile(incoming[0, i], scratch)
+    moves[2].wait()
+    start[pair * rows :] = jnp.zeros((FIELD_ROWS, rows), jnp.float32)
     for kind in range(fields.shape[0]):
         for i in range(pair):
             line = fields[kind, pl.ds(pair * odd + i, 1), :]
             at = pair * rows + (kind * pair + i) * 2
-            out[at : at + 1] = line[:, :rows]
-            out[at + 1 : at + 2] = line[:, rows:]
-
-
-def prepare_kernel(backward, axial, lateral, depth, diagonal, coupling, stored, taps, weights, scratch):
-    for i in range(backward.shape[1]):
-        stored[0, i] = to_tile(backward[0, i].astype(jnp.float32), scratch)
-
-    @pl.when(pl.program_id(0) == 0)
-    def _():
-        orients = coupling.shape[0]
-        ratios = [each[w : w + 1] / each[1:2] for each in (axial, lateral, depth) for w in (0, 2)]
-        for i, ratio in enumerate(ratios + ratios[:2]):
-            taps[i : i + 1] = jnp.concatenate([ratio, ratio], axis=1)
-        square = (orients, orients)
-        same = lax.broadcasted_iota(jnp.int32, square, 0) == lax.broadcasted_iota(jnp.int32, square, 1)
-        kernel = jnp.where(same, diagonal[...], 0.0) + coupling[...]
-        kernel = kernel * (axial[1:2] * lateral[1:2] * depth[1:2])
-        upper = jnp.concatenate([kernel, jnp.zeros_like(kernel)], axis=1)
-        twice = jnp.concatenate([upper, pltpu.roll(upper, orients, 1)], axis=0).T
-        coarse = twice.astype(jnp.bfloat16)
-        fine = (twice - coarse.astype(jnp.float32)).astype(jnp.bfloat16)
-        weights[...] = jnp.concatenate(
-            [jnp.concatenate([coarse, fine], axis=1), jnp.concatenate([coarse, jnp.zeros_like(fine)], axis=1)], axis=0
-        )
-
-
-def prepare(backward, axial, lateral, depth, diagonal, coupling):
+            start[at : at + 1] = line[:, :rows]
+            start[at + 1 : at + 2] = line[:, rows:]
+    moves[0].wait()
+    steps, planes = backward.shape[:2]
+    for out, begin in ((early, 0), (late, steps // 2)):
+        for step in range(steps // 2):
+            for i in range(planes):
+                out[step, i] = to_tile(backward[begin + step, i].astype(jnp.float32), scratch)
+
+
+def prepare(backward, incoming, fields, axial, lateral, depth, diagonal, coupling):
     steps, planes, orients, cells = backward.shape
     rows, lanes = 2 * orients, cells // 2
-    small = [axial, lateral, depth, diagonal.reshape(1, -1), coupling]
+    operands = [backward, incoming, fields, axial, lateral, depth, diagonal.reshape(1, -1), coupling]
+    half = ((steps // 2, planes, rows, lanes), jnp.float32)
+    piece = ((planes // 2 * rows + FIELD_ROWS, lanes), jnp.float32)
     return pl.pallas_call(
         prepare_kernel,
-        grid=(steps,),
-        in_specs=[pl.BlockSpec((1, planes, orients, cells), lambda s: (s, 0, 0, 0))]
-        + [pl.BlockSpec(each.shape, lambda s: (0, 0)) for each in small],
-        out_specs=[
-            pl.BlockSpec((1, planes, rows, lanes), lambda s: (s, 0, 0, 0)),
-            pl.BlockSpec((8, lanes), lambda s: (0, 0)),
-            pl.BlockSpec((2 * rows, 2 * lanes), lambda s: (0, 0)),
+        in_specs=[pl.BlockSpec(memory_space=pltpu.HBM)] * len(operands),
+        out_specs=[IN_VMEM] * 5,
+        out_shape=[
+            jax.ShapeDtypeStruct(*each)
+            for each in (half, half, piece, ((8, lanes), jnp.float32), ((2 * rows, 2 * lanes), jnp.bfloat16))
         ],
-        out_shape=[
-            jax.ShapeDtypeStruct((steps, planes, rows, lanes), jnp.float32),
-            jax.ShapeDtypeStruct((8, lanes), jnp.float32),
-            jax.ShapeDtypeStruct((2 * rows, 2 * lanes), jnp.bfloat16),
-        ],
-        scratch_shapes=[pltpu.VMEM((rows, lanes), jnp.float32)],
+        scratch_shapes=[pltpu.VMEM((rows, lanes), jnp.float32)]
+        + [pltpu.VMEM(each.shape, each.dtype) for each in operands]
+        + [pltpu.SemaphoreType.DMA((len(operands),))],
         compiler_params=pltpu.CompilerParams(vmem_limit_bytes=VMEM_BYTES),
-    )(backward, *small)
+    )(*operands)
+
+
+def pack_kernel(start, moved_high, moved_low, out, scratch):
+    sec, odd = position()
+    rows = scratch.shape[0]
+    out[...] = start[...]
+
+    def fill(source):
+        for i in range(source.shape[0]):
+            out[i * rows : (i + 1) * rows] = to_tile(source[i], scratch)
+
+    pl.when(odd == 1)(lambda: fill(moved_high))
+    pl.when((sec > 0) & (odd == 0))(lambda: fill(moved_low))
 
 
 def places(odd, pair, reach):
@@ -317,9 +329,9 @@
 
 
 def early_kernel(half, *refs):
-    kinds, taps, weights, pieces, (stored, next_stored) = refs[:4], refs[4], refs[5], refs[6:14], refs[14:16]
-    middle, half_out, kept, total, factor = refs[16:21]
-    slab, other, first, second, scratch = refs[21:]
+    kinds, taps, weights, pieces, series = refs[:4], refs[4], refs[5], refs[6:14], refs[14:17]
+    middle, half_out, kept, total, factor = refs[17:22]
+    slab, other, first, second, scratch = refs[22:]
     sec, odd = position()
     planes, rows = middle.shape[:2]
     pair = planes // 2
@@ -329,14 +341,14 @@
             slab[start + i] = piece[i * rows : (i + 1) * rows]
     scratch[...] = jnp.exp(-jnp.concatenate([piece[pair * rows :] for piece in pieces], axis=0)).T
     spread_factor(reorder(scratch), factor, starts, factor.shape[0], pair)
-    steps = stored.shape[0]
+    span = series[0].shape[0]
+    steps = 2 * span
     total[...] = jnp.zeros(total.shape, jnp.float32)
 
     def after(step, state):
         @pl.when(sec == 0)
         def _():
-            source = stored if step < steps else next_stored
-            total[...] += state[half : half + planes] * source[step % steps]
+            total[...] += state[half : half + planes] * series[step // span][step % span]
             if step + 1 == steps:
                 kept[...] = state[half : half + planes]
 
@@ -348,9 +360,9 @@
 
 def late_kernel(half, last, *refs):
     kinds, taps, weights, middle, pieces, factor = refs[:4], refs[4], refs[5], refs[6], refs[7:13], refs[13]
-    kept, total_in, stored, next_stored, last_stored = refs[14:19]
-    handoff, share, to_pair, to_across, to_corner = refs[19:24]
-    slab, other, first, second, scratch, total, saved, whole = refs[24:]
+    kept, total_in, series, stored = refs[14], refs[15], refs[16:19], refs[19:21]
+    handoff, share, to_pair, to_across, to_corner = refs[21:26]
+    slab, other, first, second, scratch, total, saved, whole = refs[26:]
     sec, odd = position()
     planes, rows = middle.shape[:2]
     pair = planes // 2
@@ -359,17 +371,18 @@
     for piece, start in zip(pieces, starts[1:4] + starts[5:8]):
         for i in range(pair):
             slab[start + i] = piece[i]
-    steps = stored.shape[0]
+    span = series[0].shape[0]
+    steps = 2 * span
     total[...] = total_in[...]
     saved[...] = kept[...]
 
     def after(step, state):
+        part = step // span
         step = step + half
 
         @pl.when(sec == 0)
         def _():
-            source = next_stored if step < 2 * steps else last_stored
-            total[...] += state[half : half + planes] * source[step % steps]
+            total[...] += state[half : half + planes] * series[part][step % span]
 
         if step + 1 == 2 * steps:
 
@@ -381,7 +394,7 @@
 
             @pl.when(sec == last)
             def _():
-                total[...] += state[half : half + planes] * stored[step % steps]
+                total[...] += state[half : half + planes] * stored[step % steps // span][step % span]
 
     run_steps(kinds, steps, taps, weights, half, half, slab, other, first, second, factor, after)
     state = (slab, other)[half % 2]
@@ -439,12 +452,16 @@
         ]
         return lax.ppermute(array, ("sec", "gx"), pairs)
 
-    same, beside, across = (0, 1, 2, 3), (1, 0, 3, 2), (2, 3, 0, 1)
+    same, beside, across, crossing = (0, 1, 2, 3), (1, 0, 3, 2), (2, 3, 0, 1), (2, 1, 0, 3)
     whole = incoming[0]
-    moved_high = send(whole[pair:], (1, 3, 0, 2))
+    backward, moved = lax.optimization_barrier((backward, whole[pair:]))
+    moved_high = send(moved, (1, 3, 0, 2))
     moved_low = send(whole[:pair], (0, 2, 1, 3))
     kinds = [block_types, send(block_types, beside), send(block_types, across), send(block_types, (3, 2, 1, 0))]
-    stored, taps, weights = prepare(backward, axial_taps, lateral_taps, depth_taps, bend_diagonal, bend_coupling)
+    early_stored, late_stored, start, taps, weights = prepare(
+        backward, incoming, fields, axial_taps, lateral_taps, depth_taps, bend_diagonal, bend_coupling
+    )
+    early_next, early_last = send(early_stored, beside), send(early_stored, crossing)
 
     tile = pltpu.VMEM((rows, lanes), jnp.float32)
     slab = pltpu.VMEM((planes + 2 * half, rows, lanes), jnp.float32)
@@ -461,17 +478,17 @@
         return own, [send(each, beside) for each in own]
 
     (piece,) = call(
-        pack_kernel, [(pair * rows + FIELD_ROWS, lanes)], [tile], [whole, moved_high, moved_low, fields]
+        pack_kernel, [(pair * rows + FIELD_ROWS, lanes)], [tile], [start, moved_high, moved_low]
     )
     own, swapped = exchange(piece)
-    next_stored = send(lax.optimization_barrier((stored, piece))[0], beside)
-    last_stored = send(lax.optimization_barrier((stored, own[0]))[0], across)
+    late_stored, *swapped = lax.optimization_barrier((late_stored, *swapped))
+    late_next, late_last = send(late_stored, beside), send(late_stored, crossing)
     middle, piece, kept, total, factor = call(
         functools.partial(early_kernel, half),
         [(planes, rows, lanes), (pair, rows, lanes), (planes, rows, lanes), (planes, rows, lanes)]
         + [(fields.shape[0], planes + 2 * half, rows, lanes)],
         work,
-        [taps, weights, piece, *own, send(piece, beside), *swapped, stored, next_stored],
+        [taps, weights, piece, *own, send(piece, beside), *swapped, early_stored, late_stored, early_next],
         kinds,
     )
     own, swapped = exchange(piece)
@@ -482,7 +499,8 @@
         + [(held, cells)] * 2
         + [(held + pair * orients, cells), (pair * orients, cells)],
         work + [inner, inner, pltpu.VMEM((orients, cells), jnp.float32)],
-        [taps, weights, middle, *own, *swapped, factor, kept, total, stored, next_stored, last_stored],
+        [taps, weights, middle, *own, *swapped, factor, kept, total]
+        + [late_next, early_last, late_last, early_stored, late_stored],
         kinds,
     )
     to_pair = send(to_pair, beside)

time: 91.6 us -> 79.9 us (0.87)
  waiting for transfers between devices: 44.2 us -> 25.1 us
  starting transfers between devices: 21.7 us -> 29.1 us
    ppermute x23 -> x25, waiting for transfers between devices: 44.2 us -> 25.1 us  [send(): return lax.ppermute(array, ('sec', 'gx'), pairs)]
    ppermute x23 -> x25, starting transfers between devices: 21.7 us -> 29.1 us  [send(): return lax.ppermute(array, ('sec', 'gx'), pairs)]
  transfers between devices with their start and end apart: 23 -> 25, of which waited for: 10 -> 11; matrix products, arithmetic and copies ran while one was open for 1% -> 1% of each run, Pallas kernels for 10% -> 11%
where the time goes in v3:
time: 79.9 us; the launch traced here: 79.4 us
  starting transfers between devices  29.1 us (36%)
  waiting for transfers between devices  25.1 us (31%)
  Pallas kernels  15.2 us (19%)
  local copies, waits for them, and re-layouts  7.8 us (10%)
  other arithmetic  1.41 us (2%)
    ppermute x25, starting transfers between devices, send(): return lax.ppermute(array, ('sec', 'gx'), pairs)  29.1 us
    ppermute x25, waiting for transfers between devices, send(): return lax.ppermute(array, ('sec', 'gx'), pairs)  25.1 us
    pallas_call x3, Pallas kernels, call(): pl.pallas_call(kernel, in_specs=[IN_SMEM] * len(scalars) + [IN_VMEM] * le...  14.3 us
    unnamed x18, local copies, waits for them, and re-layouts  6.8 us
  transfers between devices with their start and end apart: 25, of which 11 were waited for; matrix products, arithmetic and copies ran while one was open for 1% of the time, Pallas kernels for 11%

profile of v3, /device:TPU:0, one launch (start us, length us, event | category | flops | bytes accessed | tf_op | source)
XLA Modules:
  0.0 79.4 jit_solution(8110913063615149030)
XLA Ops:
  0.6 1.0 %slice_bitcast_fusion = (f32[2,64,256]{2,1,0:T(8,128)S(1)}, f32[2,64,256]{2,1,0:T(8,128)S(1)}) fusion(f32[1,4,64,256]{3,2,1,0:T(8,128)} %refs_1_.1), kind=kLoop, calls=%fused_computation.2 | loop fusion | bytes 524288 | tf_op jit(solution)/shard_map/slice | solution.py:459
  1.6 0.5 collective-permute-start.3
  2.1 0.7 collective-permute-start.4
  2.8 0.0 copy-start
  2.8 0.9 %copy-done = f32[1,4,64,256]{3,2,1,0:T(8,128)S(1)} copy-done((f32[1,4,64,256]{3,2,1,0:T(8,128)S(1)}, f32[1,4,64,256]{3,2,1,0:T(8,128)}, u32[]{:S(2)}) %copy-start) | copy-done | bytes 262168
  3.7 1.0 %copy-done.1 = bf16[4,4,64,256]{3,2,1,0:T(8,128)(2,1)S(1)} copy-done((bf16[4,4,64,256]{3,2,1,0:T(8,128)(2,1)S(1)}, bf16[4,4,64,256]{3,2,1,0:T(8,128)(2,1)}, u32[]{:S(2)}) %copy-start.1) | copy-done | bytes 524312
  4.8 0.8 copy-done.2
  5.5 0.7 copy-done.3
  6.2 0.7 copy-done.4
  6.9 0.7 copy-done.5
  7.6 0.7 copy-done.6
  8.3 0.7 copy-done.8
  8.9 0.8 %shard_map.104 = (f32[2,4,128,128]{3,2,1,0:T(8,128)S(1)}, f32[2,4,128,128]{3,2,1,0:T(8,128)S(1)}, f32[272,128]{1,0:T(8,128)S(1)}, f32[8,128]{1,0:T(8,128)S(1)}, bf16[256,256]{1,0:T(8,128)(2,1)S(1)}) custom-call(bf16[4,4,64,256]{3,2,1,0:T(8,128)(2,1)S(1)} %copy-done.1, f32[1,4,64,256]{3,2,1,0:T(8,128)S(1)} %copy-done, f32[3,4,256]{2,1,0:T(4,128)S(1)} %copy-done.3, ...), custom_call_target="tpu_custom_call" | custom-call | tf_op jit(solution)/shard_map/pallas_call | solution.py:223
  9.8 0.0 collective-permute-done.3.moved_high
  9.8 0.0 collective-permute-done.4.moved_low
  9.8 5.6 %collective-permute-start.6 = (f32[272,128]{1,0:T(8,128)S(1)}, f32[272,128]{1,0:T(8,128)S(1)}, u32[]{:S(2)}, u32[]{:S(2)}) collective-permute-start(f32[272,128]{1,0:T(8,128)S(1)} %shard_map.105.refs_6_), channel_id=1, source_target_pairs={{0,7},{1,0},{2,1},{3,2},{4,3},{5,4},{6,5},{7,6},{8,15},{9,8},{10,9... | collective-permute-start | bytes 417800 | tf_op jit(solution)/shard_map/ppermute | solution.py:453
  15.4 0.4 collective-permute-start.7
  15.9 0.6 collective-permute-start.5
  16.5 2.1 %collective-permute-start.12 = (f32[2,4,128,128]{3,2,1,0:T(8,128)S(1)}, f32[2,4,128,128]{3,2,1,0:T(8,128)S(1)}, u32[]{:S(2)}, u32[]{:S(2)}) collective-permute-start(f32[2,4,128,128]{3,2,1,0:T(8,128)S(1)} %get-tuple-element.32.refs_14_.refs_19_), channel_id=1, source_target_pairs={{0,8},{1,9},{2,10},{3,11},{4,12},{5,13},{6,14},{7,15},{8,0},{9,1},... | collective-permute-start | bytes 1572872 | tf_op jit(solution)/shard_map/ppermute | solution.py:453
  18.6 3.8 %collective-permute-start.20 = (f32[2,4,128,128]{3,2,1,0:T(8,128)S(1)}, f32[2,4,128,128]{3,2,1,0:T(8,128)S(1)}, u32[]{:S(2)}, u32[]{:S(2)}) collective-permute-start(f32[2,4,128,128]{3,2,1,0:T(8,128)S(1)} %get-tuple-element.32.refs_14_.refs_19_), channel_id=1, source_target_pairs={{0,16},{1,17},{2,18},{3,19},{4,20},{5,21},{6,22},{7,23},{8,8},{9,9... | collective-permute-start | bytes 1572872 | tf_op jit(solution)/shard_map/ppermute | solution.py:453
  22.5 0.0 collective-permute-done.6.refs_8_
  22.5 0.1 collective-permute-start.10
  22.6 0.0 collective-permute-done.7.refs_9_
  22.6 1.8 %collective-permute-start.11 = (f32[272,128]{1,0:T(8,128)S(1)}, f32[272,128]{1,0:T(8,128)S(1)}, u32[]{:S(2)}, u32[]{:S(2)}) collective-permute-start(f32[272,128]{1,0:T(8,128)S(1)} %collective-permute-done.7.refs_9_), channel_id=1, source_target_pairs={{0,8},{1,9},{2,10},{3,11},{4,12},{5,13},{6,14},{7,15},{8,0},{9,1},... | collective-permute-start | bytes 417800 | tf_op jit(solution)/shard_map/ppermute | solution.py:453
  24.3 0.0 collective-permute-done.5.refs_7_
  24.3 0.9 %collective-permute-start.9 = (f32[272,128]{1,0:T(8,128)S(1)}, f32[272,128]{1,0:T(8,128)S(1)}, u32[]{:S(2)}, u32[]{:S(2)}) collective-permute-start(f32[272,128]{1,0:T(8,128)S(1)} %collective-permute-done.5.refs_7_), channel_id=1, source_target_pairs={{0,8},{1,9},{2,10},{3,11},{4,12},{5,13},{6,14},{7,15},{8,0},{9,1},... | collective-permute-start | bytes 417800 | tf_op jit(solution)/shard_map/ppermute | solution.py:453
  25.2 0.0 collective-permute-done.10.refs_12_
  25.2 0.1 collective-permute-done.11.refs_13_
  25.3 0.9 %collective-permute-done.9.refs_11_ = f32[272,128]{1,0:T(8,128)S(1)} collective-permute-done((f32[272,128]{1,0:T(8,128)S(1)}, f32[272,128]{1,0:T(8,128)S(1)}, u32[]{:S(2)}, u32[]{:S(2)}) %collective-permute-start.9) | collective-permute-done | bytes 139296 | tf_op jit(solution)/shard_map/ppermute | solution.py:453
  26.2 0.4 collective-permute-start.19
  26.6 4.5 %collective-permute-start.21 = (f32[2,4,128,128]{3,2,1,0:T(8,128)S(1)}, f32[2,4,128,128]{3,2,1,0:T(8,128)S(1)}, u32[]{:S(2)}, u32[]{:S(2)}) collective-permute-start(f32[2,4,128,128]{3,2,1,0:T(8,128)S(1)} %get-tuple-element.33.refs_15_.refs_20_), channel_id=1, source_target_pairs={{0,16},{1,17},{2,18},{3,19},{4,20},{5,21},{6,22},{7,23},{8,8},{9,9... | collective-permute-start | bytes 1572872 | tf_op jit(solution)/shard_map/ppermute | solution.py:453
  31.1 0.1 collective-permute-start
  31.2 1.2 %collective-permute-done.refs_1_ = s32[1,4]{1,0:T(1,128)S(1)} collective-permute-done((s32[1,4]{1,0:T(1,128)}, s32[1,4]{1,0:T(1,128)S(1)}, u32[]{:S(2)}, u32[]{:S(2)}) %collective-permute-start) | collective-permute-done | bytes 48 | tf_op jit(solution)/shard_map/ppermute | solution.py:453
  32.4 0.0 collective-permute-start.1
  32.4 5.9 %collective-permute-done.1.refs_2_ = s32[1,4]{1,0:T(1,128)S(1)} collective-permute-done((s32[1,4]{1,0:T(1,128)}, s32[1,4]{1,0:T(1,128)S(1)}, u32[]{:S(2)}, u32[]{:S(2)}) %collective-permute-start.1) | collective-permute-done | bytes 48 | tf_op jit(solution)/shard_map/ppermute | solution.py:453
  38.3 0.0 collective-permute-start.2
  38.3 3.1 %collective-permute-done.2.refs_3_ = s32[1,4]{1,0:T(1,128)S(1)} collective-permute-done((s32[1,4]{1,0:T(1,128)}, s32[1,4]{1,0:T(1,128)S(1)}, u32[]{:S(2)}, u32[]{:S(2)}) %collective-permute-start.2) | collective-permute-done | bytes 48 | tf_op jit(solution)/shard_map/ppermute | solution.py:453
  41.4 0.4 collective-permute-start.8
  41.8 1.0 %collective-permute-done.8.refs_10_ = f32[272,128]{1,0:T(8,128)S(1)} collective-permute-done((f32[272,128]{1,0:T(8,128)S(1)}, f32[272,128]{1,0:T(8,128)S(1)}, u32[]{:S(2)}, u32[]{:S(2)}) %collective-permute-start.8) | collective-permute-done | bytes 139296 | tf_op jit(solution)/shard_map/ppermute | solution.py:453
  42.8 0.0 collective-permute-done.12.refs_16_
  42.8 0.7 copy-done.7
  43.4 7.9 %shard_map.106 = (f32[4,128,128]{2,1,0:T(8,128)S(1)}, f32[2,128,128]{2,1,0:T(8,128)S(1)}, f32[4,128,128]{2,1,0:T(8,128)S(1)}, f32[4,128,128]{2,1,0:T(8,128)S(1)}, f32[3,16,128,128]{3,2,1,0:T(8,128)}) custom-call(s32[1,4]{1,0:T(1,128)S(1)} %copy-done.7, s32[1,4]{1,0:T(1,128)S(1)} %collective-permute-done.refs_1_, s32[1,4]{1,0:T(1,128)S(1)} %collective-permute-done.1.refs_2_, ...), custom_call_target="tpu_custom_call" | custom-call | tf_op jit(solution)/shard_map/pallas_call | solution.py:429
  51.4 0.0 collective-permute-start.13
  51.4 4.7 %collective-permute-start.14 = (f32[2,128,128]{2,1,0:T(8,128)S(1)}, f32[2,128,128]{2,1,0:T(8,128)S(1)}, u32[]{:S(2)}, u32[]{:S(2)}) collective-permute-start(f32[2,128,128]{2,1,0:T(8,128)S(1)} %get-tuple-element.35), channel_id=1, source_target_pairs={{0,7},{1,0},{2,1},{3,2},{4,3},{5,4},{6,5},{7,6},{8,15},{9,8},{10,9... | collective-permute-start | bytes 393224 | tf_op jit(solution)/shard_map/ppermute | solution.py:453
  56.1 0.0 collective-permute-done.20.refs_17_
  56.1 0.0 collective-permute-start.15
  56.1 4.5 %collective-permute-done.13.refs_7_ = f32[2,128,128]{2,1,0:T(8,128)S(1)} collective-permute-done((f32[2,128,128]{2,1,0:T(8,128)S(1)}, f32[2,128,128]{2,1,0:T(8,128)S(1)}, u32[]{:S(2)}, u32[]{:S(2)}) %collective-permute-start.13) | collective-permute-done | bytes 131104 | tf_op jit(solution)/shard_map/ppermute | solution.py:453
  60.6 0.0 collective-permute-start.16
  60.6 0.0 collective-permute-done.14.refs_8_
  60.6 0.5 collective-permute-start.17
  61.1 1.4 %collective-permute-done.15.refs_9_ = f32[2,128,128]{2,1,0:T(8,128)S(1)} collective-permute-done((f32[2,128,128]{2,1,0:T(8,128)S(1)}, f32[2,128,128]{2,1,0:T(8,128)S(1)}, u32[]{:S(2)}, u32[]{:S(2)}) %collective-permute-start.15) | collective-permute-done | bytes 131104 | tf_op jit(solution)/shard_map/ppermute | solution.py:453
  62.5 0.0 collective-permute-start.18
  62.5 0.0 collective-permute-done.16.refs_10_
  62.5 0.0 collective-permute-done.17.refs_11_
  62.5 1.3 %collective-permute-done.18.refs_12_ = f32[2,128,128]{2,1,0:T(8,128)S(1)} collective-permute-done((f32[2,128,128]{2,1,0:T(8,128)S(1)}, f32[2,128,128]{2,1,0:T(8,128)S(1)}, u32[]{:S(2)}, u32[]{:S(2)}) %collective-permute-start.18) | collective-permute-done | bytes 131104 | tf_op jit(solution)/shard_map/ppermute | solution.py:453
  63.8 6.3 %shard_map.107 = (f32[4,64,256]{2,1,0:T(8,128)S(1)}, f32[64,256]{1,0:T(8,128)S(1)}, f32[64,256]{1,0:T(8,128)S(1)}, f32[192,256]{1,0:T(8,128)S(1)}, f32[128,256]{1,0:T(8,128)S(1)}) custom-call(s32[1,4]{1,0:T(1,128)S(1)} %copy-done.7, s32[1,4]{1,0:T(1,128)S(1)} %collective-permute-done.refs_1_, s32[1,4]{1,0:T(1,128)S(1)} %collective-permute-done.1.refs_2_, ...), custom_call_target="tpu_custom_call" | custom-call | tf_op jit(solution)/shard_map/pallas_call | solution.py:429
  70.2 1.6 %collective-permute-start.22 = (f32[192,256]{1,0:T(8,128)S(1)}, f32[192,256]{1,0:T(8,128)S(1)}, u32[]{:S(2)}, u32[]{:S(2)}) collective-permute-start(f32[192,256]{1,0:T(8,128)S(1)} %get-tuple-element.39), channel_id=1, source_target_pairs={{0,16},{1,17},{2,18},{3,19},{4,20},{5,21},{6,22},{7,23},{8,0},{9,1... | collective-permute-start | bytes 589832 | tf_op jit(solution)/shard_map/ppermute | solution.py:453
  71.8 0.1 collective-permute-start.23
  71.9 0.4 collective-permute-start.24
  72.3 3.9 %collective-permute-done.22 = f32[192,256]{1,0:T(8,128)S(1)} collective-permute-done((f32[192,256]{1,0:T(8,128)S(1)}, f32[192,256]{1,0:T(8,128)S(1)}, u32[]{:S(2)}, u32[]{:S(2)}) %collective-permute-start.22) | collective-permute-done | bytes 196640 | tf_op jit(solution)/shard_map/ppermute | solution.py:453
  76.2 1.7 %collective-permute-done.23 = f32[128,256]{1,0:T(8,128)S(1)} collective-permute-done((f32[128,256]{1,0:T(8,128)S(1)}, f32[128,256]{1,0:T(8,128)S(1)}, u32[]{:S(2)}, u32[]{:S(2)}) %collective-permute-start.23) | collective-permute-done | bytes 131104 | tf_op jit(solution)/shard_map/ppermute | solution.py:453
  78.0 0.7 select_bitcast_fusion
  78.7 0.0 collective-permute-done.24
  78.7 0.7 fusion.1
  (13 shorter events, 0.1 us)
Async XLA Ops:
  1.6 8.2 %collective-permute-start.3 = (f32[2,64,256]{2,1,0:T(8,128)S(1)}, f32[2,64,256]{2,1,0:T(8,128)S(1)}, u32[]{:S(2)}, u32[]{:S(2)}) collective-permute-start(f32[2,64,256]{2,1,0:T(8,128)S(1)} %get-tuple-element.27), channel_id=1, source_target_pairs={{0,8},{1,9},{2,10},{3,11},{4,12},{5,13},{6,14},{7,15},{8,24},{9,25... | collective-permute-start | bytes 393224 | tf_op jit(solution)/shard_map/ppermute | solution.py:453
  2.1 7.7 %collective-permute-start.4 = (f32[2,64,256]{2,1,0:T(8,128)S(1)}, f32[2,64,256]{2,1,0:T(8,128)S(1)}, u32[]{:S(2)}, u32[]{:S(2)}) collective-permute-start(f32[2,64,256]{2,1,0:T(8,128)S(1)} %get-tuple-element.44), channel_id=1, source_target_pairs={{0,0},{1,1},{2,2},{3,3},{4,4},{5,5},{6,6},{7,7},{8,16},{9,17},{10,... | collective-permute-start | bytes 393224 | tf_op jit(solution)/shard_map/ppermute | solution.py:453
  2.8 1.0 %copy-start = (f32[1,4,64,256]{3,2,1,0:T(8,128)S(1)}, f32[1,4,64,256]{3,2,1,0:T(8,128)}, u32[]{:S(2)}) copy-start(f32[1,4,64,256]{3,2,1,0:T(8,128)} %refs_1_.1) | copy-start | bytes 786436
  3.7 1.0 %copy-start.1 = (bf16[4,4,64,256]{3,2,1,0:T(8,128)(2,1)S(1)}, bf16[4,4,64,256]{3,2,1,0:T(8,128)(2,1)}, u32[]{:S(2)}) copy-start(bf16[4,4,64,256]{3,2,1,0:T(8,128)(2,1)} %refs_0_.2) | copy-start | bytes 1572868
  4.8 0.8 copy-start.2
  5.5 0.7 copy-start.3
  6.2 0.7 copy-start.4
  6.9 0.7 copy-start.5
  7.6 0.7 copy-start.6
  8.3 0.7 copy-start.8
  9.8 12.6 %collective-permute-start.6 = (f32[272,128]{1,0:T(8,128)S(1)}, f32[272,128]{1,0:T(8,128)S(1)}, u32[]{:S(2)}, u32[]{:S(2)}) collective-permute-start(f32[272,128]{1,0:T(8,128)S(1)} %shard_map.105.refs_6_), channel_id=1, source_target_pairs={{0,7},{1,0},{2,1},{3,2},{4,3},{5,4},{6,5},{7,6},{8,15},{9,8},{10,9... | collective-permute-start | bytes 417800 | tf_op jit(solution)/shard_map/ppermute | solution.py:453
  15.4 7.1 %collective-permute-start.7 = (f32[272,128]{1,0:T(8,128)S(1)}, f32[272,128]{1,0:T(8,128)S(1)}, u32[]{:S(2)}, u32[]{:S(2)}) collective-permute-start(f32[272,128]{1,0:T(8,128)S(1)} %shard_map.105.refs_6_), channel_id=1, source_target_pairs={{0,6},{1,7},{2,0},{3,1},{4,2},{5,3},{6,4},{7,5},{8,10},{9,11},{10,... | collective-permute-start | bytes 417800 | tf_op jit(solution)/shard_map/ppermute | solution.py:453
  15.9 8.4 %collective-permute-start.5 = (f32[272,128]{1,0:T(8,128)S(1)}, f32[272,128]{1,0:T(8,128)S(1)}, u32[]{:S(2)}, u32[]{:S(2)}) collective-permute-start(f32[272,128]{1,0:T(8,128)S(1)} %shard_map.105.refs_6_), channel_id=1, source_target_pairs={{0,1},{1,2},{2,3},{3,4},{4,5},{5,6},{6,7},{7,0},{8,9},{9,10},{10,1... | collective-permute-start | bytes 417800 | tf_op jit(solution)/shard_map/ppermute | solution.py:453
  16.5 26.2 %collective-permute-start.12 = (f32[2,4,128,128]{3,2,1,0:T(8,128)S(1)}, f32[2,4,128,128]{3,2,1,0:T(8,128)S(1)}, u32[]{:S(2)}, u32[]{:S(2)}) collective-permute-start(f32[2,4,128,128]{3,2,1,0:T(8,128)S(1)} %get-tuple-element.32.refs_14_.refs_19_), channel_id=1, source_target_pairs={{0,8},{1,9},{2,10},{3,11},{4,12},{5,13},{6,14},{7,15},{8,0},{9,1},... | collective-permute-start | bytes 1572872 | tf_op jit(solution)/shard_map/ppermute | solution.py:453
  18.6 37.5 %collective-permute-start.20 = (f32[2,4,128,128]{3,2,1,0:T(8,128)S(1)}, f32[2,4,128,128]{3,2,1,0:T(8,128)S(1)}, u32[]{:S(2)}, u32[]{:S(2)}) collective-permute-start(f32[2,4,128,128]{3,2,1,0:T(8,128)S(1)} %get-tuple-element.32.refs_14_.refs_19_), channel_id=1, source_target_pairs={{0,16},{1,17},{2,18},{3,19},{4,20},{5,21},{6,22},{7,23},{8,8},{9,9... | collective-permute-start | bytes 1572872 | tf_op jit(solution)/shard_map/ppermute | solution.py:453
  22.5 2.7 %collective-permute-start.10 = (f32[272,128]{1,0:T(8,128)S(1)}, f32[272,128]{1,0:T(8,128)S(1)}, u32[]{:S(2)}, u32[]{:S(2)}) collective-permute-start(f32[272,128]{1,0:T(8,128)S(1)} %collective-permute-done.6.refs_8_), channel_id=1, source_target_pairs={{0,8},{1,9},{2,10},{3,11},{4,12},{5,13},{6,14},{7,15},{8,0},{9,1},... | collective-permute-start | bytes 417800 | tf_op jit(solution)/shard_map/ppermute | solution.py:453
  22.6 2.8 %collective-permute-start.11 = (f32[272,128]{1,0:T(8,128)S(1)}, f32[272,128]{1,0:T(8,128)S(1)}, u32[]{:S(2)}, u32[]{:S(2)}) collective-permute-start(f32[272,128]{1,0:T(8,128)S(1)} %collective-permute-done.7.refs_9_), channel_id=1, source_target_pairs={{0,8},{1,9},{2,10},{3,11},{4,12},{5,13},{6,14},{7,15},{8,0},{9,1},... | collective-permute-start | bytes 417800 | tf_op jit(solution)/shard_map/ppermute | solution.py:453
  24.3 1.9 %collective-permute-start.9 = (f32[272,128]{1,0:T(8,128)S(1)}, f32[272,128]{1,0:T(8,128)S(1)}, u32[]{:S(2)}, u32[]{:S(2)}) collective-permute-start(f32[272,128]{1,0:T(8,128)S(1)} %collective-permute-done.5.refs_7_), channel_id=1, source_target_pairs={{0,8},{1,9},{2,10},{3,11},{4,12},{5,13},{6,14},{7,15},{8,0},{9,1},... | collective-permute-start | bytes 417800 | tf_op jit(solution)/shard_map/ppermute | solution.py:453
  26.2 37.6 %collective-permute-start.19 = (f32[2,4,128,128]{3,2,1,0:T(8,128)S(1)}, f32[2,4,128,128]{3,2,1,0:T(8,128)S(1)}, u32[]{:S(2)}, u32[]{:S(2)}) collective-permute-start(f32[2,4,128,128]{3,2,1,0:T(8,128)S(1)} %get-tuple-element.33.refs_15_.refs_20_), channel_id=1, source_target_pairs={{0,8},{1,9},{2,10},{3,11},{4,12},{5,13},{6,14},{7,15},{8,0},{9,1},... | collective-permute-start | bytes 1572872 | tf_op jit(solution)/shard_map/ppermute | solution.py:453
  26.6 37.3 %collective-permute-start.21 = (f32[2,4,128,128]{3,2,1,0:T(8,128)S(1)}, f32[2,4,128,128]{3,2,1,0:T(8,128)S(1)}, u32[]{:S(2)}, u32[]{:S(2)}) collective-permute-start(f32[2,4,128,128]{3,2,1,0:T(8,128)S(1)} %get-tuple-element.33.refs_15_.refs_20_), channel_id=1, source_target_pairs={{0,16},{1,17},{2,18},{3,19},{4,20},{5,21},{6,22},{7,23},{8,8},{9,9... | collective-permute-start | bytes 1572872 | tf_op jit(solution)/shard_map/ppermute | solution.py:453
  31.1 1.3 %collective-permute-start = (s32[1,4]{1,0:T(1,128)}, s32[1,4]{1,0:T(1,128)S(1)}, u32[]{:S(2)}, u32[]{:S(2)}) collective-permute-start(s32[1,4]{1,0:T(1,128)} %refs_0_.4), channel_id=1, source_target_pairs={{0,8},{1,9},{2,10},{3,11},{4,12},{5,13},{6,14},{7,15},{8,0},{9,1},... | collective-permute-start | bytes 56 | tf_op jit(solution)/shard_map/ppermute | solution.py:453
  32.4 5.9 %collective-permute-start.1 = (s32[1,4]{1,0:T(1,128)}, s32[1,4]{1,0:T(1,128)S(1)}, u32[]{:S(2)}, u32[]{:S(2)}) collective-permute-start(s32[1,4]{1,0:T(1,128)} %refs_0_.4), channel_id=1, source_target_pairs={{0,16},{1,17},{2,18},{3,19},{4,20},{5,21},{6,22},{7,23},{8,24},{9,... | collective-permute-start | bytes 56 | tf_op jit(solution)/shard_map/ppermute | solution.py:453
  38.3 3.1 %collective-permute-start.2 = (s32[1,4]{1,0:T(1,128)}, s32[1,4]{1,0:T(1,128)S(1)}, u32[]{:S(2)}, u32[]{:S(2)}) collective-permute-start(s32[1,4]{1,0:T(1,128)} %refs_0_.4), channel_id=1, source_target_pairs={{0,24},{1,25},{2,26},{3,27},{4,28},{5,29},{6,30},{7,31},{8,16},{9,... | collective-permute-start | bytes 56 | tf_op jit(solution)/shard_map/ppermute | solution.py:453
  41.4 1.4 %collective-permute-start.8 = (f32[272,128]{1,0:T(8,128)S(1)}, f32[272,128]{1,0:T(8,128)S(1)}, u32[]{:S(2)}, u32[]{:S(2)}) collective-permute-start(f32[272,128]{1,0:T(8,128)S(1)} %shard_map.105.refs_6_), channel_id=1, source_target_pairs={{0,8},{1,9},{2,10},{3,11},{4,12},{5,13},{6,14},{7,15},{8,0},{9,1},... | collective-permute-start | bytes 417800 | tf_op jit(solution)/shard_map/ppermute | solution.py:453
  42.8 0.7 copy-start.7
  51.4 9.2 %collective-permute-start.13 = (f32[2,128,128]{2,1,0:T(8,128)S(1)}, f32[2,128,128]{2,1,0:T(8,128)S(1)}, u32[]{:S(2)}, u32[]{:S(2)}) collective-permute-start(f32[2,128,128]{2,1,0:T(8,128)S(1)} %get-tuple-element.35), channel_id=1, source_target_pairs={{0,1},{1,2},{2,3},{3,4},{4,5},{5,6},{6,7},{7,0},{8,9},{9,10},{10,1... | collective-permute-start | bytes 393224 | tf_op jit(solution)/shard_map/ppermute | solution.py:453
  51.4 9.2 %collective-permute-start.14 = (f32[2,128,128]{2,1,0:T(8,128)S(1)}, f32[2,128,128]{2,1,0:T(8,128)S(1)}, u32[]{:S(2)}, u32[]{:S(2)}) collective-permute-start(f32[2,128,128]{2,1,0:T(8,128)S(1)} %get-tuple-element.35), channel_id=1, source_target_pairs={{0,7},{1,0},{2,1},{3,2},{4,3},{5,4},{6,5},{7,6},{8,15},{9,8},{10,9... | collective-permute-start | bytes 393224 | tf_op jit(solution)/shard_map/ppermute | solution.py:453
  56.1 6.4 %collective-permute-start.15 = (f32[2,128,128]{2,1,0:T(8,128)S(1)}, f32[2,128,128]{2,1,0:T(8,128)S(1)}, u32[]{:S(2)}, u32[]{:S(2)}) collective-permute-start(f32[2,128,128]{2,1,0:T(8,128)S(1)} %get-tuple-element.35), channel_id=1, source_target_pairs={{0,6},{1,7},{2,0},{3,1},{4,2},{5,3},{6,4},{7,5},{8,10},{9,11},{10,... | collective-permute-start | bytes 393224 | tf_op jit(solution)/shard_map/ppermute | solution.py:453
  60.6 1.9 %collective-permute-start.16 = (f32[2,128,128]{2,1,0:T(8,128)S(1)}, f32[2,128,128]{2,1,0:T(8,128)S(1)}, u32[]{:S(2)}, u32[]{:S(2)}) collective-permute-start(f32[2,128,128]{2,1,0:T(8,128)S(1)} %collective-permute-done.13.refs_7_), channel_id=1, source_target_pairs={{0,8},{1,9},{2,10},{3,11},{4,12},{5,13},{6,14},{7,15},{8,0},{9,1},... | collective-permute-start | bytes 393224 | tf_op jit(solution)/shard_map/ppermute | solution.py:453
  60.6 1.9 %collective-permute-start.17 = (f32[2,128,128]{2,1,0:T(8,128)S(1)}, f32[2,128,128]{2,1,0:T(8,128)S(1)}, u32[]{:S(2)}, u32[]{:S(2)}) collective-permute-start(f32[2,128,128]{2,1,0:T(8,128)S(1)} %collective-permute-done.14.refs_8_), channel_id=1, source_target_pairs={{0,8},{1,9},{2,10},{3,11},{4,12},{5,13},{6,14},{7,15},{8,0},{9,1},... | collective-permute-start | bytes 393224 | tf_op jit(solution)/shard_map/ppermute | solution.py:453
  62.5 1.3 %collective-permute-start.18 = (f32[2,128,128]{2,1,0:T(8,128)S(1)}, f32[2,128,128]{2,1,0:T(8,128)S(1)}, u32[]{:S(2)}, u32[]{:S(2)}) collective-permute-start(f32[2,128,128]{2,1,0:T(8,128)S(1)} %collective-permute-done.15.refs_9_), channel_id=1, source_target_pairs={{0,8},{1,9},{2,10},{3,11},{4,12},{5,13},{6,14},{7,15},{8,0},{9,1},... | collective-permute-start | bytes 393224 | tf_op jit(solution)/shard_map/ppermute | solution.py:453
  70.2 6.0 %collective-permute-start.22 = (f32[192,256]{1,0:T(8,128)S(1)}, f32[192,256]{1,0:T(8,128)S(1)}, u32[]{:S(2)}, u32[]{:S(2)}) collective-permute-start(f32[192,256]{1,0:T(8,128)S(1)} %get-tuple-element.39), channel_id=1, source_target_pairs={{0,16},{1,17},{2,18},{3,19},{4,20},{5,21},{6,22},{7,23},{8,0},{9,1... | collective-permute-start | bytes 589832 | tf_op jit(solution)/shard_map/ppermute | solution.py:453
  71.8 6.2 %collective-permute-start.23 = (f32[128,256]{1,0:T(8,128)S(1)}, f32[128,256]{1,0:T(8,128)S(1)}, u32[]{:S(2)}, u32[]{:S(2)}) collective-permute-start(f32[128,256]{1,0:T(8,128)S(1)} %get-tuple-element.40), channel_id=1, source_target_pairs={{0,24},{1,25},{2,26},{3,27},{4,28},{5,29},{6,30},{7,31},{8,16},{9,... | collective-permute-start | bytes 393224 | tf_op jit(solution)/shard_map/ppermute | solution.py:453
  71.9 6.8 %collective-permute-start.24 = (f32[64,256]{1,0:T(8,128)S(1)}, f32[64,256]{1,0:T(8,128)S(1)}, u32[]{:S(2)}, u32[]{:S(2)}) collective-permute-start(f32[64,256]{1,0:T(8,128)S(1)} %get-tuple-element.43), channel_id=1, source_target_pairs={{0,8},{1,9},{2,10},{3,11},{4,12},{5,13},{6,14},{7,15},{8,0},{9,1},... | collective-permute-start | bytes 196616 | tf_op jit(solution)/shard_map/ppermute | solution.py:453

commit v4 on v3

--- a/solution.py
+++ b/solution.py
@@ -11,7 +11,8 @@
 CZ = 64
 GROUP = 4
 FIELD_ROWS = 16
-VMEM_BYTES = 48 * 2**20
+VMEM_BYTES = 16 * 2**20
+WHOLE_VMEM_BYTES = 62 * 2**20
 IN_VMEM = pl.BlockSpec(memory_space=pltpu.VMEM)
 IN_SMEM = pl.BlockSpec(memory_space=pltpu.SMEM)
 
@@ -231,14 +232,18 @@
         scratch_shapes=[pltpu.VMEM((rows, lanes), jnp.float32)]
         + [pltpu.VMEM(each.shape, each.dtype) for each in operands]
         + [pltpu.SemaphoreType.DMA((len(operands),))],
-        compiler_params=pltpu.CompilerParams(vmem_limit_bytes=VMEM_BYTES),
+        compiler_params=pltpu.CompilerParams(vmem_limit_bytes=WHOLE_VMEM_BYTES),
     )(*operands)
 
 
-def pack_kernel(start, moved_high, moved_low, out, scratch):
+def pack_kernel(*refs):
+    kinds, start, moved_high, moved_low, out, info, scratch = refs[:4], *refs[4:]
     sec, odd = position()
     rows = scratch.shape[0]
     out[...] = start[...]
+    steps = kinds[0].shape[1]
+    for step in range(info.shape[1]):
+        info[0, step] = kind_of(kinds, step, steps)
 
     def fill(source):
         for i in range(source.shape[0]):
@@ -271,7 +276,7 @@
     )
 
 
-def run_steps(kinds, steps, taps, weights, begun, count, slab, other, first, second, factor, after):
+def run_steps(info, taps, weights, begun, count, slab, other, first, second, factor, after):
     tap = [taps[i : i + 1, :] for i in range(6)]
     extent, rows, lanes = slab.shape
     buffers = (slab, other)
@@ -293,7 +298,7 @@
         source, target = buffers[step % 2], buffers[1 - step % 2]
         begin, width = step + 1, extent - 2 * step - 2
         groups = -(-width // GROUP)
-        kind = kind_of(kinds, begun + step, steps)
+        kind = info[0, begun + step]
 
         def at(i, begin=begin, width=width):
             return jnp.minimum(begin + i * GROUP, begin + width - GROUP)
@@ -329,9 +334,9 @@
 
 
 def early_kernel(half, *refs):
-    kinds, taps, weights, pieces, series = refs[:4], refs[4], refs[5], refs[6:14], refs[14:17]
-    middle, half_out, kept, total, factor = refs[17:22]
-    slab, other, first, second, scratch = refs[22:]
+    info, taps, weights, pieces, stored = refs[0], refs[1], refs[2], refs[3:11], refs[11:13]
+    middle, half_out, kept, total, factor = refs[13:18]
+    slab, other, first, second, scratch = refs[18:]
     sec, odd = position()
     planes, rows = middle.shape[:2]
     pair = planes // 2
@@ -341,28 +346,28 @@
             slab[start + i] = piece[i * rows : (i + 1) * rows]
     scratch[...] = jnp.exp(-jnp.concatenate([piece[pair * rows :] for piece in pieces], axis=0)).T
     spread_factor(reorder(scratch), factor, starts, factor.shape[0], pair)
-    span = series[0].shape[0]
+    span = stored[0].shape[0]
     steps = 2 * span
     total[...] = jnp.zeros(total.shape, jnp.float32)
 
     def after(step, state):
-        @pl.when(sec == 0)
+        @pl.when(sec == step // steps)
         def _():
-            total[...] += state[half : half + planes] * series[step // span][step % span]
+            total[...] += state[half : half + planes] * stored[step % steps // span][step % span]
             if step + 1 == steps:
                 kept[...] = state[half : half + planes]
 
-    run_steps(kinds, steps, taps, weights, 0, half, slab, other, first, second, factor, after)
+    run_steps(info, taps, weights, 0, half, slab, other, first, second, factor, after)
     state = (slab, other)[half % 2]
     middle[...] = state[half : half + planes]
     half_out[...] = state[pl.ds(half + pair * odd, pair)]
 
 
 def late_kernel(half, last, *refs):
-    kinds, taps, weights, middle, pieces, factor = refs[:4], refs[4], refs[5], refs[6], refs[7:13], refs[13]
-    kept, total_in, series, stored = refs[14], refs[15], refs[16:19], refs[19:21]
-    handoff, share, to_pair, to_across, to_corner = refs[21:26]
-    slab, other, first, second, scratch, total, saved, whole = refs[26:]
+    info, taps, weights, middle, pieces, factor = refs[0], refs[1], refs[2], refs[3], refs[4:10], refs[10]
+    kept, total_in, total_beside, series, stored = refs[11], refs[12], refs[13], refs[14:17], refs[17:19]
+    handoff, share, to_pair, to_across, to_corner = refs[19:24]
+    slab, other, first, second, scratch, total, saved, whole = refs[24:]
     sec, odd = position()
     planes, rows = middle.shape[:2]
     pair = planes // 2
@@ -373,7 +378,12 @@
             slab[start + i] = piece[i]
     span = series[0].shape[0]
     steps = 2 * span
-    total[...] = total_in[...]
+    total[...] = jnp.zeros(total.shape, jnp.float32)
+
+    @pl.when(sec == 0)
+    def _():
+        total[...] = total_in[...] + total_beside[...]
+
     saved[...] = kept[...]
 
     def after(step, state):
@@ -396,7 +406,7 @@
             def _():
                 total[...] += state[half : half + planes] * stored[step % steps // span][step % span]
 
-    run_steps(kinds, steps, taps, weights, half, half, slab, other, first, second, factor, after)
+    run_steps(info, taps, weights, half, half, slab, other, first, second, factor, after)
     state = (slab, other)[half % 2]
 
     @pl.when(sec == last)
@@ -461,7 +471,7 @@
     early_stored, late_stored, start, taps, weights = prepare(
         backward, incoming, fields, axial_taps, lateral_taps, depth_taps, bend_diagonal, bend_coupling
     )
-    early_next, early_last = send(early_stored, beside), send(early_stored, crossing)
+    early_last = send(early_stored, crossing)
 
     tile = pltpu.VMEM((rows, lanes), jnp.float32)
     slab = pltpu.VMEM((planes + 2 * half, rows, lanes), jnp.float32)
@@ -477,9 +487,17 @@
         ]
         return own, [send(each, beside) for each in own]
 
-    (piece,) = call(
-        pack_kernel, [(pair * rows + FIELD_ROWS, lanes)], [tile], [start, moved_high, moved_low]
-    )
+    piece, info = pl.pallas_call(
+        pack_kernel,
+        in_specs=[IN_SMEM] * 4 + [IN_VMEM] * 3,
+        out_specs=[IN_VMEM, IN_SMEM],
+        out_shape=[
+            jax.ShapeDtypeStruct(start.shape, jnp.float32),
+            jax.ShapeDtypeStruct((1, TICKS * steps), jnp.int32),
+        ],
+        scratch_shapes=[tile],
+        compiler_params=pltpu.CompilerParams(vmem_limit_bytes=VMEM_BYTES),
+    )(*kinds, start, moved_high, moved_low)
     own, swapped = exchange(piece)
     late_stored, *swapped = lax.optimization_barrier((late_stored, *swapped))
     late_next, late_last = send(late_stored, beside), send(late_stored, crossing)
@@ -488,8 +506,8 @@
         [(planes, rows, lanes), (pair, rows, lanes), (planes, rows, lanes), (planes, rows, lanes)]
         + [(fields.shape[0], planes + 2 * half, rows, lanes)],
         work,
-        [taps, weights, piece, *own, send(piece, beside), *swapped, early_stored, late_stored, early_next],
-        kinds,
+        [taps, weights, piece, *own, send(piece, beside), *swapped, early_stored, late_stored],
+        [info],
     )
     own, swapped = exchange(piece)
     held = planes * (orients // n_sec)
@@ -499,9 +517,9 @@
         + [(held, cells)] * 2
         + [(held + pair * orients, cells), (pair * orients, cells)],
         work + [inner, inner, pltpu.VMEM((orients, cells), jnp.float32)],
-        [taps, weights, middle, *own, *swapped, factor, kept, total]
+        [taps, weights, middle, *own, *swapped, factor, kept, total, send(total, beside)]
         + [late_next, early_last, late_last, early_stored, late_stored],
-        kinds,
+        [info],
     )
     to_pair = send(to_pair, beside)
     to_across = send(to_across, (2, 0, 3, 1))

time: 79.9 us -> 68.6 us (0.86)
  waiting for transfers between devices: 25.1 us -> 16.4 us
  local copies, waits for them, and re-layouts: 7.8 us -> 6.22 us
  starting transfers between devices: 29.1 us -> 28.2 us
    ppermute x25, waiting for transfers between devices: 25.1 us -> 16.4 us  [send(): return lax.ppermute(array, ('sec', 'gx'), pairs)]
    pallas_call x3 -> x2, Pallas kernels: 14.3 us -> 11.3 us  [call(): pl.pallas_call(kernel, in_specs=[IN_SMEM] * len(scalars) + [IN_VMEM] * le...]
    pallas_call x1, Pallas kernels: 0.84 us -> 2.68 us  [prepare(): pl.pallas_call(prepare_kernel, in_specs=[pl.BlockSpec(memory_space=pltpu....]
    unnamed x18 -> x12, local copies, waits for them, and re-layouts: 6.8 us -> 5.23 us
    pallas_call x0 -> x1, Pallas kernels: none -> 1.2 us  [paired(): pl.pallas_call(pack_kernel, in_specs=[IN_SMEM] * 4 + [IN_VMEM] * 3, out_s...]
    ppermute x25, starting transfers between devices: 29.1 us -> 28.2 us  [send(): return lax.ppermute(array, ('sec', 'gx'), pairs)]
  transfers between devices with their start and end apart: 25 -> 25, of which waited for: 11 -> 10; matrix products, arithmetic and copies ran while one was open for 1% -> 1% of each run, Pallas kernels for 11% -> 13%
where the time goes in v4:
time: 68.6 us; the launch traced here: 68.2 us
  starting transfers between devices  28.2 us (41%)
  waiting for transfers between devices  16.4 us (24%)
  Pallas kernels  15.2 us (22%)
  local copies, waits for them, and re-layouts  6.22 us (9%)
  other arithmetic  1.41 us (2%)
  between operations  0.78 us (1%)
    ppermute x25, starting transfers between devices, send(): return lax.ppermute(array, ('sec', 'gx'), pairs)  28.2 us
    ppermute x25, waiting for transfers between devices, send(): return lax.ppermute(array, ('sec', 'gx'), pairs)  16.4 us
    pallas_call x2, Pallas kernels, call(): pl.pallas_call(kernel, in_specs=[IN_SMEM] * len(scalars) + [IN_VMEM] * le...  11.3 us
    unnamed x12, local copies, waits for them, and re-layouts  5.23 us
    pallas_call x1, Pallas kernels, prepare(): pl.pallas_call(prepare_kernel, in_specs=[pl.BlockSpec(memory_space=pltpu....  2.68 us
  transfers between devices with their start and end apart: 25, of which 10 were waited for; matrix products, arithmetic and copies ran while one was open for 1% of the time, Pallas kernels for 13%

profile of v4, /device:TPU:0, one launch (start us, length us, event | category | flops | bytes accessed | tf_op | source)
XLA Modules:
  0.0 68.2 jit_solution(10700692736276607192)
XLA Ops:
  0.6 1.0 %slice_bitcast_fusion = (f32[2,64,256]{2,1,0:T(8,128)S(1)}, f32[2,64,256]{2,1,0:T(8,128)S(1)}) fusion(f32[1,4,64,256]{3,2,1,0:T(8,128)} %refs_1_.1), kind=kLoop, calls=%fused_computation.2 | loop fusion | bytes 524288 | tf_op jit(solution)/shard_map/slice | solution.py:469
  1.6 0.5 collective-permute-start.3
  2.1 0.7 collective-permute-start.4
  2.8 4.0 %collective-permute-start = (s32[1,4]{1,0:T(1,128)}, s32[1,4]{1,0:T(1,128)S(1)}, u32[]{:S(2)}, u32[]{:S(2)}) collective-permute-start(s32[1,4]{1,0:T(1,128)} %refs_0_.2), channel_id=1, source_target_pairs={{0,8},{1,9},{2,10},{3,11},{4,12},{5,13},{6,14},{7,15},{8,0},{9,1},... | collective-permute-start | bytes 56 | tf_op jit(solution)/shard_map/ppermute | solution.py:463
  6.7 1.1 %collective-permute-start.1 = (s32[1,4]{1,0:T(1,128)}, s32[1,4]{1,0:T(1,128)S(1)}, u32[]{:S(2)}, u32[]{:S(2)}) collective-permute-start(s32[1,4]{1,0:T(1,128)} %refs_0_.2), channel_id=1, source_target_pairs={{0,16},{1,17},{2,18},{3,19},{4,20},{5,21},{6,22},{7,23},{8,24},{9,... | collective-permute-start | bytes 56 | tf_op jit(solution)/shard_map/ppermute | solution.py:463
  7.8 0.3 collective-permute-start.2
  8.1 2.7 %shard_map.104 = (f32[2,4,128,128]{3,2,1,0:T(8,128)}, f32[2,4,128,128]{3,2,1,0:T(8,128)}, f32[272,128]{1,0:T(8,128)}, f32[8,128]{1,0:T(8,128)}, bf16[256,256]{1,0:T(8,128)(2,1)}) custom-call(bf16[4,4,64,256]{3,2,1,0:T(8,128)(2,1)} %refs_0_.1, f32[1,4,64,256]{3,2,1,0:T(8,128)} %refs_1_.1, f32[3,4,256]{2,1,0:T(4,128)} %refs_2_.1, f32[3,64]{1,0:T(4,128)} %refs_3_.1, ...), custom_call_target="tpu_custom_call" | custom-call | tf_op jit(solution)/shard_map/pallas_call | solution.py:224
  10.8 0.0 collective-permute-done.refs_1_
  10.8 0.0 collective-permute-done.1.refs_2_
  10.9 0.1 collective-permute-done.2.refs_3_
  10.9 0.0 collective-permute-done.3.refs_5_
  10.9 0.0 collective-permute-done.4.refs_6_
  11.0 0.9 %copy-done.3 = f32[272,128]{1,0:T(8,128)S(1)} copy-done((f32[272,128]{1,0:T(8,128)S(1)}, f32[272,128]{1,0:T(8,128)}, u32[]{:S(2)}) %copy-start.3) | copy-done | bytes 139288
  11.9 0.7 copy-done.5
  12.5 1.2 %shard_map.105 = (f32[272,128]{1,0:T(8,128)S(1)}, s32[1,12]{1,0:T(1,128)S(1)}) custom-call(s32[1,4]{1,0:T(1,128)S(1)} %copy-done.5, s32[1,4]{1,0:T(1,128)S(1)} %collective-permute-done.refs_1_, s32[1,4]{1,0:T(1,128)S(1)} %collective-permute-done.1.refs_2_, s32[1,4]{1,0:T(1,128)S(1)} %collective-permute-done.2.refs_3_, f32[272,128]{1,0:T(8,128)S(1)} %copy-done.3, ...), custom_call_target="tpu_custom_call" | custom-call | tf_op jit(solution)/shard_map/pallas_call | solution.py:490
  13.7 5.0 %collective-permute-start.6 = (f32[272,128]{1,0:T(8,128)S(1)}, f32[272,128]{1,0:T(8,128)S(1)}, u32[]{:S(2)}, u32[]{:S(2)}) collective-permute-start(f32[272,128]{1,0:T(8,128)S(1)} %get-tuple-element.31.refs_3_), channel_id=1, source_target_pairs={{0,7},{1,0},{2,1},{3,2},{4,3},{5,4},{6,5},{7,6},{8,15},{9,8},{10,9... | collective-permute-start | bytes 417800 | tf_op jit(solution)/shard_map/ppermute | solution.py:463
  18.7 0.4 collective-permute-start.7
  19.2 0.6 collective-permute-start.5
  19.8 3.0 %collective-permute-start.20 = (f32[2,4,128,128]{3,2,1,0:T(8,128)}, f32[2,4,128,128]{3,2,1,0:T(8,128)S(1)}, u32[]{:S(2)}, u32[]{:S(2)}) collective-permute-start(f32[2,4,128,128]{3,2,1,0:T(8,128)} %get-tuple-element.36.refs_11_.refs_17_), channel_id=1, source_target_pairs={{0,16},{1,17},{2,18},{3,19},{4,20},{5,21},{6,22},{7,23},{8,8},{9,9... | collective-permute-start | bytes 1572872 | tf_op jit(solution)/shard_map/ppermute | solution.py:463
  22.9 0.0 collective-permute-done.6.refs_5_
  22.9 0.1 collective-permute-start.10
  22.9 2.7 %collective-permute-done.7.refs_6_ = f32[272,128]{1,0:T(8,128)S(1)} collective-permute-done((f32[272,128]{1,0:T(8,128)S(1)}, f32[272,128]{1,0:T(8,128)S(1)}, u32[]{:S(2)}, u32[]{:S(2)}) %collective-permute-start.7) | collective-permute-done | bytes 139296 | tf_op jit(solution)/shard_map/ppermute | solution.py:463
  25.6 1.1 %collective-permute-start.11 = (f32[272,128]{1,0:T(8,128)S(1)}, f32[272,128]{1,0:T(8,128)S(1)}, u32[]{:S(2)}, u32[]{:S(2)}) collective-permute-start(f32[272,128]{1,0:T(8,128)S(1)} %collective-permute-done.7.refs_6_), channel_id=1, source_target_pairs={{0,8},{1,9},{2,10},{3,11},{4,12},{5,13},{6,14},{7,15},{8,0},{9,1},... | collective-permute-start | bytes 417800 | tf_op jit(solution)/shard_map/ppermute | solution.py:463
  26.7 0.9 %collective-permute-done.5.refs_4_ = f32[272,128]{1,0:T(8,128)S(1)} collective-permute-done((f32[272,128]{1,0:T(8,128)S(1)}, f32[272,128]{1,0:T(8,128)S(1)}, u32[]{:S(2)}, u32[]{:S(2)}) %collective-permute-start.5) | collective-permute-done | bytes 139296 | tf_op jit(solution)/shard_map/ppermute | solution.py:463
  27.5 0.0 collective-permute-start.9
  27.5 0.5 collective-permute-start.8
  28.0 0.0 collective-permute-done.10.refs_9_
  28.0 0.0 collective-permute-done.11.refs_10_
  28.1 0.8 %collective-permute-done.9.refs_8_ = f32[272,128]{1,0:T(8,128)S(1)} collective-permute-done((f32[272,128]{1,0:T(8,128)S(1)}, f32[272,128]{1,0:T(8,128)S(1)}, u32[]{:S(2)}, u32[]{:S(2)}) %collective-permute-start.9) | collective-permute-done | bytes 139296 | tf_op jit(solution)/shard_map/ppermute | solution.py:463
  28.9 0.1 collective-permute-start.19
  29.0 2.5 %collective-permute-start.21 = (f32[2,4,128,128]{3,2,1,0:T(8,128)}, f32[2,4,128,128]{3,2,1,0:T(8,128)S(1)}, u32[]{:S(2)}, u32[]{:S(2)}) collective-permute-start(f32[2,4,128,128]{3,2,1,0:T(8,128)} %get-tuple-element.37.refs_12_.refs_18_), channel_id=1, source_target_pairs={{0,16},{1,17},{2,18},{3,19},{4,20},{5,21},{6,22},{7,23},{8,8},{9,9... | collective-permute-start | bytes 1572872 | tf_op jit(solution)/shard_map/ppermute | solution.py:463
  31.6 0.0 collective-permute-done.8.refs_7_
  31.6 0.0 copy-start
  31.6 1.0 %copy-done = f32[2,4,128,128]{3,2,1,0:T(8,128)S(1)} copy-done((f32[2,4,128,128]{3,2,1,0:T(8,128)S(1)}, f32[2,4,128,128]{3,2,1,0:T(8,128)}, u32[]{:S(2)}) %copy-start) | copy-done | bytes 524312
  32.6 1.0 %copy-done.1 = f32[2,4,128,128]{3,2,1,0:T(8,128)S(1)} copy-done((f32[2,4,128,128]{3,2,1,0:T(8,128)S(1)}, f32[2,4,128,128]{3,2,1,0:T(8,128)}, u32[]{:S(2)}) %copy-start.1) | copy-done | bytes 524312
  33.7 0.9 %copy-done.2 = bf16[256,256]{1,0:T(8,128)(2,1)S(1)} copy-done((bf16[256,256]{1,0:T(8,128)(2,1)S(1)}, bf16[256,256]{1,0:T(8,128)(2,1)}, u32[]{:S(2)}) %copy-start.2) | copy-done | bytes 131096
  34.6 0.7 %copy-done.4 = f32[8,128]{1,0:T(8,128)S(1)} copy-done((f32[8,128]{1,0:T(8,128)S(1)}, f32[8,128]{1,0:T(8,128)}, u32[]{:S(2)}) %copy-start.4) | copy-done | bytes 4120
  35.3 6.3 %shard_map.106 = (f32[4,128,128]{2,1,0:T(8,128)S(1)}, f32[2,128,128]{2,1,0:T(8,128)S(1)}, f32[4,128,128]{2,1,0:T(8,128)S(1)}, f32[4,128,128]{2,1,0:T(8,128)S(1)}, f32[3,16,128,128]{3,2,1,0:T(8,128)S(1)}) custom-call(s32[1,12]{1,0:T(1,128)S(1)} %get-tuple-element.28.refs_0_, f32[8,128]{1,0:T(8,128)S(1)} %copy-done.4, bf16[256,256]{1,0:T(8,128)(2,1)S(1)} %copy-done.2, ...), custom_call_target="tpu_custom_call" | custom-call | tf_op jit(solution)/shard_map/pallas_call | solution.py:439
  41.6 0.1 collective-permute-start.12
  41.7 4.7 %collective-permute-start.13 = (f32[2,128,128]{2,1,0:T(8,128)S(1)}, f32[2,128,128]{2,1,0:T(8,128)S(1)}, u32[]{:S(2)}, u32[]{:S(2)}) collective-permute-start(f32[2,128,128]{2,1,0:T(8,128)S(1)} %get-tuple-element.39), channel_id=1, source_target_pairs={{0,7},{1,0},{2,1},{3,2},{4,3},{5,4},{6,5},{7,6},{8,15},{9,8},{10,9... | collective-permute-start | bytes 393224 | tf_op jit(solution)/shard_map/ppermute | solution.py:463
  46.4 0.0 collective-permute-done.20.refs_15_
  46.4 0.9 %collective-permute-start.14 = (f32[2,128,128]{2,1,0:T(8,128)S(1)}, f32[2,128,128]{2,1,0:T(8,128)S(1)}, u32[]{:S(2)}, u32[]{:S(2)}) collective-permute-start(f32[2,128,128]{2,1,0:T(8,128)S(1)} %get-tuple-element.39), channel_id=1, source_target_pairs={{0,6},{1,7},{2,0},{3,1},{4,2},{5,3},{6,4},{7,5},{8,10},{9,11},{10,... | collective-permute-start | bytes 393224 | tf_op jit(solution)/shard_map/ppermute | solution.py:463
  47.3 3.4 %collective-permute-done.12.refs_4_ = f32[2,128,128]{2,1,0:T(8,128)S(1)} collective-permute-done((f32[2,128,128]{2,1,0:T(8,128)S(1)}, f32[2,128,128]{2,1,0:T(8,128)S(1)}, u32[]{:S(2)}, u32[]{:S(2)}) %collective-permute-start.12) | collective-permute-done | bytes 131104 | tf_op jit(solution)/shard_map/ppermute | solution.py:463
  50.7 0.0 collective-permute-start.15
  50.7 0.0 collective-permute-done.13.refs_5_
  50.7 0.5 collective-permute-start.18
  51.2 1.3 %collective-permute-done.14.refs_6_ = f32[2,128,128]{2,1,0:T(8,128)S(1)} collective-permute-done((f32[2,128,128]{2,1,0:T(8,128)S(1)}, f32[2,128,128]{2,1,0:T(8,128)S(1)}, u32[]{:S(2)}, u32[]{:S(2)}) %collective-permute-start.14) | collective-permute-done | bytes 131104 | tf_op jit(solution)/shard_map/ppermute | solution.py:463
  52.6 0.0 collective-permute-start.16
  52.6 0.0 collective-permute-done.15.refs_7_
  52.6 0.5 collective-permute-start.17
  53.1 0.8 %collective-permute-done.16.refs_8_ = f32[2,128,128]{2,1,0:T(8,128)S(1)} collective-permute-done((f32[2,128,128]{2,1,0:T(8,128)S(1)}, f32[2,128,128]{2,1,0:T(8,128)S(1)}, u32[]{:S(2)}, u32[]{:S(2)}) %collective-permute-start.16) | collective-permute-done | bytes 131104 | tf_op jit(solution)/shard_map/ppermute | solution.py:463
  53.9 0.2 collective-permute-done.17.refs_9_
  54.1 0.0 collective-permute-done.18.refs_13_
  54.1 0.0 collective-permute-done.19.refs_14_
  54.1 0.0 collective-permute-done.21.refs_16_
  54.1 5.0 %shard_map.107 = (f32[4,64,256]{2,1,0:T(8,128)S(1)}, f32[64,256]{1,0:T(8,128)S(1)}, f32[64,256]{1,0:T(8,128)S(1)}, f32[192,256]{1,0:T(8,128)S(1)}, f32[128,256]{1,0:T(8,128)S(1)}) custom-call(s32[1,12]{1,0:T(1,128)S(1)} %get-tuple-element.28.refs_0_, f32[8,128]{1,0:T(8,128)S(1)} %copy-done.4, bf16[256,256]{1,0:T(8,128)(2,1)S(1)} %copy-done.2, ...), custom_call_target="tpu_custom_call" | custom-call | tf_op jit(solution)/shard_map/pallas_call | solution.py:439
  59.1 0.8 %collective-permute-start.22 = (f32[192,256]{1,0:T(8,128)S(1)}, f32[192,256]{1,0:T(8,128)S(1)}, u32[]{:S(2)}, u32[]{:S(2)}) collective-permute-start(f32[192,256]{1,0:T(8,128)S(1)} %get-tuple-element.43), channel_id=1, source_target_pairs={{0,16},{1,17},{2,18},{3,19},{4,20},{5,21},{6,22},{7,23},{8,0},{9,1... | collective-permute-start | bytes 589832 | tf_op jit(solution)/shard_map/ppermute | solution.py:463
  59.8 0.8 %collective-permute-start.23 = (f32[128,256]{1,0:T(8,128)S(1)}, f32[128,256]{1,0:T(8,128)S(1)}, u32[]{:S(2)}, u32[]{:S(2)}) collective-permute-start(f32[128,256]{1,0:T(8,128)S(1)} %get-tuple-element.44), channel_id=1, source_target_pairs={{0,24},{1,25},{2,26},{3,27},{4,28},{5,29},{6,30},{7,31},{8,16},{9,... | collective-permute-start | bytes 393224 | tf_op jit(solution)/shard_map/ppermute | solution.py:463
  60.6 0.0 collective-permute-start.24
  60.6 3.7 %collective-permute-done.22 = f32[192,256]{1,0:T(8,128)S(1)} collective-permute-done((f32[192,256]{1,0:T(8,128)S(1)}, f32[192,256]{1,0:T(8,128)S(1)}, u32[]{:S(2)}, u32[]{:S(2)}) %collective-permute-start.22) | collective-permute-done | bytes 196640 | tf_op jit(solution)/shard_map/ppermute | solution.py:463
  64.4 2.4 %collective-permute-done.23 = f32[128,256]{1,0:T(8,128)S(1)} collective-permute-done((f32[128,256]{1,0:T(8,128)S(1)}, f32[128,256]{1,0:T(8,128)S(1)}, u32[]{:S(2)}, u32[]{:S(2)}) %collective-permute-start.23) | collective-permute-done | bytes 131104 | tf_op jit(solution)/shard_map/ppermute | solution.py:463
  66.8 0.7 %select_bitcast_fusion = f32[1,4,64,256]{3,2,1,0:T(8,128)} fusion(f32[4,64,256]{2,1,0:T(8,128)S(1)} %bitcast.9, f32[4,64,256]{2,1,0:T(8,128)S(1)} %get-tuple-element.45, pred[]{:T(512)S(6)} %eq.3), kind=kLoop, calls=%fused_computation.1 | loop fusion | flops 65536 | bytes 786433 | tf_op jit(solution)/shard_map/broadcast_in_dim | solution.py:531
  67.5 0.0 collective-permute-done.24
  67.5 0.7 fusion.1
  (7 shorter events, 0.0 us)
Async XLA Ops:
  1.6 9.3 %collective-permute-start.3 = (f32[2,64,256]{2,1,0:T(8,128)S(1)}, f32[2,64,256]{2,1,0:T(8,128)S(1)}, u32[]{:S(2)}, u32[]{:S(2)}) collective-permute-start(f32[2,64,256]{2,1,0:T(8,128)S(1)} %get-tuple-element.27), channel_id=1, source_target_pairs={{0,8},{1,9},{2,10},{3,11},{4,12},{5,13},{6,14},{7,15},{8,24},{9,25... | collective-permute-start | bytes 393224 | tf_op jit(solution)/shard_map/ppermute | solution.py:463
  2.1 8.9 %collective-permute-start.4 = (f32[2,64,256]{2,1,0:T(8,128)S(1)}, f32[2,64,256]{2,1,0:T(8,128)S(1)}, u32[]{:S(2)}, u32[]{:S(2)}) collective-permute-start(f32[2,64,256]{2,1,0:T(8,128)S(1)} %get-tuple-element.48), channel_id=1, source_target_pairs={{0,0},{1,1},{2,2},{3,3},{4,4},{5,5},{6,6},{7,7},{8,16},{9,17},{10,... | collective-permute-start | bytes 393224 | tf_op jit(solution)/shard_map/ppermute | solution.py:463
  2.8 8.1 %collective-permute-start = (s32[1,4]{1,0:T(1,128)}, s32[1,4]{1,0:T(1,128)S(1)}, u32[]{:S(2)}, u32[]{:S(2)}) collective-permute-start(s32[1,4]{1,0:T(1,128)} %refs_0_.2), channel_id=1, source_target_pairs={{0,8},{1,9},{2,10},{3,11},{4,12},{5,13},{6,14},{7,15},{8,0},{9,1},... | collective-permute-start | bytes 56 | tf_op jit(solution)/shard_map/ppermute | solution.py:463
  6.7 4.1 %collective-permute-start.1 = (s32[1,4]{1,0:T(1,128)}, s32[1,4]{1,0:T(1,128)S(1)}, u32[]{:S(2)}, u32[]{:S(2)}) collective-permute-start(s32[1,4]{1,0:T(1,128)} %refs_0_.2), channel_id=1, source_target_pairs={{0,16},{1,17},{2,18},{3,19},{4,20},{5,21},{6,22},{7,23},{8,24},{9,... | collective-permute-start | bytes 56 | tf_op jit(solution)/shard_map/ppermute | solution.py:463
  7.8 3.1 %collective-permute-start.2 = (s32[1,4]{1,0:T(1,128)}, s32[1,4]{1,0:T(1,128)S(1)}, u32[]{:S(2)}, u32[]{:S(2)}) collective-permute-start(s32[1,4]{1,0:T(1,128)} %refs_0_.2), channel_id=1, source_target_pairs={{0,24},{1,25},{2,26},{3,27},{4,28},{5,29},{6,30},{7,31},{8,16},{9,... | collective-permute-start | bytes 56 | tf_op jit(solution)/shard_map/ppermute | solution.py:463
  10.9 0.9 %copy-start.3 = (f32[272,128]{1,0:T(8,128)S(1)}, f32[272,128]{1,0:T(8,128)}, u32[]{:S(2)}) copy-start(f32[272,128]{1,0:T(8,128)} %get-tuple-element.26.refs_4_) | copy-start | bytes 417796
  11.9 0.7 copy-start.5
  13.7 9.1 %collective-permute-start.6 = (f32[272,128]{1,0:T(8,128)S(1)}, f32[272,128]{1,0:T(8,128)S(1)}, u32[]{:S(2)}, u32[]{:S(2)}) collective-permute-start(f32[272,128]{1,0:T(8,128)S(1)} %get-tuple-element.31.refs_3_), channel_id=1, source_target_pairs={{0,7},{1,0},{2,1},{3,2},{4,3},{5,4},{6,5},{7,6},{8,15},{9,8},{10,9... | collective-permute-start | bytes 417800 | tf_op jit(solution)/shard_map/ppermute | solution.py:463
  18.7 6.9 %collective-permute-start.7 = (f32[272,128]{1,0:T(8,128)S(1)}, f32[272,128]{1,0:T(8,128)S(1)}, u32[]{:S(2)}, u32[]{:S(2)}) collective-permute-start(f32[272,128]{1,0:T(8,128)S(1)} %get-tuple-element.31.refs_3_), channel_id=1, source_target_pairs={{0,6},{1,7},{2,0},{3,1},{4,2},{5,3},{6,4},{7,5},{8,10},{9,11},{10,... | collective-permute-start | bytes 417800 | tf_op jit(solution)/shard_map/ppermute | solution.py:463
  19.2 8.4 %collective-permute-start.5 = (f32[272,128]{1,0:T(8,128)S(1)}, f32[272,128]{1,0:T(8,128)S(1)}, u32[]{:S(2)}, u32[]{:S(2)}) collective-permute-start(f32[272,128]{1,0:T(8,128)S(1)} %get-tuple-element.31.refs_3_), channel_id=1, source_target_pairs={{0,1},{1,2},{2,3},{3,4},{4,5},{5,6},{6,7},{7,0},{8,9},{9,10},{10,1... | collective-permute-start | bytes 417800 | tf_op jit(solution)/shard_map/ppermute | solution.py:463
  19.8 26.5 %collective-permute-start.20 = (f32[2,4,128,128]{3,2,1,0:T(8,128)}, f32[2,4,128,128]{3,2,1,0:T(8,128)S(1)}, u32[]{:S(2)}, u32[]{:S(2)}) collective-permute-start(f32[2,4,128,128]{3,2,1,0:T(8,128)} %get-tuple-element.36.refs_11_.refs_17_), channel_id=1, source_target_pairs={{0,16},{1,17},{2,18},{3,19},{4,20},{5,21},{6,22},{7,23},{8,8},{9,9... | collective-permute-start | bytes 1572872 | tf_op jit(solution)/shard_map/ppermute | solution.py:463
  22.9 5.2 %collective-permute-start.10 = (f32[272,128]{1,0:T(8,128)S(1)}, f32[272,128]{1,0:T(8,128)S(1)}, u32[]{:S(2)}, u32[]{:S(2)}) collective-permute-start(f32[272,128]{1,0:T(8,128)S(1)} %collective-permute-done.6.refs_5_), channel_id=1, source_target_pairs={{0,8},{1,9},{2,10},{3,11},{4,12},{5,13},{6,14},{7,15},{8,0},{9,1},... | collective-permute-start | bytes 417800 | tf_op jit(solution)/shard_map/ppermute | solution.py:463
  25.6 2.4 %collective-permute-start.11 = (f32[272,128]{1,0:T(8,128)S(1)}, f32[272,128]{1,0:T(8,128)S(1)}, u32[]{:S(2)}, u32[]{:S(2)}) collective-permute-start(f32[272,128]{1,0:T(8,128)S(1)} %collective-permute-done.7.refs_6_), channel_id=1, source_target_pairs={{0,8},{1,9},{2,10},{3,11},{4,12},{5,13},{6,14},{7,15},{8,0},{9,1},... | collective-permute-start | bytes 417800 | tf_op jit(solution)/shard_map/ppermute | solution.py:463
  27.5 1.4 %collective-permute-start.9 = (f32[272,128]{1,0:T(8,128)S(1)}, f32[272,128]{1,0:T(8,128)S(1)}, u32[]{:S(2)}, u32[]{:S(2)}) collective-permute-start(f32[272,128]{1,0:T(8,128)S(1)} %collective-permute-done.5.refs_4_), channel_id=1, source_target_pairs={{0,8},{1,9},{2,10},{3,11},{4,12},{5,13},{6,14},{7,15},{8,0},{9,1},... | collective-permute-start | bytes 417800 | tf_op jit(solution)/shard_map/ppermute | solution.py:463
  27.5 4.1 %collective-permute-start.8 = (f32[272,128]{1,0:T(8,128)S(1)}, f32[272,128]{1,0:T(8,128)S(1)}, u32[]{:S(2)}, u32[]{:S(2)}) collective-permute-start(f32[272,128]{1,0:T(8,128)S(1)} %get-tuple-element.31.refs_3_), channel_id=1, source_target_pairs={{0,8},{1,9},{2,10},{3,11},{4,12},{5,13},{6,14},{7,15},{8,0},{9,1},... | collective-permute-start | bytes 417800 | tf_op jit(solution)/shard_map/ppermute | solution.py:463
  28.9 25.2 %collective-permute-start.19 = (f32[2,4,128,128]{3,2,1,0:T(8,128)}, f32[2,4,128,128]{3,2,1,0:T(8,128)S(1)}, u32[]{:S(2)}, u32[]{:S(2)}) collective-permute-start(f32[2,4,128,128]{3,2,1,0:T(8,128)} %get-tuple-element.37.refs_12_.refs_18_), channel_id=1, source_target_pairs={{0,8},{1,9},{2,10},{3,11},{4,12},{5,13},{6,14},{7,15},{8,0},{9,1},... | collective-permute-start | bytes 1572872 | tf_op jit(solution)/shard_map/ppermute | solution.py:463
  29.0 25.1 %collective-permute-start.21 = (f32[2,4,128,128]{3,2,1,0:T(8,128)}, f32[2,4,128,128]{3,2,1,0:T(8,128)S(1)}, u32[]{:S(2)}, u32[]{:S(2)}) collective-permute-start(f32[2,4,128,128]{3,2,1,0:T(8,128)} %get-tuple-element.37.refs_12_.refs_18_), channel_id=1, source_target_pairs={{0,16},{1,17},{2,18},{3,19},{4,20},{5,21},{6,22},{7,23},{8,8},{9,9... | collective-permute-start | bytes 1572872 | tf_op jit(solution)/shard_map/ppermute | solution.py:463
  31.6 1.0 %copy-start = (f32[2,4,128,128]{3,2,1,0:T(8,128)S(1)}, f32[2,4,128,128]{3,2,1,0:T(8,128)}, u32[]{:S(2)}) copy-start(f32[2,4,128,128]{3,2,1,0:T(8,128)} %get-tuple-element.36.refs_11_.refs_17_) | copy-start | bytes 1572868
  32.6 1.0 %copy-start.1 = (f32[2,4,128,128]{3,2,1,0:T(8,128)S(1)}, f32[2,4,128,128]{3,2,1,0:T(8,128)}, u32[]{:S(2)}) copy-start(f32[2,4,128,128]{3,2,1,0:T(8,128)} %get-tuple-element.37.refs_12_.refs_18_) | copy-start | bytes 1572868
  33.7 0.9 %copy-start.2 = (bf16[256,256]{1,0:T(8,128)(2,1)S(1)}, bf16[256,256]{1,0:T(8,128)(2,1)}, u32[]{:S(2)}) copy-start(bf16[256,256]{1,0:T(8,128)(2,1)} %get-tuple-element.30.refs_2_) | copy-start | bytes 393220
  34.6 0.7 %copy-start.4 = (f32[8,128]{1,0:T(8,128)S(1)}, f32[8,128]{1,0:T(8,128)}, u32[]{:S(2)}) copy-start(f32[8,128]{1,0:T(8,128)} %get-tuple-element.29.refs_1_) | copy-start | bytes 12292
  41.6 9.1 %collective-permute-start.12 = (f32[2,128,128]{2,1,0:T(8,128)S(1)}, f32[2,128,128]{2,1,0:T(8,128)S(1)}, u32[]{:S(2)}, u32[]{:S(2)}) collective-permute-start(f32[2,128,128]{2,1,0:T(8,128)S(1)} %get-tuple-element.39), channel_id=1, source_target_pairs={{0,1},{1,2},{2,3},{3,4},{4,5},{5,6},{6,7},{7,0},{8,9},{9,10},{10,1... | collective-permute-start | bytes 393224 | tf_op jit(solution)/shard_map/ppermute | solution.py:463
  41.7 9.1 %collective-permute-start.13 = (f32[2,128,128]{2,1,0:T(8,128)S(1)}, f32[2,128,128]{2,1,0:T(8,128)S(1)}, u32[]{:S(2)}, u32[]{:S(2)}) collective-permute-start(f32[2,128,128]{2,1,0:T(8,128)S(1)} %get-tuple-element.39), channel_id=1, source_target_pairs={{0,7},{1,0},{2,1},{3,2},{4,3},{5,4},{6,5},{7,6},{8,15},{9,8},{10,9... | collective-permute-start | bytes 393224 | tf_op jit(solution)/shard_map/ppermute | solution.py:463
  46.4 6.2 %collective-permute-start.14 = (f32[2,128,128]{2,1,0:T(8,128)S(1)}, f32[2,128,128]{2,1,0:T(8,128)S(1)}, u32[]{:S(2)}, u32[]{:S(2)}) collective-permute-start(f32[2,128,128]{2,1,0:T(8,128)S(1)} %get-tuple-element.39), channel_id=1, source_target_pairs={{0,6},{1,7},{2,0},{3,1},{4,2},{5,3},{6,4},{7,5},{8,10},{9,11},{10,... | collective-permute-start | bytes 393224 | tf_op jit(solution)/shard_map/ppermute | solution.py:463
  50.7 1.9 %collective-permute-start.15 = (f32[2,128,128]{2,1,0:T(8,128)S(1)}, f32[2,128,128]{2,1,0:T(8,128)S(1)}, u32[]{:S(2)}, u32[]{:S(2)}) collective-permute-start(f32[2,128,128]{2,1,0:T(8,128)S(1)} %collective-permute-done.12.refs_4_), channel_id=1, source_target_pairs={{0,8},{1,9},{2,10},{3,11},{4,12},{5,13},{6,14},{7,15},{8,0},{9,1},... | collective-permute-start | bytes 393224 | tf_op jit(solution)/shard_map/ppermute | solution.py:463
  50.7 3.4 %collective-permute-start.18 = (f32[4,128,128]{2,1,0:T(8,128)S(1)}, f32[4,128,128]{2,1,0:T(8,128)S(1)}, u32[]{:S(2)}, u32[]{:S(2)}) collective-permute-start(f32[4,128,128]{2,1,0:T(8,128)S(1)} %get-tuple-element.42.refs_12_), channel_id=1, source_target_pairs={{0,8},{1,9},{2,10},{3,11},{4,12},{5,13},{6,14},{7,15},{8,0},{9,1},... | collective-permute-start | bytes 786440 | tf_op jit(solution)/shard_map/ppermute | solution.py:463
  52.6 1.3 %collective-permute-start.16 = (f32[2,128,128]{2,1,0:T(8,128)S(1)}, f32[2,128,128]{2,1,0:T(8,128)S(1)}, u32[]{:S(2)}, u32[]{:S(2)}) collective-permute-start(f32[2,128,128]{2,1,0:T(8,128)S(1)} %collective-permute-done.13.refs_5_), channel_id=1, source_target_pairs={{0,8},{1,9},{2,10},{3,11},{4,12},{5,13},{6,14},{7,15},{8,0},{9,1},... | collective-permute-start | bytes 393224 | tf_op jit(solution)/shard_map/ppermute | solution.py:463
  52.6 1.5 %collective-permute-start.17 = (f32[2,128,128]{2,1,0:T(8,128)S(1)}, f32[2,128,128]{2,1,0:T(8,128)S(1)}, u32[]{:S(2)}, u32[]{:S(2)}) collective-permute-start(f32[2,128,128]{2,1,0:T(8,128)S(1)} %collective-permute-done.14.refs_6_), channel_id=1, source_target_pairs={{0,8},{1,9},{2,10},{3,11},{4,12},{5,13},{6,14},{7,15},{8,0},{9,1},... | collective-permute-start | bytes 393224 | tf_op jit(solution)/shard_map/ppermute | solution.py:463
  59.1 5.3 %collective-permute-start.22 = (f32[192,256]{1,0:T(8,128)S(1)}, f32[192,256]{1,0:T(8,128)S(1)}, u32[]{:S(2)}, u32[]{:S(2)}) collective-permute-start(f32[192,256]{1,0:T(8,128)S(1)} %get-tuple-element.43), channel_id=1, source_target_pairs={{0,16},{1,17},{2,18},{3,19},{4,20},{5,21},{6,22},{7,23},{8,0},{9,1... | collective-permute-start | bytes 589832 | tf_op jit(solution)/shard_map/ppermute | solution.py:463
  59.8 6.9 %collective-permute-start.23 = (f32[128,256]{1,0:T(8,128)S(1)}, f32[128,256]{1,0:T(8,128)S(1)}, u32[]{:S(2)}, u32[]{:S(2)}) collective-permute-start(f32[128,256]{1,0:T(8,128)S(1)} %get-tuple-element.44), channel_id=1, source_target_pairs={{0,24},{1,25},{2,26},{3,27},{4,28},{5,29},{6,30},{7,31},{8,16},{9,... | collective-permute-start | bytes 393224 | tf_op jit(solution)/shard_map/ppermute | solution.py:463
  60.6 6.9 %collective-permute-start.24 = (f32[64,256]{1,0:T(8,128)S(1)}, f32[64,256]{1,0:T(8,128)S(1)}, u32[]{:S(2)}, u32[]{:S(2)}) collective-permute-start(f32[64,256]{1,0:T(8,128)S(1)} %get-tuple-element.47), channel_id=1, source_target_pairs={{0,8},{1,9},{2,10},{3,11},{4,12},{5,13},{6,14},{7,15},{8,0},{9,1},... | collective-permute-start | bytes 196616 | tf_op jit(solution)/shard_map/ppermute | solution.py:463

commit v5 on v3

--- a/solution.py
+++ b/solution.py
@@ -11,9 +11,11 @@
 CZ = 64
 GROUP = 4
 FIELD_ROWS = 16
-VMEM_BYTES = 48 * 2**20
+OWN_KINDS, FIRST_KINDS, ACROSS_KINDS = 12, 13, 14
+LEAD = 1
+VMEM_BYTES = 16 * 2**20
+WHOLE_VMEM_BYTES = 62 * 2**20
 IN_VMEM = pl.BlockSpec(memory_space=pltpu.VMEM)
-IN_SMEM = pl.BlockSpec(memory_space=pltpu.SMEM)
 
 
 def padded_2(block, sides, width):
@@ -169,13 +171,13 @@
 
 
 def prepare_kernel(*refs):
-    sources, (early, late, start, taps, weights) = refs[:8], refs[8:13]
-    scratch, copies, sems = refs[13], refs[14:22], refs[22]
+    sources, (early, late, taps, weights) = refs[:6], refs[6:10]
+    scratch, copies, sems = refs[10], refs[11:17], refs[17]
     moves = [pltpu.make_async_copy(s, c, sems.at[i]) for i, (s, c) in enumerate(zip(sources, copies))]
     for move in moves:
         move.start()
-    backward, incoming, fields, axial, lateral, depth, diagonal, coupling = copies
-    for move in moves[3:]:
+    backward, axial, lateral, depth, diagonal, coupling = copies
+    for move in moves[1:]:
         move.wait()
     orients = coupling.shape[0]
     ratios = [each[w : w + 1] / each[1:2] for each in (axial, lateral, depth) for w in (0, 2)]
@@ -192,86 +194,71 @@
     weights[...] = jnp.concatenate(
         [jnp.concatenate([coarse, fine], axis=1), jnp.concatenate([coarse, jnp.zeros_like(fine)], axis=1)], axis=0
     )
-    odd = position()[1]
-    rows = scratch.shape[0]
-    pair = incoming.shape[1] // 2
-    moves[1].wait()
-    for i in range(pair):
-        start[i * rows : (i + 1) * rows] = to_tile(incoming[0, i], scratch)
-    moves[2].wait()
-    start[pair * rows :] = jnp.zeros((FIELD_ROWS, rows), jnp.float32)
-    for kind in range(fields.shape[0]):
-        for i in range(pair):
-            line = fields[kind, pl.ds(pair * odd + i, 1), :]
-            at = pair * rows + (kind * pair + i) * 2
-            start[at : at + 1] = line[:, :rows]
-            start[at + 1 : at + 2] = line[:, rows:]
     moves[0].wait()
-    steps, planes = backward.shape[:2]
-    for out, begin in ((early, 0), (late, steps // 2)):
-        for step in range(steps // 2):
-            for i in range(planes):
+    for out, begin in ((early, 0), (late, LEAD)):
+        for step in range(out.shape[0]):
+            for i in range(out.shape[1]):
                 out[step, i] = to_tile(backward[begin + step, i].astype(jnp.float32), scratch)
 
 
-def prepare(backward, incoming, fields, axial, lateral, depth, diagonal, coupling):
+def prepare(backward, axial, lateral, depth, diagonal, coupling):
     steps, planes, orients, cells = backward.shape
     rows, lanes = 2 * orients, cells // 2
-    operands = [backward, incoming, fields, axial, lateral, depth, diagonal.reshape(1, -1), coupling]
-    half = ((steps // 2, planes, rows, lanes), jnp.float32)
-    piece = ((planes // 2 * rows + FIELD_ROWS, lanes), jnp.float32)
+    operands = [backward, axial, lateral, depth, diagonal.reshape(1, -1), coupling]
+    first, rest = (((count, planes, rows, lanes), jnp.float32) for count in (LEAD, steps - LEAD))
     return pl.pallas_call(
         prepare_kernel,
         in_specs=[pl.BlockSpec(memory_space=pltpu.HBM)] * len(operands),
-        out_specs=[IN_VMEM] * 5,
+        out_specs=[IN_VMEM] * 4,
         out_shape=[
             jax.ShapeDtypeStruct(*each)
-            for each in (half, half, piece, ((8, lanes), jnp.float32), ((2 * rows, 2 * lanes), jnp.bfloat16))
+            for each in (first, rest, ((8, lanes), jnp.float32), ((2 * rows, 2 * lanes), jnp.bfloat16))
         ],
         scratch_shapes=[pltpu.VMEM((rows, lanes), jnp.float32)]
         + [pltpu.VMEM(each.shape, each.dtype) for each in operands]
         + [pltpu.SemaphoreType.DMA((len(operands),))],
-        compiler_params=pltpu.CompilerParams(vmem_limit_bytes=VMEM_BYTES),
+        compiler_params=pltpu.CompilerParams(vmem_limit_bytes=WHOLE_VMEM_BYTES),
     )(*operands)
 
 
-def pack_kernel(start, moved_high, moved_low, out, scratch):
+def settle_kernel(*refs):
+    for source, out in zip(refs[: len(refs) // 2], refs[len(refs) // 2 :]):
+        out[...] = source[...]
+
+
+def pack_kernel(low, moved_high, moved_low, across, fields, out, scratch):
     sec, odd = position()
     rows = scratch.shape[0]
-    out[...] = start[...]
+    orients = rows // 2
+    pair = low.shape[0] // orients
+    count = fields.shape[0]
+    out[pair * rows :] = jnp.zeros((FIELD_ROWS, rows), jnp.float32)
+    for i in range(count):
+        out[pair * rows + 2 * i : pair * rows + 2 * i + 1] = fields[i : i + 1, :rows]
+        out[pair * rows + 2 * i + 1 : pair * rows + 2 * i + 2] = fields[i : i + 1, rows:]
+    out[OWN_KINDS + pair * rows : OWN_KINDS + pair * rows + 1] = low[pair * orients : pair * orients + 1, :rows]
+    out[ACROSS_KINDS + pair * rows : ACROSS_KINDS + pair * rows + 1] = across[:1, :rows]
 
     def fill(source):
-        for i in range(source.shape[0]):
-            out[i * rows : (i + 1) * rows] = to_tile(source[i], scratch)
-
+        for i in range(pair):
+            out[i * rows : (i + 1) * rows] = to_tile(source[i * orients : (i + 1) * orients], scratch)
+        out[FIRST_KINDS + pair * rows : FIRST_KINDS + pair * rows + 1] = source[pair * orients : pair * orients + 1, :rows]
+
+    pl.when(sec == 0)(lambda: fill(low))
     pl.when(odd == 1)(lambda: fill(moved_high))
     pl.when((sec > 0) & (odd == 0))(lambda: fill(moved_low))
 
 
-def places(odd, pair, reach):
-    width = 2 * pair
-    far = reach - width
-    starts = []
-    for core in (odd, 1 - odd):
-        starts += [
-            reach + pair * core,
-            far + pair * core,
-            reach + width + pair * core,
-            jnp.where(core == 0, reach + 2 * width, 0),
-        ]
-    return starts
-
-
-def kind_of(kinds, step, steps):
-    sec = lax.axis_index("sec")
-    apart = sec ^ (sec // 2 + step // steps)
-    each = [ref[0, step % steps] for ref in kinds]
-    return jnp.where(
-        apart == 0, each[0], jnp.where(apart == 1, each[1], jnp.where(apart == 2, each[2], each[3]))
-    )
-
-
-def run_steps(kinds, steps, taps, weights, begun, count, slab, other, first, second, factor, after):
+def scalars_of(row, count):
+    lane = lax.broadcasted_iota(jnp.int32, row.shape, 1)
+    return [jnp.sum(jnp.where(lane == i, row, 0.0)).astype(jnp.int32) for i in range(count)]
+
+
+def places(odd, planes, reach, blocks):
+    return [reach + block * planes + planes // 2 * core for core in (odd, 1 - odd) for block in blocks]
+
+
+def run_steps(kinds, taps, weights, count, slab, other, first, second, factor, offset, after):
     tap = [taps[i : i + 1, :] for i in range(6)]
     extent, rows, lanes = slab.shape
     buffers = (slab, other)
@@ -287,13 +274,13 @@
         product = jnp.dot(packed[...], weights[...], preferred_element_type=jnp.float32)
         product = product[:, :lanes] + product[:, lanes:]
         for i in range(GROUP):
-            target[at + i] = product[i * rows : (i + 1) * rows] * factor[kind, at + i]
+            target[at + i] = product[i * rows : (i + 1) * rows] * factor[kind, at + i + offset]
 
     for step in range(count):
         source, target = buffers[step % 2], buffers[1 - step % 2]
         begin, width = step + 1, extent - 2 * step - 2
         groups = -(-width // GROUP)
-        kind = kind_of(kinds, begun + step, steps)
+        kind = kinds[step]
 
         def at(i, begin=begin, width=width):
             return jnp.minimum(begin + i * GROUP, begin + width - GROUP)
@@ -318,90 +305,99 @@
         after(step, target)
 
 
-def spread_factor(columns, factor, starts, kinds, pair):
+def spread_factor(columns, factor, starts, width):
     rows, lanes = factor.shape[2:]
-    left = lax.broadcasted_iota(jnp.int32, (rows, lanes), 1) < lanes // 2
+    pair = factor.shape[1] // len(starts)
+    right = (lax.broadcasted_iota(jnp.int32, (rows, lanes), 1) >= lanes // 2).astype(jnp.int32)
     for piece, start in enumerate(starts):
-        for kind in range(kinds):
+        for kind in range(factor.shape[0]):
             for i in range(pair):
-                at = piece * FIELD_ROWS + (kind * pair + i) * 2
-                factor[kind, start + i] = jnp.where(left, columns[:, at : at + 1], columns[:, at + 1 : at + 2])
-
-
-def early_kernel(half, *refs):
-    kinds, taps, weights, pieces, series = refs[:4], refs[4], refs[5], refs[6:14], refs[14:17]
-    middle, half_out, kept, total, factor = refs[17:22]
-    slab, other, first, second, scratch = refs[22:]
+                at = piece * width + (kind * pair + i) * 2
+                factor[kind, start + i] = jnp.take_along_axis(columns, right + at, axis=1, mode="promise_in_bounds")
+
+
+def early_kernel(blocks, taps, weights, *refs):
+    pieces, refs = refs[: 2 * len(blocks)], refs[2 * len(blocks) :]
+    stored, (middle, half_out, kept, total, factor) = refs[:2], refs[2:7]
+    slab, other, first, second, scratch = refs[7:]
     sec, odd = position()
     planes, rows = middle.shape[:2]
     pair = planes // 2
-    starts = places(odd, pair, half)
+    reach = (slab.shape[0] - planes) // 2
+    starts = places(odd, planes, reach, blocks)
     for piece, start in zip(pieces, starts):
         for i in range(pair):
             slab[start + i] = piece[i * rows : (i + 1) * rows]
-    scratch[...] = jnp.exp(-jnp.concatenate([piece[pair * rows :] for piece in pieces], axis=0)).T
-    spread_factor(reorder(scratch), factor, starts, factor.shape[0], pair)
-    span = series[0].shape[0]
-    steps = 2 * span
+    at = pair * rows
+    mine, others = (piece[at + OWN_KINDS : at + OWN_KINDS + 1] for piece in (pieces[0], pieces[len(blocks)]))
+    steps = LEAD + stored[1].shape[0]
+    second_kinds = jnp.where((sec == 1) | (sec == 2), mine, others)
+    kinds = scalars_of(pieces[0][at + FIRST_KINDS : at + FIRST_KINDS + 1], steps) + scalars_of(second_kinds, steps)
+    width = 2 * pair * factor.shape[0]
+    lines = [piece[pair * rows : pair * rows + width] for piece in pieces]
+    lines.append(jnp.zeros((rows - width * len(pieces), rows), jnp.float32))
+    scratch[...] = jnp.exp(-jnp.concatenate(lines, axis=0)).T
+    spread_factor(reorder(scratch), factor, starts, width)
     total[...] = jnp.zeros(total.shape, jnp.float32)
+    kept[...] = jnp.zeros(kept.shape, jnp.float32)
 
     def after(step, state):
-        @pl.when(sec == 0)
+        @pl.when(sec == step // steps)
         def _():
-            total[...] += state[half : half + planes] * series[step // span][step % span]
-            if step + 1 == steps:
-                kept[...] = state[half : half + planes]
-
-    run_steps(kinds, steps, taps, weights, 0, half, slab, other, first, second, factor, after)
-    state = (slab, other)[half % 2]
-    middle[...] = state[half : half + planes]
-    half_out[...] = state[pl.ds(half + pair * odd, pair)]
-
-
-def late_kernel(half, last, *refs):
-    kinds, taps, weights, middle, pieces, factor = refs[:4], refs[4], refs[5], refs[6], refs[7:13], refs[13]
-    kept, total_in, series, stored = refs[14], refs[15], refs[16:19], refs[19:21]
-    handoff, share, to_pair, to_across, to_corner = refs[21:26]
-    slab, other, first, second, scratch, total, saved, whole = refs[26:]
+            j = step % steps
+            source = stored[0][j] if j < LEAD else stored[1][j - LEAD]
+            total[...] += state[reach : reach + planes] * source
+            if j + 1 == steps:
+                kept[...] = state[reach : reach + planes]
+
+    run_steps(kinds, taps, weights, reach, slab, other, first, second, factor, 0, after)
+    state = (slab, other)[reach % 2]
+    middle[...] = state[reach : reach + planes]
+    half_out[...] = state[pl.ds(reach + pair * odd, pair)]
+
+
+def late_kernel(blocks, last, taps, weights, first_own, first_swapped, middle, *refs):
+    pieces, refs = refs[: 2 * len(blocks)], refs[2 * len(blocks) :]
+    factor, kept, total_in, total_beside, series, stored = refs[0], refs[1], refs[2], refs[3], refs[4:6], refs[6:8]
+    handoff, share, to_pair, to_across, to_corner = refs[8:13]
+    slab, other, first, second, scratch, total, saved, whole = refs[13:]
     sec, odd = position()
     planes, rows = middle.shape[:2]
     pair = planes // 2
-    starts = places(odd, pair, half)
-    slab[half : half + planes] = middle[...]
-    for piece, start in zip(pieces, starts[1:4] + starts[5:8]):
+    reach = (slab.shape[0] - planes) // 2
+    begun = (factor.shape[1] - planes) // 2
+    own, others = (
+        [each[pair * rows + at : pair * rows + at + 1] for at in (OWN_KINDS, ACROSS_KINDS)]
+        for each in (first_own, first_swapped)
+    )
+    row = jnp.where(sec < 2, jnp.where(odd == 0, own[1], others[1]), jnp.where(odd == 0, others[0], own[0]))
+    kinds = scalars_of(row, reach)
+    slab[reach : reach + planes] = middle[...]
+    for piece, start in zip(pieces, places(odd, planes, reach, blocks)):
         for i in range(pair):
             slab[start + i] = piece[i]
-    span = series[0].shape[0]
-    steps = 2 * span
-    total[...] = total_in[...]
+    total[...] = jnp.zeros(total.shape, jnp.float32)
+
+    @pl.when(sec == 0)
+    def _():
+        total[...] = total_in[...] + total_beside[...]
+
     saved[...] = kept[...]
 
     def after(step, state):
-        part = step // span
-        step = step + half
-
-        @pl.when(sec == 0)
-        def _():
-            total[...] += state[half : half + planes] * series[part][step % span]
-
-        if step + 1 == 2 * steps:
-
-            @pl.when(sec == 1)
-            def _():
-                saved[...] = state[half : half + planes]
-
-        if step >= 2 * steps:
-
-            @pl.when(sec == last)
-            def _():
-                total[...] += state[half : half + planes] * stored[step % steps // span][step % span]
-
-    run_steps(kinds, steps, taps, weights, half, half, slab, other, first, second, factor, after)
-    state = (slab, other)[half % 2]
+        for where, source in ((sec == 0, series), (sec == last, stored)):
+
+            @pl.when(where)
+            def _(source=source):
+                part = source[0][step] if step < LEAD else source[1][step - LEAD]
+                total[...] += state[reach : reach + planes] * part
+
+    run_steps(kinds, taps, weights, reach, slab, other, first, second, factor, begun - reach, after)
+    state = (slab, other)[reach % 2]
 
     @pl.when(sec == last)
     def _():
-        saved[...] = state[half : half + planes]
+        saved[...] = state[reach : reach + planes]
 
     orients = handoff.shape[1]
     count = orients // (last + 1)
@@ -418,29 +414,30 @@
         ):
             piece[i * count : (i + 1) * count] = whole[pl.ds(pl.multiple_of(who * count, count), count)]
     for i in range(pair):
-        to_across[held + i * orients : held + (i + 1) * orients] = from_tile(state[half + pair * odd + i], scratch)
+        to_across[held + i * orients : held + (i + 1) * orients] = from_tile(state[reach + pair * odd + i], scratch)
 
     @pl.when(sec == 1)
     def _():
         to_corner[...] = to_across[held:]
 
 
-def call(kernel, out_shape, scratch, operands, scalars=()):
+def call(kernel, out_shape, scratch, operands):
     return pl.pallas_call(
         kernel,
-        in_specs=[IN_SMEM] * len(scalars) + [IN_VMEM] * len(operands),
+        in_specs=[IN_VMEM] * len(operands),
         out_specs=[IN_VMEM] * len(out_shape),
         out_shape=[jax.ShapeDtypeStruct(shape, jnp.float32) for shape in out_shape],
         scratch_shapes=scratch,
         compiler_params=pltpu.CompilerParams(vmem_limit_bytes=VMEM_BYTES),
-    )(*scalars, *operands)
+    )(*operands)
 
 
 def paired(incoming, backward, fields, block_types, axial_taps, lateral_taps, depth_taps, bend_diagonal, bend_coupling):
     n_sec, n_gx = lax.axis_size("sec"), lax.axis_size("gx")
     steps, planes, orients, cells = backward.shape
     pair = planes // 2
-    half = TICKS * steps // 2
+    reach = (TICKS - 1) * steps, steps
+    near, far = (1, -1), (1, -1, 2, -2)
     rows = 2 * orients
     lanes = cells // 2
     sec = lax.axis_index("sec")
@@ -454,54 +451,61 @@
 
     same, beside, across, crossing = (0, 1, 2, 3), (1, 0, 3, 2), (2, 3, 0, 1), (2, 1, 0, 3)
     whole = incoming[0]
-    backward, moved = lax.optimization_barrier((backward, whole[pair:]))
-    moved_high = send(moved, (1, 3, 0, 2))
-    moved_low = send(whole[:pair], (0, 2, 1, 3))
-    kinds = [block_types, send(block_types, beside), send(block_types, across), send(block_types, (3, 2, 1, 0))]
-    early_stored, late_stored, start, taps, weights = prepare(
-        backward, incoming, fields, axial_taps, lateral_taps, depth_taps, bend_diagonal, bend_coupling
-    )
-    early_next, early_last = send(early_stored, beside), send(early_stored, crossing)
+    types = jnp.pad(block_types.astype(jnp.float32), ((0, 7), (0, cells - steps)))
+    low, high = (jnp.concatenate([each.reshape(-1, cells), types]) for each in (whole[:pair], whole[pair:]))
+    backward, high, low = lax.optimization_barrier((backward, high, low))
+    moved_high = send(high, (1, 3, 0, 2))
+    moved_low = send(low, (0, 2, 1, 3))
+    across_types = send(types, across)
+    lines = lax.dynamic_slice_in_dim(fields, sec % 2 * pair, pair, axis=1).reshape(-1, cells)
+    settled = prepare(backward, axial_taps, lateral_taps, depth_taps, bend_diagonal, bend_coupling)
+    early_stored, late_stored = settled[:2]
 
     tile = pltpu.VMEM((rows, lanes), jnp.float32)
-    slab = pltpu.VMEM((planes + 2 * half, rows, lanes), jnp.float32)
     packed = pltpu.VMEM((GROUP * rows, 2 * lanes), jnp.bfloat16)
     inner = pltpu.VMEM((planes, rows, lanes), jnp.float32)
-    work = [slab, slab, packed, packed, tile]
-
-    def exchange(piece):
-        own = [
-            send(piece, same, lambda s: 1),
-            send(piece, same, lambda s: -1),
-            send(piece, same, lambda s: -2 if s % 2 == 0 else 2),
-        ]
-        return own, [send(each, beside) for each in own]
+
+    def work(extent):
+        slab = pltpu.VMEM((planes + 2 * extent, rows, lanes), jnp.float32)
+        return [slab, slab, packed, packed, tile]
 
     (piece,) = call(
-        pack_kernel, [(pair * rows + FIELD_ROWS, lanes)], [tile], [start, moved_high, moved_low]
-    )
-    own, swapped = exchange(piece)
+        pack_kernel, [(pair * rows + FIELD_ROWS, lanes)], [tile], [low, moved_high, moved_low, across_types, lines]
+    )
+    own = [send(piece, same, lambda s: shift) for shift in far]
+    early_last = send(early_stored, crossing)
+    settled = pl.pallas_call(
+        settle_kernel,
+        in_specs=[IN_VMEM] * len(settled),
+        out_specs=[IN_VMEM] * len(settled),
+        out_shape=[jax.ShapeDtypeStruct(each.shape, each.dtype) for each in settled],
+        compiler_params=pltpu.CompilerParams(vmem_limit_bytes=VMEM_BYTES),
+    )(*settled)
+    own[-1], *settled = lax.optimization_barrier((own[-1], *settled))
+    stored, (taps, weights) = settled[:2], settled[2:]
+    swapped = [send(each, beside) for each in [piece] + own]
     late_stored, *swapped = lax.optimization_barrier((late_stored, *swapped))
-    late_next, late_last = send(late_stored, beside), send(late_stored, crossing)
+    late_last = send(late_stored, crossing)
+    firsts = [piece, swapped[0]]
     middle, piece, kept, total, factor = call(
-        functools.partial(early_kernel, half),
+        functools.partial(early_kernel, tuple(-shift for shift in (0,) + far)),
         [(planes, rows, lanes), (pair, rows, lanes), (planes, rows, lanes), (planes, rows, lanes)]
-        + [(fields.shape[0], planes + 2 * half, rows, lanes)],
-        work,
-        [taps, weights, piece, *own, send(piece, beside), *swapped, early_stored, late_stored, early_next],
-        kinds,
-    )
-    own, swapped = exchange(piece)
+        + [(fields.shape[0], planes + 2 * reach[0], rows, lanes)],
+        work(reach[0]),
+        [taps, weights, piece, *own, *swapped, *stored],
+    )
+    own = [send(piece, same, lambda s: shift) for shift in near]
+    beside_total = send(total, beside)
+    swapped = [send(each, beside) for each in own]
     held = planes * (orients // n_sec)
     handoff, share, to_pair, to_across, to_corner = call(
-        functools.partial(late_kernel, half, last),
+        functools.partial(late_kernel, tuple(-shift for shift in near), last),
         [(planes, orients, cells)]
         + [(held, cells)] * 2
         + [(held + pair * orients, cells), (pair * orients, cells)],
-        work + [inner, inner, pltpu.VMEM((orients, cells), jnp.float32)],
-        [taps, weights, middle, *own, *swapped, factor, kept, total]
-        + [late_next, early_last, late_last, early_stored, late_stored],
-        kinds,
+        work(reach[1]) + [inner, inner, pltpu.VMEM((orients, cells), jnp.float32)],
+        [taps, weights, *firsts, middle, *own, *swapped, factor, kept, total, beside_total]
+        + [early_last, late_last, *stored],
     )
     to_pair = send(to_pair, beside)
     to_across = send(to_across, (2, 0, 3, 1))
@@ -518,9 +522,8 @@
         n_sec == TICKS + 1 == 4
         and planes == steps
         and planes % 2 == 0
-        and TICKS * steps == 2 * (planes + planes // 2)
         and 2 * orients == 2 * CZ == cells // 2 == 128
-        and kinds * planes <= FIELD_ROWS
+        and kinds * planes <= FIELD_ROWS and 10 * kinds * planes <= 2 * orients
         and planes >= GROUP
     )
 

time: 79.9 us -> 68.3 us (0.85)
  waiting for transfers between devices: 25.1 us -> 19.6 us
  local copies, waits for them, and re-layouts: 7.8 us -> 4.69 us
  Pallas kernels: 15.2 us -> 13.1 us
  starting transfers between devices: 29.1 us -> 27.5 us
    ppermute x25 -> x22, waiting for transfers between devices: 25.1 us -> 19.6 us  [send(): return lax.ppermute(array, ('sec', 'gx'), pairs)]
    pallas_call x3 -> x4, Pallas kernels: 14.3 us -> 10.7 us  [the longest x3 10.6 us: call(): pl.pallas_call(kernel, in_specs=[IN_VMEM] * len(operands), out_specs=[IN_...]
    unnamed x18 -> x10, local copies, waits for them, and re-layouts: 6.8 us -> 3.68 us
    pallas_call x1, Pallas kernels: 0.84 us -> 2.44 us  [prepare(): pl.pallas_call(prepare_kernel, in_specs=[pl.BlockSpec(memory_space=pltpu....]
    ppermute x25 -> x22, starting transfers between devices: 29.1 us -> 27.5 us  [send(): return lax.ppermute(array, ('sec', 'gx'), pairs)]
  transfers between devices with their start and end apart: 25 -> 22, of which waited for: 11 -> 8; matrix products, arithmetic and copies ran while one was open for 1% -> 1% of each run, Pallas kernels for 11% -> 15%
where the time goes in v5:
time: 68.3 us; the launch traced here: 67.9 us
  starting transfers between devices  27.5 us (40%)
  waiting for transfers between devices  19.6 us (29%)
  Pallas kernels  13.1 us (19%)
  local copies, waits for them, and re-layouts  4.69 us (7%)
  other arithmetic  2.09 us (3%)
  between operations  0.81 us (1%)
    ppermute x22, starting transfers between devices, send(): return lax.ppermute(array, ('sec', 'gx'), pairs)  27.5 us
    ppermute x22, waiting for transfers between devices, send(): return lax.ppermute(array, ('sec', 'gx'), pairs)  19.6 us
    pallas_call x3, Pallas kernels, call(): pl.pallas_call(kernel, in_specs=[IN_VMEM] * len(operands), out_specs=[IN_...  10.6 us
    unnamed x10, local copies, waits for them, and re-layouts  3.68 us
    pallas_call x1, Pallas kernels, prepare(): pl.pallas_call(prepare_kernel, in_specs=[pl.BlockSpec(memory_space=pltpu....  2.44 us
  transfers between devices with their start and end apart: 22, of which 8 were waited for; matrix products, arithmetic and copies ran while one was open for 1% of the time, Pallas kernels for 15%

profile of v5, /device:TPU:0, one launch (start us, length us, event | category | flops | bytes accessed | tf_op | source)
XLA Modules:
  0.0 67.9 jit_solution(18222523142302481942)
XLA Ops:
  0.6 0.0 copy-start
  0.6 0.7 convert_element_type.5
  1.3 1.0 %fusion.2 = (f32[1,2,64,256]{3,2,1,0:T(8,128)S(1)}, f32[1,2,64,256]{3,2,1,0:T(8,128)S(1)}) fusion(f32[1,4,64,256]{3,2,1,0:T(8,128)} %param.9), kind=kLoop, calls=%fused_computation.9 | loop fusion | bytes 524288 | tf_op jit(solution)/shard_map/slice | solution.py:455
  2.3 0.5 collective-permute-start
  2.8 0.7 collective-permute-start.1
  3.5 5.0 %collective-permute-start.2 = (f32[8,256]{1,0:T(8,128)S(1)}, f32[8,256]{1,0:T(8,128)S(1)}, u32[]{:S(2)}, u32[]{:S(2)}) collective-permute-start(f32[8,256]{1,0:T(8,128)S(1)} %pad.4), channel_id=1, source_target_pairs={{0,16},{1,17},{2,18},{3,19},{4,20},{5,21},{6,22},{7,23},{8,24},{9,... | collective-permute-start | bytes 24584 | tf_op jit(solution)/shard_map/ppermute | solution.py:450
  8.5 0.0 copy-done
  8.5 3.1 %collective-permute-done.2.across = f32[8,256]{1,0:T(8,128)S(1)} collective-permute-done((f32[8,256]{1,0:T(8,128)S(1)}, f32[8,256]{1,0:T(8,128)S(1)}, u32[]{:S(2)}, u32[]{:S(2)}) %collective-permute-start.2) | collective-permute-done | bytes 8224 | tf_op jit(solution)/shard_map/ppermute | solution.py:450
  11.6 0.0 collective-permute-done.moved_high
  11.6 0.0 collective-permute-done.1.moved_low
  11.6 0.1 shard_map.104.refs_0_.first_own
  11.7 3.7 %collective-permute-start.3 = (f32[272,128]{1,0:T(8,128)S(1)}, f32[272,128]{1,0:T(8,128)S(1)}, u32[]{:S(2)}, u32[]{:S(2)}) collective-permute-start(f32[272,128]{1,0:T(8,128)S(1)} %shard_map.104.refs_0_.first_own), channel_id=1, source_target_pairs={{0,6},{1,7},{2,0},{3,1},{4,2},{5,3},{6,4},{7,5},{8,14},{9,15},{10,... | collective-permute-start | bytes 417800 | tf_op jit(solution)/shard_map/ppermute | solution.py:450
  15.4 0.0 collective-permute-start.9
  15.4 4.7 %collective-permute-start.7 = (f32[272,128]{1,0:T(8,128)S(1)}, f32[272,128]{1,0:T(8,128)S(1)}, u32[]{:S(2)}, u32[]{:S(2)}) collective-permute-start(f32[272,128]{1,0:T(8,128)S(1)} %shard_map.104.refs_0_.first_own), channel_id=1, source_target_pairs={{0,7},{1,0},{2,1},{3,2},{4,3},{5,4},{6,5},{7,6},{8,15},{9,8},{10,9... | collective-permute-start | bytes 417800 | tf_op jit(solution)/shard_map/ppermute | solution.py:450
  20.2 0.0 collective-permute-start.5
  20.2 2.4 %shard_map.105 = (f32[1,4,128,128]{3,2,1,0:T(8,128)}, f32[3,4,128,128]{3,2,1,0:T(8,128)}, f32[8,128]{1,0:T(8,128)}, bf16[256,256]{1,0:T(8,128)(2,1)}) custom-call(bf16[4,4,64,256]{3,2,1,0:T(8,128)(2,1)} %refs_0_, f32[3,64]{1,0:T(4,128)} %refs_1_.1, f32[3,64]{1,0:T(4,128)} %refs_2_.1, f32[3,64]{1,0:T(4,128)} %refs_3_.1, f32[1,64]{1,0:T(1,128)} %bitcast.11, ...), custom_call_target="tpu_custom_call" | custom-call | tf_op jit(solution)/shard_map/pallas_call | solution.py:209
  22.6 0.0 copy-start.1
  22.6 1.1 %copy-done.1 = f32[3,4,128,128]{3,2,1,0:T(8,128)S(1)} copy-done((f32[3,4,128,128]{3,2,1,0:T(8,128)S(1)}, f32[3,4,128,128]{3,2,1,0:T(8,128)}, u32[]{:S(2)}) %copy-start.1) | copy-done | bytes 786456
  23.7 0.0 copy-start.2
  23.7 0.9 %copy-done.2 = f32[1,4,128,128]{3,2,1,0:T(8,128)S(1)} copy-done((f32[1,4,128,128]{3,2,1,0:T(8,128)S(1)}, f32[1,4,128,128]{3,2,1,0:T(8,128)}, u32[]{:S(2)}) %copy-start.2) | copy-done | bytes 262168
  24.7 0.0 copy-start.3
  24.7 0.9 %copy-done.3 = bf16[256,256]{1,0:T(8,128)(2,1)S(1)} copy-done((bf16[256,256]{1,0:T(8,128)(2,1)S(1)}, bf16[256,256]{1,0:T(8,128)(2,1)}, u32[]{:S(2)}) %copy-start.3) | copy-done | bytes 131096
  25.6 0.0 copy-start.4
  25.6 0.7 %copy-done.4 = f32[8,128]{1,0:T(8,128)S(1)} copy-done((f32[8,128]{1,0:T(8,128)S(1)}, f32[8,128]{1,0:T(8,128)}, u32[]{:S(2)}) %copy-start.4) | copy-done | bytes 4120
  26.3 0.1 shard_map.106
  26.4 0.1 collective-permute-start.4
  26.4 0.0 collective-permute-done.3.refs_4_
  26.5 0.0 collective-permute-done.9.refs_3_
  26.5 0.5 collective-permute-start.10
  26.9 0.0 collective-permute-done.7.refs_2_
  27.0 0.1 collective-permute-start.8
  27.0 0.9 %collective-permute-done.5.refs_1_ = f32[272,128]{1,0:T(8,128)S(1)} collective-permute-done((f32[272,128]{1,0:T(8,128)S(1)}, f32[272,128]{1,0:T(8,128)S(1)}, u32[]{:S(2)}, u32[]{:S(2)}) %collective-permute-start.5) | collective-permute-done | bytes 139296 | tf_op jit(solution)/shard_map/ppermute | solution.py:450
  27.9 0.0 collective-permute-start.6
  27.9 0.5 collective-permute-start.11
  28.4 0.0 collective-permute-done.4.refs_5_.first_swapped
  28.4 0.0 collective-permute-done.10.refs_8_
  28.4 0.0 collective-permute-done.8.refs_7_
  28.4 0.8 %collective-permute-done.6.refs_6_ = f32[272,128]{1,0:T(8,128)S(1)} collective-permute-done((f32[272,128]{1,0:T(8,128)S(1)}, f32[272,128]{1,0:T(8,128)S(1)}, u32[]{:S(2)}, u32[]{:S(2)}) %collective-permute-start.6) | collective-permute-done | bytes 139296 | tf_op jit(solution)/shard_map/ppermute | solution.py:450
  29.3 0.2 collective-permute-done.11.refs_9_
  29.5 2.6 %collective-permute-start.18 = (f32[3,4,128,128]{3,2,1,0:T(8,128)}, f32[3,4,128,128]{3,2,1,0:T(8,128)S(1)}, u32[]{:S(2)}, u32[]{:S(2)}) collective-permute-start(f32[3,4,128,128]{3,2,1,0:T(8,128)} %get-tuple-element.60.refs_1_), channel_id=1, source_target_pairs={{0,16},{1,17},{2,18},{3,19},{4,20},{5,21},{6,22},{7,23},{8,8},{9,9... | collective-permute-start | bytes 2359304 | tf_op jit(solution)/shard_map/ppermute | solution.py:450
  32.0 7.8 %shard_map.107 = (f32[4,128,128]{2,1,0:T(8,128)S(1)}, f32[2,128,128]{2,1,0:T(8,128)S(1)}, f32[4,128,128]{2,1,0:T(8,128)S(1)}, f32[4,128,128]{2,1,0:T(8,128)S(1)}, f32[3,20,128,128]{3,2,1,0:T(8,128)S(1)}) custom-call(f32[8,128]{1,0:T(8,128)S(1)} %get-tuple-element.45.taps, bf16[256,256]{1,0:T(8,128)(2,1)S(1)} %get-tuple-element.46.weights, ...), custom_call_target="tpu_custom_call" | custom-call | tf_op jit(solution)/shard_map/pallas_call | solution.py:425
  39.8 4.1 %collective-permute-start.13 = (f32[2,128,128]{2,1,0:T(8,128)S(1)}, f32[2,128,128]{2,1,0:T(8,128)S(1)}, u32[]{:S(2)}, u32[]{:S(2)}) collective-permute-start(f32[2,128,128]{2,1,0:T(8,128)S(1)} %get-tuple-element.56), channel_id=1, source_target_pairs={{0,7},{1,0},{2,1},{3,2},{4,3},{5,4},{6,5},{7,6},{8,15},{9,8},{10,9... | collective-permute-start | bytes 393224 | tf_op jit(solution)/shard_map/ppermute | solution.py:450
  43.9 3.1 %collective-permute-start.17 = (f32[1,4,128,128]{3,2,1,0:T(8,128)}, f32[1,4,128,128]{3,2,1,0:T(8,128)S(1)}, u32[]{:S(2)}, u32[]{:S(2)}) collective-permute-start(f32[1,4,128,128]{3,2,1,0:T(8,128)} %get-tuple-element.37.refs_0_), channel_id=1, source_target_pairs={{0,16},{1,17},{2,18},{3,19},{4,20},{5,21},{6,22},{7,23},{8,8},{9,9... | collective-permute-start | bytes 786440 | tf_op jit(solution)/shard_map/ppermute | solution.py:450
  47.1 0.1 collective-permute-start.12
  47.1 0.1 collective-permute-start.16
  47.2 0.0 collective-permute-done.13.refs_1_
  47.2 0.5 collective-permute-start.15
  47.7 7.1 %collective-permute-done.12.refs_0_ = f32[2,128,128]{2,1,0:T(8,128)S(1)} collective-permute-done((f32[2,128,128]{2,1,0:T(8,128)S(1)}, f32[2,128,128]{2,1,0:T(8,128)S(1)}, u32[]{:S(2)}, u32[]{:S(2)}) %collective-permute-start.12) | collective-permute-done | bytes 131104 | tf_op jit(solution)/shard_map/ppermute | solution.py:450
  54.8 0.0 collective-permute-start.14
  54.8 0.0 collective-permute-done.17.refs_8_
  54.8 0.0 collective-permute-done.15.refs_3_
  54.8 1.3 %collective-permute-done.14.refs_2_ = f32[2,128,128]{2,1,0:T(8,128)S(1)} collective-permute-done((f32[2,128,128]{2,1,0:T(8,128)S(1)}, f32[2,128,128]{2,1,0:T(8,128)S(1)}, u32[]{:S(2)}, u32[]{:S(2)}) %collective-permute-start.14) | collective-permute-done | bytes 131104 | tf_op jit(solution)/shard_map/ppermute | solution.py:450
  56.1 0.0 collective-permute-done.16.refs_7_
  56.1 0.0 collective-permute-done.18.refs_9_
  56.1 2.7 %shard_map.108 = (f32[4,64,256]{2,1,0:T(8,128)S(1)}, f32[64,256]{1,0:T(8,128)S(1)}, f32[64,256]{1,0:T(8,128)S(1)}, f32[192,256]{1,0:T(8,128)S(1)}, f32[128,256]{1,0:T(8,128)S(1)}) custom-call(f32[8,128]{1,0:T(8,128)S(1)} %get-tuple-element.45.taps, bf16[256,256]{1,0:T(8,128)(2,1)S(1)} %get-tuple-element.46.weights, ...), custom_call_target="tpu_custom_call" | custom-call | tf_op jit(solution)/shard_map/pallas_call | solution.py:425
  58.9 0.7 %collective-permute-start.19 = (f32[192,256]{1,0:T(8,128)S(1)}, f32[192,256]{1,0:T(8,128)S(1)}, u32[]{:S(2)}, u32[]{:S(2)}) collective-permute-start(f32[192,256]{1,0:T(8,128)S(1)} %get-tuple-element.61), channel_id=1, source_target_pairs={{0,16},{1,17},{2,18},{3,19},{4,20},{5,21},{6,22},{7,23},{8,0},{9,1... | collective-permute-start | bytes 589832 | tf_op jit(solution)/shard_map/ppermute | solution.py:450
  59.6 0.7 %collective-permute-start.20 = (f32[128,256]{1,0:T(8,128)S(1)}, f32[128,256]{1,0:T(8,128)S(1)}, u32[]{:S(2)}, u32[]{:S(2)}) collective-permute-start(f32[128,256]{1,0:T(8,128)S(1)} %get-tuple-element.62), channel_id=1, source_target_pairs={{0,24},{1,25},{2,26},{3,27},{4,28},{5,29},{6,30},{7,31},{8,16},{9,... | collective-permute-start | bytes 393224 | tf_op jit(solution)/shard_map/ppermute | solution.py:450
  60.3 0.0 collective-permute-start.21
  60.3 3.6 %collective-permute-done.19 = f32[192,256]{1,0:T(8,128)S(1)} collective-permute-done((f32[192,256]{1,0:T(8,128)S(1)}, f32[192,256]{1,0:T(8,128)S(1)}, u32[]{:S(2)}, u32[]{:S(2)}) %collective-permute-start.19) | collective-permute-done | bytes 196640 | tf_op jit(solution)/shard_map/ppermute | solution.py:450
  63.9 2.5 %collective-permute-done.20 = f32[128,256]{1,0:T(8,128)S(1)} collective-permute-done((f32[128,256]{1,0:T(8,128)S(1)}, f32[128,256]{1,0:T(8,128)S(1)}, u32[]{:S(2)}, u32[]{:S(2)}) %collective-permute-start.20) | collective-permute-done | bytes 131104 | tf_op jit(solution)/shard_map/ppermute | solution.py:450
  66.5 0.7 %select_bitcast_fusion = f32[1,4,64,256]{3,2,1,0:T(8,128)} fusion(f32[4,64,256]{2,1,0:T(8,128)S(1)} %bitcast.7, f32[4,64,256]{2,1,0:T(8,128)S(1)} %get-tuple-element.63, pred[]{:T(512)S(6)} %eq.5), kind=kLoop, calls=%fused_computation.1 | loop fusion | flops 65536 | bytes 786433 | tf_op jit(solution)/shard_map/broadcast_in_dim | solution.py:517
  67.2 0.0 collective-permute-done.21
  67.2 0.7 fusion.1
  (6 shorter events, 0.1 us)
Async XLA Ops:
  0.6 7.9 %copy-start = (f32[3,4,256]{2,1,0:T(4,128)S(1)}, f32[3,4,256]{2,1,0:T(4,128)}, u32[]{:S(2)}) copy-start(f32[3,4,256]{2,1,0:T(4,128)} %param.11) | copy-start | bytes 36868
  2.3 9.3 %collective-permute-start = (f32[136,256]{1,0:T(8,128)S(1)}, f32[136,256]{1,0:T(8,128)S(1)}, u32[]{:S(2)}, u32[]{:S(2)}) collective-permute-start(f32[136,256]{1,0:T(8,128)S(1)} %get-tuple-element.35), channel_id=1, source_target_pairs={{0,8},{1,9},{2,10},{3,11},{4,12},{5,13},{6,14},{7,15},{8,24},{9,25... | collective-permute-start | bytes 417800 | tf_op jit(solution)/shard_map/ppermute | solution.py:450
  2.8 8.8 %collective-permute-start.1 = (f32[136,256]{1,0:T(8,128)S(1)}, f32[136,256]{1,0:T(8,128)S(1)}, u32[]{:S(2)}, u32[]{:S(2)}) collective-permute-start(f32[136,256]{1,0:T(8,128)S(1)} %get-tuple-element.34.low), channel_id=1, source_target_pairs={{0,0},{1,1},{2,2},{3,3},{4,4},{5,5},{6,6},{7,7},{8,16},{9,17},{10,... | collective-permute-start | bytes 417800 | tf_op jit(solution)/shard_map/ppermute | solution.py:450
  3.5 8.1 %collective-permute-start.2 = (f32[8,256]{1,0:T(8,128)S(1)}, f32[8,256]{1,0:T(8,128)S(1)}, u32[]{:S(2)}, u32[]{:S(2)}) collective-permute-start(f32[8,256]{1,0:T(8,128)S(1)} %pad.4), channel_id=1, source_target_pairs={{0,16},{1,17},{2,18},{3,19},{4,20},{5,21},{6,22},{7,23},{8,24},{9,... | collective-permute-start | bytes 24584 | tf_op jit(solution)/shard_map/ppermute | solution.py:450
  11.7 14.7 %collective-permute-start.3 = (f32[272,128]{1,0:T(8,128)S(1)}, f32[272,128]{1,0:T(8,128)S(1)}, u32[]{:S(2)}, u32[]{:S(2)}) collective-permute-start(f32[272,128]{1,0:T(8,128)S(1)} %shard_map.104.refs_0_.first_own), channel_id=1, source_target_pairs={{0,6},{1,7},{2,0},{3,1},{4,2},{5,3},{6,4},{7,5},{8,14},{9,15},{10,... | collective-permute-start | bytes 417800 | tf_op jit(solution)/shard_map/ppermute | solution.py:450
  15.4 11.1 %collective-permute-start.9 = (f32[272,128]{1,0:T(8,128)S(1)}, f32[272,128]{1,0:T(8,128)S(1)}, u32[]{:S(2)}, u32[]{:S(2)}) collective-permute-start(f32[272,128]{1,0:T(8,128)S(1)} %shard_map.104.refs_0_.first_own), channel_id=1, source_target_pairs={{0,2},{1,3},{2,4},{3,5},{4,6},{5,7},{6,0},{7,1},{8,10},{9,11},{10,... | collective-permute-start | bytes 417800 | tf_op jit(solution)/shard_map/ppermute | solution.py:450
  15.4 11.5 %collective-permute-start.7 = (f32[272,128]{1,0:T(8,128)S(1)}, f32[272,128]{1,0:T(8,128)S(1)}, u32[]{:S(2)}, u32[]{:S(2)}) collective-permute-start(f32[272,128]{1,0:T(8,128)S(1)} %shard_map.104.refs_0_.first_own), channel_id=1, source_target_pairs={{0,7},{1,0},{2,1},{3,2},{4,3},{5,4},{6,5},{7,6},{8,15},{9,8},{10,9... | collective-permute-start | bytes 417800 | tf_op jit(solution)/shard_map/ppermute | solution.py:450
  20.2 7.8 %collective-permute-start.5 = (f32[272,128]{1,0:T(8,128)S(1)}, f32[272,128]{1,0:T(8,128)S(1)}, u32[]{:S(2)}, u32[]{:S(2)}) collective-permute-start(f32[272,128]{1,0:T(8,128)S(1)} %shard_map.104.refs_0_.first_own), channel_id=1, source_target_pairs={{0,1},{1,2},{2,3},{3,4},{4,5},{5,6},{6,7},{7,0},{8,9},{9,10},{10,1... | collective-permute-start | bytes 417800 | tf_op jit(solution)/shard_map/ppermute | solution.py:450
  22.6 1.1 %copy-start.1 = (f32[3,4,128,128]{3,2,1,0:T(8,128)S(1)}, f32[3,4,128,128]{3,2,1,0:T(8,128)}, u32[]{:S(2)}) copy-start(f32[3,4,128,128]{3,2,1,0:T(8,128)} %get-tuple-element.60.refs_1_) | copy-start | bytes 2359300
  23.7 0.9 %copy-start.2 = (f32[1,4,128,128]{3,2,1,0:T(8,128)S(1)}, f32[1,4,128,128]{3,2,1,0:T(8,128)}, u32[]{:S(2)}) copy-start(f32[1,4,128,128]{3,2,1,0:T(8,128)} %get-tuple-element.37.refs_0_) | copy-start | bytes 786436
  24.7 0.9 %copy-start.3 = (bf16[256,256]{1,0:T(8,128)(2,1)S(1)}, bf16[256,256]{1,0:T(8,128)(2,1)}, u32[]{:S(2)}) copy-start(bf16[256,256]{1,0:T(8,128)(2,1)} %get-tuple-element.40.refs_3_) | copy-start | bytes 393220
  25.6 0.7 %copy-start.4 = (f32[8,128]{1,0:T(8,128)S(1)}, f32[8,128]{1,0:T(8,128)}, u32[]{:S(2)}) copy-start(f32[8,128]{1,0:T(8,128)} %get-tuple-element.39.refs_2_) | copy-start | bytes 12292
  26.4 2.1 %collective-permute-start.4 = (f32[272,128]{1,0:T(8,128)S(1)}, f32[272,128]{1,0:T(8,128)S(1)}, u32[]{:S(2)}, u32[]{:S(2)}) collective-permute-start(f32[272,128]{1,0:T(8,128)S(1)} %shard_map.104.refs_0_.first_own), channel_id=1, source_target_pairs={{0,8},{1,9},{2,10},{3,11},{4,12},{5,13},{6,14},{7,15},{8,0},{9,1},... | collective-permute-start | bytes 417800 | tf_op jit(solution)/shard_map/ppermute | solution.py:450
  26.5 2.0 %collective-permute-start.10 = (f32[272,128]{1,0:T(8,128)S(1)}, f32[272,128]{1,0:T(8,128)S(1)}, u32[]{:S(2)}, u32[]{:S(2)}) collective-permute-start(f32[272,128]{1,0:T(8,128)S(1)} %collective-permute-done.9.refs_3_), channel_id=1, source_target_pairs={{0,8},{1,9},{2,10},{3,11},{4,12},{5,13},{6,14},{7,15},{8,0},{9,1},... | collective-permute-start | bytes 417800 | tf_op jit(solution)/shard_map/ppermute | solution.py:450
  27.0 1.5 %collective-permute-start.8 = (f32[272,128]{1,0:T(8,128)S(1)}, f32[272,128]{1,0:T(8,128)S(1)}, u32[]{:S(2)}, u32[]{:S(2)}) collective-permute-start(f32[272,128]{1,0:T(8,128)S(1)} %collective-permute-done.7.refs_2_), channel_id=1, source_target_pairs={{0,8},{1,9},{2,10},{3,11},{4,12},{5,13},{6,14},{7,15},{8,0},{9,1},... | collective-permute-start | bytes 417800 | tf_op jit(solution)/shard_map/ppermute | solution.py:450
  27.9 1.4 %collective-permute-start.6 = (f32[272,128]{1,0:T(8,128)S(1)}, f32[272,128]{1,0:T(8,128)S(1)}, u32[]{:S(2)}, u32[]{:S(2)}) collective-permute-start(f32[272,128]{1,0:T(8,128)S(1)} %collective-permute-done.5.refs_1_), channel_id=1, source_target_pairs={{0,8},{1,9},{2,10},{3,11},{4,12},{5,13},{6,14},{7,15},{8,0},{9,1},... | collective-permute-start | bytes 417800 | tf_op jit(solution)/shard_map/ppermute | solution.py:450
  27.9 1.6 %collective-permute-start.11 = (f32[272,128]{1,0:T(8,128)S(1)}, f32[272,128]{1,0:T(8,128)S(1)}, u32[]{:S(2)}, u32[]{:S(2)}) collective-permute-start(f32[272,128]{1,0:T(8,128)S(1)} %collective-permute-done.3.refs_4_), channel_id=1, source_target_pairs={{0,8},{1,9},{2,10},{3,11},{4,12},{5,13},{6,14},{7,15},{8,0},{9,1},... | collective-permute-start | bytes 417800 | tf_op jit(solution)/shard_map/ppermute | solution.py:450
  29.5 26.7 %collective-permute-start.18 = (f32[3,4,128,128]{3,2,1,0:T(8,128)}, f32[3,4,128,128]{3,2,1,0:T(8,128)S(1)}, u32[]{:S(2)}, u32[]{:S(2)}) collective-permute-start(f32[3,4,128,128]{3,2,1,0:T(8,128)} %get-tuple-element.60.refs_1_), channel_id=1, source_target_pairs={{0,16},{1,17},{2,18},{3,19},{4,20},{5,21},{6,22},{7,23},{8,8},{9,9... | collective-permute-start | bytes 2359304 | tf_op jit(solution)/shard_map/ppermute | solution.py:450
  39.8 7.4 %collective-permute-start.13 = (f32[2,128,128]{2,1,0:T(8,128)S(1)}, f32[2,128,128]{2,1,0:T(8,128)S(1)}, u32[]{:S(2)}, u32[]{:S(2)}) collective-permute-start(f32[2,128,128]{2,1,0:T(8,128)S(1)} %get-tuple-element.56), channel_id=1, source_target_pairs={{0,7},{1,0},{2,1},{3,2},{4,3},{5,4},{6,5},{7,6},{8,15},{9,8},{10,9... | collective-permute-start | bytes 393224 | tf_op jit(solution)/shard_map/ppermute | solution.py:450
  43.9 10.9 %collective-permute-start.17 = (f32[1,4,128,128]{3,2,1,0:T(8,128)}, f32[1,4,128,128]{3,2,1,0:T(8,128)S(1)}, u32[]{:S(2)}, u32[]{:S(2)}) collective-permute-start(f32[1,4,128,128]{3,2,1,0:T(8,128)} %get-tuple-element.37.refs_0_), channel_id=1, source_target_pairs={{0,16},{1,17},{2,18},{3,19},{4,20},{5,21},{6,22},{7,23},{8,8},{9,9... | collective-permute-start | bytes 786440 | tf_op jit(solution)/shard_map/ppermute | solution.py:450
  47.1 7.7 %collective-permute-start.12 = (f32[2,128,128]{2,1,0:T(8,128)S(1)}, f32[2,128,128]{2,1,0:T(8,128)S(1)}, u32[]{:S(2)}, u32[]{:S(2)}) collective-permute-start(f32[2,128,128]{2,1,0:T(8,128)S(1)} %get-tuple-element.56), channel_id=1, source_target_pairs={{0,1},{1,2},{2,3},{3,4},{4,5},{5,6},{6,7},{7,0},{8,9},{9,10},{10,1... | collective-permute-start | bytes 393224 | tf_op jit(solution)/shard_map/ppermute | solution.py:450
  47.1 9.0 %collective-permute-start.16 = (f32[4,128,128]{2,1,0:T(8,128)S(1)}, f32[4,128,128]{2,1,0:T(8,128)S(1)}, u32[]{:S(2)}, u32[]{:S(2)}) collective-permute-start(f32[4,128,128]{2,1,0:T(8,128)S(1)} %get-tuple-element.59.refs_6_), channel_id=1, source_target_pairs={{0,8},{1,9},{2,10},{3,11},{4,12},{5,13},{6,14},{7,15},{8,0},{9,1},... | collective-permute-start | bytes 786440 | tf_op jit(solution)/shard_map/ppermute | solution.py:450
  47.2 7.6 %collective-permute-start.15 = (f32[2,128,128]{2,1,0:T(8,128)S(1)}, f32[2,128,128]{2,1,0:T(8,128)S(1)}, u32[]{:S(2)}, u32[]{:S(2)}) collective-permute-start(f32[2,128,128]{2,1,0:T(8,128)S(1)} %collective-permute-done.13.refs_1_), channel_id=1, source_target_pairs={{0,8},{1,9},{2,10},{3,11},{4,12},{5,13},{6,14},{7,15},{8,0},{9,1},... | collective-permute-start | bytes 393224 | tf_op jit(solution)/shard_map/ppermute | solution.py:450
  54.8 1.3 %collective-permute-start.14 = (f32[2,128,128]{2,1,0:T(8,128)S(1)}, f32[2,128,128]{2,1,0:T(8,128)S(1)}, u32[]{:S(2)}, u32[]{:S(2)}) collective-permute-start(f32[2,128,128]{2,1,0:T(8,128)S(1)} %collective-permute-done.12.refs_0_), channel_id=1, source_target_pairs={{0,8},{1,9},{2,10},{3,11},{4,12},{5,13},{6,14},{7,15},{8,0},{9,1},... | collective-permute-start | bytes 393224 | tf_op jit(solution)/shard_map/ppermute | solution.py:450
  58.9 5.0 %collective-permute-start.19 = (f32[192,256]{1,0:T(8,128)S(1)}, f32[192,256]{1,0:T(8,128)S(1)}, u32[]{:S(2)}, u32[]{:S(2)}) collective-permute-start(f32[192,256]{1,0:T(8,128)S(1)} %get-tuple-element.61), channel_id=1, source_target_pairs={{0,16},{1,17},{2,18},{3,19},{4,20},{5,21},{6,22},{7,23},{8,0},{9,1... | collective-permute-start | bytes 589832 | tf_op jit(solution)/shard_map/ppermute | solution.py:450
  59.6 6.9 %collective-permute-start.20 = (f32[128,256]{1,0:T(8,128)S(1)}, f32[128,256]{1,0:T(8,128)S(1)}, u32[]{:S(2)}, u32[]{:S(2)}) collective-permute-start(f32[128,256]{1,0:T(8,128)S(1)} %get-tuple-element.62), channel_id=1, source_target_pairs={{0,24},{1,25},{2,26},{3,27},{4,28},{5,29},{6,30},{7,31},{8,16},{9,... | collective-permute-start | bytes 393224 | tf_op jit(solution)/shard_map/ppermute | solution.py:450
  60.3 6.9 %collective-permute-start.21 = (f32[64,256]{1,0:T(8,128)S(1)}, f32[64,256]{1,0:T(8,128)S(1)}, u32[]{:S(2)}, u32[]{:S(2)}) collective-permute-start(f32[64,256]{1,0:T(8,128)S(1)} %get-tuple-element.65), channel_id=1, source_target_pairs={{0,8},{1,9},{2,10},{3,11},{4,12},{5,13},{6,14},{7,15},{8,0},{9,1},... | collective-permute-start | bytes 196616 | tf_op jit(solution)/shard_map/ppermute | solution.py:450

commit v6 on v5

--- a/solution.py
+++ b/solution.py
@@ -9,7 +9,7 @@
 
 TICKS = 3
 CZ = 64
-GROUP = 4
+GROUP = 6
 FIELD_ROWS = 16
 OWN_KINDS, FIRST_KINDS, ACROSS_KINDS = 12, 13, 14
 LEAD = 1
@@ -385,12 +385,16 @@
     saved[...] = kept[...]
 
     def after(step, state):
-        for where, source in ((sec == 0, series), (sec == last, stored)):
-
-            @pl.when(where)
-            def _(source=source):
-                part = source[0][step] if step < LEAD else source[1][step - LEAD]
-                total[...] += state[reach : reach + planes] * part
+        @pl.when(sec == 0)
+        def _():
+            for i in range(planes):
+                part = series[1][step - LEAD, i] if step >= LEAD else to_tile(series[0][step, i], scratch)
+                total[i] += state[reach + i] * part
+
+        @pl.when(sec == last)
+        def _():
+            part = stored[0][step] if step < LEAD else stored[1][step - LEAD]
+            total[...] += state[reach : reach + planes] * part
 
     run_steps(kinds, taps, weights, reach, slab, other, first, second, factor, begun - reach, after)
     state = (slab, other)[reach % 2]
@@ -443,23 +447,24 @@
     sec = lax.axis_index("sec")
     last = n_sec - 1
 
-    def send(array, by_sec, shift=lambda s: 0):
-        pairs = [
-            (s * n_gx + g, t * n_gx + (g + shift(s)) % n_gx) for s, t in enumerate(by_sec) for g in range(n_gx)
-        ]
+    def send(array, by_sec, shift=0):
+        by_sec = by_sec.items() if isinstance(by_sec, dict) else enumerate(by_sec)
+        pairs = [(s * n_gx + g, t * n_gx + (g + shift) % n_gx) for s, t in by_sec for g in range(n_gx)]
         return lax.ppermute(array, ("sec", "gx"), pairs)
 
-    same, beside, across, crossing = (0, 1, 2, 3), (1, 0, 3, 2), (2, 3, 0, 1), (2, 1, 0, 3)
+    same, beside, across = (0, 1, 2, 3), (1, 0, 3, 2), (2, 3, 0, 1)
     whole = incoming[0]
     types = jnp.pad(block_types.astype(jnp.float32), ((0, 7), (0, cells - steps)))
     low, high = (jnp.concatenate([each.reshape(-1, cells), types]) for each in (whole[:pair], whole[pair:]))
-    backward, high, low = lax.optimization_barrier((backward, high, low))
+    lead = backward[:LEAD]
+    backward, lead, high, low = lax.optimization_barrier((backward, lead, high, low))
     moved_high = send(high, (1, 3, 0, 2))
     moved_low = send(low, (0, 2, 1, 3))
-    across_types = send(types, across)
+    across_types = send(high[pair * orients :], across)
+    early_last = send(lead.astype(jnp.float32), {2: 0})
     lines = lax.dynamic_slice_in_dim(fields, sec % 2 * pair, pair, axis=1).reshape(-1, cells)
     settled = prepare(backward, axial_taps, lateral_taps, depth_taps, bend_diagonal, bend_coupling)
-    early_stored, late_stored = settled[:2]
+    lines, early_last, *settled = lax.optimization_barrier((lines, early_last, *settled))
 
     tile = pltpu.VMEM((rows, lanes), jnp.float32)
     packed = pltpu.VMEM((GROUP * rows, 2 * lanes), jnp.bfloat16)
@@ -472,8 +477,7 @@
     (piece,) = call(
         pack_kernel, [(pair * rows + FIELD_ROWS, lanes)], [tile], [low, moved_high, moved_low, across_types, lines]
     )
-    own = [send(piece, same, lambda s: shift) for shift in far]
-    early_last = send(early_stored, crossing)
+    own = [send(piece, same, shift) for shift in far]
     settled = pl.pallas_call(
         settle_kernel,
         in_specs=[IN_VMEM] * len(settled),
@@ -484,8 +488,8 @@
     own[-1], *settled = lax.optimization_barrier((own[-1], *settled))
     stored, (taps, weights) = settled[:2], settled[2:]
     swapped = [send(each, beside) for each in [piece] + own]
-    late_stored, *swapped = lax.optimization_barrier((late_stored, *swapped))
-    late_last = send(late_stored, crossing)
+    late_stored, *swapped = lax.optimization_barrier((stored[1], *swapped))
+    late_last = send(late_stored, {2: 0})
     firsts = [piece, swapped[0]]
     middle, piece, kept, total, factor = call(
         functools.partial(early_kernel, tuple(-shift for shift in (0,) + far)),
@@ -494,7 +498,7 @@
         work(reach[0]),
         [taps, weights, piece, *own, *swapped, *stored],
     )
-    own = [send(piece, same, lambda s: shift) for shift in near]
+    own = [send(piece, same, shift) for shift in near]
     beside_total = send(total, beside)
     swapped = [send(each, beside) for each in own]
     held = planes * (orients // n_sec)
@@ -524,7 +528,7 @@
         and planes % 2 == 0
         and 2 * orients == 2 * CZ == cells // 2 == 128
         and kinds * planes <= FIELD_ROWS and 10 * kinds * planes <= 2 * orients
-        and planes >= GROUP
+        and GROUP < 2 * planes
     )
 
 

time: 68.3 us -> 68 us (level)
  starting transfers between devices: 27.5 us -> 23.2 us
  waiting for transfers between devices: 19.6 us -> 22.5 us
  local copies, waits for them, and re-layouts: 4.69 us -> 5.61 us
    ppermute x22, starting transfers between devices: 27.5 us -> 23.2 us  [send(): return lax.ppermute(array, ('sec', 'gx'), pairs)]
    ppermute x22, waiting for transfers between devices: 19.6 us -> 22.5 us  [send(): return lax.ppermute(array, ('sec', 'gx'), pairs)]
    slice x0 -> x2, local copies, waits for them, and re-layouts: none -> 0.91 us  [the longest x1 0.91 us: paired(): lead = backward[:LEAD]]
  transfers between devices with their start and end apart: 22 -> 22, of which waited for: 8 -> 9; matrix products, arithmetic and copies ran while one was open for 1% -> 1% of each run, Pallas kernels for 15% -> 15%
where the time goes in v6:
time: 68 us; the launch traced here: 67.6 us
  starting transfers between devices  23.2 us (34%)
  waiting for transfers between devices  22.5 us (33%)
  Pallas kernels  13.4 us (20%)
  local copies, waits for them, and re-layouts  5.61 us (8%)
  other arithmetic  2.11 us (3%)
  between operations  0.79 us (1%)
    ppermute x22, starting transfers between devices, send(): return lax.ppermute(array, ('sec', 'gx'), pairs)  23.2 us
    ppermute x22, waiting for transfers between devices, send(): return lax.ppermute(array, ('sec', 'gx'), pairs)  22.5 us
    pallas_call x3, Pallas kernels, call(): pl.pallas_call(kernel, in_specs=[IN_VMEM] * len(operands), out_specs=[IN_...  10.8 us
    unnamed x10, local copies, waits for them, and re-layouts  3.68 us
    pallas_call x1, Pallas kernels, prepare(): pl.pallas_call(prepare_kernel, in_specs=[pl.BlockSpec(memory_space=pltpu....  2.45 us
  transfers between devices with their start and end apart: 22, of which 9 were waited for; matrix products, arithmetic and copies ran while one was open for 1% of the time, Pallas kernels for 15%

profile of v6, /device:TPU:0, one launch (start us, length us, event | category | flops | bytes accessed | tf_op | source)
XLA Modules:
  0.0 67.6 jit_solution(1420484041604568443)
XLA Ops:
  0.6 0.0 copy-start
  0.6 0.7 convert_element_type.8
  1.3 0.9 %slice.23 = bf16[1,4,64,256]{3,2,1,0:T(8,128)(2,1)S(1)} slice(bf16[4,4,64,256]{3,2,1,0:T(8,128)(2,1)} %refs_0_), slice={[0:1], [0:4], [0:64], [0:256]} | slice | bytes 262144 | tf_op jit(solution)/shard_map/slice | solution.py:459
  2.2 1.0 %fusion.4 = (f32[1,2,64,256]{3,2,1,0:T(8,128)S(1)}, f32[1,2,64,256]{3,2,1,0:T(8,128)S(1)}) fusion(f32[1,4,64,256]{3,2,1,0:T(8,128)} %param.9), kind=kLoop, calls=%fused_computation.11 | loop fusion | bytes 524288 | tf_op jit(solution)/shard_map/slice | solution.py:458
  3.3 1.3 %collective-permute-start.3 = (f32[1,4,64,256]{3,2,1,0:T(8,128)S(1)}, f32[1,4,64,256]{3,2,1,0:T(8,128)S(1)}, u32[]{:S(2)}, u32[]{:S(2)}) collective-permute-start(f32[1,4,64,256]{3,2,1,0:T(8,128)S(1)} %convert_element_type.9), channel_id=1, source_target_pairs={{16,0},{17,1},{18,2},{19,3},{20,4},{21,5},{22,6},{23,7}} | collective-permute-start | bytes 786440 | tf_op jit(solution)/shard_map/ppermute | solution.py:453
  4.6 0.7 collective-permute-start.1
  5.3 4.4 %collective-permute-start = (f32[136,256]{1,0:T(8,128)S(1)}, f32[136,256]{1,0:T(8,128)S(1)}, u32[]{:S(2)}, u32[]{:S(2)}) collective-permute-start(f32[136,256]{1,0:T(8,128)S(1)} %get-tuple-element.42), channel_id=1, source_target_pairs={{0,8},{1,9},{2,10},{3,11},{4,12},{5,13},{6,14},{7,15},{8,24},{9,25... | collective-permute-start | bytes 417800 | tf_op jit(solution)/shard_map/ppermute | solution.py:453
  9.6 0.0 collective-permute-start.2
  9.6 0.0 copy-done
  9.6 2.4 %shard_map.104 = (f32[1,4,128,128]{3,2,1,0:T(8,128)}, f32[3,4,128,128]{3,2,1,0:T(8,128)}, f32[8,128]{1,0:T(8,128)}, bf16[256,256]{1,0:T(8,128)(2,1)}) custom-call(bf16[4,4,64,256]{3,2,1,0:T(8,128)(2,1)} %refs_0_, f32[3,64]{1,0:T(4,128)} %refs_1_.1, f32[3,64]{1,0:T(4,128)} %refs_2_.1, f32[3,64]{1,0:T(4,128)} %refs_3_.1, f32[1,64]{1,0:T(1,128)} %bitcast.11, ...), custom_call_target="tpu_custom_call" | custom-call | tf_op jit(solution)/shard_map/pallas_call | solution.py:209
  12.1 0.0 collective-permute-done.3.refs_8_
  12.1 2.9 %collective-permute-done.2.across = f32[8,256]{1,0:T(8,128)S(1)} collective-permute-done((f32[8,256]{1,0:T(8,128)S(1)}, f32[8,256]{1,0:T(8,128)S(1)}, u32[]{:S(2)}, u32[]{:S(2)}) %collective-permute-start.2) | collective-permute-done | bytes 8224 | tf_op jit(solution)/shard_map/ppermute | solution.py:453
  15.0 0.0 collective-permute-done.1.moved_low
  15.0 0.0 collective-permute-done.moved_high
  15.0 0.1 shard_map.105.refs_0_.first_own
  15.2 4.8 %collective-permute-start.4 = (f32[272,128]{1,0:T(8,128)S(1)}, f32[272,128]{1,0:T(8,128)S(1)}, u32[]{:S(2)}, u32[]{:S(2)}) collective-permute-start(f32[272,128]{1,0:T(8,128)S(1)} %shard_map.105.refs_0_.first_own), channel_id=1, source_target_pairs={{0,6},{1,7},{2,0},{3,1},{4,2},{5,3},{6,4},{7,5},{8,14},{9,15},{10,... | collective-permute-start | bytes 417800 | tf_op jit(solution)/shard_map/ppermute | solution.py:453
  20.0 0.0 collective-permute-start.10
  20.0 4.7 %collective-permute-start.8 = (f32[272,128]{1,0:T(8,128)S(1)}, f32[272,128]{1,0:T(8,128)S(1)}, u32[]{:S(2)}, u32[]{:S(2)}) collective-permute-start(f32[272,128]{1,0:T(8,128)S(1)} %shard_map.105.refs_0_.first_own), channel_id=1, source_target_pairs={{0,7},{1,0},{2,1},{3,2},{4,3},{5,4},{6,5},{7,6},{8,15},{9,8},{10,9... | collective-permute-start | bytes 417800 | tf_op jit(solution)/shard_map/ppermute | solution.py:453
  24.7 0.0 collective-permute-start.6
  24.7 0.0 collective-permute-start.5
  24.7 0.0 copy-start.1
  24.7 1.1 %copy-done.1 = f32[3,4,128,128]{3,2,1,0:T(8,128)S(1)} copy-done((f32[3,4,128,128]{3,2,1,0:T(8,128)S(1)}, f32[3,4,128,128]{3,2,1,0:T(8,128)}, u32[]{:S(2)}) %copy-start.1) | copy-done | bytes 786456
  25.8 0.0 copy-start.2
  25.8 0.9 %copy-done.2 = f32[1,4,128,128]{3,2,1,0:T(8,128)S(1)} copy-done((f32[1,4,128,128]{3,2,1,0:T(8,128)S(1)}, f32[1,4,128,128]{3,2,1,0:T(8,128)}, u32[]{:S(2)}) %copy-start.2) | copy-done | bytes 262168
  26.8 0.0 copy-start.3
  26.8 0.9 %copy-done.3 = bf16[256,256]{1,0:T(8,128)(2,1)S(1)} copy-done((bf16[256,256]{1,0:T(8,128)(2,1)S(1)}, bf16[256,256]{1,0:T(8,128)(2,1)}, u32[]{:S(2)}) %copy-start.3) | copy-done | bytes 131096
  27.7 0.0 copy-start.4
  27.7 0.7 %copy-done.4 = f32[8,128]{1,0:T(8,128)S(1)} copy-done((f32[8,128]{1,0:T(8,128)S(1)}, f32[8,128]{1,0:T(8,128)}, u32[]{:S(2)}) %copy-start.4) | copy-done | bytes 4120
  28.4 0.1 shard_map.106
  28.5 0.0 collective-permute-done.4.refs_4_
  28.5 0.0 collective-permute-done.10.refs_3_
  28.5 0.6 collective-permute-start.11
  29.1 0.0 collective-permute-done.8.refs_2_
  29.1 0.1 collective-permute-start.9
  29.2 3.3 %collective-permute-done.6.refs_1_ = f32[272,128]{1,0:T(8,128)S(1)} collective-permute-done((f32[272,128]{1,0:T(8,128)S(1)}, f32[272,128]{1,0:T(8,128)S(1)}, u32[]{:S(2)}, u32[]{:S(2)}) %collective-permute-start.6) | collective-permute-done | bytes 139296 | tf_op jit(solution)/shard_map/ppermute | solution.py:453
  32.5 0.0 collective-permute-start.7
  32.5 0.5 collective-permute-start.12
  33.0 0.0 collective-permute-done.5.refs_5_.first_swapped
  33.0 0.0 collective-permute-done.11.refs_8_
  33.0 0.0 collective-permute-done.9.refs_7_
  33.0 0.8 %collective-permute-done.7.refs_6_ = f32[272,128]{1,0:T(8,128)S(1)} collective-permute-done((f32[272,128]{1,0:T(8,128)S(1)}, f32[272,128]{1,0:T(8,128)S(1)}, u32[]{:S(2)}, u32[]{:S(2)}) %collective-permute-start.7) | collective-permute-done | bytes 139296 | tf_op jit(solution)/shard_map/ppermute | solution.py:453
  33.8 0.2 collective-permute-done.12.refs_9_
  34.0 1.3 %collective-permute-start.18 = (f32[3,4,128,128]{3,2,1,0:T(8,128)S(1)}, f32[3,4,128,128]{3,2,1,0:T(8,128)S(1)}, u32[]{:S(2)}, u32[]{:S(2)}) collective-permute-start(f32[3,4,128,128]{3,2,1,0:T(8,128)S(1)} %get-tuple-element.74.refs_11_), channel_id=1, source_target_pairs={{16,0},{17,1},{18,2},{19,3},{20,4},{21,5},{22,6},{23,7}} | collective-permute-start | bytes 2359304 | tf_op jit(solution)/shard_map/ppermute | solution.py:453
  35.3 7.7 %shard_map.107 = (f32[4,128,128]{2,1,0:T(8,128)S(1)}, f32[2,128,128]{2,1,0:T(8,128)S(1)}, f32[4,128,128]{2,1,0:T(8,128)S(1)}, f32[4,128,128]{2,1,0:T(8,128)S(1)}, f32[3,20,128,128]{3,2,1,0:T(8,128)S(1)}) custom-call(f32[8,128]{1,0:T(8,128)S(1)} %get-tuple-element.58.taps, bf16[256,256]{1,0:T(8,128)(2,1)S(1)} %get-tuple-element.59.weights, ...), custom_call_target="tpu_custom_call" | custom-call | tf_op jit(solution)/shard_map/pallas_call | solution.py:429
  43.0 1.7 %collective-permute-start.14 = (f32[2,128,128]{2,1,0:T(8,128)S(1)}, f32[2,128,128]{2,1,0:T(8,128)S(1)}, u32[]{:S(2)}, u32[]{:S(2)}) collective-permute-start(f32[2,128,128]{2,1,0:T(8,128)S(1)} %get-tuple-element.69), channel_id=1, source_target_pairs={{0,7},{1,0},{2,1},{3,2},{4,3},{5,4},{6,5},{7,6},{8,15},{9,8},{10,9... | collective-permute-start | bytes 393224 | tf_op jit(solution)/shard_map/ppermute | solution.py:453
  44.7 0.0 collective-permute-start.17
  44.7 0.4 collective-permute-start.13
  45.1 3.1 %collective-permute-done.14.refs_1_ = f32[2,128,128]{2,1,0:T(8,128)S(1)} collective-permute-done((f32[2,128,128]{2,1,0:T(8,128)S(1)}, f32[2,128,128]{2,1,0:T(8,128)S(1)}, u32[]{:S(2)}, u32[]{:S(2)}) %collective-permute-start.14) | collective-permute-done | bytes 131104 | tf_op jit(solution)/shard_map/ppermute | solution.py:453
  48.2 0.0 collective-permute-start.16
  48.2 5.1 %collective-permute-done.13.refs_0_ = f32[2,128,128]{2,1,0:T(8,128)S(1)} collective-permute-done((f32[2,128,128]{2,1,0:T(8,128)S(1)}, f32[2,128,128]{2,1,0:T(8,128)S(1)}, u32[]{:S(2)}, u32[]{:S(2)}) %collective-permute-start.13) | collective-permute-done | bytes 131104 | tf_op jit(solution)/shard_map/ppermute | solution.py:453
  53.3 0.0 collective-permute-start.15
  53.3 0.0 collective-permute-done.17.refs_7_
  53.4 0.0 collective-permute-done.16.refs_3_
  53.4 1.3 %collective-permute-done.15.refs_2_ = f32[2,128,128]{2,1,0:T(8,128)S(1)} collective-permute-done((f32[2,128,128]{2,1,0:T(8,128)S(1)}, f32[2,128,128]{2,1,0:T(8,128)S(1)}, u32[]{:S(2)}, u32[]{:S(2)}) %collective-permute-start.15) | collective-permute-done | bytes 131104 | tf_op jit(solution)/shard_map/ppermute | solution.py:453
  54.7 0.0 collective-permute-done.18.refs_9_
  54.7 3.0 %shard_map.108 = (f32[4,64,256]{2,1,0:T(8,128)S(1)}, f32[64,256]{1,0:T(8,128)S(1)}, f32[64,256]{1,0:T(8,128)S(1)}, f32[192,256]{1,0:T(8,128)S(1)}, f32[128,256]{1,0:T(8,128)S(1)}) custom-call(f32[8,128]{1,0:T(8,128)S(1)} %get-tuple-element.58.taps, bf16[256,256]{1,0:T(8,128)(2,1)S(1)} %get-tuple-element.59.weights, ...), custom_call_target="tpu_custom_call" | custom-call | tf_op jit(solution)/shard_map/pallas_call | solution.py:429
  57.7 2.4 %collective-permute-start.19 = (f32[192,256]{1,0:T(8,128)S(1)}, f32[192,256]{1,0:T(8,128)S(1)}, u32[]{:S(2)}, u32[]{:S(2)}) collective-permute-start(f32[192,256]{1,0:T(8,128)S(1)} %get-tuple-element.75), channel_id=1, source_target_pairs={{0,16},{1,17},{2,18},{3,19},{4,20},{5,21},{6,22},{7,23},{8,0},{9,1... | collective-permute-start | bytes 589832 | tf_op jit(solution)/shard_map/ppermute | solution.py:453
  60.1 0.0 collective-permute-start.20
  60.1 0.4 collective-permute-start.21
  60.5 3.9 %collective-permute-done.19 = f32[192,256]{1,0:T(8,128)S(1)} collective-permute-done((f32[192,256]{1,0:T(8,128)S(1)}, f32[192,256]{1,0:T(8,128)S(1)}, u32[]{:S(2)}, u32[]{:S(2)}) %collective-permute-start.19) | collective-permute-done | bytes 196640 | tf_op jit(solution)/shard_map/ppermute | solution.py:453
  64.4 1.7 %collective-permute-done.20 = f32[128,256]{1,0:T(8,128)S(1)} collective-permute-done((f32[128,256]{1,0:T(8,128)S(1)}, f32[128,256]{1,0:T(8,128)S(1)}, u32[]{:S(2)}, u32[]{:S(2)}) %collective-permute-start.20) | collective-permute-done | bytes 131104 | tf_op jit(solution)/shard_map/ppermute | solution.py:453
  66.2 0.7 %select_bitcast_fusion = f32[1,4,64,256]{3,2,1,0:T(8,128)} fusion(f32[4,64,256]{2,1,0:T(8,128)S(1)} %bitcast.7, f32[4,64,256]{2,1,0:T(8,128)S(1)} %get-tuple-element.77, pred[]{:T(512)S(6)} %eq.5), kind=kLoop, calls=%fused_computation.1 | loop fusion | flops 65536 | bytes 786433 | tf_op jit(solution)/shard_map/broadcast_in_dim | solution.py:521
  66.9 0.0 collective-permute-done.21
  66.9 0.6 fusion.3
  (7 shorter events, 0.1 us)
Async XLA Ops:
  0.6 9.0 %copy-start = (f32[3,4,256]{2,1,0:T(4,128)S(1)}, f32[3,4,256]{2,1,0:T(4,128)}, u32[]{:S(2)}) copy-start(f32[3,4,256]{2,1,0:T(4,128)} %param.11) | copy-start | bytes 36868
  3.3 8.8 %collective-permute-start.3 = (f32[1,4,64,256]{3,2,1,0:T(8,128)S(1)}, f32[1,4,64,256]{3,2,1,0:T(8,128)S(1)}, u32[]{:S(2)}, u32[]{:S(2)}) collective-permute-start(f32[1,4,64,256]{3,2,1,0:T(8,128)S(1)} %convert_element_type.9), channel_id=1, source_target_pairs={{16,0},{17,1},{18,2},{19,3},{20,4},{21,5},{22,6},{23,7}} | collective-permute-start | bytes 786440 | tf_op jit(solution)/shard_map/ppermute | solution.py:453
  4.6 10.5 %collective-permute-start.1 = (f32[136,256]{1,0:T(8,128)S(1)}, f32[136,256]{1,0:T(8,128)S(1)}, u32[]{:S(2)}, u32[]{:S(2)}) collective-permute-start(f32[136,256]{1,0:T(8,128)S(1)} %get-tuple-element.41.low), channel_id=1, source_target_pairs={{0,0},{1,1},{2,2},{3,3},{4,4},{5,5},{6,6},{7,7},{8,16},{9,17},{10,... | collective-permute-start | bytes 417800 | tf_op jit(solution)/shard_map/ppermute | solution.py:453
  5.3 9.8 %collective-permute-start = (f32[136,256]{1,0:T(8,128)S(1)}, f32[136,256]{1,0:T(8,128)S(1)}, u32[]{:S(2)}, u32[]{:S(2)}) collective-permute-start(f32[136,256]{1,0:T(8,128)S(1)} %get-tuple-element.42), channel_id=1, source_target_pairs={{0,8},{1,9},{2,10},{3,11},{4,12},{5,13},{6,14},{7,15},{8,24},{9,25... | collective-permute-start | bytes 417800 | tf_op jit(solution)/shard_map/ppermute | solution.py:453
  9.6 5.4 %collective-permute-start.2 = (f32[8,256]{1,0:T(8,128)S(1)}, f32[8,256]{1,0:T(8,128)S(1)}, u32[]{:S(2)}, u32[]{:S(2)}) collective-permute-start(f32[8,256]{1,0:T(8,128)S(1)} %slice.26), channel_id=1, source_target_pairs={{0,16},{1,17},{2,18},{3,19},{4,20},{5,21},{6,22},{7,23},{8,24},{9,... | collective-permute-start | bytes 24584 | tf_op jit(solution)/shard_map/ppermute | solution.py:453
  15.2 13.3 %collective-permute-start.4 = (f32[272,128]{1,0:T(8,128)S(1)}, f32[272,128]{1,0:T(8,128)S(1)}, u32[]{:S(2)}, u32[]{:S(2)}) collective-permute-start(f32[272,128]{1,0:T(8,128)S(1)} %shard_map.105.refs_0_.first_own), channel_id=1, source_target_pairs={{0,6},{1,7},{2,0},{3,1},{4,2},{5,3},{6,4},{7,5},{8,14},{9,15},{10,... | collective-permute-start | bytes 417800 | tf_op jit(solution)/shard_map/ppermute | solution.py:453
  20.0 8.5 %collective-permute-start.10 = (f32[272,128]{1,0:T(8,128)S(1)}, f32[272,128]{1,0:T(8,128)S(1)}, u32[]{:S(2)}, u32[]{:S(2)}) collective-permute-start(f32[272,128]{1,0:T(8,128)S(1)} %shard_map.105.refs_0_.first_own), channel_id=1, source_target_pairs={{0,2},{1,3},{2,4},{3,5},{4,6},{5,7},{6,0},{7,1},{8,10},{9,11},{10,... | collective-permute-start | bytes 417800 | tf_op jit(solution)/shard_map/ppermute | solution.py:453
  20.0 9.1 %collective-permute-start.8 = (f32[272,128]{1,0:T(8,128)S(1)}, f32[272,128]{1,0:T(8,128)S(1)}, u32[]{:S(2)}, u32[]{:S(2)}) collective-permute-start(f32[272,128]{1,0:T(8,128)S(1)} %shard_map.105.refs_0_.first_own), channel_id=1, source_target_pairs={{0,7},{1,0},{2,1},{3,2},{4,3},{5,4},{6,5},{7,6},{8,15},{9,8},{10,9... | collective-permute-start | bytes 417800 | tf_op jit(solution)/shard_map/ppermute | solution.py:453
  24.7 7.8 %collective-permute-start.6 = (f32[272,128]{1,0:T(8,128)S(1)}, f32[272,128]{1,0:T(8,128)S(1)}, u32[]{:S(2)}, u32[]{:S(2)}) collective-permute-start(f32[272,128]{1,0:T(8,128)S(1)} %shard_map.105.refs_0_.first_own), channel_id=1, source_target_pairs={{0,1},{1,2},{2,3},{3,4},{4,5},{5,6},{6,7},{7,0},{8,9},{9,10},{10,1... | collective-permute-start | bytes 417800 | tf_op jit(solution)/shard_map/ppermute | solution.py:453
  24.7 8.3 %collective-permute-start.5 = (f32[272,128]{1,0:T(8,128)S(1)}, f32[272,128]{1,0:T(8,128)S(1)}, u32[]{:S(2)}, u32[]{:S(2)}) collective-permute-start(f32[272,128]{1,0:T(8,128)S(1)} %shard_map.105.refs_0_.first_own), channel_id=1, source_target_pairs={{0,8},{1,9},{2,10},{3,11},{4,12},{5,13},{6,14},{7,15},{8,0},{9,1},... | collective-permute-start | bytes 417800 | tf_op jit(solution)/shard_map/ppermute | solution.py:453
  24.7 1.1 %copy-start.1 = (f32[3,4,128,128]{3,2,1,0:T(8,128)S(1)}, f32[3,4,128,128]{3,2,1,0:T(8,128)}, u32[]{:S(2)}) copy-start(f32[3,4,128,128]{3,2,1,0:T(8,128)} %get-tuple-element.51.refs_1_) | copy-start | bytes 2359300
  25.8 0.9 %copy-start.2 = (f32[1,4,128,128]{3,2,1,0:T(8,128)S(1)}, f32[1,4,128,128]{3,2,1,0:T(8,128)}, u32[]{:S(2)}) copy-start(f32[1,4,128,128]{3,2,1,0:T(8,128)} %get-tuple-element.50.refs_0_) | copy-start | bytes 786436
  26.8 0.9 %copy-start.3 = (bf16[256,256]{1,0:T(8,128)(2,1)S(1)}, bf16[256,256]{1,0:T(8,128)(2,1)}, u32[]{:S(2)}) copy-start(bf16[256,256]{1,0:T(8,128)(2,1)} %get-tuple-element.53.refs_3_) | copy-start | bytes 393220
  27.7 0.7 %copy-start.4 = (f32[8,128]{1,0:T(8,128)S(1)}, f32[8,128]{1,0:T(8,128)}, u32[]{:S(2)}) copy-start(f32[8,128]{1,0:T(8,128)} %get-tuple-element.52.refs_2_) | copy-start | bytes 12292
  28.5 4.5 %collective-permute-start.11 = (f32[272,128]{1,0:T(8,128)S(1)}, f32[272,128]{1,0:T(8,128)S(1)}, u32[]{:S(2)}, u32[]{:S(2)}) collective-permute-start(f32[272,128]{1,0:T(8,128)S(1)} %collective-permute-done.10.refs_3_), channel_id=1, source_target_pairs={{0,8},{1,9},{2,10},{3,11},{4,12},{5,13},{6,14},{7,15},{8,0},{9,1},... | collective-permute-start | bytes 417800 | tf_op jit(solution)/shard_map/ppermute | solution.py:453
  29.1 3.9 %collective-permute-start.9 = (f32[272,128]{1,0:T(8,128)S(1)}, f32[272,128]{1,0:T(8,128)S(1)}, u32[]{:S(2)}, u32[]{:S(2)}) collective-permute-start(f32[272,128]{1,0:T(8,128)S(1)} %collective-permute-done.8.refs_2_), channel_id=1, source_target_pairs={{0,8},{1,9},{2,10},{3,11},{4,12},{5,13},{6,14},{7,15},{8,0},{9,1},... | collective-permute-start | bytes 417800 | tf_op jit(solution)/shard_map/ppermute | solution.py:453
  32.5 1.4 %collective-permute-start.7 = (f32[272,128]{1,0:T(8,128)S(1)}, f32[272,128]{1,0:T(8,128)S(1)}, u32[]{:S(2)}, u32[]{:S(2)}) collective-permute-start(f32[272,128]{1,0:T(8,128)S(1)} %collective-permute-done.6.refs_1_), channel_id=1, source_target_pairs={{0,8},{1,9},{2,10},{3,11},{4,12},{5,13},{6,14},{7,15},{8,0},{9,1},... | collective-permute-start | bytes 417800 | tf_op jit(solution)/shard_map/ppermute | solution.py:453
  32.5 1.6 %collective-permute-start.12 = (f32[272,128]{1,0:T(8,128)S(1)}, f32[272,128]{1,0:T(8,128)S(1)}, u32[]{:S(2)}, u32[]{:S(2)}) collective-permute-start(f32[272,128]{1,0:T(8,128)S(1)} %collective-permute-done.4.refs_4_), channel_id=1, source_target_pairs={{0,8},{1,9},{2,10},{3,11},{4,12},{5,13},{6,14},{7,15},{8,0},{9,1},... | collective-permute-start | bytes 417800 | tf_op jit(solution)/shard_map/ppermute | solution.py:453
  34.0 20.7 %collective-permute-start.18 = (f32[3,4,128,128]{3,2,1,0:T(8,128)S(1)}, f32[3,4,128,128]{3,2,1,0:T(8,128)S(1)}, u32[]{:S(2)}, u32[]{:S(2)}) collective-permute-start(f32[3,4,128,128]{3,2,1,0:T(8,128)S(1)} %get-tuple-element.74.refs_11_), channel_id=1, source_target_pairs={{16,0},{17,1},{18,2},{19,3},{20,4},{21,5},{22,6},{23,7}} | collective-permute-start | bytes 2359304 | tf_op jit(solution)/shard_map/ppermute | solution.py:453
  43.0 5.2 %collective-permute-start.14 = (f32[2,128,128]{2,1,0:T(8,128)S(1)}, f32[2,128,128]{2,1,0:T(8,128)S(1)}, u32[]{:S(2)}, u32[]{:S(2)}) collective-permute-start(f32[2,128,128]{2,1,0:T(8,128)S(1)} %get-tuple-element.69), channel_id=1, source_target_pairs={{0,7},{1,0},{2,1},{3,2},{4,3},{5,4},{6,5},{7,6},{8,15},{9,8},{10,9... | collective-permute-start | bytes 393224 | tf_op jit(solution)/shard_map/ppermute | solution.py:453
  44.7 8.6 %collective-permute-start.17 = (f32[4,128,128]{2,1,0:T(8,128)S(1)}, f32[4,128,128]{2,1,0:T(8,128)S(1)}, u32[]{:S(2)}, u32[]{:S(2)}) collective-permute-start(f32[4,128,128]{2,1,0:T(8,128)S(1)} %get-tuple-element.72.refs_6_), channel_id=1, source_target_pairs={{0,8},{1,9},{2,10},{3,11},{4,12},{5,13},{6,14},{7,15},{8,0},{9,1},... | collective-permute-start | bytes 786440 | tf_op jit(solution)/shard_map/ppermute | solution.py:453
  44.7 8.6 %collective-permute-start.13 = (f32[2,128,128]{2,1,0:T(8,128)S(1)}, f32[2,128,128]{2,1,0:T(8,128)S(1)}, u32[]{:S(2)}, u32[]{:S(2)}) collective-permute-start(f32[2,128,128]{2,1,0:T(8,128)S(1)} %get-tuple-element.69), channel_id=1, source_target_pairs={{0,1},{1,2},{2,3},{3,4},{4,5},{5,6},{6,7},{7,0},{8,9},{9,10},{10,1... | collective-permute-start | bytes 393224 | tf_op jit(solution)/shard_map/ppermute | solution.py:453
  48.2 5.1 %collective-permute-start.16 = (f32[2,128,128]{2,1,0:T(8,128)S(1)}, f32[2,128,128]{2,1,0:T(8,128)S(1)}, u32[]{:S(2)}, u32[]{:S(2)}) collective-permute-start(f32[2,128,128]{2,1,0:T(8,128)S(1)} %collective-permute-done.14.refs_1_), channel_id=1, source_target_pairs={{0,8},{1,9},{2,10},{3,11},{4,12},{5,13},{6,14},{7,15},{8,0},{9,1},... | collective-permute-start | bytes 393224 | tf_op jit(solution)/shard_map/ppermute | solution.py:453
  53.3 1.3 %collective-permute-start.15 = (f32[2,128,128]{2,1,0:T(8,128)S(1)}, f32[2,128,128]{2,1,0:T(8,128)S(1)}, u32[]{:S(2)}, u32[]{:S(2)}) collective-permute-start(f32[2,128,128]{2,1,0:T(8,128)S(1)} %collective-permute-done.13.refs_0_), channel_id=1, source_target_pairs={{0,8},{1,9},{2,10},{3,11},{4,12},{5,13},{6,14},{7,15},{8,0},{9,1},... | collective-permute-start | bytes 393224 | tf_op jit(solution)/shard_map/ppermute | solution.py:453
  57.7 6.7 %collective-permute-start.19 = (f32[192,256]{1,0:T(8,128)S(1)}, f32[192,256]{1,0:T(8,128)S(1)}, u32[]{:S(2)}, u32[]{:S(2)}) collective-permute-start(f32[192,256]{1,0:T(8,128)S(1)} %get-tuple-element.75), channel_id=1, source_target_pairs={{0,16},{1,17},{2,18},{3,19},{4,20},{5,21},{6,22},{7,23},{8,0},{9,1... | collective-permute-start | bytes 589832 | tf_op jit(solution)/shard_map/ppermute | solution.py:453
  60.1 6.1 %collective-permute-start.20 = (f32[128,256]{1,0:T(8,128)S(1)}, f32[128,256]{1,0:T(8,128)S(1)}, u32[]{:S(2)}, u32[]{:S(2)}) collective-permute-start(f32[128,256]{1,0:T(8,128)S(1)} %get-tuple-element.76), channel_id=1, source_target_pairs={{0,24},{1,25},{2,26},{3,27},{4,28},{5,29},{6,30},{7,31},{8,16},{9,... | collective-permute-start | bytes 393224 | tf_op jit(solution)/shard_map/ppermute | solution.py:453
  60.1 6.8 %collective-permute-start.21 = (f32[64,256]{1,0:T(8,128)S(1)}, f32[64,256]{1,0:T(8,128)S(1)}, u32[]{:S(2)}, u32[]{:S(2)}) collective-permute-start(f32[64,256]{1,0:T(8,128)S(1)} %get-tuple-element.79), channel_id=1, source_target_pairs={{0,8},{1,9},{2,10},{3,11},{4,12},{5,13},{6,14},{7,15},{8,0},{9,1},... | collective-permute-start | bytes 196616 | tf_op jit(solution)/shard_map/ppermute | solution.py:453

commit v7 on v6

--- a/solution.py
+++ b/solution.py
@@ -11,10 +11,9 @@
 CZ = 64
 GROUP = 6
 FIELD_ROWS = 16
-OWN_KINDS, FIRST_KINDS, ACROSS_KINDS = 12, 13, 14
+OWN_KINDS, ACROSS_KINDS = 12, 13
 LEAD = 1
 VMEM_BYTES = 16 * 2**20
-WHOLE_VMEM_BYTES = 62 * 2**20
 IN_VMEM = pl.BlockSpec(memory_space=pltpu.VMEM)
 
 
@@ -170,22 +169,15 @@
     return sec, lax.rem(sec, 2)
 
 
-def prepare_kernel(*refs):
-    sources, (early, late, taps, weights) = refs[:6], refs[6:10]
-    scratch, copies, sems = refs[10], refs[11:17], refs[17]
-    moves = [pltpu.make_async_copy(s, c, sems.at[i]) for i, (s, c) in enumerate(zip(sources, copies))]
-    for move in moves:
-        move.start()
-    backward, axial, lateral, depth, diagonal, coupling = copies
-    for move in moves[1:]:
-        move.wait()
-    orients = coupling.shape[0]
+def prepare_kernel(backward, table, early, late, taps, weights, scratch):
+    orients = table.shape[1]
+    axial, lateral, depth, diagonal, coupling = (table[i : i + n] for i, n in ((0, 3), (3, 3), (6, 3), (9, 1), (16, orients)))
     ratios = [each[w : w + 1] / each[1:2] for each in (axial, lateral, depth) for w in (0, 2)]
     for i, ratio in enumerate(ratios + ratios[:2]):
         taps[i : i + 1] = jnp.concatenate([ratio, ratio], axis=1)
     square = (orients, orients)
     same = lax.broadcasted_iota(jnp.int32, square, 0) == lax.broadcasted_iota(jnp.int32, square, 1)
-    kernel = jnp.where(same, diagonal[...], 0.0) + coupling[...]
+    kernel = jnp.where(same, diagonal, 0.0) + coupling
     kernel = kernel * (axial[1:2] * lateral[1:2] * depth[1:2])
     upper = jnp.concatenate([kernel, jnp.zeros_like(kernel)], axis=1)
     twice = jnp.concatenate([upper, pltpu.roll(upper, orients, 1)], axis=0).T
@@ -194,7 +186,6 @@
     weights[...] = jnp.concatenate(
         [jnp.concatenate([coarse, fine], axis=1), jnp.concatenate([coarse, jnp.zeros_like(fine)], axis=1)], axis=0
     )
-    moves[0].wait()
     for out, begin in ((early, 0), (late, LEAD)):
         for step in range(out.shape[0]):
             for i in range(out.shape[1]):
@@ -204,54 +195,55 @@
 def prepare(backward, axial, lateral, depth, diagonal, coupling):
     steps, planes, orients, cells = backward.shape
     rows, lanes = 2 * orients, cells // 2
-    operands = [backward, axial, lateral, depth, diagonal.reshape(1, -1), coupling]
+    table = jnp.concatenate([axial, lateral, depth, jnp.broadcast_to(diagonal, (7, orients)), coupling])
     first, rest = (((count, planes, rows, lanes), jnp.float32) for count in (LEAD, steps - LEAD))
     return pl.pallas_call(
         prepare_kernel,
-        in_specs=[pl.BlockSpec(memory_space=pltpu.HBM)] * len(operands),
+        in_specs=[IN_VMEM] * 2,
         out_specs=[IN_VMEM] * 4,
         out_shape=[
             jax.ShapeDtypeStruct(*each)
             for each in (first, rest, ((8, lanes), jnp.float32), ((2 * rows, 2 * lanes), jnp.bfloat16))
         ],
-        scratch_shapes=[pltpu.VMEM((rows, lanes), jnp.float32)]
-        + [pltpu.VMEM(each.shape, each.dtype) for each in operands]
-        + [pltpu.SemaphoreType.DMA((len(operands),))],
-        compiler_params=pltpu.CompilerParams(vmem_limit_bytes=WHOLE_VMEM_BYTES),
-    )(*operands)
-
-
-def settle_kernel(*refs):
-    for source, out in zip(refs[: len(refs) // 2], refs[len(refs) // 2 :]):
-        out[...] = source[...]
-
-
-def pack_kernel(low, moved_high, moved_low, across, fields, out, scratch):
+        scratch_shapes=[pltpu.VMEM((rows, lanes), jnp.float32)],
+        compiler_params=pltpu.CompilerParams(vmem_limit_bytes=VMEM_BYTES),
+    )(backward, table)
+
+
+def pack_kernel(low, moved_high, moved_low, kinds, across, fields, out, scratch):
     sec, odd = position()
     rows = scratch.shape[0]
-    orients = rows // 2
-    pair = low.shape[0] // orients
+    at = low.shape[0] * rows
     count = fields.shape[0]
-    out[pair * rows :] = jnp.zeros((FIELD_ROWS, rows), jnp.float32)
+    out[at:] = jnp.zeros((FIELD_ROWS, rows), jnp.float32)
     for i in range(count):
-        out[pair * rows + 2 * i : pair * rows + 2 * i + 1] = fields[i : i + 1, :rows]
-        out[pair * rows + 2 * i + 1 : pair * rows + 2 * i + 2] = fields[i : i + 1, rows:]
-    out[OWN_KINDS + pair * rows : OWN_KINDS + pair * rows + 1] = low[pair * orients : pair * orients + 1, :rows]
-    out[ACROSS_KINDS + pair * rows : ACROSS_KINDS + pair * rows + 1] = across[:1, :rows]
+        out[at + 2 * i : at + 2 * i + 1] = fields[i : i + 1, :rows]
+        out[at + 2 * i + 1 : at + 2 * i + 2] = fields[i : i + 1, rows:]
+    out[at + OWN_KINDS : at + OWN_KINDS + 1] = kinds[:1]
+    out[at + ACROSS_KINDS : at + ACROSS_KINDS + 1] = across[:1]
 
     def fill(source):
-        for i in range(pair):
-            out[i * rows : (i + 1) * rows] = to_tile(source[i * orients : (i + 1) * orients], scratch)
-        out[FIRST_KINDS + pair * rows : FIRST_KINDS + pair * rows + 1] = source[pair * orients : pair * orients + 1, :rows]
+        for i in range(source.shape[0]):
+            out[i * rows : (i + 1) * rows] = to_tile(source[i], scratch)
 
     pl.when(sec == 0)(lambda: fill(low))
     pl.when(odd == 1)(lambda: fill(moved_high))
     pl.when((sec > 0) & (odd == 0))(lambda: fill(moved_low))
 
 
-def scalars_of(row, count):
+def kinds_at(pieces, at, which):
+    sec, odd = position()
+    own, others = ([each[at + i : at + i + 1] for i in (OWN_KINDS, ACROSS_KINDS)] for each in pieces)
+    even_core, odd_core = (
+        [jnp.where(odd == core, mine, theirs) for mine, theirs in zip(own, others)] for core in (0, 1)
+    )
+    row = jnp.where(
+        sec < 2,
+        (even_core[0], odd_core[0], even_core[1])[which],
+        (odd_core[1], even_core[0], odd_core[0])[which],
+    )
     lane = lax.broadcasted_iota(jnp.int32, row.shape, 1)
-    return [jnp.sum(jnp.where(lane == i, row, 0.0)).astype(jnp.int32) for i in range(count)]
+    return lambda count: [jnp.sum(jnp.where(lane == i, row, 0.0)).astype(jnp.int32) for i in range(count)]
 
 
 def places(odd, planes, reach, blocks):
@@ -328,11 +320,9 @@
     for piece, start in zip(pieces, starts):
         for i in range(pair):
             slab[start + i] = piece[i * rows : (i + 1) * rows]
-    at = pair * rows
-    mine, others = (piece[at + OWN_KINDS : at + OWN_KINDS + 1] for piece in (pieces[0], pieces[len(blocks)]))
     steps = LEAD + stored[1].shape[0]
-    second_kinds = jnp.where((sec == 1) | (sec == 2), mine, others)
-    kinds = scalars_of(pieces[0][at + FIRST_KINDS : at + FIRST_KINDS + 1], steps) + scalars_of(second_kinds, steps)
+    centre = (pieces[0], pieces[len(blocks)])
+    kinds = [kind for which in (0, 1) for kind in kinds_at(centre, pair * rows, which)(steps)]
     width = 2 * pair * factor.shape[0]
     lines = [piece[pair * rows : pair * rows + width] for piece in pieces]
     lines.append(jnp.zeros((rows - width * len(pieces), rows), jnp.float32))
@@ -366,12 +356,7 @@
     pair = planes // 2
     reach = (slab.shape[0] - planes) // 2
     begun = (factor.shape[1] - planes) // 2
-    own, others = (
-        [each[pair * rows + at : pair * rows + at + 1] for at in (OWN_KINDS, ACROSS_KINDS)]
-        for each in (first_own, first_swapped)
-    )
-    row = jnp.where(sec < 2, jnp.where(odd == 0, own[1], others[1]), jnp.where(odd == 0, others[0], own[0]))
-    kinds = scalars_of(row, reach)
+    kinds = kinds_at((first_own, first_swapped), pair * rows, 2)(reach)
     slab[reach : reach + planes] = middle[...]
     for piece, start in zip(pieces, places(odd, planes, reach, blocks)):
         for i in range(pair):
@@ -454,17 +439,19 @@
 
     same, beside, across = (0, 1, 2, 3), (1, 0, 3, 2), (2, 3, 0, 1)
     whole = incoming[0]
-    types = jnp.pad(block_types.astype(jnp.float32), ((0, 7), (0, cells - steps)))
-    low, high = (jnp.concatenate([each.reshape(-1, cells), types]) for each in (whole[:pair], whole[pair:]))
-    lead = backward[:LEAD]
-    backward, lead, high, low = lax.optimization_barrier((backward, lead, high, low))
+    backward, fields, block_types, high, low = lax.optimization_barrier(
+        (backward, fields, block_types, whole[pair:], whole[:pair])
+    )
     moved_high = send(high, (1, 3, 0, 2))
     moved_low = send(low, (0, 2, 1, 3))
-    across_types = send(high[pair * orients :], across)
-    early_last = send(lead.astype(jnp.float32), {2: 0})
+    types = jnp.pad(block_types.astype(jnp.float32), ((0, 7), (0, lanes - steps)))
+    across_types = send(types, across)
     lines = lax.dynamic_slice_in_dim(fields, sec % 2 * pair, pair, axis=1).reshape(-1, cells)
+    lines, backward = lax.optimization_barrier((lines, backward))
+    early_last = send(backward[:LEAD].astype(jnp.float32), {2: 0})
     settled = prepare(backward, axial_taps, lateral_taps, depth_taps, bend_diagonal, bend_coupling)
     lines, early_last, *settled = lax.optimization_barrier((lines, early_last, *settled))
+    stored, (taps, weights) = settled[:2], settled[2:]
 
     tile = pltpu.VMEM((rows, lanes), jnp.float32)
     packed = pltpu.VMEM((GROUP * rows, 2 * lanes), jnp.bfloat16)
@@ -475,18 +462,9 @@
         return [slab, slab, packed, packed, tile]
 
     (piece,) = call(
-        pack_kernel, [(pair * rows + FIELD_ROWS, lanes)], [tile], [low, moved_high, moved_low, across_types, lines]
+        pack_kernel, [(pair * rows + FIELD_ROWS, lanes)], [tile], [low, moved_high, moved_low, types, across_types, lines]
     )
     own = [send(piece, same, shift) for shift in far]
-    settled = pl.pallas_call(
-        settle_kernel,
-        in_specs=[IN_VMEM] * len(settled),
-        out_specs=[IN_VMEM] * len(settled),
-        out_shape=[jax.ShapeDtypeStruct(each.shape, each.dtype) for each in settled],
-        compiler_params=pltpu.CompilerParams(vmem_limit_bytes=VMEM_BYTES),
-    )(*settled)
-    own[-1], *settled = lax.optimization_barrier((own[-1], *settled))
-    stored, (taps, weights) = settled[:2], settled[2:]
     swapped = [send(each, beside) for each in [piece] + own]
     late_stored, *swapped = lax.optimization_barrier((stored[1], *swapped))
     late_last = send(late_stored, {2: 0})

time: 68 us -> 67.1 us (0.987)
  Pallas kernels: 13.4 us -> 11.3 us
  waiting for transfers between devices: 22.5 us -> 24.1 us
  other arithmetic: 2.11 us -> 2.99 us
    unnamed x10 -> x4, local copies, waits for them, and re-layouts: 3.68 us -> 1.05 us
    concatenate x0 -> x1, local copies, waits for them, and re-layouts: none -> 2.26 us  [prepare(): jnp.concatenate([axial, lateral, depth, jnp.broadcast_to(diagonal, (7, or...]
    pallas_call x2 -> x1, Pallas kernels: 2.53 us -> 0.41 us  [prepare(): pl.pallas_call(prepare_kernel, in_specs=[IN_VMEM] * 2, out_specs=[IN_VMEM...]
    ppermute x22, waiting for transfers between devices: 22.5 us -> 24.1 us  [send(): return lax.ppermute(array, ('sec', 'gx'), pairs)]
    slice x2 -> x0, local copies, waits for them, and re-layouts: 0.91 us -> none  [the longest x1 0.91 us: paired(): lead = backward[:LEAD]]
    convert_element_type x1, other arithmetic: 0.02 us -> 0.93 us  [paired(): early_last = send(backward[:LEAD].astype(jnp.float32), {2: 0})]
  transfers between devices with their start and end apart: 22 -> 22, of which waited for: 9 -> 9; matrix products, arithmetic and copies ran while one was open for 1% -> 7% of each run, Pallas kernels for 15% -> 12%
where the time goes in v7:
time: 67.1 us; the launch traced here: 66.8 us
  waiting for transfers between devices  24.1 us (36%)
  starting transfers between devices  22.6 us (34%)
  Pallas kernels  11.3 us (17%)
  local copies, waits for them, and re-layouts  4.99 us (7%)
  other arithmetic  2.99 us (4%)
  between operations  0.83 us (1%)
    ppermute x22, waiting for transfers between devices, send(): return lax.ppermute(array, ('sec', 'gx'), pairs)  24.1 us
    ppermute x22, starting transfers between devices, send(): return lax.ppermute(array, ('sec', 'gx'), pairs)  22.6 us
    pallas_call x3, Pallas kernels, call(): pl.pallas_call(kernel, in_specs=[IN_VMEM] * len(operands), out_specs=[IN_...  10.9 us
    concatenate x1, local copies, waits for them, and re-layouts, prepare(): jnp.concatenate([axial, lateral, depth, jnp.broadcast_to(diagonal, (7, or...  2.26 us
  transfers between devices with their start and end apart: 22, of which 9 were waited for; matrix products, arithmetic and copies ran while one was open for 7% of the time, Pallas kernels for 12%

profile of v7, /device:TPU:0, one launch (start us, length us, event | category | flops | bytes accessed | tf_op | source)
XLA Modules:
  0.0 66.8 jit_solution(15769384265716361350)
XLA Ops:
  0.6 0.0 copy-start
  0.7 1.0 %slice_bitcast_fusion = (f32[2,64,256]{2,1,0:T(8,128)S(1)}, f32[2,64,256]{2,1,0:T(8,128)S(1)}) fusion(f32[1,4,64,256]{3,2,1,0:T(8,128)} %param.9), kind=kLoop, calls=%fused_computation.3 | loop fusion | bytes 524288 | tf_op jit(solution)/shard_map/slice | solution.py:443
  1.7 0.0 copy-done
  1.7 0.9 %slice_convert_fusion = f32[1,4,64,256]{3,2,1,0:T(8,128)S(1)} fusion(bf16[4,4,64,256]{3,2,1,0:T(8,128)(2,1)} %backward), kind=kLoop, calls=%fused_computation.2 | loop fusion | flops 65536 | bytes 393216 | tf_op jit(solution)/shard_map/convert_element_type | solution.py:451
  2.6 1.3 %collective-permute-start = (f32[1,4,64,256]{3,2,1,0:T(8,128)S(1)}, f32[1,4,64,256]{3,2,1,0:T(8,128)S(1)}, u32[]{:S(2)}, u32[]{:S(2)}) collective-permute-start(f32[1,4,64,256]{3,2,1,0:T(8,128)S(1)} %slice_convert_fusion), channel_id=1, source_target_pairs={{16,0},{17,1},{18,2},{19,3},{20,4},{21,5},{22,6},{23,7}} | collective-permute-start | bytes 786440 | tf_op jit(solution)/shard_map/ppermute | solution.py:438
  3.9 0.0 collective-permute-start.1
  4.0 0.7 %collective-permute-start.2 = (f32[2,64,256]{2,1,0:T(8,128)S(1)}, f32[2,64,256]{2,1,0:T(8,128)S(1)}, u32[]{:S(2)}, u32[]{:S(2)}) collective-permute-start(f32[2,64,256]{2,1,0:T(8,128)S(1)} %get-tuple-element.45.low), channel_id=1, source_target_pairs={{0,0},{1,1},{2,2},{3,3},{4,4},{5,5},{6,6},{7,7},{8,16},{9,17},{10,... | collective-permute-start | bytes 393224 | tf_op jit(solution)/shard_map/ppermute | solution.py:438
  4.6 0.7 convert_element_type.9
  5.3 4.8 %collective-permute-start.3 = (f32[8,128]{1,0:T(8,128)S(1)}, f32[8,128]{1,0:T(8,128)S(1)}, u32[]{:S(2)}, u32[]{:S(2)}) collective-permute-start(f32[8,128]{1,0:T(8,128)S(1)} %pad.4.kinds), channel_id=1, source_target_pairs={{0,16},{1,17},{2,18},{3,19},{4,20},{5,21},{6,22},{7,23},{8,24},{9,... | collective-permute-start | bytes 12296 | tf_op jit(solution)/shard_map/ppermute | solution.py:438
  10.1 0.7 broadcast_in_dim.10
  10.7 2.3 %concatenate.6.table = f32[80,64]{1,0:T(8,128)S(1)} concatenate(f32[3,64]{1,0:T(4,128)} %param.13, f32[3,64]{1,0:T(4,128)} %param.14, f32[3,64]{1,0:T(4,128)} %param.15, f32[7,64]{1,0:T(8,128)S(1)} %broadcast_in_dim.10, f32[64,64]{1,0:T(8,128)} %param.17), dimensions={0} | concatenate | bytes 40960 | tf_op jit(solution)/shard_map/concatenate | solution.py:198
  13.0 0.0 copy-start.1
  13.0 1.0 %copy-done.1 = bf16[4,4,64,256]{3,2,1,0:T(8,128)(2,1)S(1)} copy-done((bf16[4,4,64,256]{3,2,1,0:T(8,128)(2,1)S(1)}, bf16[4,4,64,256]{3,2,1,0:T(8,128)(2,1)}, u32[]{:S(2)}) %copy-start.1) | copy-done | bytes 524312
  14.0 0.4 shard_map.104
  14.4 0.0 collective-permute-done.refs_8_
  14.4 0.0 collective-permute-done.3.across
  14.4 0.0 collective-permute-done.1.moved_high
  14.5 0.0 collective-permute-done.2.moved_low
  14.5 0.1 shard_map.105.refs_0_.first_own
  14.6 4.4 %collective-permute-start.11 = (f32[272,128]{1,0:T(8,128)S(1)}, f32[272,128]{1,0:T(8,128)S(1)}, u32[]{:S(2)}, u32[]{:S(2)}) collective-permute-start(f32[272,128]{1,0:T(8,128)S(1)} %shard_map.105.refs_0_.first_own), channel_id=1, source_target_pairs={{0,6},{1,7},{2,0},{3,1},{4,2},{5,3},{6,4},{7,5},{8,14},{9,15},{10,... | collective-permute-start | bytes 417800 | tf_op jit(solution)/shard_map/ppermute | solution.py:438
  19.0 0.0 collective-permute-start.9
  19.0 4.7 %collective-permute-start.7 = (f32[272,128]{1,0:T(8,128)S(1)}, f32[272,128]{1,0:T(8,128)S(1)}, u32[]{:S(2)}, u32[]{:S(2)}) collective-permute-start(f32[272,128]{1,0:T(8,128)S(1)} %shard_map.105.refs_0_.first_own), channel_id=1, source_target_pairs={{0,7},{1,0},{2,1},{3,2},{4,3},{5,4},{6,5},{7,6},{8,15},{9,8},{10,9... | collective-permute-start | bytes 417800 | tf_op jit(solution)/shard_map/ppermute | solution.py:438
  23.8 0.0 collective-permute-start.5
  23.8 0.0 collective-permute-start.4
  23.8 0.0 collective-permute-done.11.refs_4_
  23.8 0.5 collective-permute-start.12
  24.3 3.1 %collective-permute-done.9.refs_3_ = f32[272,128]{1,0:T(8,128)S(1)} collective-permute-done((f32[272,128]{1,0:T(8,128)S(1)}, f32[272,128]{1,0:T(8,128)S(1)}, u32[]{:S(2)}, u32[]{:S(2)}) %collective-permute-start.9) | collective-permute-done | bytes 139296 | tf_op jit(solution)/shard_map/ppermute | solution.py:438
  27.4 0.0 collective-permute-start.10
  27.4 0.7 collective-permute-done.7.refs_2_
  28.1 0.0 collective-permute-start.8
  28.1 3.5 %collective-permute-done.5.refs_1_ = f32[272,128]{1,0:T(8,128)S(1)} collective-permute-done((f32[272,128]{1,0:T(8,128)S(1)}, f32[272,128]{1,0:T(8,128)S(1)}, u32[]{:S(2)}, u32[]{:S(2)}) %collective-permute-start.5) | collective-permute-done | bytes 139296 | tf_op jit(solution)/shard_map/ppermute | solution.py:438
  31.5 0.0 collective-permute-start.6
  31.6 0.0 collective-permute-done.4.refs_5_.first_swapped
  31.6 0.0 collective-permute-done.12.refs_9_
  31.6 0.0 collective-permute-done.10.refs_8_
  31.6 0.0 collective-permute-done.8.refs_7_
  31.6 1.3 %collective-permute-done.6.refs_6_ = f32[272,128]{1,0:T(8,128)S(1)} collective-permute-done((f32[272,128]{1,0:T(8,128)S(1)}, f32[272,128]{1,0:T(8,128)S(1)}, u32[]{:S(2)}, u32[]{:S(2)}) %collective-permute-start.6) | collective-permute-done | bytes 139296 | tf_op jit(solution)/shard_map/ppermute | solution.py:438
  32.9 1.3 %collective-permute-start.18 = (f32[3,4,128,128]{3,2,1,0:T(8,128)S(1)}, f32[3,4,128,128]{3,2,1,0:T(8,128)S(1)}, u32[]{:S(2)}, u32[]{:S(2)}) collective-permute-start(f32[3,4,128,128]{3,2,1,0:T(8,128)S(1)} %get-tuple-element.62.refs_11_), channel_id=1, source_target_pairs={{16,0},{17,1},{18,2},{19,3},{20,4},{21,5},{22,6},{23,7}} | collective-permute-start | bytes 2359304 | tf_op jit(solution)/shard_map/ppermute | solution.py:438
  34.2 7.7 %shard_map.106 = (f32[4,128,128]{2,1,0:T(8,128)S(1)}, f32[2,128,128]{2,1,0:T(8,128)S(1)}, f32[4,128,128]{2,1,0:T(8,128)S(1)}, f32[4,128,128]{2,1,0:T(8,128)S(1)}, f32[3,20,128,128]{3,2,1,0:T(8,128)S(1)}) custom-call(f32[8,128]{1,0:T(8,128)S(1)} %get-tuple-element.43.taps, bf16[256,256]{1,0:T(8,128)(2,1)S(1)} %get-tuple-element.44.weights, ...), custom_call_target="tpu_custom_call" | custom-call | tf_op jit(solution)/shard_map/pallas_call | solution.py:414
  41.9 2.0 %collective-permute-start.14 = (f32[2,128,128]{2,1,0:T(8,128)S(1)}, f32[2,128,128]{2,1,0:T(8,128)S(1)}, u32[]{:S(2)}, u32[]{:S(2)}) collective-permute-start(f32[2,128,128]{2,1,0:T(8,128)S(1)} %get-tuple-element.57), channel_id=1, source_target_pairs={{0,7},{1,0},{2,1},{3,2},{4,3},{5,4},{6,5},{7,6},{8,15},{9,8},{10,9... | collective-permute-start | bytes 393224 | tf_op jit(solution)/shard_map/ppermute | solution.py:438
  43.9 0.0 collective-permute-start.17
  43.9 0.1 collective-permute-start.13
  44.0 2.9 %collective-permute-done.14.refs_1_ = f32[2,128,128]{2,1,0:T(8,128)S(1)} collective-permute-done((f32[2,128,128]{2,1,0:T(8,128)S(1)}, f32[2,128,128]{2,1,0:T(8,128)S(1)}, u32[]{:S(2)}, u32[]{:S(2)}) %collective-permute-start.14) | collective-permute-done | bytes 131104 | tf_op jit(solution)/shard_map/ppermute | solution.py:438
  47.0 0.0 collective-permute-start.16
  47.0 5.6 %collective-permute-done.13.refs_0_ = f32[2,128,128]{2,1,0:T(8,128)S(1)} collective-permute-done((f32[2,128,128]{2,1,0:T(8,128)S(1)}, f32[2,128,128]{2,1,0:T(8,128)S(1)}, u32[]{:S(2)}, u32[]{:S(2)}) %collective-permute-start.13) | collective-permute-done | bytes 131104 | tf_op jit(solution)/shard_map/ppermute | solution.py:438
  52.5 0.0 collective-permute-start.15
  52.5 0.0 collective-permute-done.17.refs_7_
  52.5 0.0 collective-permute-done.16.refs_3_
  52.5 1.3 %collective-permute-done.15.refs_2_ = f32[2,128,128]{2,1,0:T(8,128)S(1)} collective-permute-done((f32[2,128,128]{2,1,0:T(8,128)S(1)}, f32[2,128,128]{2,1,0:T(8,128)S(1)}, u32[]{:S(2)}, u32[]{:S(2)}) %collective-permute-start.15) | collective-permute-done | bytes 131104 | tf_op jit(solution)/shard_map/ppermute | solution.py:438
  53.9 0.0 collective-permute-done.18.refs_9_
  53.9 3.0 %shard_map.107 = (f32[4,64,256]{2,1,0:T(8,128)S(1)}, f32[64,256]{1,0:T(8,128)S(1)}, f32[64,256]{1,0:T(8,128)S(1)}, f32[192,256]{1,0:T(8,128)S(1)}, f32[128,256]{1,0:T(8,128)S(1)}) custom-call(f32[8,128]{1,0:T(8,128)S(1)} %get-tuple-element.43.taps, bf16[256,256]{1,0:T(8,128)(2,1)S(1)} %get-tuple-element.44.weights, ...), custom_call_target="tpu_custom_call" | custom-call | tf_op jit(solution)/shard_map/pallas_call | solution.py:414
  56.9 2.4 %collective-permute-start.19 = (f32[192,256]{1,0:T(8,128)S(1)}, f32[192,256]{1,0:T(8,128)S(1)}, u32[]{:S(2)}, u32[]{:S(2)}) collective-permute-start(f32[192,256]{1,0:T(8,128)S(1)} %get-tuple-element.63), channel_id=1, source_target_pairs={{0,16},{1,17},{2,18},{3,19},{4,20},{5,21},{6,22},{7,23},{8,0},{9,1... | collective-permute-start | bytes 589832 | tf_op jit(solution)/shard_map/ppermute | solution.py:438
  59.2 0.0 collective-permute-start.20
  59.3 0.4 collective-permute-start.21
  59.7 3.9 %collective-permute-done.19 = f32[192,256]{1,0:T(8,128)S(1)} collective-permute-done((f32[192,256]{1,0:T(8,128)S(1)}, f32[192,256]{1,0:T(8,128)S(1)}, u32[]{:S(2)}, u32[]{:S(2)}) %collective-permute-start.19) | collective-permute-done | bytes 196640 | tf_op jit(solution)/shard_map/ppermute | solution.py:438
  63.6 1.7 %collective-permute-done.20 = f32[128,256]{1,0:T(8,128)S(1)} collective-permute-done((f32[128,256]{1,0:T(8,128)S(1)}, f32[128,256]{1,0:T(8,128)S(1)}, u32[]{:S(2)}, u32[]{:S(2)}) %collective-permute-start.20) | collective-permute-done | bytes 131104 | tf_op jit(solution)/shard_map/ppermute | solution.py:438
  65.4 0.7 %select_bitcast_fusion = f32[1,4,64,256]{3,2,1,0:T(8,128)} fusion(f32[4,64,256]{2,1,0:T(8,128)S(1)} %bitcast.8, f32[4,64,256]{2,1,0:T(8,128)S(1)} %get-tuple-element.65, pred[]{:T(512)S(6)} %eq.5), kind=kLoop, calls=%fused_computation.1 | loop fusion | flops 65536 | bytes 786433 | tf_op jit(solution)/shard_map/broadcast_in_dim | solution.py:499
  66.1 0.0 collective-permute-done.21
  66.1 0.6 fusion.1
  (5 shorter events, 0.1 us)
Async XLA Ops:
  0.6 1.0 %copy-start = (f32[3,4,256]{2,1,0:T(4,128)S(1)}, f32[3,4,256]{2,1,0:T(4,128)}, u32[]{:S(2)}) copy-start(f32[3,4,256]{2,1,0:T(4,128)} %param.11) | copy-start | bytes 36868
  2.6 11.8 %collective-permute-start = (f32[1,4,64,256]{3,2,1,0:T(8,128)S(1)}, f32[1,4,64,256]{3,2,1,0:T(8,128)S(1)}, u32[]{:S(2)}, u32[]{:S(2)}) collective-permute-start(f32[1,4,64,256]{3,2,1,0:T(8,128)S(1)} %slice_convert_fusion), channel_id=1, source_target_pairs={{16,0},{17,1},{18,2},{19,3},{20,4},{21,5},{22,6},{23,7}} | collective-permute-start | bytes 786440 | tf_op jit(solution)/shard_map/ppermute | solution.py:438
  3.9 10.5 %collective-permute-start.1 = (f32[2,64,256]{2,1,0:T(8,128)S(1)}, f32[2,64,256]{2,1,0:T(8,128)S(1)}, u32[]{:S(2)}, u32[]{:S(2)}) collective-permute-start(f32[2,64,256]{2,1,0:T(8,128)S(1)} %get-tuple-element.46), channel_id=1, source_target_pairs={{0,8},{1,9},{2,10},{3,11},{4,12},{5,13},{6,14},{7,15},{8,24},{9,25... | collective-permute-start | bytes 393224 | tf_op jit(solution)/shard_map/ppermute | solution.py:438
  4.0 10.5 %collective-permute-start.2 = (f32[2,64,256]{2,1,0:T(8,128)S(1)}, f32[2,64,256]{2,1,0:T(8,128)S(1)}, u32[]{:S(2)}, u32[]{:S(2)}) collective-permute-start(f32[2,64,256]{2,1,0:T(8,128)S(1)} %get-tuple-element.45.low), channel_id=1, source_target_pairs={{0,0},{1,1},{2,2},{3,3},{4,4},{5,5},{6,6},{7,7},{8,16},{9,17},{10,... | collective-permute-start | bytes 393224 | tf_op jit(solution)/shard_map/ppermute | solution.py:438
  5.3 9.1 %collective-permute-start.3 = (f32[8,128]{1,0:T(8,128)S(1)}, f32[8,128]{1,0:T(8,128)S(1)}, u32[]{:S(2)}, u32[]{:S(2)}) collective-permute-start(f32[8,128]{1,0:T(8,128)S(1)} %pad.4.kinds), channel_id=1, source_target_pairs={{0,16},{1,17},{2,18},{3,19},{4,20},{5,21},{6,22},{7,23},{8,24},{9,... | collective-permute-start | bytes 12296 | tf_op jit(solution)/shard_map/ppermute | solution.py:438
  13.0 1.0 %copy-start.1 = (bf16[4,4,64,256]{3,2,1,0:T(8,128)(2,1)S(1)}, bf16[4,4,64,256]{3,2,1,0:T(8,128)(2,1)}, u32[]{:S(2)}) copy-start(bf16[4,4,64,256]{3,2,1,0:T(8,128)(2,1)} %backward) | copy-start | bytes 1572868
  14.6 9.2 %collective-permute-start.11 = (f32[272,128]{1,0:T(8,128)S(1)}, f32[272,128]{1,0:T(8,128)S(1)}, u32[]{:S(2)}, u32[]{:S(2)}) collective-permute-start(f32[272,128]{1,0:T(8,128)S(1)} %shard_map.105.refs_0_.first_own), channel_id=1, source_target_pairs={{0,6},{1,7},{2,0},{3,1},{4,2},{5,3},{6,4},{7,5},{8,14},{9,15},{10,... | collective-permute-start | bytes 417800 | tf_op jit(solution)/shard_map/ppermute | solution.py:438
  19.0 8.4 %collective-permute-start.9 = (f32[272,128]{1,0:T(8,128)S(1)}, f32[272,128]{1,0:T(8,128)S(1)}, u32[]{:S(2)}, u32[]{:S(2)}) collective-permute-start(f32[272,128]{1,0:T(8,128)S(1)} %shard_map.105.refs_0_.first_own), channel_id=1, source_target_pairs={{0,2},{1,3},{2,4},{3,5},{4,6},{5,7},{6,0},{7,1},{8,10},{9,11},{10,... | collective-permute-start | bytes 417800 | tf_op jit(solution)/shard_map/ppermute | solution.py:438
  19.0 9.0 %collective-permute-start.7 = (f32[272,128]{1,0:T(8,128)S(1)}, f32[272,128]{1,0:T(8,128)S(1)}, u32[]{:S(2)}, u32[]{:S(2)}) collective-permute-start(f32[272,128]{1,0:T(8,128)S(1)} %shard_map.105.refs_0_.first_own), channel_id=1, source_target_pairs={{0,7},{1,0},{2,1},{3,2},{4,3},{5,4},{6,5},{7,6},{8,15},{9,8},{10,9... | collective-permute-start | bytes 417800 | tf_op jit(solution)/shard_map/ppermute | solution.py:438
  23.8 7.8 %collective-permute-start.5 = (f32[272,128]{1,0:T(8,128)S(1)}, f32[272,128]{1,0:T(8,128)S(1)}, u32[]{:S(2)}, u32[]{:S(2)}) collective-permute-start(f32[272,128]{1,0:T(8,128)S(1)} %shard_map.105.refs_0_.first_own), channel_id=1, source_target_pairs={{0,1},{1,2},{2,3},{3,4},{4,5},{5,6},{6,7},{7,0},{8,9},{9,10},{10,1... | collective-permute-start | bytes 417800 | tf_op jit(solution)/shard_map/ppermute | solution.py:438
  23.8 7.8 %collective-permute-start.4 = (f32[272,128]{1,0:T(8,128)S(1)}, f32[272,128]{1,0:T(8,128)S(1)}, u32[]{:S(2)}, u32[]{:S(2)}) collective-permute-start(f32[272,128]{1,0:T(8,128)S(1)} %shard_map.105.refs_0_.first_own), channel_id=1, source_target_pairs={{0,8},{1,9},{2,10},{3,11},{4,12},{5,13},{6,14},{7,15},{8,0},{9,1},... | collective-permute-start | bytes 417800 | tf_op jit(solution)/shard_map/ppermute | solution.py:438
  23.8 7.8 %collective-permute-start.12 = (f32[272,128]{1,0:T(8,128)S(1)}, f32[272,128]{1,0:T(8,128)S(1)}, u32[]{:S(2)}, u32[]{:S(2)}) collective-permute-start(f32[272,128]{1,0:T(8,128)S(1)} %collective-permute-done.11.refs_4_), channel_id=1, source_target_pairs={{0,8},{1,9},{2,10},{3,11},{4,12},{5,13},{6,14},{7,15},{8,0},{9,1},... | collective-permute-start | bytes 417800 | tf_op jit(solution)/shard_map/ppermute | solution.py:438
  27.4 4.1 %collective-permute-start.10 = (f32[272,128]{1,0:T(8,128)S(1)}, f32[272,128]{1,0:T(8,128)S(1)}, u32[]{:S(2)}, u32[]{:S(2)}) collective-permute-start(f32[272,128]{1,0:T(8,128)S(1)} %collective-permute-done.9.refs_3_), channel_id=1, source_target_pairs={{0,8},{1,9},{2,10},{3,11},{4,12},{5,13},{6,14},{7,15},{8,0},{9,1},... | collective-permute-start | bytes 417800 | tf_op jit(solution)/shard_map/ppermute | solution.py:438
  28.1 3.5 %collective-permute-start.8 = (f32[272,128]{1,0:T(8,128)S(1)}, f32[272,128]{1,0:T(8,128)S(1)}, u32[]{:S(2)}, u32[]{:S(2)}) collective-permute-start(f32[272,128]{1,0:T(8,128)S(1)} %collective-permute-done.7.refs_2_), channel_id=1, source_target_pairs={{0,8},{1,9},{2,10},{3,11},{4,12},{5,13},{6,14},{7,15},{8,0},{9,1},... | collective-permute-start | bytes 417800 | tf_op jit(solution)/shard_map/ppermute | solution.py:438
  31.5 1.4 %collective-permute-start.6 = (f32[272,128]{1,0:T(8,128)S(1)}, f32[272,128]{1,0:T(8,128)S(1)}, u32[]{:S(2)}, u32[]{:S(2)}) collective-permute-start(f32[272,128]{1,0:T(8,128)S(1)} %collective-permute-done.5.refs_1_), channel_id=1, source_target_pairs={{0,8},{1,9},{2,10},{3,11},{4,12},{5,13},{6,14},{7,15},{8,0},{9,1},... | collective-permute-start | bytes 417800 | tf_op jit(solution)/shard_map/ppermute | solution.py:438
  32.9 21.0 %collective-permute-start.18 = (f32[3,4,128,128]{3,2,1,0:T(8,128)S(1)}, f32[3,4,128,128]{3,2,1,0:T(8,128)S(1)}, u32[]{:S(2)}, u32[]{:S(2)}) collective-permute-start(f32[3,4,128,128]{3,2,1,0:T(8,128)S(1)} %get-tuple-element.62.refs_11_), channel_id=1, source_target_pairs={{16,0},{17,1},{18,2},{19,3},{20,4},{21,5},{22,6},{23,7}} | collective-permute-start | bytes 2359304 | tf_op jit(solution)/shard_map/ppermute | solution.py:438
  41.9 5.0 %collective-permute-start.14 = (f32[2,128,128]{2,1,0:T(8,128)S(1)}, f32[2,128,128]{2,1,0:T(8,128)S(1)}, u32[]{:S(2)}, u32[]{:S(2)}) collective-permute-start(f32[2,128,128]{2,1,0:T(8,128)S(1)} %get-tuple-element.57), channel_id=1, source_target_pairs={{0,7},{1,0},{2,1},{3,2},{4,3},{5,4},{6,5},{7,6},{8,15},{9,8},{10,9... | collective-permute-start | bytes 393224 | tf_op jit(solution)/shard_map/ppermute | solution.py:438
  43.9 8.6 %collective-permute-start.17 = (f32[4,128,128]{2,1,0:T(8,128)S(1)}, f32[4,128,128]{2,1,0:T(8,128)S(1)}, u32[]{:S(2)}, u32[]{:S(2)}) collective-permute-start(f32[4,128,128]{2,1,0:T(8,128)S(1)} %get-tuple-element.60.refs_6_), channel_id=1, source_target_pairs={{0,8},{1,9},{2,10},{3,11},{4,12},{5,13},{6,14},{7,15},{8,0},{9,1},... | collective-permute-start | bytes 786440 | tf_op jit(solution)/shard_map/ppermute | solution.py:438
  43.9 8.6 %collective-permute-start.13 = (f32[2,128,128]{2,1,0:T(8,128)S(1)}, f32[2,128,128]{2,1,0:T(8,128)S(1)}, u32[]{:S(2)}, u32[]{:S(2)}) collective-permute-start(f32[2,128,128]{2,1,0:T(8,128)S(1)} %get-tuple-element.57), channel_id=1, source_target_pairs={{0,1},{1,2},{2,3},{3,4},{4,5},{5,6},{6,7},{7,0},{8,9},{9,10},{10,1... | collective-permute-start | bytes 393224 | tf_op jit(solution)/shard_map/ppermute | solution.py:438
  47.0 5.6 %collective-permute-start.16 = (f32[2,128,128]{2,1,0:T(8,128)S(1)}, f32[2,128,128]{2,1,0:T(8,128)S(1)}, u32[]{:S(2)}, u32[]{:S(2)}) collective-permute-start(f32[2,128,128]{2,1,0:T(8,128)S(1)} %collective-permute-done.14.refs_1_), channel_id=1, source_target_pairs={{0,8},{1,9},{2,10},{3,11},{4,12},{5,13},{6,14},{7,15},{8,0},{9,1},... | collective-permute-start | bytes 393224 | tf_op jit(solution)/shard_map/ppermute | solution.py:438
  52.5 1.3 %collective-permute-start.15 = (f32[2,128,128]{2,1,0:T(8,128)S(1)}, f32[2,128,128]{2,1,0:T(8,128)S(1)}, u32[]{:S(2)}, u32[]{:S(2)}) collective-permute-start(f32[2,128,128]{2,1,0:T(8,128)S(1)} %collective-permute-done.13.refs_0_), channel_id=1, source_target_pairs={{0,8},{1,9},{2,10},{3,11},{4,12},{5,13},{6,14},{7,15},{8,0},{9,1},... | collective-permute-start | bytes 393224 | tf_op jit(solution)/shard_map/ppermute | solution.py:438
  56.9 6.7 %collective-permute-start.19 = (f32[192,256]{1,0:T(8,128)S(1)}, f32[192,256]{1,0:T(8,128)S(1)}, u32[]{:S(2)}, u32[]{:S(2)}) collective-permute-start(f32[192,256]{1,0:T(8,128)S(1)} %get-tuple-element.63), channel_id=1, source_target_pairs={{0,16},{1,17},{2,18},{3,19},{4,20},{5,21},{6,22},{7,23},{8,0},{9,1... | collective-permute-start | bytes 589832 | tf_op jit(solution)/shard_map/ppermute | solution.py:438
  59.2 6.1 %collective-permute-start.20 = (f32[128,256]{1,0:T(8,128)S(1)}, f32[128,256]{1,0:T(8,128)S(1)}, u32[]{:S(2)}, u32[]{:S(2)}) collective-permute-start(f32[128,256]{1,0:T(8,128)S(1)} %get-tuple-element.64), channel_id=1, source_target_pairs={{0,24},{1,25},{2,26},{3,27},{4,28},{5,29},{6,30},{7,31},{8,16},{9,... | collective-permute-start | bytes 393224 | tf_op jit(solution)/shard_map/ppermute | solution.py:438
  59.3 6.8 %collective-permute-start.21 = (f32[64,256]{1,0:T(8,128)S(1)}, f32[64,256]{1,0:T(8,128)S(1)}, u32[]{:S(2)}, u32[]{:S(2)}) collective-permute-start(f32[64,256]{1,0:T(8,128)S(1)} %get-tuple-element.67), channel_id=1, source_target_pairs={{0,8},{1,9},{2,10},{3,11},{4,12},{5,13},{6,14},{7,15},{8,0},{9,1},... | collective-permute-start | bytes 196616 | tf_op jit(solution)/shard_map/ppermute | solution.py:438

commit v8 on v7

--- a/solution.py
+++ b/solution.py
@@ -11,9 +11,11 @@
 CZ = 64
 GROUP = 6
 FIELD_ROWS = 16
-OWN_KINDS, ACROSS_KINDS = 12, 13
+TAP_ROWS = 8
+OWN_KINDS, FIRST_KINDS, ACROSS_KINDS = 12, 13, 14
 LEAD = 1
 VMEM_BYTES = 16 * 2**20
+WHOLE_VMEM_BYTES = 62 * 2**20
 IN_VMEM = pl.BlockSpec(memory_space=pltpu.VMEM)
 
 
@@ -169,79 +171,124 @@
     return sec, lax.rem(sec, 2)
 
 
-def prepare_kernel(backward, table, early, late, taps, weights, scratch):
-    orients = table.shape[1]
-    axial, lateral, depth, diagonal, coupling = (table[i : i + n] for i, n in ((0, 3), (3, 3), (6, 3), (9, 1), (16, orients)))
+def launch_kernel(*refs):
+    sources, (high, low, lead, bundle) = refs[:9], refs[9:13]
+    scratch, copies, sems = refs[13], refs[14:23], refs[23]
+    moves = [
+        pltpu.make_async_copy(source.at[pl.ds(0, copy.shape[0])], copy, sems.at[i])
+        for i, (source, copy) in enumerate(zip(sources, copies))
+    ]
+    for move in moves:
+        move.start()
+    incoming, stored, fields, kinds, axial, lateral, depth, diagonal, coupling = copies
+    for move in moves[2:]:
+        move.wait()
+    rows, cells = scratch.shape[0], high.shape[1]
+    orients = rows // 2
     ratios = [each[w : w + 1] / each[1:2] for each in (axial, lateral, depth) for w in (0, 2)]
     for i, ratio in enumerate(ratios + ratios[:2]):
-        taps[i : i + 1] = jnp.concatenate([ratio, ratio], axis=1)
+        bundle[i : i + 1] = jnp.concatenate([ratio, ratio], axis=1)
     square = (orients, orients)
     same = lax.broadcasted_iota(jnp.int32, square, 0) == lax.broadcasted_iota(jnp.int32, square, 1)
-    kernel = jnp.where(same, diagonal, 0.0) + coupling
+    kernel = jnp.where(same, diagonal[...], 0.0) + coupling[...]
     kernel = kernel * (axial[1:2] * lateral[1:2] * depth[1:2])
     upper = jnp.concatenate([kernel, jnp.zeros_like(kernel)], axis=1)
-    twice = jnp.concatenate([upper, pltpu.roll(upper, orients, 1)], axis=0).T
+    bundle[TAP_ROWS : TAP_ROWS + rows] = jnp.concatenate([upper, pltpu.roll(upper, orients, 1)], axis=0).T
+    types = kinds[...].astype(jnp.float32)
+    types = jnp.concatenate([types, jnp.zeros((1, cells - types.shape[1]), jnp.float32)], axis=1)
+    odd = position()[1]
+    pair = incoming.shape[1] // 2
+    at = TAP_ROWS + rows
+    bundle[at : at + FIELD_ROWS] = jnp.zeros((FIELD_ROWS, rows), jnp.float32)
+    for kind in range(fields.shape[0]):
+        for i in range(pair):
+            line = fields[kind, pl.ds(pair * odd + i, 1), :]
+            here = at + (kind * pair + i) * 2
+            bundle[here : here + 1] = line[:, :rows]
+            bundle[here + 1 : here + 2] = line[:, rows:]
+    bundle[at + OWN_KINDS : at + OWN_KINDS + 1] = types[:, :rows]
+    moves[0].wait()
+    for i in range(pair):
+        low[i * orients : (i + 1) * orients] = incoming[0, i]
+        high[i * orients : (i + 1) * orients] = incoming[0, pair + i]
+        here = at + FIELD_ROWS + i * rows
+        bundle[here : here + rows] = to_tile(incoming[0, i], scratch)
+    moves[1].wait()
+    planes = stored.shape[1]
+    for step in range(LEAD):
+        for i in range(planes):
+            here = (step * planes + i) * orients
+            lead[here : here + orients] = stored[step, i].astype(jnp.float32)
+    for out in (high, low, lead):
+        out[out.shape[0] - 8 :] = jnp.broadcast_to(types, (8, cells))
+
+
+def launch(incoming, backward, fields, kinds, axial, lateral, depth, diagonal, coupling):
+    planes, orients, cells = backward.shape[1:]
+    rows = 2 * orients
+    operands = [incoming, backward, fields, kinds, axial, lateral, depth, diagonal.reshape(1, -1), coupling]
+    half = (planes // 2 * orients + 8, cells)
+    shapes = [half, half, (LEAD * planes * orients + 8, cells), (TAP_ROWS + rows + FIELD_ROWS + planes // 2 * rows, rows)]
+    taken = [(LEAD,) + each.shape[1:] if i == 1 else each.shape for i, each in enumerate(operands)]
+    return pl.pallas_call(
+        launch_kernel,
+        in_specs=[pl.BlockSpec(memory_space=pltpu.HBM)] * len(operands),
+        out_specs=[IN_VMEM] * len(shapes),
+        out_shape=[jax.ShapeDtypeStruct(shape, jnp.float32) for shape in shapes],
+        scratch_shapes=[pltpu.VMEM((rows, rows), jnp.float32)]
+        + [pltpu.VMEM(shape, each.dtype) for shape, each in zip(taken, operands)]
+        + [pltpu.SemaphoreType.DMA((len(operands),))],
+        compiler_params=pltpu.CompilerParams(vmem_limit_bytes=WHOLE_VMEM_BYTES),
+    )(*operands)
+
+
+def turn_kernel(backward, early, late, scratch):
+    for out, begin in ((early, 0), (late, LEAD)):
+        for step in range(out.shape[0]):
+            for i in range(out.shape[1]):
+                out[step, i] = to_tile(backward[begin + step, i].astype(jnp.float32), scratch)
+
+
+def pack_kernel(bundle, moved_high, moved_low, lead, out, taps, weights, scratch):
+    sec, odd = position()
+    rows = scratch.shape[0]
+    orients = rows // 2
+    taps[...] = bundle[:TAP_ROWS]
+    twice = bundle[TAP_ROWS : TAP_ROWS + rows]
     coarse = twice.astype(jnp.bfloat16)
     fine = (twice - coarse.astype(jnp.float32)).astype(jnp.bfloat16)
     weights[...] = jnp.concatenate(
         [jnp.concatenate([coarse, fine], axis=1), jnp.concatenate([coarse, jnp.zeros_like(fine)], axis=1)], axis=0
     )
-    for out, begin in ((early, 0), (late, LEAD)):
-        for step in range(out.shape[0]):
-            for i in range(out.shape[1]):
-                out[step, i] = to_tile(backward[begin + step, i].astype(jnp.float32), scratch)
-
-
-def prepare(backward, axial, lateral, depth, diagonal, coupling):
-    steps, planes, orients, cells = backward.shape
-    rows, lanes = 2 * orients, cells // 2
-    table = jnp.concatenate([axial, lateral, depth, jnp.broadcast_to(diagonal, (7, orients)), coupling])
-    first, rest = (((count, planes, rows, lanes), jnp.float32) for count in (LEAD, steps - LEAD))
-    return pl.pallas_call(
-        prepare_kernel,
-        in_specs=[IN_VMEM] * 2,
-        out_specs=[IN_VMEM] * 4,
-        out_shape=[
-            jax.ShapeDtypeStruct(*each)
-            for each in (first, rest, ((8, lanes), jnp.float32), ((2 * rows, 2 * lanes), jnp.bfloat16))
-        ],
-        scratch_shapes=[pltpu.VMEM((rows, lanes), jnp.float32)],
-        compiler_params=pltpu.CompilerParams(vmem_limit_bytes=VMEM_BYTES),
-    )(backward, table)
-
-
-def pack_kernel(low, moved_high, moved_low, kinds, across, fields, out, scratch):
-    sec, odd = position()
-    rows = scratch.shape[0]
-    at = low.shape[0] * rows
-    count = fields.shape[0]
-    out[at:] = jnp.zeros((FIELD_ROWS, rows), jnp.float32)
-    for i in range(count):
-        out[at + 2 * i : at + 2 * i + 1] = fields[i : i + 1, :rows]
-        out[at + 2 * i + 1 : at + 2 * i + 2] = fields[i : i + 1, rows:]
-    out[at + OWN_KINDS : at + OWN_KINDS + 1] = kinds[:1]
-    out[at + ACROSS_KINDS : at + ACROSS_KINDS + 1] = across[:1]
+    at = out.shape[0] - FIELD_ROWS
+    lines = TAP_ROWS + rows
+    out[at:] = bundle[lines : lines + FIELD_ROWS]
+    out[at + ACROSS_KINDS : at + ACROSS_KINDS + 1] = lead[lead.shape[0] - 8 : lead.shape[0] - 7, :rows]
+
+    @pl.when(sec == 0)
+    def _():
+        out[:at] = bundle[lines + FIELD_ROWS :]
+        out[at + FIRST_KINDS : at + FIRST_KINDS + 1] = out[at + OWN_KINDS : at + OWN_KINDS + 1]
 
     def fill(source):
-        for i in range(source.shape[0]):
-            out[i * rows : (i + 1) * rows] = to_tile(source[i], scratch)
-
-    pl.when(sec == 0)(lambda: fill(low))
+        for i in range(at // rows):
+            out[i * rows : (i + 1) * rows] = to_tile(source[i * orients : (i + 1) * orients], scratch)
+        here = source.shape[0] - 8
+        out[at + FIRST_KINDS : at + FIRST_KINDS + 1] = source[here : here + 1, :rows]
+
     pl.when(odd == 1)(lambda: fill(moved_high))
     pl.when((sec > 0) & (odd == 0))(lambda: fill(moved_low))
 
 
 def kinds_at(pieces, at, which):
     sec, odd = position()
-    own, others = ([each[at + i : at + i + 1] for i in (OWN_KINDS, ACROSS_KINDS)] for each in pieces)
+    own, others = ([each[at + i : at + i + 1] for i in (OWN_KINDS, FIRST_KINDS, ACROSS_KINDS)] for each in pieces)
     even_core, odd_core = (
         [jnp.where(odd == core, mine, theirs) for mine, theirs in zip(own, others)] for core in (0, 1)
     )
-    row = jnp.where(
-        sec < 2,
-        (even_core[0], odd_core[0], even_core[1])[which],
-        (odd_core[1], even_core[0], odd_core[0])[which],
-    )
+    row = own[1]
+    if which > 0:
+        row = jnp.where(sec < 2, (odd_core[0], even_core[2])[which - 1], (even_core[0], odd_core[0])[which - 1])
     lane = lax.broadcasted_iota(jnp.int32, row.shape, 1)
     return lambda count: [jnp.sum(jnp.where(lane == i, row, 0.0)).astype(jnp.int32) for i in range(count)]
 
@@ -369,11 +416,14 @@
 
     saved[...] = kept[...]
 
+    def lead_plane(i):
+        return series[0][i * rows // 2 : (i + 1) * rows // 2]
+
     def after(step, state):
         @pl.when(sec == 0)
         def _():
             for i in range(planes):
-                part = series[1][step - LEAD, i] if step >= LEAD else to_tile(series[0][step, i], scratch)
+                part = series[1][step - LEAD, i] if step >= LEAD else to_tile(lead_plane(step * planes + i), scratch)
                 total[i] += state[reach + i] * part
 
         @pl.when(sec == last)
@@ -410,12 +460,31 @@
         to_corner[...] = to_across[held:]
 
 
-def call(kernel, out_shape, scratch, operands):
+def finish_kernel(contour, handoff_in, share, to_pair, to_across, to_corner, handoff, density):
+    sec = lax.axis_index("sec")
+    planes, count = density.shape[:2]
+    held = planes * count
+    corner = jnp.where(sec == 2, 0.0, to_corner[:held])
+    total = (share[...] + to_pair[...] + to_across[:held] + corner) / contour
+    for i in range(planes):
+        density[i] = total[i * count : (i + 1) * count]
+    handoff[0] = handoff_in[...]
+
+    @pl.when(sec == 2)
+    def _():
+        orients = handoff.shape[2]
+        pair = planes // 2
+        for i in range(pair):
+            handoff[0, i] = to_across[held + i * orients : held + (i + 1) * orients]
+            handoff[0, pair + i] = to_corner[i * orients : (i + 1) * orients]
+
+
+def call(kernel, out_shape, scratch, operands, dtypes=None):
     return pl.pallas_call(
         kernel,
         in_specs=[IN_VMEM] * len(operands),
         out_specs=[IN_VMEM] * len(out_shape),
-        out_shape=[jax.ShapeDtypeStruct(shape, jnp.float32) for shape in out_shape],
+        out_shape=[jax.ShapeDtypeStruct(shape, (dtypes or {}).get(i, jnp.float32)) for i, shape in enumerate(out_shape)],
         scratch_shapes=scratch,
         compiler_params=pltpu.CompilerParams(vmem_limit_bytes=VMEM_BYTES),
     )(*operands)
@@ -429,7 +498,6 @@
     near, far = (1, -1), (1, -1, 2, -2)
     rows = 2 * orients
     lanes = cells // 2
-    sec = lax.axis_index("sec")
     last = n_sec - 1
 
     def send(array, by_sec, shift=0):
@@ -437,21 +505,13 @@
         pairs = [(s * n_gx + g, t * n_gx + (g + shift) % n_gx) for s, t in by_sec for g in range(n_gx)]
         return lax.ppermute(array, ("sec", "gx"), pairs)
 
-    same, beside, across = (0, 1, 2, 3), (1, 0, 3, 2), (2, 3, 0, 1)
-    whole = incoming[0]
-    backward, fields, block_types, high, low = lax.optimization_barrier(
-        (backward, fields, block_types, whole[pair:], whole[:pair])
-    )
-    moved_high = send(high, (1, 3, 0, 2))
-    moved_low = send(low, (0, 2, 1, 3))
-    types = jnp.pad(block_types.astype(jnp.float32), ((0, 7), (0, lanes - steps)))
-    across_types = send(types, across)
-    lines = lax.dynamic_slice_in_dim(fields, sec % 2 * pair, pair, axis=1).reshape(-1, cells)
-    lines, backward = lax.optimization_barrier((lines, backward))
-    early_last = send(backward[:LEAD].astype(jnp.float32), {2: 0})
-    settled = prepare(backward, axial_taps, lateral_taps, depth_taps, bend_diagonal, bend_coupling)
-    lines, early_last, *settled = lax.optimization_barrier((lines, early_last, *settled))
-    stored, (taps, weights) = settled[:2], settled[2:]
+    same, beside = (0, 1, 2, 3), (1, 0, 3, 2)
+    high, low, lead, bundle = launch(
+        incoming, backward, fields, block_types, axial_taps, lateral_taps, depth_taps, bend_diagonal, bend_coupling
+    )
+    moved_high = send(high, {0: 1, 1: 3})
+    moved_low = send(low, {1: 2})
+    early_last = send(lead, {2: 0})
 
     tile = pltpu.VMEM((rows, lanes), jnp.float32)
     packed = pltpu.VMEM((GROUP * rows, 2 * lanes), jnp.bfloat16)
@@ -461,10 +521,17 @@
         slab = pltpu.VMEM((planes + 2 * extent, rows, lanes), jnp.float32)
         return [slab, slab, packed, packed, tile]
 
-    (piece,) = call(
-        pack_kernel, [(pair * rows + FIELD_ROWS, lanes)], [tile], [low, moved_high, moved_low, types, across_types, lines]
+    piece, taps, weights = call(
+        pack_kernel,
+        [(pair * rows + FIELD_ROWS, lanes), (TAP_ROWS, lanes), (2 * rows, 2 * lanes)],
+        [tile],
+        [bundle, moved_high, moved_low, early_last],
+        {2: jnp.bfloat16},
     )
     own = [send(piece, same, shift) for shift in far]
+    backward, _ = lax.optimization_barrier((backward, piece))
+    stored = call(turn_kernel, [(count, planes, rows, lanes) for count in (LEAD, steps - LEAD)], [tile], [backward])
+    own[-1], *stored = lax.optimization_barrier((own[-1], *stored))
     swapped = [send(each, beside) for each in [piece] + own]
     late_stored, *swapped = lax.optimization_barrier((stored[1], *swapped))
     late_last = send(late_stored, {2: 0})
@@ -492,11 +559,13 @@
     to_pair = send(to_pair, beside)
     to_across = send(to_across, (2, 0, 3, 1))
     to_corner = send(to_corner, (3, 2, 1, 0))
-    third = sec == 2
-    density = share + to_pair + to_across[:held] + jnp.where(third, 0.0, to_corner[:held])
-    arrived = jnp.concatenate([to_across[held:], to_corner]).reshape(handoff.shape)
-    handoff = jnp.where(third, arrived, handoff)
-    return handoff[None], density.reshape(planes, -1, cells) / (n_sec * steps)
+    handoff, density = call(
+        functools.partial(finish_kernel, n_sec * steps),
+        [(1,) + handoff.shape, (planes, orients // n_sec, cells)],
+        [],
+        [handoff, share, to_pair, to_across, to_corner],
+    )
+    return handoff, density
 
 
 def pairs_fit(n_sec, planes, steps, orients, cells, kinds):

time: 67.1 us -> 64.7 us (0.964)
  waiting for transfers between devices: 24.1 us -> 27.4 us
  local copies, waits for them, and re-layouts: 4.99 us -> 1.97 us
  other arithmetic: 2.99 us -> 0 us
  Pallas kernels: 11.3 us -> 13.9 us
  starting transfers between devices: 22.6 us -> 20.3 us
    ppermute x22 -> x21, waiting for transfers between devices: 24.1 us -> 27.4 us  [send(): return lax.ppermute(array, ('sec', 'gx'), pairs)]
    ppermute x22 -> x21, starting transfers between devices: 22.6 us -> 20.3 us  [send(): return lax.ppermute(array, ('sec', 'gx'), pairs)]
    concatenate x1 -> x0, local copies, waits for them, and re-layouts: 2.26 us -> none  [prepare(): jnp.concatenate([axial, lateral, depth, jnp.broadcast_to(diagonal, (7, or...]
    pallas_call x1, Pallas kernels: 0.41 us -> 2.22 us  [launch(): pl.pallas_call(launch_kernel, in_specs=[pl.BlockSpec(memory_space=pltpu.H...]
    convert_element_type x2 -> x0, other arithmetic: 1.59 us -> none  [the longest x1 0.93 us: paired(): early_last = send(backward[:LEAD].astype(jnp.float32), {2: 0})]
    slice x2 -> x0, local copies, waits for them, and re-layouts: 1 us -> none  [the longest x1 0.99 us: paired(): whole[:pair]]
    unnamed x4, local copies, waits for them, and re-layouts: 1.05 us -> 1.97 us
    pallas_call x3 -> x5, Pallas kernels: 10.9 us -> 11.7 us  [call(): pl.pallas_call(kernel, in_specs=[IN_VMEM] * len(operands), out_specs=[IN_...]
  transfers between devices with their start and end apart: 22 -> 21, of which waited for: 9 -> 12; matrix products, arithmetic and copies ran while one was open for 7% -> 0% of each run, Pallas kernels for 12% -> 12%
where the time goes in v8:
time: 64.7 us; the launch traced here: 64.4 us
  waiting for transfers between devices  27.4 us (42%)
  starting transfers between devices  20.3 us (31%)
  Pallas kernels  13.9 us (21%)
  local copies, waits for them, and re-layouts  1.97 us (3%)
  between operations  0.73 us (1%)
    ppermute x21, waiting for transfers between devices, send(): return lax.ppermute(array, ('sec', 'gx'), pairs)  27.4 us
    ppermute x21, starting transfers between devices, send(): return lax.ppermute(array, ('sec', 'gx'), pairs)  20.3 us
    pallas_call x5, Pallas kernels, call(): pl.pallas_call(kernel, in_specs=[IN_VMEM] * len(operands), out_specs=[IN_...  11.7 us
    pallas_call x1, Pallas kernels, launch(): pl.pallas_call(launch_kernel, in_specs=[pl.BlockSpec(memory_space=pltpu.H...  2.22 us
    unnamed x4, local copies, waits for them, and re-layouts  1.97 us
  transfers between devices with their start and end apart: 21, of which 12 were waited for; matrix products, arithmetic and copies ran while one was open for 0% of the time, Pallas kernels for 12%

profile of v8, /device:TPU:0, one launch (start us, length us, event | category | flops | bytes accessed | tf_op | source)
XLA Modules:
  0.0 64.4 jit_solution(9305726478381093364)
XLA Ops:
  0.6 2.2 %shard_map.104 = (f32[136,256]{1,0:T(8,128)}, f32[136,256]{1,0:T(8,128)}, f32[264,256]{1,0:T(8,128)}, f32[408,128]{1,0:T(8,128)}) custom-call(f32[1,4,64,256]{3,2,1,0:T(8,128)} %refs_0_.1, bf16[4,4,64,256]{3,2,1,0:T(8,128)(2,1)} %backward, f32[3,4,256]{2,1,0:T(4,128)} %refs_2_.1, s32[1,4]{1,0:T(1,128)} %refs_3_.1, f32[3,64]{1,0:T(4,128)} %refs_4_.1, ...), custom_call_target="tpu_custom_call" | custom-call | tf_op jit(solution)/shard_map/pallas_call | solution.py:233
  2.9 1.3 %collective-permute-start.2 = (f32[264,256]{1,0:T(8,128)}, f32[264,256]{1,0:T(8,128)S(1)}, u32[]{:S(2)}, u32[]{:S(2)}) collective-permute-start(f32[264,256]{1,0:T(8,128)} %get-tuple-element.34), channel_id=1, source_target_pairs={{16,0},{17,1},{18,2},{19,3},{20,4},{21,5},{22,6},{23,7}} | collective-permute-start | bytes 811016 | tf_op jit(solution)/shard_map/ppermute | solution.py:506
  4.2 1.8 %collective-permute-start = (f32[136,256]{1,0:T(8,128)}, f32[136,256]{1,0:T(8,128)S(1)}, u32[]{:S(2)}, u32[]{:S(2)}) collective-permute-start(f32[136,256]{1,0:T(8,128)} %get-tuple-element.32), channel_id=1, source_target_pairs={{0,8},{1,9},{2,10},{3,11},{4,12},{5,13},{6,14},{7,15},{8,24},{9,25... | collective-permute-start | bytes 417800 | tf_op jit(solution)/shard_map/ppermute | solution.py:506
  5.9 0.7 %collective-permute-start.1 = (f32[136,256]{1,0:T(8,128)}, f32[136,256]{1,0:T(8,128)S(1)}, u32[]{:S(2)}, u32[]{:S(2)}) collective-permute-start(f32[136,256]{1,0:T(8,128)} %get-tuple-element.33), channel_id=1, source_target_pairs={{8,16},{9,17},{10,18},{11,19},{12,20},{13,21},{14,22},{15,23}} | collective-permute-start | bytes 417800 | tf_op jit(solution)/shard_map/ppermute | solution.py:506
  6.6 0.5 collective-permute-done.moved_high
  7.1 0.0 collective-permute-done.1.moved_low
  7.1 4.6 %collective-permute-done.2.lead.refs_8_ = f32[264,256]{1,0:T(8,128)S(1)} collective-permute-done((f32[264,256]{1,0:T(8,128)}, f32[264,256]{1,0:T(8,128)S(1)}, u32[]{:S(2)}, u32[]{:S(2)}) %collective-permute-start.2) | collective-permute-done | bytes 270368 | tf_op jit(solution)/shard_map/ppermute | solution.py:506
  11.8 0.0 copy-start.1
  11.8 0.9 %copy-done.1 = f32[408,128]{1,0:T(8,128)S(1)} copy-done((f32[408,128]{1,0:T(8,128)S(1)}, f32[408,128]{1,0:T(8,128)}, u32[]{:S(2)}) %copy-start.1) | copy-done | bytes 208920
  12.7 4.8 %collective-permute-start.3 = (f32[272,128]{1,0:T(8,128)S(1)}, f32[272,128]{1,0:T(8,128)S(1)}, u32[]{:S(2)}, u32[]{:S(2)}) collective-permute-start(f32[272,128]{1,0:T(8,128)S(1)} %get-tuple-element.37.refs_0_.first_own), channel_id=1, source_target_pairs={{0,6},{1,7},{2,0},{3,1},{4,2},{5,3},{6,4},{7,5},{8,14},{9,15},{10,... | collective-permute-start | bytes 417800 | tf_op jit(solution)/shard_map/ppermute | solution.py:506
  17.5 0.0 collective-permute-start.9
  17.5 4.7 %collective-permute-start.7 = (f32[272,128]{1,0:T(8,128)S(1)}, f32[272,128]{1,0:T(8,128)S(1)}, u32[]{:S(2)}, u32[]{:S(2)}) collective-permute-start(f32[272,128]{1,0:T(8,128)S(1)} %get-tuple-element.37.refs_0_.first_own), channel_id=1, source_target_pairs={{0,7},{1,0},{2,1},{3,2},{4,3},{5,4},{6,5},{7,6},{8,15},{9,8},{10,9... | collective-permute-start | bytes 417800 | tf_op jit(solution)/shard_map/ppermute | solution.py:506
  22.2 0.0 collective-permute-start.5
  22.3 0.0 collective-permute-start.4
  22.3 0.0 copy-start
  22.3 1.0 %copy-done = bf16[4,4,64,256]{3,2,1,0:T(8,128)(2,1)S(1)} copy-done((bf16[4,4,64,256]{3,2,1,0:T(8,128)(2,1)S(1)}, bf16[4,4,64,256]{3,2,1,0:T(8,128)(2,1)}, u32[]{:S(2)}) %copy-start) | copy-done | bytes 524312
  23.3 0.3 shard_map.106
  23.7 0.0 collective-permute-done.3.refs_4_
  23.7 2.2 %collective-permute-done.9.refs_3_ = f32[272,128]{1,0:T(8,128)S(1)} collective-permute-done((f32[272,128]{1,0:T(8,128)S(1)}, f32[272,128]{1,0:T(8,128)S(1)}, u32[]{:S(2)}, u32[]{:S(2)}) %collective-permute-start.9) | collective-permute-done | bytes 139296 | tf_op jit(solution)/shard_map/ppermute | solution.py:506
  25.8 0.0 collective-permute-start.10
  25.9 1.3 %collective-permute-done.7.refs_2_ = f32[272,128]{1,0:T(8,128)S(1)} collective-permute-done((f32[272,128]{1,0:T(8,128)S(1)}, f32[272,128]{1,0:T(8,128)S(1)}, u32[]{:S(2)}, u32[]{:S(2)}) %collective-permute-start.7) | collective-permute-done | bytes 139296 | tf_op jit(solution)/shard_map/ppermute | solution.py:506
  27.1 0.0 collective-permute-start.8
  27.1 3.1 %collective-permute-done.5.refs_1_ = f32[272,128]{1,0:T(8,128)S(1)} collective-permute-done((f32[272,128]{1,0:T(8,128)S(1)}, f32[272,128]{1,0:T(8,128)S(1)}, u32[]{:S(2)}, u32[]{:S(2)}) %collective-permute-start.5) | collective-permute-done | bytes 139296 | tf_op jit(solution)/shard_map/ppermute | solution.py:506
  30.2 0.0 collective-permute-start.6
  30.2 0.5 collective-permute-start.11
  30.7 0.0 collective-permute-done.4.refs_5_.first_swapped
  30.7 0.0 collective-permute-done.10.refs_8_
  30.7 0.0 collective-permute-done.8.refs_7_
  30.7 0.8 %collective-permute-done.6.refs_6_ = f32[272,128]{1,0:T(8,128)S(1)} collective-permute-done((f32[272,128]{1,0:T(8,128)S(1)}, f32[272,128]{1,0:T(8,128)S(1)}, u32[]{:S(2)}, u32[]{:S(2)}) %collective-permute-start.6) | collective-permute-done | bytes 139296 | tf_op jit(solution)/shard_map/ppermute | solution.py:506
  31.6 0.2 collective-permute-done.11.refs_9_
  31.8 1.3 %collective-permute-start.17 = (f32[3,4,128,128]{3,2,1,0:T(8,128)S(1)}, f32[3,4,128,128]{3,2,1,0:T(8,128)S(1)}, u32[]{:S(2)}, u32[]{:S(2)}) collective-permute-start(f32[3,4,128,128]{3,2,1,0:T(8,128)S(1)} %get-tuple-element.54.refs_11_), channel_id=1, source_target_pairs={{16,0},{17,1},{18,2},{19,3},{20,4},{21,5},{22,6},{23,7}} | collective-permute-start | bytes 2359304 | tf_op jit(solution)/shard_map/ppermute | solution.py:506
  33.1 7.6 %shard_map.107 = (f32[4,128,128]{2,1,0:T(8,128)S(1)}, f32[2,128,128]{2,1,0:T(8,128)S(1)}, f32[4,128,128]{2,1,0:T(8,128)S(1)}, f32[4,128,128]{2,1,0:T(8,128)S(1)}, f32[3,20,128,128]{3,2,1,0:T(8,128)S(1)}) custom-call(f32[8,128]{1,0:T(8,128)S(1)} %get-tuple-element.35.taps, bf16[256,256]{1,0:T(8,128)(2,1)S(1)} %get-tuple-element.36.weights, ...), custom_call_target="tpu_custom_call" | custom-call | tf_op jit(solution)/shard_map/pallas_call | solution.py:483
  40.7 2.5 %collective-permute-start.13 = (f32[2,128,128]{2,1,0:T(8,128)S(1)}, f32[2,128,128]{2,1,0:T(8,128)S(1)}, u32[]{:S(2)}, u32[]{:S(2)}) collective-permute-start(f32[2,128,128]{2,1,0:T(8,128)S(1)} %get-tuple-element.50), channel_id=1, source_target_pairs={{0,7},{1,0},{2,1},{3,2},{4,3},{5,4},{6,5},{7,6},{8,15},{9,8},{10,9... | collective-permute-start | bytes 393224 | tf_op jit(solution)/shard_map/ppermute | solution.py:506
  43.2 0.0 collective-permute-start.12
  43.2 0.0 collective-permute-start.16
  43.2 2.7 %collective-permute-done.13.refs_1_ = f32[2,128,128]{2,1,0:T(8,128)S(1)} collective-permute-done((f32[2,128,128]{2,1,0:T(8,128)S(1)}, f32[2,128,128]{2,1,0:T(8,128)S(1)}, u32[]{:S(2)}, u32[]{:S(2)}) %collective-permute-start.13) | collective-permute-done | bytes 131104 | tf_op jit(solution)/shard_map/ppermute | solution.py:506
  45.9 0.0 collective-permute-start.15
  45.9 5.0 %collective-permute-done.12.refs_0_ = f32[2,128,128]{2,1,0:T(8,128)S(1)} collective-permute-done((f32[2,128,128]{2,1,0:T(8,128)S(1)}, f32[2,128,128]{2,1,0:T(8,128)S(1)}, u32[]{:S(2)}, u32[]{:S(2)}) %collective-permute-start.12) | collective-permute-done | bytes 131104 | tf_op jit(solution)/shard_map/ppermute | solution.py:506
  50.8 0.0 collective-permute-start.14
  50.8 0.0 collective-permute-done.15.refs_3_
  50.8 1.3 %collective-permute-done.14.refs_2_ = f32[2,128,128]{2,1,0:T(8,128)S(1)} collective-permute-done((f32[2,128,128]{2,1,0:T(8,128)S(1)}, f32[2,128,128]{2,1,0:T(8,128)S(1)}, u32[]{:S(2)}, u32[]{:S(2)}) %collective-permute-start.14) | collective-permute-done | bytes 131104 | tf_op jit(solution)/shard_map/ppermute | solution.py:506
  52.2 0.0 collective-permute-done.16.refs_7_
  52.2 0.0 collective-permute-done.17.refs_9_
  52.2 3.0 %shard_map.108 = (f32[4,64,256]{2,1,0:T(8,128)S(1)}, f32[64,256]{1,0:T(8,128)S(1)}, f32[64,256]{1,0:T(8,128)S(1)}, f32[192,256]{1,0:T(8,128)S(1)}, f32[128,256]{1,0:T(8,128)S(1)}) custom-call(f32[8,128]{1,0:T(8,128)S(1)} %get-tuple-element.35.taps, bf16[256,256]{1,0:T(8,128)(2,1)S(1)} %get-tuple-element.36.weights, ...), custom_call_target="tpu_custom_call" | custom-call | tf_op jit(solution)/shard_map/pallas_call | solution.py:483
  55.2 2.4 %collective-permute-start.19 = (f32[192,256]{1,0:T(8,128)S(1)}, f32[192,256]{1,0:T(8,128)S(1)}, u32[]{:S(2)}, u32[]{:S(2)}) collective-permute-start(f32[192,256]{1,0:T(8,128)S(1)} %get-tuple-element.58), channel_id=1, source_target_pairs={{0,16},{1,17},{2,18},{3,19},{4,20},{5,21},{6,22},{7,23},{8,0},{9,1... | collective-permute-start | bytes 589832 | tf_op jit(solution)/shard_map/ppermute | solution.py:506
  57.6 0.0 collective-permute-start.20
  57.6 0.4 collective-permute-start.18
  58.0 0.9 %collective-permute-done.18.to_pair = f32[64,256]{1,0:T(8,128)S(1)} collective-permute-done((f32[64,256]{1,0:T(8,128)S(1)}, f32[64,256]{1,0:T(8,128)S(1)}, u32[]{:S(2)}, u32[]{:S(2)}) %collective-permute-start.18) | collective-permute-done | bytes 65568 | tf_op jit(solution)/shard_map/ppermute | solution.py:506
  58.9 4.7 %collective-permute-done.20.to_corner = f32[128,256]{1,0:T(8,128)S(1)} collective-permute-done((f32[128,256]{1,0:T(8,128)S(1)}, f32[128,256]{1,0:T(8,128)S(1)}, u32[]{:S(2)}, u32[]{:S(2)}) %collective-permute-start.20) | collective-permute-done | bytes 131104 | tf_op jit(solution)/shard_map/ppermute | solution.py:506
  63.6 0.0 collective-permute-done.19.to_across
  63.6 0.8 %shard_map.109 = (f32[1,4,64,256]{3,2,1,0:T(8,128)}, f32[4,16,256]{2,1,0:T(8,128)}) custom-call(f32[4,64,256]{2,1,0:T(8,128)S(1)} %get-tuple-element.55.handoff_in, f32[64,256]{1,0:T(8,128)S(1)} %get-tuple-element.56.share, f32[64,256]{1,0:T(8,128)S(1)} %collective-permute-done.18.to_pair, f32[192,256]{1,0:T(8,128)S(1)} %collective-permute-done.19.to_across, ...), custom_call_target="tpu_custom_call" | custom-call | tf_op jit(solution)/shard_map/pallas_call | solution.py:483
  (1 shorter events, 0.0 us)
Async XLA Ops:
  2.9 8.9 %collective-permute-start.2 = (f32[264,256]{1,0:T(8,128)}, f32[264,256]{1,0:T(8,128)S(1)}, u32[]{:S(2)}, u32[]{:S(2)}) collective-permute-start(f32[264,256]{1,0:T(8,128)} %get-tuple-element.34), channel_id=1, source_target_pairs={{16,0},{17,1},{18,2},{19,3},{20,4},{21,5},{22,6},{23,7}} | collective-permute-start | bytes 811016 | tf_op jit(solution)/shard_map/ppermute | solution.py:506
  4.2 2.9 %collective-permute-start = (f32[136,256]{1,0:T(8,128)}, f32[136,256]{1,0:T(8,128)S(1)}, u32[]{:S(2)}, u32[]{:S(2)}) collective-permute-start(f32[136,256]{1,0:T(8,128)} %get-tuple-element.32), channel_id=1, source_target_pairs={{0,8},{1,9},{2,10},{3,11},{4,12},{5,13},{6,14},{7,15},{8,24},{9,25... | collective-permute-start | bytes 417800 | tf_op jit(solution)/shard_map/ppermute | solution.py:506
  5.9 1.2 %collective-permute-start.1 = (f32[136,256]{1,0:T(8,128)}, f32[136,256]{1,0:T(8,128)S(1)}, u32[]{:S(2)}, u32[]{:S(2)}) collective-permute-start(f32[136,256]{1,0:T(8,128)} %get-tuple-element.33), channel_id=1, source_target_pairs={{8,16},{9,17},{10,18},{11,19},{12,20},{13,21},{14,22},{15,23}} | collective-permute-start | bytes 417800 | tf_op jit(solution)/shard_map/ppermute | solution.py:506
  11.8 0.9 %copy-start.1 = (f32[408,128]{1,0:T(8,128)S(1)}, f32[408,128]{1,0:T(8,128)}, u32[]{:S(2)}) copy-start(f32[408,128]{1,0:T(8,128)} %get-tuple-element.31.bundle) | copy-start | bytes 626692
  12.7 10.9 %collective-permute-start.3 = (f32[272,128]{1,0:T(8,128)S(1)}, f32[272,128]{1,0:T(8,128)S(1)}, u32[]{:S(2)}, u32[]{:S(2)}) collective-permute-start(f32[272,128]{1,0:T(8,128)S(1)} %get-tuple-element.37.refs_0_.first_own), channel_id=1, source_target_pairs={{0,6},{1,7},{2,0},{3,1},{4,2},{5,3},{6,4},{7,5},{8,14},{9,15},{10,... | collective-permute-start | bytes 417800 | tf_op jit(solution)/shard_map/ppermute | solution.py:506
  17.5 8.4 %collective-permute-start.9 = (f32[272,128]{1,0:T(8,128)S(1)}, f32[272,128]{1,0:T(8,128)S(1)}, u32[]{:S(2)}, u32[]{:S(2)}) collective-permute-start(f32[272,128]{1,0:T(8,128)S(1)} %get-tuple-element.37.refs_0_.first_own), channel_id=1, source_target_pairs={{0,2},{1,3},{2,4},{3,5},{4,6},{5,7},{6,0},{7,1},{8,10},{9,11},{10,... | collective-permute-start | bytes 417800 | tf_op jit(solution)/shard_map/ppermute | solution.py:506
  17.5 9.6 %collective-permute-start.7 = (f32[272,128]{1,0:T(8,128)S(1)}, f32[272,128]{1,0:T(8,128)S(1)}, u32[]{:S(2)}, u32[]{:S(2)}) collective-permute-start(f32[272,128]{1,0:T(8,128)S(1)} %get-tuple-element.37.refs_0_.first_own), channel_id=1, source_target_pairs={{0,7},{1,0},{2,1},{3,2},{4,3},{5,4},{6,5},{7,6},{8,15},{9,8},{10,9... | collective-permute-start | bytes 417800 | tf_op jit(solution)/shard_map/ppermute | solution.py:506
  22.2 8.0 %collective-permute-start.5 = (f32[272,128]{1,0:T(8,128)S(1)}, f32[272,128]{1,0:T(8,128)S(1)}, u32[]{:S(2)}, u32[]{:S(2)}) collective-permute-start(f32[272,128]{1,0:T(8,128)S(1)} %get-tuple-element.37.refs_0_.first_own), channel_id=1, source_target_pairs={{0,1},{1,2},{2,3},{3,4},{4,5},{5,6},{6,7},{7,0},{8,9},{9,10},{10,1... | collective-permute-start | bytes 417800 | tf_op jit(solution)/shard_map/ppermute | solution.py:506
  22.3 8.5 %collective-permute-start.4 = (f32[272,128]{1,0:T(8,128)S(1)}, f32[272,128]{1,0:T(8,128)S(1)}, u32[]{:S(2)}, u32[]{:S(2)}) collective-permute-start(f32[272,128]{1,0:T(8,128)S(1)} %get-tuple-element.37.refs_0_.first_own), channel_id=1, source_target_pairs={{0,8},{1,9},{2,10},{3,11},{4,12},{5,13},{6,14},{7,15},{8,0},{9,1},... | collective-permute-start | bytes 417800 | tf_op jit(solution)/shard_map/ppermute | solution.py:506
  22.3 1.0 %copy-start = (bf16[4,4,64,256]{3,2,1,0:T(8,128)(2,1)S(1)}, bf16[4,4,64,256]{3,2,1,0:T(8,128)(2,1)}, u32[]{:S(2)}) copy-start(bf16[4,4,64,256]{3,2,1,0:T(8,128)(2,1)} %backward) | copy-start | bytes 1572868
  25.8 4.9 %collective-permute-start.10 = (f32[272,128]{1,0:T(8,128)S(1)}, f32[272,128]{1,0:T(8,128)S(1)}, u32[]{:S(2)}, u32[]{:S(2)}) collective-permute-start(f32[272,128]{1,0:T(8,128)S(1)} %collective-permute-done.9.refs_3_), channel_id=1, source_target_pairs={{0,8},{1,9},{2,10},{3,11},{4,12},{5,13},{6,14},{7,15},{8,0},{9,1},... | collective-permute-start | bytes 417800 | tf_op jit(solution)/shard_map/ppermute | solution.py:506
  27.1 3.6 %collective-permute-start.8 = (f32[272,128]{1,0:T(8,128)S(1)}, f32[272,128]{1,0:T(8,128)S(1)}, u32[]{:S(2)}, u32[]{:S(2)}) collective-permute-start(f32[272,128]{1,0:T(8,128)S(1)} %collective-permute-done.7.refs_2_), channel_id=1, source_target_pairs={{0,8},{1,9},{2,10},{3,11},{4,12},{5,13},{6,14},{7,15},{8,0},{9,1},... | collective-permute-start | bytes 417800 | tf_op jit(solution)/shard_map/ppermute | solution.py:506
  30.2 1.4 %collective-permute-start.6 = (f32[272,128]{1,0:T(8,128)S(1)}, f32[272,128]{1,0:T(8,128)S(1)}, u32[]{:S(2)}, u32[]{:S(2)}) collective-permute-start(f32[272,128]{1,0:T(8,128)S(1)} %collective-permute-done.5.refs_1_), channel_id=1, source_target_pairs={{0,8},{1,9},{2,10},{3,11},{4,12},{5,13},{6,14},{7,15},{8,0},{9,1},... | collective-permute-start | bytes 417800 | tf_op jit(solution)/shard_map/ppermute | solution.py:506
  30.2 1.6 %collective-permute-start.11 = (f32[272,128]{1,0:T(8,128)S(1)}, f32[272,128]{1,0:T(8,128)S(1)}, u32[]{:S(2)}, u32[]{:S(2)}) collective-permute-start(f32[272,128]{1,0:T(8,128)S(1)} %collective-permute-done.3.refs_4_), channel_id=1, source_target_pairs={{0,8},{1,9},{2,10},{3,11},{4,12},{5,13},{6,14},{7,15},{8,0},{9,1},... | collective-permute-start | bytes 417800 | tf_op jit(solution)/shard_map/ppermute | solution.py:506
  31.8 20.4 %collective-permute-start.17 = (f32[3,4,128,128]{3,2,1,0:T(8,128)S(1)}, f32[3,4,128,128]{3,2,1,0:T(8,128)S(1)}, u32[]{:S(2)}, u32[]{:S(2)}) collective-permute-start(f32[3,4,128,128]{3,2,1,0:T(8,128)S(1)} %get-tuple-element.54.refs_11_), channel_id=1, source_target_pairs={{16,0},{17,1},{18,2},{19,3},{20,4},{21,5},{22,6},{23,7}} | collective-permute-start | bytes 2359304 | tf_op jit(solution)/shard_map/ppermute | solution.py:506
  40.7 5.2 %collective-permute-start.13 = (f32[2,128,128]{2,1,0:T(8,128)S(1)}, f32[2,128,128]{2,1,0:T(8,128)S(1)}, u32[]{:S(2)}, u32[]{:S(2)}) collective-permute-start(f32[2,128,128]{2,1,0:T(8,128)S(1)} %get-tuple-element.50), channel_id=1, source_target_pairs={{0,7},{1,0},{2,1},{3,2},{4,3},{5,4},{6,5},{7,6},{8,15},{9,8},{10,9... | collective-permute-start | bytes 393224 | tf_op jit(solution)/shard_map/ppermute | solution.py:506
  43.2 7.7 %collective-permute-start.12 = (f32[2,128,128]{2,1,0:T(8,128)S(1)}, f32[2,128,128]{2,1,0:T(8,128)S(1)}, u32[]{:S(2)}, u32[]{:S(2)}) collective-permute-start(f32[2,128,128]{2,1,0:T(8,128)S(1)} %get-tuple-element.50), channel_id=1, source_target_pairs={{0,1},{1,2},{2,3},{3,4},{4,5},{5,6},{6,7},{7,0},{8,9},{9,10},{10,1... | collective-permute-start | bytes 393224 | tf_op jit(solution)/shard_map/ppermute | solution.py:506
  43.2 9.0 %collective-permute-start.16 = (f32[4,128,128]{2,1,0:T(8,128)S(1)}, f32[4,128,128]{2,1,0:T(8,128)S(1)}, u32[]{:S(2)}, u32[]{:S(2)}) collective-permute-start(f32[4,128,128]{2,1,0:T(8,128)S(1)} %get-tuple-element.53.refs_6_), channel_id=1, source_target_pairs={{0,8},{1,9},{2,10},{3,11},{4,12},{5,13},{6,14},{7,15},{8,0},{9,1},... | collective-permute-start | bytes 786440 | tf_op jit(solution)/shard_map/ppermute | solution.py:506
  45.9 5.0 %collective-permute-start.15 = (f32[2,128,128]{2,1,0:T(8,128)S(1)}, f32[2,128,128]{2,1,0:T(8,128)S(1)}, u32[]{:S(2)}, u32[]{:S(2)}) collective-permute-start(f32[2,128,128]{2,1,0:T(8,128)S(1)} %collective-permute-done.13.refs_1_), channel_id=1, source_target_pairs={{0,8},{1,9},{2,10},{3,11},{4,12},{5,13},{6,14},{7,15},{8,0},{9,1},... | collective-permute-start | bytes 393224 | tf_op jit(solution)/shard_map/ppermute | solution.py:506
  50.8 1.3 %collective-permute-start.14 = (f32[2,128,128]{2,1,0:T(8,128)S(1)}, f32[2,128,128]{2,1,0:T(8,128)S(1)}, u32[]{:S(2)}, u32[]{:S(2)}) collective-permute-start(f32[2,128,128]{2,1,0:T(8,128)S(1)} %collective-permute-done.12.refs_0_), channel_id=1, source_target_pairs={{0,8},{1,9},{2,10},{3,11},{4,12},{5,13},{6,14},{7,15},{8,0},{9,1},... | collective-permute-start | bytes 393224 | tf_op jit(solution)/shard_map/ppermute | solution.py:506
  55.2 8.5 %collective-permute-start.19 = (f32[192,256]{1,0:T(8,128)S(1)}, f32[192,256]{1,0:T(8,128)S(1)}, u32[]{:S(2)}, u32[]{:S(2)}) collective-permute-start(f32[192,256]{1,0:T(8,128)S(1)} %get-tuple-element.58), channel_id=1, source_target_pairs={{0,16},{1,17},{2,18},{3,19},{4,20},{5,21},{6,22},{7,23},{8,0},{9,1... | collective-permute-start | bytes 589832 | tf_op jit(solution)/shard_map/ppermute | solution.py:506
  57.6 6.1 %collective-permute-start.20 = (f32[128,256]{1,0:T(8,128)S(1)}, f32[128,256]{1,0:T(8,128)S(1)}, u32[]{:S(2)}, u32[]{:S(2)}) collective-permute-start(f32[128,256]{1,0:T(8,128)S(1)} %get-tuple-element.59), channel_id=1, source_target_pairs={{0,24},{1,25},{2,26},{3,27},{4,28},{5,29},{6,30},{7,31},{8,16},{9,... | collective-permute-start | bytes 393224 | tf_op jit(solution)/shard_map/ppermute | solution.py:506
  57.6 1.3 %collective-permute-start.18 = (f32[64,256]{1,0:T(8,128)S(1)}, f32[64,256]{1,0:T(8,128)S(1)}, u32[]{:S(2)}, u32[]{:S(2)}) collective-permute-start(f32[64,256]{1,0:T(8,128)S(1)} %get-tuple-element.57), channel_id=1, source_target_pairs={{0,8},{1,9},{2,10},{3,11},{4,12},{5,13},{6,14},{7,15},{8,0},{9,1},... | collective-permute-start | bytes 196616 | tf_op jit(solution)/shard_map/ppermute | solution.py:506

commit v9 on v8

--- a/solution.py
+++ b/solution.py
@@ -10,9 +10,9 @@
 TICKS = 3
 CZ = 64
 GROUP = 6
-FIELD_ROWS = 16
+FIELD_ROWS = 32
 TAP_ROWS = 8
-OWN_KINDS, FIRST_KINDS, ACROSS_KINDS = 12, 13, 14
+OWN_KINDS, FIRST_KINDS = 24, 25
 LEAD = 1
 VMEM_BYTES = 16 * 2**20
 WHOLE_VMEM_BYTES = 62 * 2**20
@@ -172,8 +172,8 @@
 
 
 def launch_kernel(*refs):
-    sources, (high, low, lead, bundle) = refs[:9], refs[9:13]
-    scratch, copies, sems = refs[13], refs[14:23], refs[23]
+    sources, (full, lead, bundle) = refs[:9], refs[9:12]
+    scratch, copies, sems = refs[12], refs[13:22], refs[22]
     moves = [
         pltpu.make_async_copy(source.at[pl.ds(0, copy.shape[0])], copy, sems.at[i])
         for i, (source, copy) in enumerate(zip(sources, copies))
@@ -183,7 +183,7 @@
     incoming, stored, fields, kinds, axial, lateral, depth, diagonal, coupling = copies
     for move in moves[2:]:
         move.wait()
-    rows, cells = scratch.shape[0], high.shape[1]
+    rows, cells = scratch.shape[0], full.shape[1]
     orients = rows // 2
     ratios = [each[w : w + 1] / each[1:2] for each in (axial, lateral, depth) for w in (0, 2)]
     for i, ratio in enumerate(ratios + ratios[:2]):
@@ -196,30 +196,27 @@
     bundle[TAP_ROWS : TAP_ROWS + rows] = jnp.concatenate([upper, pltpu.roll(upper, orients, 1)], axis=0).T
     types = kinds[...].astype(jnp.float32)
     types = jnp.concatenate([types, jnp.zeros((1, cells - types.shape[1]), jnp.float32)], axis=1)
-    odd = position()[1]
-    pair = incoming.shape[1] // 2
+    planes = incoming.shape[1]
     at = TAP_ROWS + rows
     bundle[at : at + FIELD_ROWS] = jnp.zeros((FIELD_ROWS, rows), jnp.float32)
     for kind in range(fields.shape[0]):
-        for i in range(pair):
-            line = fields[kind, pl.ds(pair * odd + i, 1), :]
-            here = at + (kind * pair + i) * 2
+        for i in range(planes):
+            line = fields[kind, i : i + 1, :]
+            here = at + (kind * planes + i) * 2
             bundle[here : here + 1] = line[:, :rows]
             bundle[here + 1 : here + 2] = line[:, rows:]
     bundle[at + OWN_KINDS : at + OWN_KINDS + 1] = types[:, :rows]
     moves[0].wait()
-    for i in range(pair):
-        low[i * orients : (i + 1) * orients] = incoming[0, i]
-        high[i * orients : (i + 1) * orients] = incoming[0, pair + i]
+    for i in range(planes):
+        full[i * orients : (i + 1) * orients] = incoming[0, i]
         here = at + FIELD_ROWS + i * rows
         bundle[here : here + rows] = to_tile(incoming[0, i], scratch)
     moves[1].wait()
-    planes = stored.shape[1]
     for step in range(LEAD):
         for i in range(planes):
             here = (step * planes + i) * orients
             lead[here : here + orients] = stored[step, i].astype(jnp.float32)
-    for out in (high, low, lead):
+    for out in (full, lead):
         out[out.shape[0] - 8 :] = jnp.broadcast_to(types, (8, cells))
 
 
@@ -227,8 +224,8 @@
     planes, orients, cells = backward.shape[1:]
     rows = 2 * orients
     operands = [incoming, backward, fields, kinds, axial, lateral, depth, diagonal.reshape(1, -1), coupling]
-    half = (planes // 2 * orients + 8, cells)
-    shapes = [half, half, (LEAD * planes * orients + 8, cells), (TAP_ROWS + rows + FIELD_ROWS + planes // 2 * rows, rows)]
+    shapes = [(count * planes * orients + 8, cells) for count in (1, LEAD)]
+    shapes.append((TAP_ROWS + rows + FIELD_ROWS + planes * rows, rows))
     taken = [(LEAD,) + each.shape[1:] if i == 1 else each.shape for i, each in enumerate(operands)]
     return pl.pallas_call(
         launch_kernel,
@@ -249,7 +246,7 @@
                 out[step, i] = to_tile(backward[begin + step, i].astype(jnp.float32), scratch)
 
 
-def pack_kernel(bundle, moved_high, moved_low, lead, out, taps, weights, scratch):
+def pack_kernel(bundle, moved, passed, out, taps, weights, scratch):
     sec, odd = position()
     rows = scratch.shape[0]
     orients = rows // 2
@@ -263,7 +260,6 @@
     at = out.shape[0] - FIELD_ROWS
     lines = TAP_ROWS + rows
     out[at:] = bundle[lines : lines + FIELD_ROWS]
-    out[at + ACROSS_KINDS : at + ACROSS_KINDS + 1] = lead[lead.shape[0] - 8 : lead.shape[0] - 7, :rows]
 
     @pl.when(sec == 0)
     def _():
@@ -276,21 +272,13 @@
         here = source.shape[0] - 8
         out[at + FIRST_KINDS : at + FIRST_KINDS + 1] = source[here : here + 1, :rows]
 
-    pl.when(odd == 1)(lambda: fill(moved_high))
-    pl.when((sec > 0) & (odd == 0))(lambda: fill(moved_low))
-
-
-def kinds_at(pieces, at, which):
-    sec, odd = position()
-    own, others = ([each[at + i : at + i + 1] for i in (OWN_KINDS, FIRST_KINDS, ACROSS_KINDS)] for each in pieces)
-    even_core, odd_core = (
-        [jnp.where(odd == core, mine, theirs) for mine, theirs in zip(own, others)] for core in (0, 1)
-    )
-    row = own[1]
-    if which > 0:
-        row = jnp.where(sec < 2, (odd_core[0], even_core[2])[which - 1], (even_core[0], odd_core[0])[which - 1])
+    pl.when(odd == 1)(lambda: fill(moved))
+    pl.when((sec > 0) & (odd == 0))(lambda: fill(passed))
+
+
+def scalars_of(row, count):
     lane = lax.broadcasted_iota(jnp.int32, row.shape, 1)
-    return lambda count: [jnp.sum(jnp.where(lane == i, row, 0.0)).astype(jnp.int32) for i in range(count)]
+    return [jnp.sum(jnp.where(lane == i, row, 0.0)).astype(jnp.int32) for i in range(count)]
 
 
 def places(odd, planes, reach, blocks):
@@ -355,23 +343,28 @@
                 factor[kind, start + i] = jnp.take_along_axis(columns, right + at, axis=1, mode="promise_in_bounds")
 
 
-def early_kernel(blocks, taps, weights, *refs):
-    pieces, refs = refs[: 2 * len(blocks)], refs[2 * len(blocks) :]
-    stored, (middle, half_out, kept, total, factor) = refs[:2], refs[2:7]
-    slab, other, first, second, scratch = refs[7:]
+def early_kernel(taps, weights, lead, *refs):
+    pieces, stored, (middle, half_out, kept, total, factor) = refs[:5], refs[5:7], refs[7:12]
+    slab, other, first, second, scratch = refs[12:]
     sec, odd = position()
     planes, rows = middle.shape[:2]
     pair = planes // 2
     reach = (slab.shape[0] - planes) // 2
-    starts = places(odd, planes, reach, blocks)
+    mine, others = (planes * (1 + core) for core in (odd, 1 - odd))
+    starts = [reach, reach - mine, reach + mine, reach - others, reach + others]
     for piece, start in zip(pieces, starts):
-        for i in range(pair):
+        for i in range(planes):
             slab[start + i] = piece[i * rows : (i + 1) * rows]
+    at = planes * rows
     steps = LEAD + stored[1].shape[0]
-    centre = (pieces[0], pieces[len(blocks)])
-    kinds = [kind for which in (0, 1) for kind in kinds_at(centre, pair * rows, which)(steps)]
-    width = 2 * pair * factor.shape[0]
-    lines = [piece[pair * rows : pair * rows + width] for piece in pieces]
+    own_kinds, first_kinds = (pieces[0][at + row : at + row + 1] for row in (OWN_KINDS, FIRST_KINDS))
+    beside_kinds = pieces[3][at + OWN_KINDS : at + OWN_KINDS + 1]
+    kinds = scalars_of(first_kinds, steps)
+    kinds += scalars_of(jnp.where((sec == 1) | (sec == 2), own_kinds, beside_kinds), steps)
+    lead_kinds = lead[lead.shape[0] - 8 : lead.shape[0], :rows]
+    half_out[pair * rows :] = jnp.where(sec == 0, lead_kinds, jnp.broadcast_to(own_kinds, lead_kinds.shape))
+    width = 2 * planes * factor.shape[0]
+    lines = [piece[at : at + width] for piece in pieces]
     lines.append(jnp.zeros((rows - width * len(pieces), rows), jnp.float32))
     scratch[...] = jnp.exp(-jnp.concatenate(lines, axis=0)).T
     spread_factor(reorder(scratch), factor, starts, width)
@@ -390,10 +383,11 @@
     run_steps(kinds, taps, weights, reach, slab, other, first, second, factor, 0, after)
     state = (slab, other)[reach % 2]
     middle[...] = state[reach : reach + planes]
-    half_out[...] = state[pl.ds(reach + pair * odd, pair)]
-
-
-def late_kernel(blocks, last, taps, weights, first_own, first_swapped, middle, *refs):
+    for i in range(pair):
+        half_out[i * rows : (i + 1) * rows] = state[reach + pair * odd + i]
+
+
+def late_kernel(blocks, last, taps, weights, middle, *refs):
     pieces, refs = refs[: 2 * len(blocks)], refs[2 * len(blocks) :]
     factor, kept, total_in, total_beside, series, stored = refs[0], refs[1], refs[2], refs[3], refs[4:6], refs[6:8]
     handoff, share, to_pair, to_across, to_corner = refs[8:13]
@@ -403,11 +397,12 @@
     pair = planes // 2
     reach = (slab.shape[0] - planes) // 2
     begun = (factor.shape[1] - planes) // 2
-    kinds = kinds_at((first_own, first_swapped), pair * rows, 2)(reach)
+    even, uneven = (jnp.where(odd == core, pieces[0][pair * rows :], pieces[len(blocks)][pair * rows :]) for core in (0, 1))
+    kinds = scalars_of(jnp.where(sec < 2, even, uneven)[:1], reach)
     slab[reach : reach + planes] = middle[...]
     for piece, start in zip(pieces, places(odd, planes, reach, blocks)):
         for i in range(pair):
-            slab[start + i] = piece[i]
+            slab[start + i] = piece[i * rows : (i + 1) * rows]
     total[...] = jnp.zeros(total.shape, jnp.float32)
 
     @pl.when(sec == 0)
@@ -495,23 +490,25 @@
     steps, planes, orients, cells = backward.shape
     pair = planes // 2
     reach = (TICKS - 1) * steps, steps
-    near, far = (1, -1), (1, -1, 2, -2)
+    near = (1, -1)
     rows = 2 * orients
     lanes = cells // 2
     last = n_sec - 1
 
-    def send(array, by_sec, shift=0):
+    def send(array, by_sec, even=0, odd=0):
         by_sec = by_sec.items() if isinstance(by_sec, dict) else enumerate(by_sec)
-        pairs = [(s * n_gx + g, t * n_gx + (g + shift) % n_gx) for s, t in by_sec for g in range(n_gx)]
+        pairs = [
+            (s * n_gx + g, t * n_gx + (g + (odd if s % 2 else even)) % n_gx) for s, t in by_sec for g in range(n_gx)
+        ]
         return lax.ppermute(array, ("sec", "gx"), pairs)
 
     same, beside = (0, 1, 2, 3), (1, 0, 3, 2)
-    high, low, lead, bundle = launch(
+    full, lead, bundle = launch(
         incoming, backward, fields, block_types, axial_taps, lateral_taps, depth_taps, bend_diagonal, bend_coupling
     )
-    moved_high = send(high, {0: 1, 1: 3})
-    moved_low = send(low, {1: 2})
-    early_last = send(lead, {2: 0})
+    moved = send(full, {0: 1, 1: 3})
+    passed = send(moved, {3: 2})
+    passed, lead = lax.optimization_barrier((passed, send(lead, {2: 0})))
 
     tile = pltpu.VMEM((rows, lanes), jnp.float32)
     packed = pltpu.VMEM((GROUP * rows, 2 * lanes), jnp.bfloat16)
@@ -523,27 +520,26 @@
 
     piece, taps, weights = call(
         pack_kernel,
-        [(pair * rows + FIELD_ROWS, lanes), (TAP_ROWS, lanes), (2 * rows, 2 * lanes)],
+        [(planes * rows + FIELD_ROWS, lanes), (TAP_ROWS, lanes), (2 * rows, 2 * lanes)],
         [tile],
-        [bundle, moved_high, moved_low, early_last],
+        [bundle, moved, passed],
         {2: jnp.bfloat16},
     )
-    own = [send(piece, same, shift) for shift in far]
+    own = [send(piece, same, shift, 2 * shift) for shift in near]
     backward, _ = lax.optimization_barrier((backward, piece))
     stored = call(turn_kernel, [(count, planes, rows, lanes) for count in (LEAD, steps - LEAD)], [tile], [backward])
     own[-1], *stored = lax.optimization_barrier((own[-1], *stored))
-    swapped = [send(each, beside) for each in [piece] + own]
+    swapped = [send(each, beside) for each in own]
     late_stored, *swapped = lax.optimization_barrier((stored[1], *swapped))
     late_last = send(late_stored, {2: 0})
-    firsts = [piece, swapped[0]]
     middle, piece, kept, total, factor = call(
-        functools.partial(early_kernel, tuple(-shift for shift in (0,) + far)),
-        [(planes, rows, lanes), (pair, rows, lanes), (planes, rows, lanes), (planes, rows, lanes)]
+        early_kernel,
+        [(planes, rows, lanes), (pair * rows + 8, lanes), (planes, rows, lanes), (planes, rows, lanes)]
         + [(fields.shape[0], planes + 2 * reach[0], rows, lanes)],
         work(reach[0]),
-        [taps, weights, piece, *own, *swapped, *stored],
-    )
-    own = [send(piece, same, shift) for shift in near]
+        [taps, weights, lead, piece, *own, *swapped, *stored],
+    )
+    own = [send(piece, same, shift, shift) for shift in near]
     beside_total = send(total, beside)
     swapped = [send(each, beside) for each in own]
     held = planes * (orients // n_sec)
@@ -553,8 +549,8 @@
         + [(held, cells)] * 2
         + [(held + pair * orients, cells), (pair * orients, cells)],
         work(reach[1]) + [inner, inner, pltpu.VMEM((orients, cells), jnp.float32)],
-        [taps, weights, *firsts, middle, *own, *swapped, factor, kept, total, beside_total]
-        + [early_last, late_last, *stored],
+        [taps, weights, middle, *own, *swapped, factor, kept, total, beside_total]
+        + [lead, late_last, *stored],
     )
     to_pair = send(to_pair, beside)
     to_across = send(to_across, (2, 0, 3, 1))
@@ -574,7 +570,7 @@
         and planes == steps
         and planes % 2 == 0
         and 2 * orients == 2 * CZ == cells // 2 == 128
-        and kinds * planes <= FIELD_ROWS and 10 * kinds * planes <= 2 * orients
+        and 2 * kinds * planes <= OWN_KINDS and 10 * kinds * planes <= 2 * orients
         and GROUP < 2 * planes
     )
 

time: 64.7 us -> 63.5 us (0.981)
  starting transfers between devices: 20.3 us -> 15.9 us
  waiting for transfers between devices: 27.4 us -> 30.4 us
    ppermute x21 -> x16, starting transfers between devices: 20.3 us -> 15.9 us  [send(): return lax.ppermute(array, ('sec', 'gx'), pairs)]
    ppermute x21 -> x16, waiting for transfers between devices: 27.4 us -> 30.4 us  [send(): return lax.ppermute(array, ('sec', 'gx'), pairs)]
  transfers between devices with their start and end apart: 21 -> 16, of which waited for: 12 -> 9; matrix products, arithmetic and copies ran while one was open for 0% -> 0% of each run, Pallas kernels for 12% -> 13%
where the time goes in v9:
time: 63.5 us; the launch traced here: 63.2 us
  waiting for transfers between devices  30.4 us (48%)
  starting transfers between devices  15.9 us (25%)
  Pallas kernels  14.2 us (22%)
  local copies, waits for them, and re-layouts  2.02 us (3%)
  between operations  0.72 us (1%)
    ppermute x16, waiting for transfers between devices, send(): return lax.ppermute(array, ('sec', 'gx'), pairs)  30.4 us
    ppermute x16, starting transfers between devices, send(): return lax.ppermute(array, ('sec', 'gx'), pairs)  15.9 us
    pallas_call x5, Pallas kernels, call(): pl.pallas_call(kernel, in_specs=[IN_VMEM] * len(operands), out_specs=[IN_...  11.9 us
    pallas_call x1, Pallas kernels, launch(): pl.pallas_call(launch_kernel, in_specs=[pl.BlockSpec(memory_space=pltpu.H...  2.33 us
    unnamed x4, local copies, waits for them, and re-layouts  2.02 us
  transfers between devices with their start and end apart: 16, of which 9 were waited for; matrix products, arithmetic and copies ran while one was open for 0% of the time, Pallas kernels for 13%

profile of v9, /device:TPU:0, one launch (start us, length us, event | category | flops | bytes accessed | tf_op | source)
XLA Modules:
  0.0 63.2 jit_solution(8759837100296115453)
XLA Ops:
  0.6 2.3 %shard_map.104 = (f32[264,256]{1,0:T(8,128)}, f32[264,256]{1,0:T(8,128)}, f32[680,128]{1,0:T(8,128)}) custom-call(f32[1,4,64,256]{3,2,1,0:T(8,128)} %refs_0_.1, bf16[4,4,64,256]{3,2,1,0:T(8,128)(2,1)} %backward, f32[3,4,256]{2,1,0:T(4,128)} %refs_2_.1, s32[1,4]{1,0:T(1,128)} %refs_3_.1, f32[3,64]{1,0:T(4,128)} %refs_4_.1, f32[3,64]{1,0:T(4,128)} %refs_5_.1, ...), custom_call_target="tpu_custom_call" | custom-call | tf_op jit(solution)/shard_map/pallas_call | solution.py:230
  3.0 2.4 %collective-permute-start = (f32[264,256]{1,0:T(8,128)}, f32[264,256]{1,0:T(8,128)S(1)}, u32[]{:S(2)}, u32[]{:S(2)}) collective-permute-start(f32[264,256]{1,0:T(8,128)} %get-tuple-element.30), channel_id=1, source_target_pairs={{0,8},{1,9},{2,10},{3,11},{4,12},{5,13},{6,14},{7,15},{8,24},{9,25... | collective-permute-start | bytes 811016 | tf_op jit(solution)/shard_map/ppermute | solution.py:503
  5.3 1.3 %collective-permute-start.2 = (f32[264,256]{1,0:T(8,128)}, f32[264,256]{1,0:T(8,128)S(1)}, u32[]{:S(2)}, u32[]{:S(2)}) collective-permute-start(f32[264,256]{1,0:T(8,128)} %get-tuple-element.31), channel_id=1, source_target_pairs={{16,0},{17,1},{18,2},{19,3},{20,4},{21,5},{22,6},{23,7}} | collective-permute-start | bytes 811016 | tf_op jit(solution)/shard_map/ppermute | solution.py:503
  6.6 0.1 collective-permute-done.moved
  6.7 0.7 %collective-permute-start.1 = (f32[264,256]{1,0:T(8,128)S(1)}, f32[264,256]{1,0:T(8,128)S(1)}, u32[]{:S(2)}, u32[]{:S(2)}) collective-permute-start(f32[264,256]{1,0:T(8,128)S(1)} %collective-permute-done.moved), channel_id=1, source_target_pairs={{24,16},{25,17},{26,18},{27,19},{28,20},{29,21},{30,22},{31,23}} | collective-permute-start | bytes 811016 | tf_op jit(solution)/shard_map/ppermute | solution.py:503
  7.4 6.5 %collective-permute-done.2.lead.refs_8_ = f32[264,256]{1,0:T(8,128)S(1)} collective-permute-done((f32[264,256]{1,0:T(8,128)}, f32[264,256]{1,0:T(8,128)S(1)}, u32[]{:S(2)}, u32[]{:S(2)}) %collective-permute-start.2) | collective-permute-done | bytes 270368 | tf_op jit(solution)/shard_map/ppermute | solution.py:503
  13.9 0.0 collective-permute-done.1.passed
  13.9 0.0 copy-start.1
  13.9 1.0 %copy-done.1 = f32[680,128]{1,0:T(8,128)S(1)} copy-done((f32[680,128]{1,0:T(8,128)S(1)}, f32[680,128]{1,0:T(8,128)}, u32[]{:S(2)}) %copy-start.1) | copy-done | bytes 348184
  14.9 5.4 %collective-permute-start.4 = (f32[544,128]{1,0:T(8,128)S(1)}, f32[544,128]{1,0:T(8,128)S(1)}, u32[]{:S(2)}, u32[]{:S(2)}) collective-permute-start(f32[544,128]{1,0:T(8,128)S(1)} %get-tuple-element.36.refs_0_), channel_id=1, source_target_pairs={{0,7},{1,0},{2,1},{3,2},{4,3},{5,4},{6,5},{7,6},{8,14},{9,15},{10,... | collective-permute-start | bytes 835592 | tf_op jit(solution)/shard_map/ppermute | solution.py:503
  20.4 0.0 collective-permute-start.3
  20.4 0.0 copy-start
  20.4 1.0 %copy-done = bf16[4,4,64,256]{3,2,1,0:T(8,128)(2,1)S(1)} copy-done((bf16[4,4,64,256]{3,2,1,0:T(8,128)(2,1)S(1)}, bf16[4,4,64,256]{3,2,1,0:T(8,128)(2,1)}, u32[]{:S(2)}) %copy-start) | copy-done | bytes 524312
  21.4 0.3 shard_map.106
  21.8 4.0 %collective-permute-done.4.refs_2_ = f32[544,128]{1,0:T(8,128)S(1)} collective-permute-done((f32[544,128]{1,0:T(8,128)S(1)}, f32[544,128]{1,0:T(8,128)S(1)}, u32[]{:S(2)}, u32[]{:S(2)}) %collective-permute-start.4) | collective-permute-done | bytes 278560 | tf_op jit(solution)/shard_map/ppermute | solution.py:503
  25.7 0.0 collective-permute-start.6
  25.7 3.9 %collective-permute-done.3.refs_1_ = f32[544,128]{1,0:T(8,128)S(1)} collective-permute-done((f32[544,128]{1,0:T(8,128)S(1)}, f32[544,128]{1,0:T(8,128)S(1)}, u32[]{:S(2)}, u32[]{:S(2)}) %collective-permute-start.3) | collective-permute-done | bytes 278560 | tf_op jit(solution)/shard_map/ppermute | solution.py:503
  29.6 0.0 collective-permute-start.5
  29.6 0.0 collective-permute-done.6.refs_4_
  29.6 1.6 %collective-permute-done.5.refs_3_ = f32[544,128]{1,0:T(8,128)S(1)} collective-permute-done((f32[544,128]{1,0:T(8,128)S(1)}, f32[544,128]{1,0:T(8,128)S(1)}, u32[]{:S(2)}, u32[]{:S(2)}) %collective-permute-start.5) | collective-permute-done | bytes 278560 | tf_op jit(solution)/shard_map/ppermute | solution.py:503
  31.2 1.3 %collective-permute-start.12 = (f32[3,4,128,128]{3,2,1,0:T(8,128)S(1)}, f32[3,4,128,128]{3,2,1,0:T(8,128)S(1)}, u32[]{:S(2)}, u32[]{:S(2)}) collective-permute-start(f32[3,4,128,128]{3,2,1,0:T(8,128)S(1)} %get-tuple-element.50.refs_6_.refs_11_), channel_id=1, source_target_pairs={{16,0},{17,1},{18,2},{19,3},{20,4},{21,5},{22,6},{23,7}} | collective-permute-start | bytes 2359304 | tf_op jit(solution)/shard_map/ppermute | solution.py:503
  32.4 7.7 %shard_map.107 = (f32[4,128,128]{2,1,0:T(8,128)S(1)}, f32[264,128]{1,0:T(8,128)S(1)}, f32[4,128,128]{2,1,0:T(8,128)S(1)}, f32[4,128,128]{2,1,0:T(8,128)S(1)}, f32[3,20,128,128]{3,2,1,0:T(8,128)S(1)}) custom-call(f32[8,128]{1,0:T(8,128)S(1)} %get-tuple-element.33.taps, bf16[256,256]{1,0:T(8,128)(2,1)S(1)} %get-tuple-element.34.weights, ...), custom_call_target="tpu_custom_call" | custom-call | tf_op jit(solution)/shard_map/pallas_call | solution.py:478
  40.2 1.8 %collective-permute-start.8 = (f32[264,128]{1,0:T(8,128)S(1)}, f32[264,128]{1,0:T(8,128)S(1)}, u32[]{:S(2)}, u32[]{:S(2)}) collective-permute-start(f32[264,128]{1,0:T(8,128)S(1)} %get-tuple-element.46), channel_id=1, source_target_pairs={{0,7},{1,0},{2,1},{3,2},{4,3},{5,4},{6,5},{7,6},{8,15},{9,8},{10,9... | collective-permute-start | bytes 405512 | tf_op jit(solution)/shard_map/ppermute | solution.py:503
  41.9 0.3 collective-permute-start.7
  42.3 0.0 collective-permute-start.11
  42.3 3.0 %collective-permute-done.8.refs_1_ = f32[264,128]{1,0:T(8,128)S(1)} collective-permute-done((f32[264,128]{1,0:T(8,128)S(1)}, f32[264,128]{1,0:T(8,128)S(1)}, u32[]{:S(2)}, u32[]{:S(2)}) %collective-permute-start.8) | collective-permute-done | bytes 135200 | tf_op jit(solution)/shard_map/ppermute | solution.py:503
  45.3 0.0 collective-permute-start.10
  45.3 4.4 %collective-permute-done.7.refs_0_ = f32[264,128]{1,0:T(8,128)S(1)} collective-permute-done((f32[264,128]{1,0:T(8,128)S(1)}, f32[264,128]{1,0:T(8,128)S(1)}, u32[]{:S(2)}, u32[]{:S(2)}) %collective-permute-start.7) | collective-permute-done | bytes 135200 | tf_op jit(solution)/shard_map/ppermute | solution.py:503
  49.6 0.0 collective-permute-start.9
  49.6 0.0 collective-permute-done.11.refs_7_
  49.6 0.0 collective-permute-done.10.refs_3_
  49.7 1.3 %collective-permute-done.9.refs_2_ = f32[264,128]{1,0:T(8,128)S(1)} collective-permute-done((f32[264,128]{1,0:T(8,128)S(1)}, f32[264,128]{1,0:T(8,128)S(1)}, u32[]{:S(2)}, u32[]{:S(2)}) %collective-permute-start.9) | collective-permute-done | bytes 135200 | tf_op jit(solution)/shard_map/ppermute | solution.py:503
  51.0 0.0 collective-permute-done.12.refs_9_
  51.0 3.0 %shard_map.108 = (f32[4,64,256]{2,1,0:T(8,128)S(1)}, f32[64,256]{1,0:T(8,128)S(1)}, f32[64,256]{1,0:T(8,128)S(1)}, f32[192,256]{1,0:T(8,128)S(1)}, f32[128,256]{1,0:T(8,128)S(1)}) custom-call(f32[8,128]{1,0:T(8,128)S(1)} %get-tuple-element.33.taps, bf16[256,256]{1,0:T(8,128)(2,1)S(1)} %get-tuple-element.34.weights, ...), custom_call_target="tpu_custom_call" | custom-call | tf_op jit(solution)/shard_map/pallas_call | solution.py:478
  54.0 2.4 %collective-permute-start.14 = (f32[192,256]{1,0:T(8,128)S(1)}, f32[192,256]{1,0:T(8,128)S(1)}, u32[]{:S(2)}, u32[]{:S(2)}) collective-permute-start(f32[192,256]{1,0:T(8,128)S(1)} %get-tuple-element.54), channel_id=1, source_target_pairs={{0,16},{1,17},{2,18},{3,19},{4,20},{5,21},{6,22},{7,23},{8,0},{9,1... | collective-permute-start | bytes 589832 | tf_op jit(solution)/shard_map/ppermute | solution.py:503
  56.4 0.0 collective-permute-start.15
  56.4 0.4 collective-permute-start.13
  56.8 0.9 %collective-permute-done.13.to_pair = f32[64,256]{1,0:T(8,128)S(1)} collective-permute-done((f32[64,256]{1,0:T(8,128)S(1)}, f32[64,256]{1,0:T(8,128)S(1)}, u32[]{:S(2)}, u32[]{:S(2)}) %collective-permute-start.13) | collective-permute-done | bytes 65568 | tf_op jit(solution)/shard_map/ppermute | solution.py:503
  57.7 4.7 %collective-permute-done.15.to_corner = f32[128,256]{1,0:T(8,128)S(1)} collective-permute-done((f32[128,256]{1,0:T(8,128)S(1)}, f32[128,256]{1,0:T(8,128)S(1)}, u32[]{:S(2)}, u32[]{:S(2)}) %collective-permute-start.15) | collective-permute-done | bytes 131104 | tf_op jit(solution)/shard_map/ppermute | solution.py:503
  62.5 0.0 collective-permute-done.14.to_across
  62.5 0.8 %shard_map.109 = (f32[1,4,64,256]{3,2,1,0:T(8,128)}, f32[4,16,256]{2,1,0:T(8,128)}) custom-call(f32[4,64,256]{2,1,0:T(8,128)S(1)} %get-tuple-element.51.handoff_in, f32[64,256]{1,0:T(8,128)S(1)} %get-tuple-element.52.share, f32[64,256]{1,0:T(8,128)S(1)} %collective-permute-done.13.to_pair, f32[192,256]{1,0:T(8,128)S(1)} %collective-permute-done.14.to_across, ...), custom_call_target="tpu_custom_call" | custom-call | tf_op jit(solution)/shard_map/pallas_call | solution.py:478
  (1 shorter events, 0.0 us)
Async XLA Ops:
  3.0 3.7 %collective-permute-start = (f32[264,256]{1,0:T(8,128)}, f32[264,256]{1,0:T(8,128)S(1)}, u32[]{:S(2)}, u32[]{:S(2)}) collective-permute-start(f32[264,256]{1,0:T(8,128)} %get-tuple-element.30), channel_id=1, source_target_pairs={{0,8},{1,9},{2,10},{3,11},{4,12},{5,13},{6,14},{7,15},{8,24},{9,25... | collective-permute-start | bytes 811016 | tf_op jit(solution)/shard_map/ppermute | solution.py:503
  5.3 8.6 %collective-permute-start.2 = (f32[264,256]{1,0:T(8,128)}, f32[264,256]{1,0:T(8,128)S(1)}, u32[]{:S(2)}, u32[]{:S(2)}) collective-permute-start(f32[264,256]{1,0:T(8,128)} %get-tuple-element.31), channel_id=1, source_target_pairs={{16,0},{17,1},{18,2},{19,3},{20,4},{21,5},{22,6},{23,7}} | collective-permute-start | bytes 811016 | tf_op jit(solution)/shard_map/ppermute | solution.py:503
  6.7 7.2 %collective-permute-start.1 = (f32[264,256]{1,0:T(8,128)S(1)}, f32[264,256]{1,0:T(8,128)S(1)}, u32[]{:S(2)}, u32[]{:S(2)}) collective-permute-start(f32[264,256]{1,0:T(8,128)S(1)} %collective-permute-done.moved), channel_id=1, source_target_pairs={{24,16},{25,17},{26,18},{27,19},{28,20},{29,21},{30,22},{31,23}} | collective-permute-start | bytes 811016 | tf_op jit(solution)/shard_map/ppermute | solution.py:503
  13.9 1.0 %copy-start.1 = (f32[680,128]{1,0:T(8,128)S(1)}, f32[680,128]{1,0:T(8,128)}, u32[]{:S(2)}) copy-start(f32[680,128]{1,0:T(8,128)} %get-tuple-element.29.bundle) | copy-start | bytes 1044484
  14.9 10.8 %collective-permute-start.4 = (f32[544,128]{1,0:T(8,128)S(1)}, f32[544,128]{1,0:T(8,128)S(1)}, u32[]{:S(2)}, u32[]{:S(2)}) collective-permute-start(f32[544,128]{1,0:T(8,128)S(1)} %get-tuple-element.36.refs_0_), channel_id=1, source_target_pairs={{0,7},{1,0},{2,1},{3,2},{4,3},{5,4},{6,5},{7,6},{8,14},{9,15},{10,... | collective-permute-start | bytes 835592 | tf_op jit(solution)/shard_map/ppermute | solution.py:503
  20.4 9.2 %collective-permute-start.3 = (f32[544,128]{1,0:T(8,128)S(1)}, f32[544,128]{1,0:T(8,128)S(1)}, u32[]{:S(2)}, u32[]{:S(2)}) collective-permute-start(f32[544,128]{1,0:T(8,128)S(1)} %get-tuple-element.36.refs_0_), channel_id=1, source_target_pairs={{0,1},{1,2},{2,3},{3,4},{4,5},{5,6},{6,7},{7,0},{8,10},{9,11},{10,... | collective-permute-start | bytes 835592 | tf_op jit(solution)/shard_map/ppermute | solution.py:503
  20.4 1.0 %copy-start = (bf16[4,4,64,256]{3,2,1,0:T(8,128)(2,1)S(1)}, bf16[4,4,64,256]{3,2,1,0:T(8,128)(2,1)}, u32[]{:S(2)}) copy-start(bf16[4,4,64,256]{3,2,1,0:T(8,128)(2,1)} %backward) | copy-start | bytes 1572868
  25.7 3.9 %collective-permute-start.6 = (f32[544,128]{1,0:T(8,128)S(1)}, f32[544,128]{1,0:T(8,128)S(1)}, u32[]{:S(2)}, u32[]{:S(2)}) collective-permute-start(f32[544,128]{1,0:T(8,128)S(1)} %collective-permute-done.4.refs_2_), channel_id=1, source_target_pairs={{0,8},{1,9},{2,10},{3,11},{4,12},{5,13},{6,14},{7,15},{8,0},{9,1},... | collective-permute-start | bytes 835592 | tf_op jit(solution)/shard_map/ppermute | solution.py:503
  29.6 1.6 %collective-permute-start.5 = (f32[544,128]{1,0:T(8,128)S(1)}, f32[544,128]{1,0:T(8,128)S(1)}, u32[]{:S(2)}, u32[]{:S(2)}) collective-permute-start(f32[544,128]{1,0:T(8,128)S(1)} %collective-permute-done.3.refs_1_), channel_id=1, source_target_pairs={{0,8},{1,9},{2,10},{3,11},{4,12},{5,13},{6,14},{7,15},{8,0},{9,1},... | collective-permute-start | bytes 835592 | tf_op jit(solution)/shard_map/ppermute | solution.py:503
  31.2 19.8 %collective-permute-start.12 = (f32[3,4,128,128]{3,2,1,0:T(8,128)S(1)}, f32[3,4,128,128]{3,2,1,0:T(8,128)S(1)}, u32[]{:S(2)}, u32[]{:S(2)}) collective-permute-start(f32[3,4,128,128]{3,2,1,0:T(8,128)S(1)} %get-tuple-element.50.refs_6_.refs_11_), channel_id=1, source_target_pairs={{16,0},{17,1},{18,2},{19,3},{20,4},{21,5},{22,6},{23,7}} | collective-permute-start | bytes 2359304 | tf_op jit(solution)/shard_map/ppermute | solution.py:503
  40.2 5.1 %collective-permute-start.8 = (f32[264,128]{1,0:T(8,128)S(1)}, f32[264,128]{1,0:T(8,128)S(1)}, u32[]{:S(2)}, u32[]{:S(2)}) collective-permute-start(f32[264,128]{1,0:T(8,128)S(1)} %get-tuple-element.46), channel_id=1, source_target_pairs={{0,7},{1,0},{2,1},{3,2},{4,3},{5,4},{6,5},{7,6},{8,15},{9,8},{10,9... | collective-permute-start | bytes 405512 | tf_op jit(solution)/shard_map/ppermute | solution.py:503
  41.9 7.7 %collective-permute-start.7 = (f32[264,128]{1,0:T(8,128)S(1)}, f32[264,128]{1,0:T(8,128)S(1)}, u32[]{:S(2)}, u32[]{:S(2)}) collective-permute-start(f32[264,128]{1,0:T(8,128)S(1)} %get-tuple-element.46), channel_id=1, source_target_pairs={{0,1},{1,2},{2,3},{3,4},{4,5},{5,6},{6,7},{7,0},{8,9},{9,10},{10,1... | collective-permute-start | bytes 405512 | tf_op jit(solution)/shard_map/ppermute | solution.py:503
  42.3 7.4 %collective-permute-start.11 = (f32[4,128,128]{2,1,0:T(8,128)S(1)}, f32[4,128,128]{2,1,0:T(8,128)S(1)}, u32[]{:S(2)}, u32[]{:S(2)}) collective-permute-start(f32[4,128,128]{2,1,0:T(8,128)S(1)} %get-tuple-element.49.refs_6_), channel_id=1, source_target_pairs={{0,8},{1,9},{2,10},{3,11},{4,12},{5,13},{6,14},{7,15},{8,0},{9,1},... | collective-permute-start | bytes 786440 | tf_op jit(solution)/shard_map/ppermute | solution.py:503
  45.3 4.4 %collective-permute-start.10 = (f32[264,128]{1,0:T(8,128)S(1)}, f32[264,128]{1,0:T(8,128)S(1)}, u32[]{:S(2)}, u32[]{:S(2)}) collective-permute-start(f32[264,128]{1,0:T(8,128)S(1)} %collective-permute-done.8.refs_1_), channel_id=1, source_target_pairs={{0,8},{1,9},{2,10},{3,11},{4,12},{5,13},{6,14},{7,15},{8,0},{9,1},... | collective-permute-start | bytes 405512 | tf_op jit(solution)/shard_map/ppermute | solution.py:503
  49.6 1.4 %collective-permute-start.9 = (f32[264,128]{1,0:T(8,128)S(1)}, f32[264,128]{1,0:T(8,128)S(1)}, u32[]{:S(2)}, u32[]{:S(2)}) collective-permute-start(f32[264,128]{1,0:T(8,128)S(1)} %collective-permute-done.7.refs_0_), channel_id=1, source_target_pairs={{0,8},{1,9},{2,10},{3,11},{4,12},{5,13},{6,14},{7,15},{8,0},{9,1},... | collective-permute-start | bytes 405512 | tf_op jit(solution)/shard_map/ppermute | solution.py:503
  54.0 8.5 %collective-permute-start.14 = (f32[192,256]{1,0:T(8,128)S(1)}, f32[192,256]{1,0:T(8,128)S(1)}, u32[]{:S(2)}, u32[]{:S(2)}) collective-permute-start(f32[192,256]{1,0:T(8,128)S(1)} %get-tuple-element.54), channel_id=1, source_target_pairs={{0,16},{1,17},{2,18},{3,19},{4,20},{5,21},{6,22},{7,23},{8,0},{9,1... | collective-permute-start | bytes 589832 | tf_op jit(solution)/shard_map/ppermute | solution.py:503
  56.4 6.1 %collective-permute-start.15 = (f32[128,256]{1,0:T(8,128)S(1)}, f32[128,256]{1,0:T(8,128)S(1)}, u32[]{:S(2)}, u32[]{:S(2)}) collective-permute-start(f32[128,256]{1,0:T(8,128)S(1)} %get-tuple-element.55), channel_id=1, source_target_pairs={{0,24},{1,25},{2,26},{3,27},{4,28},{5,29},{6,30},{7,31},{8,16},{9,... | collective-permute-start | bytes 393224 | tf_op jit(solution)/shard_map/ppermute | solution.py:503
  56.4 1.3 %collective-permute-start.13 = (f32[64,256]{1,0:T(8,128)S(1)}, f32[64,256]{1,0:T(8,128)S(1)}, u32[]{:S(2)}, u32[]{:S(2)}) collective-permute-start(f32[64,256]{1,0:T(8,128)S(1)} %get-tuple-element.53), channel_id=1, source_target_pairs={{0,8},{1,9},{2,10},{3,11},{4,12},{5,13},{6,14},{7,15},{8,0},{9,1},... | collective-permute-start | bytes 196616 | tf_op jit(solution)/shard_map/ppermute | solution.py:503

commit v10 on v9

--- a/solution.py
+++ b/solution.py
@@ -12,7 +12,7 @@
 GROUP = 6
 FIELD_ROWS = 32
 TAP_ROWS = 8
-OWN_KINDS, FIRST_KINDS = 24, 25
+OWN_KINDS, FIRST_KINDS, ACROSS_KINDS = 24, 25, 26
 LEAD = 1
 VMEM_BYTES = 16 * 2**20
 WHOLE_VMEM_BYTES = 62 * 2**20
@@ -172,8 +172,8 @@
 
 
 def launch_kernel(*refs):
-    sources, (full, lead, bundle) = refs[:9], refs[9:12]
-    scratch, copies, sems = refs[12], refs[13:22], refs[22]
+    sources, (lead, bundle) = refs[:9], refs[9:11]
+    scratch, copies, sems = refs[11], refs[12:21], refs[21]
     moves = [
         pltpu.make_async_copy(source.at[pl.ds(0, copy.shape[0])], copy, sems.at[i])
         for i, (source, copy) in enumerate(zip(sources, copies))
@@ -183,7 +183,7 @@
     incoming, stored, fields, kinds, axial, lateral, depth, diagonal, coupling = copies
     for move in moves[2:]:
         move.wait()
-    rows, cells = scratch.shape[0], full.shape[1]
+    rows = scratch.shape[0]
     orients = rows // 2
     ratios = [each[w : w + 1] / each[1:2] for each in (axial, lateral, depth) for w in (0, 2)]
     for i, ratio in enumerate(ratios + ratios[:2]):
@@ -194,8 +194,9 @@
     kernel = kernel * (axial[1:2] * lateral[1:2] * depth[1:2])
     upper = jnp.concatenate([kernel, jnp.zeros_like(kernel)], axis=1)
     bundle[TAP_ROWS : TAP_ROWS + rows] = jnp.concatenate([upper, pltpu.roll(upper, orients, 1)], axis=0).T
-    types = kinds[...].astype(jnp.float32)
-    types = jnp.concatenate([types, jnp.zeros((1, cells - types.shape[1]), jnp.float32)], axis=1)
+    line = kinds[...].astype(jnp.float32)
+    line = jnp.concatenate([line, jnp.zeros((1, rows - line.shape[1]), jnp.float32)], axis=1)
+    types = line
     planes = incoming.shape[1]
     at = TAP_ROWS + rows
     bundle[at : at + FIELD_ROWS] = jnp.zeros((FIELD_ROWS, rows), jnp.float32)
@@ -205,10 +206,9 @@
             here = at + (kind * planes + i) * 2
             bundle[here : here + 1] = line[:, :rows]
             bundle[here + 1 : here + 2] = line[:, rows:]
-    bundle[at + OWN_KINDS : at + OWN_KINDS + 1] = types[:, :rows]
+    bundle[at + OWN_KINDS : at + OWN_KINDS + 1] = types
     moves[0].wait()
     for i in range(planes):
-        full[i * orients : (i + 1) * orients] = incoming[0, i]
         here = at + FIELD_ROWS + i * rows
         bundle[here : here + rows] = to_tile(incoming[0, i], scratch)
     moves[1].wait()
@@ -216,16 +216,13 @@
         for i in range(planes):
             here = (step * planes + i) * orients
             lead[here : here + orients] = stored[step, i].astype(jnp.float32)
-    for out in (full, lead):
-        out[out.shape[0] - 8 :] = jnp.broadcast_to(types, (8, cells))
 
 
 def launch(incoming, backward, fields, kinds, axial, lateral, depth, diagonal, coupling):
     planes, orients, cells = backward.shape[1:]
     rows = 2 * orients
     operands = [incoming, backward, fields, kinds, axial, lateral, depth, diagonal.reshape(1, -1), coupling]
-    shapes = [(count * planes * orients + 8, cells) for count in (1, LEAD)]
-    shapes.append((TAP_ROWS + rows + FIELD_ROWS + planes * rows, rows))
+    shapes = [(LEAD * planes * orients, cells), (TAP_ROWS + rows + FIELD_ROWS + planes * rows, rows)]
     taken = [(LEAD,) + each.shape[1:] if i == 1 else each.shape for i, each in enumerate(operands)]
     return pl.pallas_call(
         launch_kernel,
@@ -239,17 +236,20 @@
     )(*operands)
 
 
-def turn_kernel(backward, early, late, scratch):
-    for out, begin in ((early, 0), (late, LEAD)):
-        for step in range(out.shape[0]):
-            for i in range(out.shape[1]):
-                out[step, i] = to_tile(backward[begin + step, i].astype(jnp.float32), scratch)
-
-
-def pack_kernel(bundle, moved, passed, out, taps, weights, scratch):
-    sec, odd = position()
-    rows = scratch.shape[0]
-    orients = rows // 2
+def turn_kernel(backward, lead, early, late, out, scratch):
+    orients = scratch.shape[0] // 2
+    for target, begin in ((early, 0), (late, LEAD)):
+        for step in range(target.shape[0]):
+            for i in range(target.shape[1]):
+                target[step, i] = to_tile(backward[begin + step, i].astype(jnp.float32), scratch)
+    for step in range(out.shape[0]):
+        for i in range(out.shape[1]):
+            here = (step * out.shape[1] + i) * orients
+            out[step, i] = to_tile(lead[here : here + orients], scratch)
+
+
+def unpack_kernel(bundle, out, taps, weights):
+    rows = taps.shape[1]
     taps[...] = bundle[:TAP_ROWS]
     twice = bundle[TAP_ROWS : TAP_ROWS + rows]
     coarse = twice.astype(jnp.bfloat16)
@@ -260,17 +260,26 @@
     at = out.shape[0] - FIELD_ROWS
     lines = TAP_ROWS + rows
     out[at:] = bundle[lines : lines + FIELD_ROWS]
+    out[:at] = bundle[lines + FIELD_ROWS :]
+
+
+def pack_kernel(base, moved, passed, types, out, scratch):
+    sec, odd = position()
+    rows = scratch.shape[0]
+    at = out.shape[0] - FIELD_ROWS
+    out[at:] = base[at:]
+    out[at + FIRST_KINDS : at + FIRST_KINDS + 1] = jnp.where(
+        sec == 0, base[at + OWN_KINDS : at + OWN_KINDS + 1], types[:1]
+    )
+    out[at + ACROSS_KINDS : at + ACROSS_KINDS + 1] = types[:1]
 
     @pl.when(sec == 0)
     def _():
-        out[:at] = bundle[lines + FIELD_ROWS :]
-        out[at + FIRST_KINDS : at + FIRST_KINDS + 1] = out[at + OWN_KINDS : at + OWN_KINDS + 1]
+        out[:at] = base[:at]
 
     def fill(source):
-        for i in range(at // rows):
-            out[i * rows : (i + 1) * rows] = to_tile(source[i * orients : (i + 1) * orients], scratch)
-        here = source.shape[0] - 8
-        out[at + FIRST_KINDS : at + FIRST_KINDS + 1] = source[here : here + 1, :rows]
+        for i in range(source.shape[0]):
+            out[i * rows : (i + 1) * rows] = to_tile(source[i], scratch)
 
     pl.when(odd == 1)(lambda: fill(moved))
     pl.when((sec > 0) & (odd == 0))(lambda: fill(passed))
@@ -343,7 +352,7 @@
                 factor[kind, start + i] = jnp.take_along_axis(columns, right + at, axis=1, mode="promise_in_bounds")
 
 
-def early_kernel(taps, weights, lead, *refs):
+def early_kernel(taps, weights, *refs):
     pieces, stored, (middle, half_out, kept, total, factor) = refs[:5], refs[5:7], refs[7:12]
     slab, other, first, second, scratch = refs[12:]
     sec, odd = position()
@@ -357,12 +366,14 @@
             slab[start + i] = piece[i * rows : (i + 1) * rows]
     at = planes * rows
     steps = LEAD + stored[1].shape[0]
-    own_kinds, first_kinds = (pieces[0][at + row : at + row + 1] for row in (OWN_KINDS, FIRST_KINDS))
-    beside_kinds = pieces[3][at + OWN_KINDS : at + OWN_KINDS + 1]
-    kinds = scalars_of(first_kinds, steps)
+    own_kinds, first_kinds, across_kinds = (
+        pieces[0][at + row : at + row + 1] for row in (OWN_KINDS, FIRST_KINDS, ACROSS_KINDS)
+    )
+    beside_kinds, beside_first = (pieces[3][at + row : at + row + 1] for row in (OWN_KINDS, FIRST_KINDS))
+    kinds = scalars_of(jnp.where((sec == 1) | (sec == 2), beside_first, first_kinds), steps)
     kinds += scalars_of(jnp.where((sec == 1) | (sec == 2), own_kinds, beside_kinds), steps)
-    lead_kinds = lead[lead.shape[0] - 8 : lead.shape[0], :rows]
-    half_out[pair * rows :] = jnp.where(sec == 0, lead_kinds, jnp.broadcast_to(own_kinds, lead_kinds.shape))
+    last_kinds = jnp.where(sec == 0, across_kinds, own_kinds)
+    half_out[pair * rows :] = jnp.broadcast_to(last_kinds, (8, rows))
     width = 2 * planes * factor.shape[0]
     lines = [piece[at : at + width] for piece in pieces]
     lines.append(jnp.zeros((rows - width * len(pieces), rows), jnp.float32))
@@ -411,20 +422,13 @@
 
     saved[...] = kept[...]
 
-    def lead_plane(i):
-        return series[0][i * rows // 2 : (i + 1) * rows // 2]
-
     def after(step, state):
-        @pl.when(sec == 0)
-        def _():
-            for i in range(planes):
-                part = series[1][step - LEAD, i] if step >= LEAD else to_tile(lead_plane(step * planes + i), scratch)
-                total[i] += state[reach + i] * part
-
-        @pl.when(sec == last)
-        def _():
-            part = stored[0][step] if step < LEAD else stored[1][step - LEAD]
-            total[...] += state[reach : reach + planes] * part
+        for where, source in ((sec == 0, series), (sec == last, stored)):
+
+            @pl.when(where)
+            def _(source=source):
+                part = source[0][step] if step < LEAD else source[1][step - LEAD]
+                total[...] += state[reach : reach + planes] * part
 
     run_steps(kinds, taps, weights, reach, slab, other, first, second, factor, begun - reach, after)
     state = (slab, other)[reach % 2]
@@ -503,12 +507,19 @@
         return lax.ppermute(array, ("sec", "gx"), pairs)
 
     same, beside = (0, 1, 2, 3), (1, 0, 3, 2)
-    full, lead, bundle = launch(
+    moved = send(incoming[0], {0: 1, 1: 3})
+    lead, bundle = launch(
         incoming, backward, fields, block_types, axial_taps, lateral_taps, depth_taps, bend_diagonal, bend_coupling
     )
-    moved = send(full, {0: 1, 1: 3})
+    types = jnp.pad(block_types.astype(jnp.float32), ((0, 7), (0, lanes - steps)))
+    types = send(types, {1: 3, 2: 0})
+    lead = send(lead, {2: 0})
+    size = planes * rows + FIELD_ROWS
+    base, taps, weights = call(
+        unpack_kernel, [(size, lanes), (TAP_ROWS, lanes), (2 * rows, 2 * lanes)], [], [bundle], {2: jnp.bfloat16}
+    )
+    moved, base, types = lax.optimization_barrier((moved, base, types))
     passed = send(moved, {3: 2})
-    passed, lead = lax.optimization_barrier((passed, send(lead, {2: 0})))
 
     tile = pltpu.VMEM((rows, lanes), jnp.float32)
     packed = pltpu.VMEM((GROUP * rows, 2 * lanes), jnp.bfloat16)
@@ -518,16 +529,15 @@
         slab = pltpu.VMEM((planes + 2 * extent, rows, lanes), jnp.float32)
         return [slab, slab, packed, packed, tile]
 
-    piece, taps, weights = call(
-        pack_kernel,
-        [(planes * rows + FIELD_ROWS, lanes), (TAP_ROWS, lanes), (2 * rows, 2 * lanes)],
-        [tile],
-        [bundle, moved, passed],
-        {2: jnp.bfloat16},
-    )
+    (piece,) = call(pack_kernel, [(size, lanes)], [tile], [base, moved, passed, types])
     own = [send(piece, same, shift, 2 * shift) for shift in near]
     backward, _ = lax.optimization_barrier((backward, piece))
-    stored = call(turn_kernel, [(count, planes, rows, lanes) for count in (LEAD, steps - LEAD)], [tile], [backward])
+    *stored, lead = call(
+        turn_kernel,
+        [(count, planes, rows, lanes) for count in (LEAD, steps - LEAD, LEAD)],
+        [tile],
+        [backward, lead],
+    )
     own[-1], *stored = lax.optimization_barrier((own[-1], *stored))
     swapped = [send(each, beside) for each in own]
     late_stored, *swapped = lax.optimization_barrier((stored[1], *swapped))
@@ -537,7 +547,7 @@
         [(planes, rows, lanes), (pair * rows + 8, lanes), (planes, rows, lanes), (planes, rows, lanes)]
         + [(fields.shape[0], planes + 2 * reach[0], rows, lanes)],
         work(reach[0]),
-        [taps, weights, lead, piece, *own, *swapped, *stored],
+        [taps, weights, piece, *own, *swapped, *stored],
     )
     own = [send(piece, same, shift, shift) for shift in near]
     beside_total = send(total, beside)

time: 63.5 us -> 60.3 us (0.950)
  waiting for transfers between devices: 30.4 us -> 21.4 us
  starting transfers between devices: 15.9 us -> 21.1 us
  other arithmetic: 0 us -> 0.66 us
    ppermute x16 -> x17, waiting for transfers between devices: 30.4 us -> 21.4 us  [send(): return lax.ppermute(array, ('sec', 'gx'), pairs)]
    ppermute x16 -> x17, starting transfers between devices: 15.9 us -> 21.1 us  [send(): return lax.ppermute(array, ('sec', 'gx'), pairs)]
    convert_element_type x0 -> x1, other arithmetic: none -> 0.66 us  [paired(): block_types.astype(jnp.float32)]
    pallas_call x5 -> x6, Pallas kernels: 11.9 us -> 11.9 us  [call(): pl.pallas_call(kernel, in_specs=[IN_VMEM] * len(operands), out_specs=[IN_...]
  transfers between devices with their start and end apart: 16 -> 17, of which waited for: 9 -> 9; matrix products, arithmetic and copies ran while one was open for 0% -> 1% of each run, Pallas kernels for 13% -> 17%
where the time goes in v10:
time: 60.3 us; the launch traced here: 60 us
  waiting for transfers between devices  21.4 us (35%)
  starting transfers between devices  21.1 us (35%)
  Pallas kernels  14.1 us (23%)
  local copies, waits for them, and re-layouts  2.02 us (3%)
  between operations  0.77 us (1%)
  other arithmetic  0.66 us (1%)
    ppermute x17, waiting for transfers between devices, send(): return lax.ppermute(array, ('sec', 'gx'), pairs)  21.4 us
    ppermute x17, starting transfers between devices, send(): return lax.ppermute(array, ('sec', 'gx'), pairs)  21.1 us
    pallas_call x6, Pallas kernels, call(): pl.pallas_call(kernel, in_specs=[IN_VMEM] * len(operands), out_specs=[IN_...  11.9 us
    pallas_call x1, Pallas kernels, launch(): pl.pallas_call(launch_kernel, in_specs=[pl.BlockSpec(memory_space=pltpu.H...  2.23 us
    unnamed x4, local copies, waits for them, and re-layouts  2.01 us
  transfers between devices with their start and end apart: 17, of which 9 were waited for; matrix products, arithmetic and copies ran while one was open for 1% of the time, Pallas kernels for 17%

profile of v10, /device:TPU:0, one launch (start us, length us, event | category | flops | bytes accessed | tf_op | source)
XLA Modules:
  0.0 60.0 jit_solution(14062860937557379226)
XLA Ops:
  0.6 2.4 %collective-permute-start = (f32[4,64,256]{2,1,0:T(8,128)}, f32[4,64,256]{2,1,0:T(8,128)S(1)}, u32[]{:S(2)}, u32[]{:S(2)}) collective-permute-start(f32[4,64,256]{2,1,0:T(8,128)} %bitcast.2), channel_id=1, source_target_pairs={{0,8},{1,9},{2,10},{3,11},{4,12},{5,13},{6,14},{7,15},{8,24},{9,25... | collective-permute-start | bytes 786440 | tf_op jit(solution)/shard_map/ppermute | solution.py:507
  3.0 0.7 %convert_element_type.5 = f32[1,4]{1,0:T(1,128)S(1)} convert(s32[1,4]{1,0:T(1,128)} %refs_3_.1) | non-fusion elementwise | flops 4 | bytes 32 | tf_op jit(solution)/shard_map/convert_element_type | solution.py:514
  3.7 1.3 %collective-permute-start.1 = (f32[8,128]{1,0:T(8,128)S(1)}, f32[8,128]{1,0:T(8,128)S(1)}, u32[]{:S(2)}, u32[]{:S(2)}) collective-permute-start(f32[8,128]{1,0:T(8,128)S(1)} %pad.4), channel_id=1, source_target_pairs={{8,24},{9,25},{10,26},{11,27},{12,28},{13,29},{14,30},{15,31},{16,... | collective-permute-start | bytes 12296 | tf_op jit(solution)/shard_map/ppermute | solution.py:507
  5.0 2.2 %shard_map.104 = (f32[256,256]{1,0:T(8,128)}, f32[680,128]{1,0:T(8,128)}) custom-call(f32[1,4,64,256]{3,2,1,0:T(8,128)} %refs_0_.1, bf16[4,4,64,256]{3,2,1,0:T(8,128)(2,1)} %backward, f32[3,4,256]{2,1,0:T(4,128)} %refs_2_.1, s32[1,4]{1,0:T(1,128)} %refs_3_.1, f32[3,64]{1,0:T(4,128)} %refs_4_.1, f32[3,64]{1,0:T(4,128)} %refs_5_.1, f32[3,64]{1,0:T(4,128)} %refs_6_.1, ...), custom_call_target="tpu_custom_call" | custom-call | tf_op jit(solution)/shard_map/pallas_call | solution.py:227
  7.2 0.0 copy-start.1
  7.2 1.0 %copy-done.1 = f32[680,128]{1,0:T(8,128)S(1)} copy-done((f32[680,128]{1,0:T(8,128)S(1)}, f32[680,128]{1,0:T(8,128)}, u32[]{:S(2)}) %copy-start.1) | copy-done | bytes 348184
  8.2 0.9 %collective-permute-done.1.types = f32[8,128]{1,0:T(8,128)S(1)} collective-permute-done((f32[8,128]{1,0:T(8,128)S(1)}, f32[8,128]{1,0:T(8,128)S(1)}, u32[]{:S(2)}, u32[]{:S(2)}) %collective-permute-start.1) | collective-permute-done | bytes 4128 | tf_op jit(solution)/shard_map/ppermute | solution.py:507
  9.2 0.0 collective-permute-done.moved
  9.2 0.7 %collective-permute-start.2 = (f32[4,64,256]{2,1,0:T(8,128)S(1)}, f32[4,64,256]{2,1,0:T(8,128)S(1)}, u32[]{:S(2)}, u32[]{:S(2)}) collective-permute-start(f32[4,64,256]{2,1,0:T(8,128)S(1)} %collective-permute-done.moved), channel_id=1, source_target_pairs={{24,16},{25,17},{26,18},{27,19},{28,20},{29,21},{30,22},{31,23}} | collective-permute-start | bytes 786440 | tf_op jit(solution)/shard_map/ppermute | solution.py:507
  9.8 0.0 collective-permute-done.2.passed
  9.9 5.4 %collective-permute-start.4 = (f32[544,128]{1,0:T(8,128)S(1)}, f32[544,128]{1,0:T(8,128)S(1)}, u32[]{:S(2)}, u32[]{:S(2)}) collective-permute-start(f32[544,128]{1,0:T(8,128)S(1)} %shard_map.106.refs_0_), channel_id=1, source_target_pairs={{0,7},{1,0},{2,1},{3,2},{4,3},{5,4},{6,5},{7,6},{8,14},{9,15},{10,... | collective-permute-start | bytes 835592 | tf_op jit(solution)/shard_map/ppermute | solution.py:507
  15.3 0.0 collective-permute-start.3
  15.3 1.3 %collective-permute-start.5 = (f32[256,256]{1,0:T(8,128)}, f32[256,256]{1,0:T(8,128)S(1)}, u32[]{:S(2)}, u32[]{:S(2)}) collective-permute-start(f32[256,256]{1,0:T(8,128)} %get-tuple-element.38), channel_id=1, source_target_pairs={{16,0},{17,1},{18,2},{19,3},{20,4},{21,5},{22,6},{23,7}} | collective-permute-start | bytes 786440 | tf_op jit(solution)/shard_map/ppermute | solution.py:507
  16.6 9.1 %collective-permute-done.5.lead = f32[256,256]{1,0:T(8,128)S(1)} collective-permute-done((f32[256,256]{1,0:T(8,128)}, f32[256,256]{1,0:T(8,128)S(1)}, u32[]{:S(2)}, u32[]{:S(2)}) %collective-permute-start.5) | collective-permute-done | bytes 262176 | tf_op jit(solution)/shard_map/ppermute | solution.py:507
  25.7 0.0 copy-start
  25.7 1.0 %copy-done = bf16[4,4,64,256]{3,2,1,0:T(8,128)(2,1)S(1)} copy-done((bf16[4,4,64,256]{3,2,1,0:T(8,128)(2,1)S(1)}, bf16[4,4,64,256]{3,2,1,0:T(8,128)(2,1)}, u32[]{:S(2)}) %copy-start) | copy-done | bytes 524312
  26.8 0.4 shard_map.107
  27.2 0.0 collective-permute-done.4.refs_2_
  27.2 0.1 collective-permute-start.7
  27.3 0.0 collective-permute-done.3.refs_1_
  27.3 0.5 collective-permute-start.6
  27.8 1.0 %collective-permute-done.7.refs_4_ = f32[544,128]{1,0:T(8,128)S(1)} collective-permute-done((f32[544,128]{1,0:T(8,128)S(1)}, f32[544,128]{1,0:T(8,128)S(1)}, u32[]{:S(2)}, u32[]{:S(2)}) %collective-permute-start.7) | collective-permute-done | bytes 278560 | tf_op jit(solution)/shard_map/ppermute | solution.py:507
  28.8 0.4 collective-permute-done.6.refs_3_
  29.2 1.3 %collective-permute-start.13 = (f32[3,4,128,128]{3,2,1,0:T(8,128)S(1)}, f32[3,4,128,128]{3,2,1,0:T(8,128)S(1)}, u32[]{:S(2)}, u32[]{:S(2)}) collective-permute-start(f32[3,4,128,128]{3,2,1,0:T(8,128)S(1)} %get-tuple-element.52.refs_6_.refs_11_), channel_id=1, source_target_pairs={{16,0},{17,1},{18,2},{19,3},{20,4},{21,5},{22,6},{23,7}} | collective-permute-start | bytes 2359304 | tf_op jit(solution)/shard_map/ppermute | solution.py:507
  30.5 7.7 %shard_map.108 = (f32[4,128,128]{2,1,0:T(8,128)S(1)}, f32[264,128]{1,0:T(8,128)S(1)}, f32[4,128,128]{2,1,0:T(8,128)S(1)}, f32[4,128,128]{2,1,0:T(8,128)S(1)}, f32[3,20,128,128]{3,2,1,0:T(8,128)S(1)}) custom-call(f32[8,128]{1,0:T(8,128)S(1)} %get-tuple-element.31.taps, bf16[256,256]{1,0:T(8,128)(2,1)S(1)} %get-tuple-element.32.weights, ...), custom_call_target="tpu_custom_call" | custom-call | tf_op jit(solution)/shard_map/pallas_call | solution.py:482
  38.2 0.1 collective-permute-start.8
  38.3 4.8 %collective-permute-start.9 = (f32[264,128]{1,0:T(8,128)S(1)}, f32[264,128]{1,0:T(8,128)S(1)}, u32[]{:S(2)}, u32[]{:S(2)}) collective-permute-start(f32[264,128]{1,0:T(8,128)S(1)} %get-tuple-element.47), channel_id=1, source_target_pairs={{0,7},{1,0},{2,1},{3,2},{4,3},{5,4},{6,5},{7,6},{8,15},{9,8},{10,9... | collective-permute-start | bytes 405512 | tf_op jit(solution)/shard_map/ppermute | solution.py:507
  43.1 0.0 collective-permute-start.12
  43.1 3.2 %collective-permute-done.8.refs_0_ = f32[264,128]{1,0:T(8,128)S(1)} collective-permute-done((f32[264,128]{1,0:T(8,128)S(1)}, f32[264,128]{1,0:T(8,128)S(1)}, u32[]{:S(2)}, u32[]{:S(2)}) %collective-permute-start.8) | collective-permute-done | bytes 135200 | tf_op jit(solution)/shard_map/ppermute | solution.py:507
  46.3 0.0 collective-permute-start.10
  46.3 0.0 collective-permute-done.9.refs_1_
  46.3 0.5 collective-permute-start.11
  46.8 0.0 collective-permute-done.12.refs_7_
  46.8 0.8 %collective-permute-done.10.refs_2_ = f32[264,128]{1,0:T(8,128)S(1)} collective-permute-done((f32[264,128]{1,0:T(8,128)S(1)}, f32[264,128]{1,0:T(8,128)S(1)}, u32[]{:S(2)}, u32[]{:S(2)}) %collective-permute-start.10) | collective-permute-done | bytes 135200 | tf_op jit(solution)/shard_map/ppermute | solution.py:507
  47.6 0.2 collective-permute-done.11.refs_3_
  47.8 0.0 collective-permute-done.13.refs_9_
  47.8 2.9 %shard_map.109 = (f32[4,64,256]{2,1,0:T(8,128)S(1)}, f32[64,256]{1,0:T(8,128)S(1)}, f32[64,256]{1,0:T(8,128)S(1)}, f32[192,256]{1,0:T(8,128)S(1)}, f32[128,256]{1,0:T(8,128)S(1)}) custom-call(f32[8,128]{1,0:T(8,128)S(1)} %get-tuple-element.31.taps, bf16[256,256]{1,0:T(8,128)(2,1)S(1)} %get-tuple-element.32.weights, ...), custom_call_target="tpu_custom_call" | custom-call | tf_op jit(solution)/shard_map/pallas_call | solution.py:482
  50.8 2.2 %collective-permute-start.15 = (f32[192,256]{1,0:T(8,128)S(1)}, f32[192,256]{1,0:T(8,128)S(1)}, u32[]{:S(2)}, u32[]{:S(2)}) collective-permute-start(f32[192,256]{1,0:T(8,128)S(1)} %get-tuple-element.56), channel_id=1, source_target_pairs={{0,16},{1,17},{2,18},{3,19},{4,20},{5,21},{6,22},{7,23},{8,0},{9,1... | collective-permute-start | bytes 589832 | tf_op jit(solution)/shard_map/ppermute | solution.py:507
  53.0 0.2 collective-permute-start.16
  53.2 0.4 collective-permute-start.14
  53.6 0.9 %collective-permute-done.14.to_pair = f32[64,256]{1,0:T(8,128)S(1)} collective-permute-done((f32[64,256]{1,0:T(8,128)S(1)}, f32[64,256]{1,0:T(8,128)S(1)}, u32[]{:S(2)}, u32[]{:S(2)}) %collective-permute-start.14) | collective-permute-done | bytes 65568 | tf_op jit(solution)/shard_map/ppermute | solution.py:507
  54.5 4.7 %collective-permute-done.16.to_corner = f32[128,256]{1,0:T(8,128)S(1)} collective-permute-done((f32[128,256]{1,0:T(8,128)S(1)}, f32[128,256]{1,0:T(8,128)S(1)}, u32[]{:S(2)}, u32[]{:S(2)}) %collective-permute-start.16) | collective-permute-done | bytes 131104 | tf_op jit(solution)/shard_map/ppermute | solution.py:507
  59.3 0.0 collective-permute-done.15.to_across
  59.3 0.8 %shard_map.110 = (f32[1,4,64,256]{3,2,1,0:T(8,128)}, f32[4,16,256]{2,1,0:T(8,128)}) custom-call(f32[4,64,256]{2,1,0:T(8,128)S(1)} %get-tuple-element.53.handoff_in, f32[64,256]{1,0:T(8,128)S(1)} %get-tuple-element.54.share, f32[64,256]{1,0:T(8,128)S(1)} %collective-permute-done.14.to_pair, f32[192,256]{1,0:T(8,128)S(1)} %collective-permute-done.15.to_across, ...), custom_call_target="tpu_custom_call" | custom-call | tf_op jit(solution)/shard_map/pallas_call | solution.py:482
  (3 shorter events, 0.1 us)
Async XLA Ops:
  0.6 8.5 %collective-permute-start = (f32[4,64,256]{2,1,0:T(8,128)}, f32[4,64,256]{2,1,0:T(8,128)S(1)}, u32[]{:S(2)}, u32[]{:S(2)}) collective-permute-start(f32[4,64,256]{2,1,0:T(8,128)} %bitcast.2), channel_id=1, source_target_pairs={{0,8},{1,9},{2,10},{3,11},{4,12},{5,13},{6,14},{7,15},{8,24},{9,25... | collective-permute-start | bytes 786440 | tf_op jit(solution)/shard_map/ppermute | solution.py:507
  3.7 5.5 %collective-permute-start.1 = (f32[8,128]{1,0:T(8,128)S(1)}, f32[8,128]{1,0:T(8,128)S(1)}, u32[]{:S(2)}, u32[]{:S(2)}) collective-permute-start(f32[8,128]{1,0:T(8,128)S(1)} %pad.4), channel_id=1, source_target_pairs={{8,24},{9,25},{10,26},{11,27},{12,28},{13,29},{14,30},{15,31},{16,... | collective-permute-start | bytes 12296 | tf_op jit(solution)/shard_map/ppermute | solution.py:507
  7.2 1.0 %copy-start.1 = (f32[680,128]{1,0:T(8,128)S(1)}, f32[680,128]{1,0:T(8,128)}, u32[]{:S(2)}) copy-start(f32[680,128]{1,0:T(8,128)} %get-tuple-element.30.bundle) | copy-start | bytes 1044484
  9.2 0.7 %collective-permute-start.2 = (f32[4,64,256]{2,1,0:T(8,128)S(1)}, f32[4,64,256]{2,1,0:T(8,128)S(1)}, u32[]{:S(2)}, u32[]{:S(2)}) collective-permute-start(f32[4,64,256]{2,1,0:T(8,128)S(1)} %collective-permute-done.moved), channel_id=1, source_target_pairs={{24,16},{25,17},{26,18},{27,19},{28,20},{29,21},{30,22},{31,23}} | collective-permute-start | bytes 786440 | tf_op jit(solution)/shard_map/ppermute | solution.py:507
  9.9 17.3 %collective-permute-start.4 = (f32[544,128]{1,0:T(8,128)S(1)}, f32[544,128]{1,0:T(8,128)S(1)}, u32[]{:S(2)}, u32[]{:S(2)}) collective-permute-start(f32[544,128]{1,0:T(8,128)S(1)} %shard_map.106.refs_0_), channel_id=1, source_target_pairs={{0,7},{1,0},{2,1},{3,2},{4,3},{5,4},{6,5},{7,6},{8,14},{9,15},{10,... | collective-permute-start | bytes 835592 | tf_op jit(solution)/shard_map/ppermute | solution.py:507
  15.3 12.0 %collective-permute-start.3 = (f32[544,128]{1,0:T(8,128)S(1)}, f32[544,128]{1,0:T(8,128)S(1)}, u32[]{:S(2)}, u32[]{:S(2)}) collective-permute-start(f32[544,128]{1,0:T(8,128)S(1)} %shard_map.106.refs_0_), channel_id=1, source_target_pairs={{0,1},{1,2},{2,3},{3,4},{4,5},{5,6},{6,7},{7,0},{8,10},{9,11},{10,... | collective-permute-start | bytes 835592 | tf_op jit(solution)/shard_map/ppermute | solution.py:507
  15.3 10.4 %collective-permute-start.5 = (f32[256,256]{1,0:T(8,128)}, f32[256,256]{1,0:T(8,128)S(1)}, u32[]{:S(2)}, u32[]{:S(2)}) collective-permute-start(f32[256,256]{1,0:T(8,128)} %get-tuple-element.38), channel_id=1, source_target_pairs={{16,0},{17,1},{18,2},{19,3},{20,4},{21,5},{22,6},{23,7}} | collective-permute-start | bytes 786440 | tf_op jit(solution)/shard_map/ppermute | solution.py:507
  25.7 1.0 %copy-start = (bf16[4,4,64,256]{3,2,1,0:T(8,128)(2,1)S(1)}, bf16[4,4,64,256]{3,2,1,0:T(8,128)(2,1)}, u32[]{:S(2)}) copy-start(bf16[4,4,64,256]{3,2,1,0:T(8,128)(2,1)} %backward) | copy-start | bytes 1572868
  27.2 1.6 %collective-permute-start.7 = (f32[544,128]{1,0:T(8,128)S(1)}, f32[544,128]{1,0:T(8,128)S(1)}, u32[]{:S(2)}, u32[]{:S(2)}) collective-permute-start(f32[544,128]{1,0:T(8,128)S(1)} %collective-permute-done.4.refs_2_), channel_id=1, source_target_pairs={{0,8},{1,9},{2,10},{3,11},{4,12},{5,13},{6,14},{7,15},{8,0},{9,1},... | collective-permute-start | bytes 835592 | tf_op jit(solution)/shard_map/ppermute | solution.py:507
  27.3 1.9 %collective-permute-start.6 = (f32[544,128]{1,0:T(8,128)S(1)}, f32[544,128]{1,0:T(8,128)S(1)}, u32[]{:S(2)}, u32[]{:S(2)}) collective-permute-start(f32[544,128]{1,0:T(8,128)S(1)} %collective-permute-done.3.refs_1_), channel_id=1, source_target_pairs={{0,8},{1,9},{2,10},{3,11},{4,12},{5,13},{6,14},{7,15},{8,0},{9,1},... | collective-permute-start | bytes 835592 | tf_op jit(solution)/shard_map/ppermute | solution.py:507
  29.2 18.6 %collective-permute-start.13 = (f32[3,4,128,128]{3,2,1,0:T(8,128)S(1)}, f32[3,4,128,128]{3,2,1,0:T(8,128)S(1)}, u32[]{:S(2)}, u32[]{:S(2)}) collective-permute-start(f32[3,4,128,128]{3,2,1,0:T(8,128)S(1)} %get-tuple-element.52.refs_6_.refs_11_), channel_id=1, source_target_pairs={{16,0},{17,1},{18,2},{19,3},{20,4},{21,5},{22,6},{23,7}} | collective-permute-start | bytes 2359304 | tf_op jit(solution)/shard_map/ppermute | solution.py:507
  38.2 8.1 %collective-permute-start.8 = (f32[264,128]{1,0:T(8,128)S(1)}, f32[264,128]{1,0:T(8,128)S(1)}, u32[]{:S(2)}, u32[]{:S(2)}) collective-permute-start(f32[264,128]{1,0:T(8,128)S(1)} %get-tuple-element.47), channel_id=1, source_target_pairs={{0,1},{1,2},{2,3},{3,4},{4,5},{5,6},{6,7},{7,0},{8,9},{9,10},{10,1... | collective-permute-start | bytes 405512 | tf_op jit(solution)/shard_map/ppermute | solution.py:507
  38.3 8.0 %collective-permute-start.9 = (f32[264,128]{1,0:T(8,128)S(1)}, f32[264,128]{1,0:T(8,128)S(1)}, u32[]{:S(2)}, u32[]{:S(2)}) collective-permute-start(f32[264,128]{1,0:T(8,128)S(1)} %get-tuple-element.47), channel_id=1, source_target_pairs={{0,7},{1,0},{2,1},{3,2},{4,3},{5,4},{6,5},{7,6},{8,15},{9,8},{10,9... | collective-permute-start | bytes 405512 | tf_op jit(solution)/shard_map/ppermute | solution.py:507
  43.1 3.7 %collective-permute-start.12 = (f32[4,128,128]{2,1,0:T(8,128)S(1)}, f32[4,128,128]{2,1,0:T(8,128)S(1)}, u32[]{:S(2)}, u32[]{:S(2)}) collective-permute-start(f32[4,128,128]{2,1,0:T(8,128)S(1)} %get-tuple-element.50.refs_6_), channel_id=1, source_target_pairs={{0,8},{1,9},{2,10},{3,11},{4,12},{5,13},{6,14},{7,15},{8,0},{9,1},... | collective-permute-start | bytes 786440 | tf_op jit(solution)/shard_map/ppermute | solution.py:507
  46.3 1.4 %collective-permute-start.10 = (f32[264,128]{1,0:T(8,128)S(1)}, f32[264,128]{1,0:T(8,128)S(1)}, u32[]{:S(2)}, u32[]{:S(2)}) collective-permute-start(f32[264,128]{1,0:T(8,128)S(1)} %collective-permute-done.8.refs_0_), channel_id=1, source_target_pairs={{0,8},{1,9},{2,10},{3,11},{4,12},{5,13},{6,14},{7,15},{8,0},{9,1},... | collective-permute-start | bytes 405512 | tf_op jit(solution)/shard_map/ppermute | solution.py:507
  46.3 1.5 %collective-permute-start.11 = (f32[264,128]{1,0:T(8,128)S(1)}, f32[264,128]{1,0:T(8,128)S(1)}, u32[]{:S(2)}, u32[]{:S(2)}) collective-permute-start(f32[264,128]{1,0:T(8,128)S(1)} %collective-permute-done.9.refs_1_), channel_id=1, source_target_pairs={{0,8},{1,9},{2,10},{3,11},{4,12},{5,13},{6,14},{7,15},{8,0},{9,1},... | collective-permute-start | bytes 405512 | tf_op jit(solution)/shard_map/ppermute | solution.py:507
  50.8 8.5 %collective-permute-start.15 = (f32[192,256]{1,0:T(8,128)S(1)}, f32[192,256]{1,0:T(8,128)S(1)}, u32[]{:S(2)}, u32[]{:S(2)}) collective-permute-start(f32[192,256]{1,0:T(8,128)S(1)} %get-tuple-element.56), channel_id=1, source_target_pairs={{0,16},{1,17},{2,18},{3,19},{4,20},{5,21},{6,22},{7,23},{8,0},{9,1... | collective-permute-start | bytes 589832 | tf_op jit(solution)/shard_map/ppermute | solution.py:507
  53.0 6.3 %collective-permute-start.16 = (f32[128,256]{1,0:T(8,128)S(1)}, f32[128,256]{1,0:T(8,128)S(1)}, u32[]{:S(2)}, u32[]{:S(2)}) collective-permute-start(f32[128,256]{1,0:T(8,128)S(1)} %get-tuple-element.57), channel_id=1, source_target_pairs={{0,24},{1,25},{2,26},{3,27},{4,28},{5,29},{6,30},{7,31},{8,16},{9,... | collective-permute-start | bytes 393224 | tf_op jit(solution)/shard_map/ppermute | solution.py:507
  53.2 1.3 %collective-permute-start.14 = (f32[64,256]{1,0:T(8,128)S(1)}, f32[64,256]{1,0:T(8,128)S(1)}, u32[]{:S(2)}, u32[]{:S(2)}) collective-permute-start(f32[64,256]{1,0:T(8,128)S(1)} %get-tuple-element.55), channel_id=1, source_target_pairs={{0,8},{1,9},{2,10},{3,11},{4,12},{5,13},{6,14},{7,15},{8,0},{9,1},... | collective-permute-start | bytes 196616 | tf_op jit(solution)/shard_map/ppermute | solution.py:507

commit v11 on v10

--- a/solution.py
+++ b/solution.py
@@ -12,8 +12,7 @@
 GROUP = 6
 FIELD_ROWS = 32
 TAP_ROWS = 8
-OWN_KINDS, FIRST_KINDS, ACROSS_KINDS = 24, 25, 26
-LEAD = 1
+OWN_KINDS, FIRST_KINDS = 24, 25
 VMEM_BYTES = 16 * 2**20
 WHOLE_VMEM_BYTES = 62 * 2**20
 IN_VMEM = pl.BlockSpec(memory_space=pltpu.VMEM)
@@ -172,16 +171,12 @@
 
 
 def launch_kernel(*refs):
-    sources, (lead, bundle) = refs[:9], refs[9:11]
-    scratch, copies, sems = refs[11], refs[12:21], refs[21]
-    moves = [
-        pltpu.make_async_copy(source.at[pl.ds(0, copy.shape[0])], copy, sems.at[i])
-        for i, (source, copy) in enumerate(zip(sources, copies))
-    ]
+    sources, bundle, scratch, copies, sems = refs[:8], refs[8], refs[9], refs[10:18], refs[18]
+    moves = [pltpu.make_async_copy(s, c, sems.at[i]) for i, (s, c) in enumerate(zip(sources, copies))]
     for move in moves:
         move.start()
-    incoming, stored, fields, kinds, axial, lateral, depth, diagonal, coupling = copies
-    for move in moves[2:]:
+    incoming, fields, kinds, axial, lateral, depth, diagonal, coupling = copies
+    for move in moves[1:]:
         move.wait()
     rows = scratch.shape[0]
     orients = rows // 2
@@ -211,41 +206,28 @@
     for i in range(planes):
         here = at + FIELD_ROWS + i * rows
         bundle[here : here + rows] = to_tile(incoming[0, i], scratch)
-    moves[1].wait()
-    for step in range(LEAD):
-        for i in range(planes):
-            here = (step * planes + i) * orients
-            lead[here : here + orients] = stored[step, i].astype(jnp.float32)
-
-
-def launch(incoming, backward, fields, kinds, axial, lateral, depth, diagonal, coupling):
-    planes, orients, cells = backward.shape[1:]
+
+
+def launch(incoming, fields, kinds, axial, lateral, depth, diagonal, coupling):
+    planes, orients, cells = incoming.shape[1:]
     rows = 2 * orients
-    operands = [incoming, backward, fields, kinds, axial, lateral, depth, diagonal.reshape(1, -1), coupling]
-    shapes = [(LEAD * planes * orients, cells), (TAP_ROWS + rows + FIELD_ROWS + planes * rows, rows)]
-    taken = [(LEAD,) + each.shape[1:] if i == 1 else each.shape for i, each in enumerate(operands)]
+    operands = [incoming, fields, kinds, axial, lateral, depth, diagonal.reshape(1, -1), coupling]
     return pl.pallas_call(
         launch_kernel,
         in_specs=[pl.BlockSpec(memory_space=pltpu.HBM)] * len(operands),
-        out_specs=[IN_VMEM] * len(shapes),
-        out_shape=[jax.ShapeDtypeStruct(shape, jnp.float32) for shape in shapes],
+        out_specs=IN_VMEM,
+        out_shape=jax.ShapeDtypeStruct((TAP_ROWS + rows + FIELD_ROWS + planes * rows, rows), jnp.float32),
         scratch_shapes=[pltpu.VMEM((rows, rows), jnp.float32)]
-        + [pltpu.VMEM(shape, each.dtype) for shape, each in zip(taken, operands)]
+        + [pltpu.VMEM(each.shape, each.dtype) for each in operands]
         + [pltpu.SemaphoreType.DMA((len(operands),))],
         compiler_params=pltpu.CompilerParams(vmem_limit_bytes=WHOLE_VMEM_BYTES),
     )(*operands)
 
 
-def turn_kernel(backward, lead, early, late, out, scratch):
-    orients = scratch.shape[0] // 2
-    for target, begin in ((early, 0), (late, LEAD)):
-        for step in range(target.shape[0]):
-            for i in range(target.shape[1]):
-                target[step, i] = to_tile(backward[begin + step, i].astype(jnp.float32), scratch)
+def turn_kernel(backward, out, scratch):
     for step in range(out.shape[0]):
         for i in range(out.shape[1]):
-            here = (step * out.shape[1] + i) * orients
-            out[step, i] = to_tile(lead[here : here + orients], scratch)
+            out[step, i] = to_tile(backward[step, i].astype(jnp.float32), scratch)
 
 
 def unpack_kernel(bundle, out, taps, weights):
@@ -271,7 +253,6 @@
     out[at + FIRST_KINDS : at + FIRST_KINDS + 1] = jnp.where(
         sec == 0, base[at + OWN_KINDS : at + OWN_KINDS + 1], types[:1]
     )
-    out[at + ACROSS_KINDS : at + ACROSS_KINDS + 1] = types[:1]
 
     @pl.when(sec == 0)
     def _():
@@ -352,9 +333,9 @@
                 factor[kind, start + i] = jnp.take_along_axis(columns, right + at, axis=1, mode="promise_in_bounds")
 
 
-def early_kernel(taps, weights, *refs):
-    pieces, stored, (middle, half_out, kept, total, factor) = refs[:5], refs[5:7], refs[7:12]
-    slab, other, first, second, scratch = refs[12:]
+def early_kernel(taps, weights, across, *refs):
+    pieces, stored, (middle, half_out, kept, total, factor) = refs[:5], refs[5], refs[6:11]
+    slab, other, first, second, scratch = refs[11:]
     sec, odd = position()
     planes, rows = middle.shape[:2]
     pair = planes // 2
@@ -365,14 +346,12 @@
         for i in range(planes):
             slab[start + i] = piece[i * rows : (i + 1) * rows]
     at = planes * rows
-    steps = LEAD + stored[1].shape[0]
-    own_kinds, first_kinds, across_kinds = (
-        pieces[0][at + row : at + row + 1] for row in (OWN_KINDS, FIRST_KINDS, ACROSS_KINDS)
-    )
+    steps = stored.shape[0]
+    own_kinds, first_kinds = (pieces[0][at + row : at + row + 1] for row in (OWN_KINDS, FIRST_KINDS))
     beside_kinds, beside_first = (pieces[3][at + row : at + row + 1] for row in (OWN_KINDS, FIRST_KINDS))
     kinds = scalars_of(jnp.where((sec == 1) | (sec == 2), beside_first, first_kinds), steps)
     kinds += scalars_of(jnp.where((sec == 1) | (sec == 2), own_kinds, beside_kinds), steps)
-    last_kinds = jnp.where(sec == 0, across_kinds, own_kinds)
+    last_kinds = jnp.where(sec == 0, across[:1], own_kinds)
     half_out[pair * rows :] = jnp.broadcast_to(last_kinds, (8, rows))
     width = 2 * planes * factor.shape[0]
     lines = [piece[at : at + width] for piece in pieces]
@@ -385,10 +364,8 @@
     def after(step, state):
         @pl.when(sec == step // steps)
         def _():
-            j = step % steps
-            source = stored[0][j] if j < LEAD else stored[1][j - LEAD]
-            total[...] += state[reach : reach + planes] * source
-            if j + 1 == steps:
+            total[...] += state[reach : reach + planes] * stored[step % steps]
+            if (step + 1) % steps == 0:
                 kept[...] = state[reach : reach + planes]
 
     run_steps(kinds, taps, weights, reach, slab, other, first, second, factor, 0, after)
@@ -400,9 +377,9 @@
 
 def late_kernel(blocks, last, taps, weights, middle, *refs):
     pieces, refs = refs[: 2 * len(blocks)], refs[2 * len(blocks) :]
-    factor, kept, total_in, total_beside, series, stored = refs[0], refs[1], refs[2], refs[3], refs[4:6], refs[6:8]
-    handoff, share, to_pair, to_across, to_corner = refs[8:13]
-    slab, other, first, second, scratch, total, saved, whole = refs[13:]
+    factor, kept, total_in, total_beside, series, stored = refs[:6]
+    handoff, onward, share, to_pair, to_across, to_corner = refs[6:12]
+    slab, other, first, second, scratch, total, whole = refs[12:]
     sec, odd = position()
     planes, rows = middle.shape[:2]
     pair = planes // 2
@@ -420,29 +397,31 @@
     def _():
         total[...] = total_in[...] + total_beside[...]
 
-    saved[...] = kept[...]
-
     def after(step, state):
         for where, source in ((sec == 0, series), (sec == last, stored)):
 
             @pl.when(where)
             def _(source=source):
-                part = source[0][step] if step < LEAD else source[1][step - LEAD]
-                total[...] += state[reach : reach + planes] * part
+                total[...] += state[reach : reach + planes] * source[step]
 
     run_steps(kinds, taps, weights, reach, slab, other, first, second, factor, begun - reach, after)
     state = (slab, other)[reach % 2]
 
-    @pl.when(sec == last)
-    def _():
-        saved[...] = state[reach : reach + planes]
-
     orients = handoff.shape[1]
     count = orients // (last + 1)
-    held = planes * count
-    to_corner[...] = jnp.zeros(to_corner.shape, jnp.float32)
     for i in range(planes):
-        handoff[i] = from_tile(saved[i], scratch)
+        onward[i] = from_tile(state[reach + i], scratch)
+
+    @pl.when(sec < 2)
+    def _():
+        for i in range(planes):
+            handoff[i] = from_tile(kept[i], scratch)
+
+    @pl.when(sec >= 2)
+    def _():
+        handoff[...] = onward[...]
+
+    for i in range(planes):
         whole[...] = from_tile(total[i], scratch)
         for piece, who in (
             (share, sec),
@@ -451,31 +430,22 @@
             (to_corner, last - sec),
         ):
             piece[i * count : (i + 1) * count] = whole[pl.ds(pl.multiple_of(who * count, count), count)]
-    for i in range(pair):
-        to_across[held + i * orients : held + (i + 1) * orients] = from_tile(state[reach + pair * odd + i], scratch)
-
-    @pl.when(sec == 1)
-    def _():
-        to_corner[...] = to_across[held:]
-
-
-def finish_kernel(contour, handoff_in, share, to_pair, to_across, to_corner, handoff, density):
+
+
+def finish_kernel(contour, handoff_in, onward, share, to_pair, to_across, to_corner, handoff, density):
     sec = lax.axis_index("sec")
     planes, count = density.shape[:2]
-    held = planes * count
-    corner = jnp.where(sec == 2, 0.0, to_corner[:held])
-    total = (share[...] + to_pair[...] + to_across[:held] + corner) / contour
+    total = (share[...] + to_pair[...] + to_across[...] + to_corner[...]) / contour
     for i in range(planes):
         density[i] = total[i * count : (i + 1) * count]
-    handoff[0] = handoff_in[...]
 
     @pl.when(sec == 2)
     def _():
-        orients = handoff.shape[2]
-        pair = planes // 2
-        for i in range(pair):
-            handoff[0, i] = to_across[held + i * orients : held + (i + 1) * orients]
-            handoff[0, pair + i] = to_corner[i * orients : (i + 1) * orients]
+        handoff[0] = onward[...]
+
+    @pl.when(sec != 2)
+    def _():
+        handoff[0] = handoff_in[...]
 
 
 def call(kernel, out_shape, scratch, operands, dtypes=None):
@@ -508,12 +478,11 @@
 
     same, beside = (0, 1, 2, 3), (1, 0, 3, 2)
     moved = send(incoming[0], {0: 1, 1: 3})
-    lead, bundle = launch(
-        incoming, backward, fields, block_types, axial_taps, lateral_taps, depth_taps, bend_diagonal, bend_coupling
-    )
-    types = jnp.pad(block_types.astype(jnp.float32), ((0, 7), (0, lanes - steps)))
-    types = send(types, {1: 3, 2: 0})
-    lead = send(lead, {2: 0})
+    bundle = launch(
+        incoming, fields, block_types, axial_taps, lateral_taps, depth_taps, bend_diagonal, bend_coupling
+    )
+    own_types = jnp.pad(block_types.astype(jnp.float32), ((0, 7), (0, lanes - steps)))
+    types = send(own_types, {1: 3})
     size = planes * rows + FIELD_ROWS
     base, taps, weights = call(
         unpack_kernel, [(size, lanes), (TAP_ROWS, lanes), (2 * rows, 2 * lanes)], [], [bundle], {2: jnp.bfloat16}
@@ -531,45 +500,39 @@
 
     (piece,) = call(pack_kernel, [(size, lanes)], [tile], [base, moved, passed, types])
     own = [send(piece, same, shift, 2 * shift) for shift in near]
-    backward, _ = lax.optimization_barrier((backward, piece))
-    *stored, lead = call(
-        turn_kernel,
-        [(count, planes, rows, lanes) for count in (LEAD, steps - LEAD, LEAD)],
-        [tile],
-        [backward, lead],
-    )
-    own[-1], *stored = lax.optimization_barrier((own[-1], *stored))
+    backward, own_types, _ = lax.optimization_barrier((backward, own_types, piece))
+    across_types = send(own_types, {2: 0})
+    (stored,) = call(turn_kernel, [(steps, planes, rows, lanes)], [tile], [backward])
+    own[-1], stored, across_types = lax.optimization_barrier((own[-1], stored, across_types))
     swapped = [send(each, beside) for each in own]
-    late_stored, *swapped = lax.optimization_barrier((stored[1], *swapped))
-    late_last = send(late_stored, {2: 0})
+    leaving, *swapped = lax.optimization_barrier((stored, *swapped))
+    arrived = send(leaving, {2: 0})
     middle, piece, kept, total, factor = call(
         early_kernel,
         [(planes, rows, lanes), (pair * rows + 8, lanes), (planes, rows, lanes), (planes, rows, lanes)]
         + [(fields.shape[0], planes + 2 * reach[0], rows, lanes)],
         work(reach[0]),
-        [taps, weights, piece, *own, *swapped, *stored],
+        [taps, weights, across_types, piece, *own, *swapped, stored],
     )
     own = [send(piece, same, shift, shift) for shift in near]
     beside_total = send(total, beside)
     swapped = [send(each, beside) for each in own]
-    held = planes * (orients // n_sec)
-    handoff, share, to_pair, to_across, to_corner = call(
+    held = planes * (orients // n_sec), cells
+    handoff, onward, share, to_pair, to_across, to_corner = call(
         functools.partial(late_kernel, tuple(-shift for shift in near), last),
-        [(planes, orients, cells)]
-        + [(held, cells)] * 2
-        + [(held + pair * orients, cells), (pair * orients, cells)],
-        work(reach[1]) + [inner, inner, pltpu.VMEM((orients, cells), jnp.float32)],
-        [taps, weights, middle, *own, *swapped, factor, kept, total, beside_total]
-        + [lead, late_last, *stored],
-    )
+        [(planes, orients, cells)] * 2 + [held] * 4,
+        work(reach[1]) + [inner, pltpu.VMEM((orients, cells), jnp.float32)],
+        [taps, weights, middle, *own, *swapped, factor, kept, total, beside_total, arrived, stored],
+    )
+    onward = send(onward, {1: 2})
+    to_corner = send(to_corner, (3, 2, 1, 0))
+    to_across = send(to_across, (2, 0, 3, 1))
     to_pair = send(to_pair, beside)
-    to_across = send(to_across, (2, 0, 3, 1))
-    to_corner = send(to_corner, (3, 2, 1, 0))
     handoff, density = call(
         functools.partial(finish_kernel, n_sec * steps),
         [(1,) + handoff.shape, (planes, orients // n_sec, cells)],
         [],
-        [handoff, share, to_pair, to_across, to_corner],
+        [handoff, onward, share, to_pair, to_across, to_corner],
     )
     return handoff, density
 

time: 60.3 us -> 61.1 us (1.013)
    ppermute x17 -> x18, waiting for transfers between devices: 21.4 us -> 21.8 us  [send(): return lax.ppermute(array, ('sec', 'gx'), pairs)]
    ppermute x17 -> x18, starting transfers between devices: 21.1 us -> 20.9 us  [send(): return lax.ppermute(array, ('sec', 'gx'), pairs)]
  transfers between devices with their start and end apart: 17 -> 18, of which waited for: 9 -> 9; matrix products, arithmetic and copies ran while one was open for 1% -> 1% of each run, Pallas kernels for 17% -> 17%
where the time goes in v11:
time: 61.1 us; the launch traced here: 60.2 us
  waiting for transfers between devices  21.8 us (36%)
  starting transfers between devices  20.9 us (34%)
  Pallas kernels  14.1 us (23%)
  local copies, waits for them, and re-layouts  2.02 us (3%)
  between operations  0.77 us (1%)
  other arithmetic  0.66 us (1%)
    ppermute x18, waiting for transfers between devices, send(): return lax.ppermute(array, ('sec', 'gx'), pairs)  21.8 us
    ppermute x18, starting transfers between devices, send(): return lax.ppermute(array, ('sec', 'gx'), pairs)  20.9 us
    pallas_call x6, Pallas kernels, call(): pl.pallas_call(kernel, in_specs=[IN_VMEM] * len(operands), out_specs=[IN_...  12 us
    pallas_call x1, Pallas kernels, launch(): pl.pallas_call(launch_kernel, in_specs=[pl.BlockSpec(memory_space=pltpu.H...  2.06 us
    unnamed x4, local copies, waits for them, and re-layouts  2.01 us
  transfers between devices with their start and end apart: 18, of which 9 were waited for; matrix products, arithmetic and copies ran while one was open for 1% of the time, Pallas kernels for 17%

profile of v11, /device:TPU:0, one launch (start us, length us, event | category | flops | bytes accessed | tf_op | source)
XLA Modules:
  0.0 60.2 jit_solution(258105060119464563)
XLA Ops:
  0.6 2.4 %collective-permute-start = (f32[4,64,256]{2,1,0:T(8,128)}, f32[4,64,256]{2,1,0:T(8,128)S(1)}, u32[]{:S(2)}, u32[]{:S(2)}) collective-permute-start(f32[4,64,256]{2,1,0:T(8,128)} %bitcast.2), channel_id=1, source_target_pairs={{0,8},{1,9},{2,10},{3,11},{4,12},{5,13},{6,14},{7,15},{8,24},{9,25... | collective-permute-start | bytes 786440 | tf_op jit(solution)/shard_map/ppermute | solution.py:477
  3.0 0.7 %convert_element_type.5 = f32[1,4]{1,0:T(1,128)S(1)} convert(s32[1,4]{1,0:T(1,128)} %refs_2_.1) | non-fusion elementwise | flops 4 | bytes 32 | tf_op jit(solution)/shard_map/convert_element_type | solution.py:484
  3.7 0.6 %collective-permute-start.1 = (f32[8,128]{1,0:T(8,128)S(1)}, f32[8,128]{1,0:T(8,128)S(1)}, u32[]{:S(2)}, u32[]{:S(2)}) collective-permute-start(f32[8,128]{1,0:T(8,128)S(1)} %pad.4), channel_id=1, source_target_pairs={{8,24},{9,25},{10,26},{11,27},{12,28},{13,29},{14,30},{15,31}} | collective-permute-start | bytes 12296 | tf_op jit(solution)/shard_map/ppermute | solution.py:477
  4.3 2.1 %shard_map.104.bundle = f32[680,128]{1,0:T(8,128)} custom-call(f32[1,4,64,256]{3,2,1,0:T(8,128)} %refs_0_.1, f32[3,4,256]{2,1,0:T(4,128)} %refs_1_.1, s32[1,4]{1,0:T(1,128)} %refs_2_.1, f32[3,64]{1,0:T(4,128)} %refs_3_.1, f32[3,64]{1,0:T(4,128)} %refs_4_.1, f32[3,64]{1,0:T(4,128)} %refs_5_.1, f32[1,64]{1,0:T(1,128)} %bitcast.3, f32[64,64]{1,0:T(8,128)} %refs_7_.1), custom_call_target="tpu_custom_call" | custom-call | tf_op jit(solution)/shard_map/pallas_call | solution.py:215
  6.4 0.0 copy-start
  6.4 1.0 %copy-done = f32[680,128]{1,0:T(8,128)S(1)} copy-done((f32[680,128]{1,0:T(8,128)S(1)}, f32[680,128]{1,0:T(8,128)}, u32[]{:S(2)}) %copy-start) | copy-done | bytes 348184
  7.4 0.0 collective-permute-done.1.types
  7.4 0.0 collective-permute-done.moved
  7.4 0.7 %collective-permute-start.2 = (f32[4,64,256]{2,1,0:T(8,128)S(1)}, f32[4,64,256]{2,1,0:T(8,128)S(1)}, u32[]{:S(2)}, u32[]{:S(2)}) collective-permute-start(f32[4,64,256]{2,1,0:T(8,128)S(1)} %collective-permute-done.moved), channel_id=1, source_target_pairs={{24,16},{25,17},{26,18},{27,19},{28,20},{29,21},{30,22},{31,23}} | collective-permute-start | bytes 786440 | tf_op jit(solution)/shard_map/ppermute | solution.py:477
  8.1 0.0 collective-permute-done.2.passed
  8.2 5.4 %collective-permute-start.3 = (f32[544,128]{1,0:T(8,128)S(1)}, f32[544,128]{1,0:T(8,128)S(1)}, u32[]{:S(2)}, u32[]{:S(2)}) collective-permute-start(f32[544,128]{1,0:T(8,128)S(1)} %shard_map.106.refs_0_), channel_id=1, source_target_pairs={{0,7},{1,0},{2,1},{3,2},{4,3},{5,4},{6,5},{7,6},{8,14},{9,15},{10,... | collective-permute-start | bytes 835592 | tf_op jit(solution)/shard_map/ppermute | solution.py:477
  13.6 0.0 collective-permute-start.5
  13.6 1.3 %collective-permute-start.4 = (f32[8,128]{1,0:T(8,128)S(1)}, f32[8,128]{1,0:T(8,128)S(1)}, u32[]{:S(2)}, u32[]{:S(2)}) collective-permute-start(f32[8,128]{1,0:T(8,128)S(1)} %pad.4), channel_id=1, source_target_pairs={{16,0},{17,1},{18,2},{19,3},{20,4},{21,5},{22,6},{23,7}} | collective-permute-start | bytes 12296 | tf_op jit(solution)/shard_map/ppermute | solution.py:477
  14.9 0.0 copy-start.1
  14.9 1.0 %copy-done.1 = bf16[4,4,64,256]{3,2,1,0:T(8,128)(2,1)S(1)} copy-done((bf16[4,4,64,256]{3,2,1,0:T(8,128)(2,1)S(1)}, bf16[4,4,64,256]{3,2,1,0:T(8,128)(2,1)}, u32[]{:S(2)}) %copy-start.1) | copy-done | bytes 524312
  15.9 0.3 shard_map.107.refs_5_.refs_9_
  16.3 4.4 %collective-permute-done.4.across = f32[8,128]{1,0:T(8,128)S(1)} collective-permute-done((f32[8,128]{1,0:T(8,128)S(1)}, f32[8,128]{1,0:T(8,128)S(1)}, u32[]{:S(2)}, u32[]{:S(2)}) %collective-permute-start.4) | collective-permute-done | bytes 4128 | tf_op jit(solution)/shard_map/ppermute | solution.py:477
  20.7 0.0 collective-permute-done.3.refs_2_
  20.7 5.0 %collective-permute-done.5.refs_1_ = f32[544,128]{1,0:T(8,128)S(1)} collective-permute-done((f32[544,128]{1,0:T(8,128)S(1)}, f32[544,128]{1,0:T(8,128)S(1)}, u32[]{:S(2)}, u32[]{:S(2)}) %collective-permute-start.5) | collective-permute-done | bytes 278560 | tf_op jit(solution)/shard_map/ppermute | solution.py:477
  25.7 0.0 collective-permute-start.6
  25.7 0.5 collective-permute-start.7
  26.2 1.0 %collective-permute-done.6.refs_3_ = f32[544,128]{1,0:T(8,128)S(1)} collective-permute-done((f32[544,128]{1,0:T(8,128)S(1)}, f32[544,128]{1,0:T(8,128)S(1)}, u32[]{:S(2)}, u32[]{:S(2)}) %collective-permute-start.6) | collective-permute-done | bytes 278560 | tf_op jit(solution)/shard_map/ppermute | solution.py:477
  27.2 0.4 collective-permute-done.7.refs_4_
  27.6 1.3 %collective-permute-start.13 = (f32[4,4,128,128]{3,2,1,0:T(8,128)S(1)}, f32[4,4,128,128]{3,2,1,0:T(8,128)S(1)}, u32[]{:S(2)}, u32[]{:S(2)}) collective-permute-start(f32[4,4,128,128]{3,2,1,0:T(8,128)S(1)} %shard_map.107.refs_5_.refs_9_), channel_id=1, source_target_pairs={{16,0},{17,1},{18,2},{19,3},{20,4},{21,5},{22,6},{23,7}} | collective-permute-start | bytes 3145736 | tf_op jit(solution)/shard_map/ppermute | solution.py:477
  28.9 7.8 %shard_map.108 = (f32[4,128,128]{2,1,0:T(8,128)S(1)}, f32[264,128]{1,0:T(8,128)S(1)}, f32[4,128,128]{2,1,0:T(8,128)S(1)}, f32[4,128,128]{2,1,0:T(8,128)S(1)}, f32[3,20,128,128]{3,2,1,0:T(8,128)S(1)}) custom-call(f32[8,128]{1,0:T(8,128)S(1)} %get-tuple-element.27.taps, bf16[256,256]{1,0:T(8,128)(2,1)S(1)} %get-tuple-element.28.weights, ...), custom_call_target="tpu_custom_call" | custom-call | tf_op jit(solution)/shard_map/pallas_call | solution.py:452
  36.7 1.0 %collective-permute-start.9 = (f32[264,128]{1,0:T(8,128)S(1)}, f32[264,128]{1,0:T(8,128)S(1)}, u32[]{:S(2)}, u32[]{:S(2)}) collective-permute-start(f32[264,128]{1,0:T(8,128)S(1)} %get-tuple-element.41), channel_id=1, source_target_pairs={{0,7},{1,0},{2,1},{3,2},{4,3},{5,4},{6,5},{7,6},{8,15},{9,8},{10,9... | collective-permute-start | bytes 405512 | tf_op jit(solution)/shard_map/ppermute | solution.py:477
  37.7 1.1 %collective-permute-start.8 = (f32[264,128]{1,0:T(8,128)S(1)}, f32[264,128]{1,0:T(8,128)S(1)}, u32[]{:S(2)}, u32[]{:S(2)}) collective-permute-start(f32[264,128]{1,0:T(8,128)S(1)} %get-tuple-element.41), channel_id=1, source_target_pairs={{0,1},{1,2},{2,3},{3,4},{4,5},{5,6},{6,7},{7,0},{8,9},{9,10},{10,1... | collective-permute-start | bytes 405512 | tf_op jit(solution)/shard_map/ppermute | solution.py:477
  38.8 0.0 collective-permute-start.12
  38.8 3.0 %collective-permute-done.9.refs_1_ = f32[264,128]{1,0:T(8,128)S(1)} collective-permute-done((f32[264,128]{1,0:T(8,128)S(1)}, f32[264,128]{1,0:T(8,128)S(1)}, u32[]{:S(2)}, u32[]{:S(2)}) %collective-permute-start.9) | collective-permute-done | bytes 135200 | tf_op jit(solution)/shard_map/ppermute | solution.py:477
  41.8 0.0 collective-permute-start.11
  41.8 3.6 %collective-permute-done.8.refs_0_ = f32[264,128]{1,0:T(8,128)S(1)} collective-permute-done((f32[264,128]{1,0:T(8,128)S(1)}, f32[264,128]{1,0:T(8,128)S(1)}, u32[]{:S(2)}, u32[]{:S(2)}) %collective-permute-start.8) | collective-permute-done | bytes 135200 | tf_op jit(solution)/shard_map/ppermute | solution.py:477
  45.4 0.0 collective-permute-start.10
  45.4 0.0 collective-permute-done.12.refs_7_
  45.4 0.0 collective-permute-done.11.refs_3_
  45.4 1.3 %collective-permute-done.10.refs_2_ = f32[264,128]{1,0:T(8,128)S(1)} collective-permute-done((f32[264,128]{1,0:T(8,128)S(1)}, f32[264,128]{1,0:T(8,128)S(1)}, u32[]{:S(2)}, u32[]{:S(2)}) %collective-permute-start.10) | collective-permute-done | bytes 135200 | tf_op jit(solution)/shard_map/ppermute | solution.py:477
  46.8 0.0 collective-permute-done.13.refs_8_
  46.8 3.0 %shard_map.109 = (f32[4,64,256]{2,1,0:T(8,128)S(1)}, f32[4,64,256]{2,1,0:T(8,128)S(1)}, f32[64,256]{1,0:T(8,128)S(1)}, f32[64,256]{1,0:T(8,128)S(1)}, f32[64,256]{1,0:T(8,128)S(1)}, /*index=5*/f32[64,256]{1,0:T(8,128)S(1)}) custom-call(f32[8,128]{1,0:T(8,128)S(1)} %get-tuple-element.27.taps, bf16[256,256]{1,0:T(8,128)(2,1)S(1)} %get-tuple-element.28.weights, ...), custom_call_target="tpu_custom_call" | custom-call | tf_op jit(solution)/shard_map/pallas_call | solution.py:452
  49.8 0.7 %collective-permute-start.14 = (f32[4,64,256]{2,1,0:T(8,128)S(1)}, f32[4,64,256]{2,1,0:T(8,128)S(1)}, u32[]{:S(2)}, u32[]{:S(2)}) collective-permute-start(f32[4,64,256]{2,1,0:T(8,128)S(1)} %get-tuple-element.47), channel_id=1, source_target_pairs={{8,16},{9,17},{10,18},{11,19},{12,20},{13,21},{14,22},{15,23}} | collective-permute-start | bytes 786440 | tf_op jit(solution)/shard_map/ppermute | solution.py:477
  50.5 4.6 %collective-permute-start.15 = (f32[64,256]{1,0:T(8,128)S(1)}, f32[64,256]{1,0:T(8,128)S(1)}, u32[]{:S(2)}, u32[]{:S(2)}) collective-permute-start(f32[64,256]{1,0:T(8,128)S(1)} %get-tuple-element.49), channel_id=1, source_target_pairs={{0,8},{1,9},{2,10},{3,11},{4,12},{5,13},{6,14},{7,15},{8,0},{9,1},... | collective-permute-start | bytes 196616 | tf_op jit(solution)/shard_map/ppermute | solution.py:477
  55.1 0.0 collective-permute-start.16
  55.1 1.4 %collective-permute-start.17 = (f32[64,256]{1,0:T(8,128)S(1)}, f32[64,256]{1,0:T(8,128)S(1)}, u32[]{:S(2)}, u32[]{:S(2)}) collective-permute-start(f32[64,256]{1,0:T(8,128)S(1)} %get-tuple-element.51), channel_id=1, source_target_pairs={{0,24},{1,25},{2,26},{3,27},{4,28},{5,29},{6,30},{7,31},{8,16},{9,... | collective-permute-start | bytes 196616 | tf_op jit(solution)/shard_map/ppermute | solution.py:477
  56.5 0.0 collective-permute-done.15.to_pair
  56.5 1.1 %collective-permute-done.16.to_across = f32[64,256]{1,0:T(8,128)S(1)} collective-permute-done((f32[64,256]{1,0:T(8,128)S(1)}, f32[64,256]{1,0:T(8,128)S(1)}, u32[]{:S(2)}, u32[]{:S(2)}) %collective-permute-start.16) | collective-permute-done | bytes 65568 | tf_op jit(solution)/shard_map/ppermute | solution.py:477
  57.6 1.9 %collective-permute-done.17.to_corner = f32[64,256]{1,0:T(8,128)S(1)} collective-permute-done((f32[64,256]{1,0:T(8,128)S(1)}, f32[64,256]{1,0:T(8,128)S(1)}, u32[]{:S(2)}, u32[]{:S(2)}) %collective-permute-start.17) | collective-permute-done | bytes 65568 | tf_op jit(solution)/shard_map/ppermute | solution.py:477
  59.5 0.0 collective-permute-done.14.onward
  59.5 0.8 %shard_map.110 = (f32[1,4,64,256]{3,2,1,0:T(8,128)}, f32[4,16,256]{2,1,0:T(8,128)}) custom-call(f32[4,64,256]{2,1,0:T(8,128)S(1)} %get-tuple-element.46.handoff_in, f32[4,64,256]{2,1,0:T(8,128)S(1)} %collective-permute-done.14.onward, f32[64,256]{1,0:T(8,128)S(1)} %get-tuple-element.48.share, f32[64,256]{1,0:T(8,128)S(1)} %collective-permute-done.15.to_pair, ...), custom_call_target="tpu_custom_call" | custom-call | tf_op jit(solution)/shard_map/pallas_call | solution.py:452
  (3 shorter events, 0.1 us)
Async XLA Ops:
  0.6 6.8 %collective-permute-start = (f32[4,64,256]{2,1,0:T(8,128)}, f32[4,64,256]{2,1,0:T(8,128)S(1)}, u32[]{:S(2)}, u32[]{:S(2)}) collective-permute-start(f32[4,64,256]{2,1,0:T(8,128)} %bitcast.2), channel_id=1, source_target_pairs={{0,8},{1,9},{2,10},{3,11},{4,12},{5,13},{6,14},{7,15},{8,24},{9,25... | collective-permute-start | bytes 786440 | tf_op jit(solution)/shard_map/ppermute | solution.py:477
  3.7 3.7 %collective-permute-start.1 = (f32[8,128]{1,0:T(8,128)S(1)}, f32[8,128]{1,0:T(8,128)S(1)}, u32[]{:S(2)}, u32[]{:S(2)}) collective-permute-start(f32[8,128]{1,0:T(8,128)S(1)} %pad.4), channel_id=1, source_target_pairs={{8,24},{9,25},{10,26},{11,27},{12,28},{13,29},{14,30},{15,31}} | collective-permute-start | bytes 12296 | tf_op jit(solution)/shard_map/ppermute | solution.py:477
  6.4 1.0 %copy-start = (f32[680,128]{1,0:T(8,128)S(1)}, f32[680,128]{1,0:T(8,128)}, u32[]{:S(2)}) copy-start(f32[680,128]{1,0:T(8,128)} %shard_map.104.bundle) | copy-start | bytes 1044484
  7.4 0.7 %collective-permute-start.2 = (f32[4,64,256]{2,1,0:T(8,128)S(1)}, f32[4,64,256]{2,1,0:T(8,128)S(1)}, u32[]{:S(2)}, u32[]{:S(2)}) collective-permute-start(f32[4,64,256]{2,1,0:T(8,128)S(1)} %collective-permute-done.moved), channel_id=1, source_target_pairs={{24,16},{25,17},{26,18},{27,19},{28,20},{29,21},{30,22},{31,23}} | collective-permute-start | bytes 786440 | tf_op jit(solution)/shard_map/ppermute | solution.py:477
  8.2 12.5 %collective-permute-start.3 = (f32[544,128]{1,0:T(8,128)S(1)}, f32[544,128]{1,0:T(8,128)S(1)}, u32[]{:S(2)}, u32[]{:S(2)}) collective-permute-start(f32[544,128]{1,0:T(8,128)S(1)} %shard_map.106.refs_0_), channel_id=1, source_target_pairs={{0,7},{1,0},{2,1},{3,2},{4,3},{5,4},{6,5},{7,6},{8,14},{9,15},{10,... | collective-permute-start | bytes 835592 | tf_op jit(solution)/shard_map/ppermute | solution.py:477
  13.6 12.1 %collective-permute-start.5 = (f32[544,128]{1,0:T(8,128)S(1)}, f32[544,128]{1,0:T(8,128)S(1)}, u32[]{:S(2)}, u32[]{:S(2)}) collective-permute-start(f32[544,128]{1,0:T(8,128)S(1)} %shard_map.106.refs_0_), channel_id=1, source_target_pairs={{0,1},{1,2},{2,3},{3,4},{4,5},{5,6},{6,7},{7,0},{8,10},{9,11},{10,... | collective-permute-start | bytes 835592 | tf_op jit(solution)/shard_map/ppermute | solution.py:477
  13.6 7.1 %collective-permute-start.4 = (f32[8,128]{1,0:T(8,128)S(1)}, f32[8,128]{1,0:T(8,128)S(1)}, u32[]{:S(2)}, u32[]{:S(2)}) collective-permute-start(f32[8,128]{1,0:T(8,128)S(1)} %pad.4), channel_id=1, source_target_pairs={{16,0},{17,1},{18,2},{19,3},{20,4},{21,5},{22,6},{23,7}} | collective-permute-start | bytes 12296 | tf_op jit(solution)/shard_map/ppermute | solution.py:477
  14.9 1.0 %copy-start.1 = (bf16[4,4,64,256]{3,2,1,0:T(8,128)(2,1)S(1)}, bf16[4,4,64,256]{3,2,1,0:T(8,128)(2,1)}, u32[]{:S(2)}) copy-start(bf16[4,4,64,256]{3,2,1,0:T(8,128)(2,1)} %backward) | copy-start | bytes 1572868
  25.7 1.6 %collective-permute-start.6 = (f32[544,128]{1,0:T(8,128)S(1)}, f32[544,128]{1,0:T(8,128)S(1)}, u32[]{:S(2)}, u32[]{:S(2)}) collective-permute-start(f32[544,128]{1,0:T(8,128)S(1)} %collective-permute-done.5.refs_1_), channel_id=1, source_target_pairs={{0,8},{1,9},{2,10},{3,11},{4,12},{5,13},{6,14},{7,15},{8,0},{9,1},... | collective-permute-start | bytes 835592 | tf_op jit(solution)/shard_map/ppermute | solution.py:477
  25.7 2.0 %collective-permute-start.7 = (f32[544,128]{1,0:T(8,128)S(1)}, f32[544,128]{1,0:T(8,128)S(1)}, u32[]{:S(2)}, u32[]{:S(2)}) collective-permute-start(f32[544,128]{1,0:T(8,128)S(1)} %collective-permute-done.3.refs_2_), channel_id=1, source_target_pairs={{0,8},{1,9},{2,10},{3,11},{4,12},{5,13},{6,14},{7,15},{8,0},{9,1},... | collective-permute-start | bytes 835592 | tf_op jit(solution)/shard_map/ppermute | solution.py:477
  27.6 19.2 %collective-permute-start.13 = (f32[4,4,128,128]{3,2,1,0:T(8,128)S(1)}, f32[4,4,128,128]{3,2,1,0:T(8,128)S(1)}, u32[]{:S(2)}, u32[]{:S(2)}) collective-permute-start(f32[4,4,128,128]{3,2,1,0:T(8,128)S(1)} %shard_map.107.refs_5_.refs_9_), channel_id=1, source_target_pairs={{16,0},{17,1},{18,2},{19,3},{20,4},{21,5},{22,6},{23,7}} | collective-permute-start | bytes 3145736 | tf_op jit(solution)/shard_map/ppermute | solution.py:477
  36.7 5.1 %collective-permute-start.9 = (f32[264,128]{1,0:T(8,128)S(1)}, f32[264,128]{1,0:T(8,128)S(1)}, u32[]{:S(2)}, u32[]{:S(2)}) collective-permute-start(f32[264,128]{1,0:T(8,128)S(1)} %get-tuple-element.41), channel_id=1, source_target_pairs={{0,7},{1,0},{2,1},{3,2},{4,3},{5,4},{6,5},{7,6},{8,15},{9,8},{10,9... | collective-permute-start | bytes 405512 | tf_op jit(solution)/shard_map/ppermute | solution.py:477
  37.7 7.7 %collective-permute-start.8 = (f32[264,128]{1,0:T(8,128)S(1)}, f32[264,128]{1,0:T(8,128)S(1)}, u32[]{:S(2)}, u32[]{:S(2)}) collective-permute-start(f32[264,128]{1,0:T(8,128)S(1)} %get-tuple-element.41), channel_id=1, source_target_pairs={{0,1},{1,2},{2,3},{3,4},{4,5},{5,6},{6,7},{7,0},{8,9},{9,10},{10,1... | collective-permute-start | bytes 405512 | tf_op jit(solution)/shard_map/ppermute | solution.py:477
  38.8 6.6 %collective-permute-start.12 = (f32[4,128,128]{2,1,0:T(8,128)S(1)}, f32[4,128,128]{2,1,0:T(8,128)S(1)}, u32[]{:S(2)}, u32[]{:S(2)}) collective-permute-start(f32[4,128,128]{2,1,0:T(8,128)S(1)} %get-tuple-element.44.refs_6_), channel_id=1, source_target_pairs={{0,8},{1,9},{2,10},{3,11},{4,12},{5,13},{6,14},{7,15},{8,0},{9,1},... | collective-permute-start | bytes 786440 | tf_op jit(solution)/shard_map/ppermute | solution.py:477
  41.8 3.6 %collective-permute-start.11 = (f32[264,128]{1,0:T(8,128)S(1)}, f32[264,128]{1,0:T(8,128)S(1)}, u32[]{:S(2)}, u32[]{:S(2)}) collective-permute-start(f32[264,128]{1,0:T(8,128)S(1)} %collective-permute-done.9.refs_1_), channel_id=1, source_target_pairs={{0,8},{1,9},{2,10},{3,11},{4,12},{5,13},{6,14},{7,15},{8,0},{9,1},... | collective-permute-start | bytes 405512 | tf_op jit(solution)/shard_map/ppermute | solution.py:477
  45.4 1.4 %collective-permute-start.10 = (f32[264,128]{1,0:T(8,128)S(1)}, f32[264,128]{1,0:T(8,128)S(1)}, u32[]{:S(2)}, u32[]{:S(2)}) collective-permute-start(f32[264,128]{1,0:T(8,128)S(1)} %collective-permute-done.8.refs_0_), channel_id=1, source_target_pairs={{0,8},{1,9},{2,10},{3,11},{4,12},{5,13},{6,14},{7,15},{8,0},{9,1},... | collective-permute-start | bytes 405512 | tf_op jit(solution)/shard_map/ppermute | solution.py:477
  49.8 9.7 %collective-permute-start.14 = (f32[4,64,256]{2,1,0:T(8,128)S(1)}, f32[4,64,256]{2,1,0:T(8,128)S(1)}, u32[]{:S(2)}, u32[]{:S(2)}) collective-permute-start(f32[4,64,256]{2,1,0:T(8,128)S(1)} %get-tuple-element.47), channel_id=1, source_target_pairs={{8,16},{9,17},{10,18},{11,19},{12,20},{13,21},{14,22},{15,23}} | collective-permute-start | bytes 786440 | tf_op jit(solution)/shard_map/ppermute | solution.py:477
  50.5 6.0 %collective-permute-start.15 = (f32[64,256]{1,0:T(8,128)S(1)}, f32[64,256]{1,0:T(8,128)S(1)}, u32[]{:S(2)}, u32[]{:S(2)}) collective-permute-start(f32[64,256]{1,0:T(8,128)S(1)} %get-tuple-element.49), channel_id=1, source_target_pairs={{0,8},{1,9},{2,10},{3,11},{4,12},{5,13},{6,14},{7,15},{8,0},{9,1},... | collective-permute-start | bytes 196616 | tf_op jit(solution)/shard_map/ppermute | solution.py:477
  55.1 2.5 %collective-permute-start.16 = (f32[64,256]{1,0:T(8,128)S(1)}, f32[64,256]{1,0:T(8,128)S(1)}, u32[]{:S(2)}, u32[]{:S(2)}) collective-permute-start(f32[64,256]{1,0:T(8,128)S(1)} %get-tuple-element.50), channel_id=1, source_target_pairs={{0,16},{1,17},{2,18},{3,19},{4,20},{5,21},{6,22},{7,23},{8,0},{9,1... | collective-permute-start | bytes 196616 | tf_op jit(solution)/shard_map/ppermute | solution.py:477
  55.1 4.4 %collective-permute-start.17 = (f32[64,256]{1,0:T(8,128)S(1)}, f32[64,256]{1,0:T(8,128)S(1)}, u32[]{:S(2)}, u32[]{:S(2)}) collective-permute-start(f32[64,256]{1,0:T(8,128)S(1)} %get-tuple-element.51), channel_id=1, source_target_pairs={{0,24},{1,25},{2,26},{3,27},{4,28},{5,29},{6,30},{7,31},{8,16},{9,... | collective-permute-start | bytes 196616 | tf_op jit(solution)/shard_map/ppermute | solution.py:477

commit v12 on v11

--- a/solution.py
+++ b/solution.py
@@ -11,8 +11,10 @@
 CZ = 64
 GROUP = 6
 FIELD_ROWS = 32
+PIECE_ROWS = 16
 TAP_ROWS = 8
-OWN_KINDS, FIRST_KINDS = 24, 25
+OWN_KINDS = 24
+PIECE_OWN, PIECE_FIRST = 12, 13
 VMEM_BYTES = 16 * 2**20
 WHOLE_VMEM_BYTES = 62 * 2**20
 IN_VMEM = pl.BlockSpec(memory_space=pltpu.VMEM)
@@ -224,10 +226,11 @@
     )(*operands)
 
 
-def turn_kernel(backward, out, scratch):
-    for step in range(out.shape[0]):
-        for i in range(out.shape[1]):
-            out[step, i] = to_tile(backward[step, i].astype(jnp.float32), scratch)
+def turn_kernel(backward, early, late, scratch):
+    for out, begin in ((early, 0), (late, early.shape[0])):
+        for step in range(out.shape[0]):
+            for i in range(out.shape[1]):
+                out[step, i] = to_tile(backward[begin + step, i].astype(jnp.float32), scratch)
 
 
 def unpack_kernel(bundle, out, taps, weights):
@@ -245,25 +248,34 @@
     out[:at] = bundle[lines + FIELD_ROWS :]
 
 
-def pack_kernel(base, moved, passed, types, out, scratch):
+def pack_kernel(base, moved, passed, types, middle, piece, scratch):
     sec, odd = position()
-    rows = scratch.shape[0]
-    at = out.shape[0] - FIELD_ROWS
-    out[at:] = base[at:]
-    out[at + FIRST_KINDS : at + FIRST_KINDS + 1] = jnp.where(
-        sec == 0, base[at + OWN_KINDS : at + OWN_KINDS + 1], types[:1]
-    )
+    planes, rows = middle.shape[:2]
+    pair = planes // 2
+    at = planes * rows
 
     @pl.when(sec == 0)
     def _():
-        out[:at] = base[:at]
+        for i in range(planes):
+            middle[i] = base[i * rows : (i + 1) * rows]
 
     def fill(source):
-        for i in range(source.shape[0]):
-            out[i * rows : (i + 1) * rows] = to_tile(source[i], scratch)
+        for i in range(planes):
+            middle[i] = to_tile(source[i], scratch)
 
     pl.when(odd == 1)(lambda: fill(moved))
     pl.when((sec > 0) & (odd == 0))(lambda: fill(passed))
+    for i in range(pair):
+        piece[i * rows : (i + 1) * rows] = middle[pair * odd + i]
+    here = pair * rows
+    piece[here:] = jnp.zeros((PIECE_ROWS, rows), jnp.float32)
+    for kind in range(OWN_KINDS // (2 * planes)):
+        for i in range(pair):
+            to = here + (kind * pair + i) * 2
+            piece[to : to + 2] = base[pl.ds(at + (kind * planes + pair * odd + i) * 2, 2)]
+    own = base[at + OWN_KINDS : at + OWN_KINDS + 1]
+    piece[here + PIECE_OWN : here + PIECE_OWN + 1] = own
+    piece[here + PIECE_FIRST : here + PIECE_FIRST + 1] = jnp.where(sec == 0, own, types[:1])
 
 
 def scalars_of(row, count):
@@ -322,104 +334,123 @@
         after(step, target)
 
 
-def spread_factor(columns, factor, starts, width):
+def spread_factor(columns, factor, begin, start, count):
     rows, lanes = factor.shape[2:]
-    pair = factor.shape[1] // len(starts)
     right = (lax.broadcasted_iota(jnp.int32, (rows, lanes), 1) >= lanes // 2).astype(jnp.int32)
-    for piece, start in enumerate(starts):
-        for kind in range(factor.shape[0]):
-            for i in range(pair):
-                at = piece * width + (kind * pair + i) * 2
-                factor[kind, start + i] = jnp.take_along_axis(columns, right + at, axis=1, mode="promise_in_bounds")
-
-
-def early_kernel(taps, weights, across, *refs):
-    pieces, stored, (middle, half_out, kept, total, factor) = refs[:5], refs[5], refs[6:11]
+    for kind in range(factor.shape[0]):
+        for i in range(count):
+            at = begin + (kind * count + i) * 2
+            factor[kind, start + i] = jnp.take_along_axis(columns, right + at, axis=1, mode="promise_in_bounds")
+
+
+def load_slab(slab, middle, pieces, odd):
+    planes, rows = middle.shape[:2]
+    pair = planes // 2
+    starts = places(odd, planes, planes, (-1, 1))
+    slab[planes : 2 * planes] = middle[...]
+    for piece, start in zip(pieces, starts):
+        for i in range(pair):
+            slab[start + i] = piece[i * rows : (i + 1) * rows]
+    return starts
+
+
+def early_kernel(taps, weights, base, middle_in, *refs):
+    pieces, stored, (middle, half_out, kept, total, factor) = refs[:4], refs[4:6], refs[6:11]
     slab, other, first, second, scratch = refs[11:]
     sec, odd = position()
     planes, rows = middle.shape[:2]
     pair = planes // 2
-    reach = (slab.shape[0] - planes) // 2
-    mine, others = (planes * (1 + core) for core in (odd, 1 - odd))
-    starts = [reach, reach - mine, reach + mine, reach - others, reach + others]
-    for piece, start in zip(pieces, starts):
-        for i in range(planes):
-            slab[start + i] = piece[i * rows : (i + 1) * rows]
-    at = planes * rows
-    steps = stored.shape[0]
-    own_kinds, first_kinds = (pieces[0][at + row : at + row + 1] for row in (OWN_KINDS, FIRST_KINDS))
-    beside_kinds, beside_first = (pieces[3][at + row : at + row + 1] for row in (OWN_KINDS, FIRST_KINDS))
-    kinds = scalars_of(jnp.where((sec == 1) | (sec == 2), beside_first, first_kinds), steps)
-    kinds += scalars_of(jnp.where((sec == 1) | (sec == 2), own_kinds, beside_kinds), steps)
-    last_kinds = jnp.where(sec == 0, across[:1], own_kinds)
-    half_out[pair * rows :] = jnp.broadcast_to(last_kinds, (8, rows))
-    width = 2 * planes * factor.shape[0]
-    lines = [piece[at : at + width] for piece in pieces]
-    lines.append(jnp.zeros((rows - width * len(pieces), rows), jnp.float32))
+    starts = load_slab(slab, middle_in, pieces, odd)
+    at = pair * rows
+    own_first, beside_first = (each[at + PIECE_FIRST : at + PIECE_FIRST + 1] for each in (pieces[0], pieces[2]))
+    kinds = scalars_of(jnp.where((sec == 0) | (sec == 3), own_first, beside_first), planes)
+    centre = base.shape[0] - FIELD_ROWS
+    lines = [base[centre : centre + OWN_KINDS]] + [piece[at : at + PIECE_OWN] for piece in pieces]
+    used = OWN_KINDS + PIECE_OWN * len(pieces)
+    lines.append(jnp.zeros((rows - used, rows), jnp.float32))
     scratch[...] = jnp.exp(-jnp.concatenate(lines, axis=0)).T
-    spread_factor(reorder(scratch), factor, starts, width)
+    columns = reorder(scratch)
+    spread_factor(columns, factor, 0, planes, planes)
+    for i, start in enumerate(starts):
+        spread_factor(columns, factor, OWN_KINDS + PIECE_OWN * i, start, pair)
+    finish_round(stored, sec == 0, kinds, taps, weights, factor, refs[6:10], refs[11:15])
+    half_out[at:] = jnp.broadcast_to(base[centre + OWN_KINDS : centre + OWN_KINDS + 1], (8, rows))
+
+
+def mid_kernel(taps, weights, across, middle_in, *refs):
+    pieces, factor, stored, (middle, half_out, kept, total) = refs[:4], refs[4], refs[5:7], refs[7:11]
+    slab, other, first, second, scratch = refs[11:]
+    sec, odd = position()
+    planes, rows = middle.shape[:2]
+    at = planes // 2 * rows
+    load_slab(slab, middle_in, pieces, odd)
+    own, beside = (each[at : at + 1] for each in (pieces[0], pieces[2]))
+    kinds = scalars_of(jnp.where((sec == 1) | (sec == 2), own, beside), planes)
+    finish_round(stored, sec == 1, kinds, taps, weights, factor, refs[7:11], refs[11:15])
+    half_out[at:] = jnp.broadcast_to(jnp.where(sec == 0, across[:1], own), (8, rows))
+
+
+def finish_round(stored, counted, kinds, taps, weights, factor, outs, work):
+    middle, half_out, kept, total = outs
+    slab, other, first, second = work
+    odd = position()[1]
+    planes, rows = middle.shape[:2]
+    pair = planes // 2
+    span = stored[0].shape[0]
     total[...] = jnp.zeros(total.shape, jnp.float32)
-    kept[...] = jnp.zeros(kept.shape, jnp.float32)
 
     def after(step, state):
-        @pl.when(sec == step // steps)
+        @pl.when(counted)
         def _():
-            total[...] += state[reach : reach + planes] * stored[step % steps]
-            if (step + 1) % steps == 0:
-                kept[...] = state[reach : reach + planes]
-
-    run_steps(kinds, taps, weights, reach, slab, other, first, second, factor, 0, after)
-    state = (slab, other)[reach % 2]
-    middle[...] = state[reach : reach + planes]
+            total[...] += state[planes : 2 * planes] * stored[step // span][step % span]
+
+    run_steps(kinds, taps, weights, planes, slab, other, first, second, factor, 0, after)
+    state = (slab, other)[planes % 2]
+    middle[...] = state[planes : 2 * planes]
+    kept[...] = state[planes : 2 * planes]
     for i in range(pair):
-        half_out[i * rows : (i + 1) * rows] = state[reach + pair * odd + i]
-
-
-def late_kernel(blocks, last, taps, weights, middle, *refs):
-    pieces, refs = refs[: 2 * len(blocks)], refs[2 * len(blocks) :]
-    factor, kept, total_in, total_beside, series, stored = refs[:6]
-    handoff, onward, share, to_pair, to_across, to_corner = refs[6:12]
-    slab, other, first, second, scratch, total, whole = refs[12:]
+        half_out[i * rows : (i + 1) * rows] = state[planes + pair * odd + i]
+
+
+def late_kernel(last, taps, weights, middle, *refs):
+    pieces, (factor, kept, beside_kept, total_in, total_beside) = refs[:4], refs[4:9]
+    series, stored = refs[9:11], refs[11:13]
+    handoff, share, to_pair, to_across, to_corner = refs[13:18]
+    slab, other, first, second, scratch, total, whole = refs[18:]
     sec, odd = position()
     planes, rows = middle.shape[:2]
     pair = planes // 2
-    reach = (slab.shape[0] - planes) // 2
-    begun = (factor.shape[1] - planes) // 2
-    even, uneven = (jnp.where(odd == core, pieces[0][pair * rows :], pieces[len(blocks)][pair * rows :]) for core in (0, 1))
-    kinds = scalars_of(jnp.where(sec < 2, even, uneven)[:1], reach)
-    slab[reach : reach + planes] = middle[...]
-    for piece, start in zip(pieces, places(odd, planes, reach, blocks)):
-        for i in range(pair):
-            slab[start + i] = piece[i * rows : (i + 1) * rows]
+    load_slab(slab, middle, pieces, odd)
+    even, uneven = (jnp.where(odd == core, pieces[0][pair * rows :], pieces[2][pair * rows :]) for core in (0, 1))
+    kinds = scalars_of(jnp.where(sec < 2, even, uneven)[:1], planes)
     total[...] = jnp.zeros(total.shape, jnp.float32)
 
     @pl.when(sec == 0)
     def _():
         total[...] = total_in[...] + total_beside[...]
 
+    span = stored[0].shape[0]
+
     def after(step, state):
         for where, source in ((sec == 0, series), (sec == last, stored)):
 
             @pl.when(where)
             def _(source=source):
-                total[...] += state[reach : reach + planes] * source[step]
-
-    run_steps(kinds, taps, weights, reach, slab, other, first, second, factor, begun - reach, after)
-    state = (slab, other)[reach % 2]
-
+                total[...] += state[planes : 2 * planes] * source[step // span][step % span]
+
+    run_steps(kinds, taps, weights, planes, slab, other, first, second, factor, 0, after)
+    state = (slab, other)[planes % 2]
     orients = handoff.shape[1]
     count = orients // (last + 1)
-    for i in range(planes):
-        onward[i] = from_tile(state[reach + i], scratch)
-
-    @pl.when(sec < 2)
-    def _():
-        for i in range(planes):
-            handoff[i] = from_tile(kept[i], scratch)
-
-    @pl.when(sec >= 2)
-    def _():
-        handoff[...] = onward[...]
+    held = planes * count
+    to_corner[...] = jnp.zeros(to_corner.shape, jnp.float32)
+    for who, source in ((0, kept), (1, beside_kept), (last, state)):
+
+        @pl.when(sec == who)
+        def _(source=source):
+            begin = planes if source is state else 0
+            for i in range(planes):
+                handoff[i] = from_tile(source[begin + i], scratch)
 
     for i in range(planes):
         whole[...] = from_tile(total[i], scratch)
@@ -430,22 +461,33 @@
             (to_corner, last - sec),
         ):
             piece[i * count : (i + 1) * count] = whole[pl.ds(pl.multiple_of(who * count, count), count)]
-
-
-def finish_kernel(contour, handoff_in, onward, share, to_pair, to_across, to_corner, handoff, density):
+    for i in range(pair):
+        to_across[held + i * orients : held + (i + 1) * orients] = from_tile(
+            state[planes + pair * odd + i], scratch
+        )
+
+    @pl.when(sec == 1)
+    def _():
+        to_corner[...] = to_across[held:]
+
+
+def finish_kernel(contour, handoff_in, share, to_pair, to_across, to_corner, handoff, density):
     sec = lax.axis_index("sec")
     planes, count = density.shape[:2]
-    total = (share[...] + to_pair[...] + to_across[...] + to_corner[...]) / contour
+    held = planes * count
+    corner = jnp.where(sec == 2, 0.0, to_corner[:held])
+    total = (share[...] + to_pair[...] + to_across[:held] + corner) / contour
     for i in range(planes):
         density[i] = total[i * count : (i + 1) * count]
+    handoff[0] = handoff_in[...]
 
     @pl.when(sec == 2)
     def _():
-        handoff[0] = onward[...]
-
-    @pl.when(sec != 2)
-    def _():
-        handoff[0] = handoff_in[...]
+        orients = handoff.shape[2]
+        pair = planes // 2
+        for i in range(pair):
+            handoff[0, i] = to_across[held + i * orients : held + (i + 1) * orients]
+            handoff[0, pair + i] = to_corner[i * orients : (i + 1) * orients]
 
 
 def call(kernel, out_shape, scratch, operands, dtypes=None):
@@ -463,17 +505,13 @@
     n_sec, n_gx = lax.axis_size("sec"), lax.axis_size("gx")
     steps, planes, orients, cells = backward.shape
     pair = planes // 2
-    reach = (TICKS - 1) * steps, steps
-    near = (1, -1)
     rows = 2 * orients
     lanes = cells // 2
     last = n_sec - 1
 
-    def send(array, by_sec, even=0, odd=0):
+    def send(array, by_sec, shift=0):
         by_sec = by_sec.items() if isinstance(by_sec, dict) else enumerate(by_sec)
-        pairs = [
-            (s * n_gx + g, t * n_gx + (g + (odd if s % 2 else even)) % n_gx) for s, t in by_sec for g in range(n_gx)
-        ]
+        pairs = [(s * n_gx + g, t * n_gx + (g + shift) % n_gx) for s, t in by_sec for g in range(n_gx)]
         return lax.ppermute(array, ("sec", "gx"), pairs)
 
     same, beside = (0, 1, 2, 3), (1, 0, 3, 2)
@@ -494,45 +532,58 @@
     packed = pltpu.VMEM((GROUP * rows, 2 * lanes), jnp.bfloat16)
     inner = pltpu.VMEM((planes, rows, lanes), jnp.float32)
 
-    def work(extent):
-        slab = pltpu.VMEM((planes + 2 * extent, rows, lanes), jnp.float32)
-        return [slab, slab, packed, packed, tile]
-
-    (piece,) = call(pack_kernel, [(size, lanes)], [tile], [base, moved, passed, types])
-    own = [send(piece, same, shift, 2 * shift) for shift in near]
-    backward, own_types, _ = lax.optimization_barrier((backward, own_types, piece))
-    across_types = send(own_types, {2: 0})
-    (stored,) = call(turn_kernel, [(steps, planes, rows, lanes)], [tile], [backward])
-    own[-1], stored, across_types = lax.optimization_barrier((own[-1], stored, across_types))
-    swapped = [send(each, beside) for each in own]
-    leaving, *swapped = lax.optimization_barrier((stored, *swapped))
-    arrived = send(leaving, {2: 0})
+    slab = pltpu.VMEM((3 * planes, rows, lanes), jnp.float32)
+    work = [slab, slab, packed, packed, tile]
+    block, half = (planes, rows, lanes), (pair * rows + 8, lanes)
+
+    def exchange(piece, *others):
+        own = [send(piece, same, shift) for shift in (1, -1)]
+        own[-1], *others = lax.optimization_barrier((own[-1], *others))
+        return own + [send(each, beside) for each in own], others
+
+    middle, piece = call(
+        pack_kernel, [block, (pair * rows + PIECE_ROWS, lanes)], [tile], [base, moved, passed, types]
+    )
+    backward, _ = lax.optimization_barrier((backward, piece))
+    stored = call(turn_kernel, [(steps // 2,) + block] * 2, [tile], [backward])
+    pieces, stored = exchange(piece, *stored)
+    leaving, *pieces = lax.optimization_barrier((stored[0], *pieces))
+    arrived = [send(leaving, {2: 0})]
     middle, piece, kept, total, factor = call(
         early_kernel,
-        [(planes, rows, lanes), (pair * rows + 8, lanes), (planes, rows, lanes), (planes, rows, lanes)]
-        + [(fields.shape[0], planes + 2 * reach[0], rows, lanes)],
-        work(reach[0]),
-        [taps, weights, across_types, piece, *own, *swapped, stored],
-    )
-    own = [send(piece, same, shift, shift) for shift in near]
-    beside_total = send(total, beside)
-    swapped = [send(each, beside) for each in own]
-    held = planes * (orients // n_sec), cells
-    handoff, onward, share, to_pair, to_across, to_corner = call(
-        functools.partial(late_kernel, tuple(-shift for shift in near), last),
-        [(planes, orients, cells)] * 2 + [held] * 4,
-        work(reach[1]) + [inner, pltpu.VMEM((orients, cells), jnp.float32)],
-        [taps, weights, middle, *own, *swapped, factor, kept, total, beside_total, arrived, stored],
-    )
-    onward = send(onward, {1: 2})
+        [block, half, block, block, (fields.shape[0], 3 * planes, rows, lanes)],
+        work,
+        [taps, weights, base, middle, *pieces, *stored],
+    )
+    own_types, piece = lax.optimization_barrier((own_types, piece))
+    pieces, (across_types,) = exchange(piece, send(own_types, {2: 0}))
+    leaving, *pieces = lax.optimization_barrier((stored[1], *pieces))
+    arrived.append(send(leaving, {2: 0}))
+    middle, piece, beside_kept, beside_total = call(
+        mid_kernel,
+        [block, half, block, block],
+        work,
+        [taps, weights, across_types, middle, *pieces, factor, *stored],
+    )
+    pieces, _ = exchange(piece)
+    beside_total = send(beside_total, beside)
+    held = planes * (orients // n_sec)
+    handoff, share, to_pair, to_across, to_corner = call(
+        functools.partial(late_kernel, last),
+        [(planes, orients, cells)]
+        + [(held, cells)] * 2
+        + [(held + pair * orients, cells), (pair * orients, cells)],
+        work + [inner, pltpu.VMEM((orients, cells), jnp.float32)],
+        [taps, weights, middle, *pieces, factor, kept, beside_kept, total, beside_total, *arrived, *stored],
+    )
+    to_pair = send(to_pair, beside)
+    to_across = send(to_across, (2, 0, 3, 1))
     to_corner = send(to_corner, (3, 2, 1, 0))
-    to_across = send(to_across, (2, 0, 3, 1))
-    to_pair = send(to_pair, beside)
     handoff, density = call(
         functools.partial(finish_kernel, n_sec * steps),
         [(1,) + handoff.shape, (planes, orients // n_sec, cells)],
         [],
-        [handoff, onward, share, to_pair, to_across, to_corner],
+        [handoff, share, to_pair, to_across, to_corner],
     )
     return handoff, density
 
@@ -543,7 +594,7 @@
         and planes == steps
         and planes % 2 == 0
         and 2 * orients == 2 * CZ == cells // 2 == 128
-        and 2 * kinds * planes <= OWN_KINDS and 10 * kinds * planes <= 2 * orients
+        and 2 * kinds * planes == OWN_KINDS and steps % 2 == 0
         and GROUP < 2 * planes
     )
 

time: 61.1 us -> 66.8 us (1.093)
  waiting for transfers between devices: 21.8 us -> 29.1 us
  Pallas kernels: 14.1 us -> 12.1 us
  starting transfers between devices: 20.9 us -> 21.8 us
    ppermute x18 -> x22, waiting for transfers between devices: 21.8 us -> 29.1 us  [send(): return lax.ppermute(array, ('sec', 'gx'), pairs)]
    pallas_call x6 -> x7, Pallas kernels: 12 us -> 10.1 us  [call(): pl.pallas_call(kernel, in_specs=[IN_VMEM] * len(operands), out_specs=[IN_...]
    ppermute x18 -> x22, starting transfers between devices: 20.9 us -> 21.8 us  [send(): return lax.ppermute(array, ('sec', 'gx'), pairs)]
  transfers between devices with their start and end apart: 18 -> 22, of which waited for: 9 -> 12; matrix products, arithmetic and copies ran while one was open for 1% -> 1% of each run, Pallas kernels for 17% -> 8%
where the time goes in v12:
time: 66.8 us; the launch traced here: 66.5 us
  waiting for transfers between devices  29.1 us (44%)
  starting transfers between devices  21.8 us (33%)
  Pallas kernels  12.1 us (18%)
  local copies, waits for them, and re-layouts  2.02 us (3%)
  between operations  0.8 us (1%)
    ppermute x22, waiting for transfers between devices, send(): return lax.ppermute(array, ('sec', 'gx'), pairs)  29.1 us
    ppermute x22, starting transfers between devices, send(): return lax.ppermute(array, ('sec', 'gx'), pairs)  21.8 us
    pallas_call x7, Pallas kernels, call(): pl.pallas_call(kernel, in_specs=[IN_VMEM] * len(operands), out_specs=[IN_...  10.1 us
    pallas_call x1, Pallas kernels, launch(): pl.pallas_call(launch_kernel, in_specs=[pl.BlockSpec(memory_space=pltpu.H...  2.07 us
    unnamed x4, local copies, waits for them, and re-layouts  2.01 us
  transfers between devices with their start and end apart: 22, of which 12 were waited for; matrix products, arithmetic and copies ran while one was open for 1% of the time, Pallas kernels for 8%

profile of v12, /device:TPU:0, one launch (start us, length us, event | category | flops | bytes accessed | tf_op | source)
XLA Modules:
  0.0 66.5 jit_solution(2904961551617660038)
XLA Ops:
  0.6 2.4 %collective-permute-start = (f32[4,64,256]{2,1,0:T(8,128)}, f32[4,64,256]{2,1,0:T(8,128)S(1)}, u32[]{:S(2)}, u32[]{:S(2)}) collective-permute-start(f32[4,64,256]{2,1,0:T(8,128)} %bitcast.2), channel_id=1, source_target_pairs={{0,8},{1,9},{2,10},{3,11},{4,12},{5,13},{6,14},{7,15},{8,24},{9,25... | collective-permute-start | bytes 786440 | tf_op jit(solution)/shard_map/ppermute | solution.py:515
  3.0 0.7 convert_element_type.5
  3.7 0.6 collective-permute-start.1
  4.3 2.1 %shard_map.104.bundle = f32[680,128]{1,0:T(8,128)} custom-call(f32[1,4,64,256]{3,2,1,0:T(8,128)} %refs_0_.1, f32[3,4,256]{2,1,0:T(4,128)} %refs_1_.1, s32[1,4]{1,0:T(1,128)} %refs_2_.1, f32[3,64]{1,0:T(4,128)} %refs_3_.1, f32[3,64]{1,0:T(4,128)} %refs_4_.1, f32[3,64]{1,0:T(4,128)} %refs_5_.1, f32[1,64]{1,0:T(1,128)} %bitcast.3, f32[64,64]{1,0:T(8,128)} %refs_7_.1), custom_call_target="tpu_custom_call" | custom-call | tf_op jit(solution)/shard_map/pallas_call | solution.py:217
  6.4 0.0 copy-start
  6.4 1.0 %copy-done = f32[680,128]{1,0:T(8,128)S(1)} copy-done((f32[680,128]{1,0:T(8,128)S(1)}, f32[680,128]{1,0:T(8,128)}, u32[]{:S(2)}) %copy-start) | copy-done | bytes 348184
  7.4 0.0 collective-permute-done.1.types
  7.4 0.0 collective-permute-done.moved
  7.4 0.7 %collective-permute-start.2 = (f32[4,64,256]{2,1,0:T(8,128)S(1)}, f32[4,64,256]{2,1,0:T(8,128)S(1)}, u32[]{:S(2)}, u32[]{:S(2)}) collective-permute-start(f32[4,64,256]{2,1,0:T(8,128)S(1)} %collective-permute-done.moved), channel_id=1, source_target_pairs={{24,16},{25,17},{26,18},{27,19},{28,20},{29,21},{30,22},{31,23}} | collective-permute-start | bytes 786440 | tf_op jit(solution)/shard_map/ppermute | solution.py:515
  8.1 0.0 collective-permute-done.2.passed
  8.1 0.1 shard_map.106
  8.2 5.4 %collective-permute-start.3 = (f32[272,128]{1,0:T(8,128)S(1)}, f32[272,128]{1,0:T(8,128)S(1)}, u32[]{:S(2)}, u32[]{:S(2)}) collective-permute-start(f32[272,128]{1,0:T(8,128)S(1)} %get-tuple-element.51), channel_id=1, source_target_pairs={{0,7},{1,0},{2,1},{3,2},{4,3},{5,4},{6,5},{7,6},{8,15},{9,8},{10,9... | collective-permute-start | bytes 417800 | tf_op jit(solution)/shard_map/ppermute | solution.py:515
  13.6 0.0 collective-permute-start.4
  13.6 0.0 copy-start.1
  13.6 1.0 %copy-done.1 = bf16[4,4,64,256]{3,2,1,0:T(8,128)(2,1)S(1)} copy-done((bf16[4,4,64,256]{3,2,1,0:T(8,128)(2,1)S(1)}, bf16[4,4,64,256]{3,2,1,0:T(8,128)(2,1)}, u32[]{:S(2)}) %copy-start.1) | copy-done | bytes 524312
  14.7 0.3 shard_map.107
  15.0 1.6 %collective-permute-done.3.refs_1_ = f32[272,128]{1,0:T(8,128)S(1)} collective-permute-done((f32[272,128]{1,0:T(8,128)S(1)}, f32[272,128]{1,0:T(8,128)S(1)}, u32[]{:S(2)}, u32[]{:S(2)}) %collective-permute-start.3) | collective-permute-done | bytes 139296 | tf_op jit(solution)/shard_map/ppermute | solution.py:515
  16.7 5.5 %collective-permute-done.4.refs_0_ = f32[272,128]{1,0:T(8,128)S(1)} collective-permute-done((f32[272,128]{1,0:T(8,128)S(1)}, f32[272,128]{1,0:T(8,128)S(1)}, u32[]{:S(2)}, u32[]{:S(2)}) %collective-permute-start.4) | collective-permute-done | bytes 139296 | tf_op jit(solution)/shard_map/ppermute | solution.py:515
  22.2 0.5 collective-permute-start.5
  22.7 0.0 collective-permute-start.6
  22.7 1.0 %collective-permute-done.5.refs_2_ = f32[272,128]{1,0:T(8,128)S(1)} collective-permute-done((f32[272,128]{1,0:T(8,128)S(1)}, f32[272,128]{1,0:T(8,128)S(1)}, u32[]{:S(2)}, u32[]{:S(2)}) %collective-permute-start.5) | collective-permute-done | bytes 139296 | tf_op jit(solution)/shard_map/ppermute | solution.py:515
  23.7 0.4 collective-permute-done.6.refs_3_
  24.0 3.3 %shard_map.108 = (f32[4,128,128]{2,1,0:T(8,128)S(1)}, f32[264,128]{1,0:T(8,128)S(1)}, f32[4,128,128]{2,1,0:T(8,128)S(1)}, f32[4,128,128]{2,1,0:T(8,128)S(1)}, f32[3,12,128,128]{3,2,1,0:T(8,128)S(1)}) custom-call(f32[8,128]{1,0:T(8,128)S(1)} %get-tuple-element.44.taps, bf16[256,256]{1,0:T(8,128)(2,1)S(1)} %get-tuple-element.45.weights, ...), custom_call_target="tpu_custom_call" | custom-call | tf_op jit(solution)/shard_map/pallas_call | solution.py:494
  27.4 0.9 %collective-permute-start.7 = (f32[264,128]{1,0:T(8,128)S(1)}, f32[264,128]{1,0:T(8,128)S(1)}, u32[]{:S(2)}, u32[]{:S(2)}) collective-permute-start(f32[264,128]{1,0:T(8,128)S(1)} %get-tuple-element.63), channel_id=1, source_target_pairs={{0,7},{1,0},{2,1},{3,2},{4,3},{5,4},{6,5},{7,6},{8,15},{9,8},{10,9... | collective-permute-start | bytes 405512 | tf_op jit(solution)/shard_map/ppermute | solution.py:515
  28.3 1.2 %collective-permute-start.9 = (f32[264,128]{1,0:T(8,128)S(1)}, f32[264,128]{1,0:T(8,128)S(1)}, u32[]{:S(2)}, u32[]{:S(2)}) collective-permute-start(f32[264,128]{1,0:T(8,128)S(1)} %get-tuple-element.63), channel_id=1, source_target_pairs={{0,1},{1,2},{2,3},{3,4},{4,5},{5,6},{6,7},{7,0},{8,9},{9,10},{10,1... | collective-permute-start | bytes 405512 | tf_op jit(solution)/shard_map/ppermute | solution.py:515
  29.5 1.3 %collective-permute-start.8 = (f32[8,128]{1,0:T(8,128)S(1)}, f32[8,128]{1,0:T(8,128)S(1)}, u32[]{:S(2)}, u32[]{:S(2)}) collective-permute-start(f32[8,128]{1,0:T(8,128)S(1)} %pad.4), channel_id=1, source_target_pairs={{16,0},{17,1},{18,2},{19,3},{20,4},{21,5},{22,6},{23,7}} | collective-permute-start | bytes 12296 | tf_op jit(solution)/shard_map/ppermute | solution.py:515
  30.8 4.9 %collective-permute-done.8.across = f32[8,128]{1,0:T(8,128)S(1)} collective-permute-done((f32[8,128]{1,0:T(8,128)S(1)}, f32[8,128]{1,0:T(8,128)S(1)}, u32[]{:S(2)}, u32[]{:S(2)}) %collective-permute-start.8) | collective-permute-done | bytes 4128 | tf_op jit(solution)/shard_map/ppermute | solution.py:515
  35.7 0.0 collective-permute-done.7.refs_1_
  35.7 0.5 collective-permute-done.9.refs_0_
  36.2 0.0 collective-permute-start.10
  36.2 0.5 collective-permute-start.11
  36.7 1.3 %collective-permute-start.17 = (f32[2,4,128,128]{3,2,1,0:T(8,128)S(1)}, f32[2,4,128,128]{3,2,1,0:T(8,128)S(1)}, u32[]{:S(2)}, u32[]{:S(2)}) collective-permute-start(f32[2,4,128,128]{3,2,1,0:T(8,128)S(1)} %get-tuple-element.79.refs_4_.refs_5_.refs_11_), channel_id=1, source_target_pairs={{16,0},{17,1},{18,2},{19,3},{20,4},{21,5},{22,6},{23,7}} | collective-permute-start | bytes 1572872 | tf_op jit(solution)/shard_map/ppermute | solution.py:515
  38.0 0.0 collective-permute-done.10.refs_2_
  38.0 0.0 collective-permute-done.11.refs_3_
  38.0 1.3 %collective-permute-start.18 = (f32[2,4,128,128]{3,2,1,0:T(8,128)S(1)}, f32[2,4,128,128]{3,2,1,0:T(8,128)S(1)}, u32[]{:S(2)}, u32[]{:S(2)}) collective-permute-start(f32[2,4,128,128]{3,2,1,0:T(8,128)S(1)} %get-tuple-element.80.refs_5_.refs_6_.refs_12_), channel_id=1, source_target_pairs={{16,0},{17,1},{18,2},{19,3},{20,4},{21,5},{22,6},{23,7}} | collective-permute-start | bytes 1572872 | tf_op jit(solution)/shard_map/ppermute | solution.py:515
  39.3 2.5 %shard_map.109 = (f32[4,128,128]{2,1,0:T(8,128)S(1)}, f32[264,128]{1,0:T(8,128)S(1)}, f32[4,128,128]{2,1,0:T(8,128)S(1)}, f32[4,128,128]{2,1,0:T(8,128)S(1)}) custom-call(f32[8,128]{1,0:T(8,128)S(1)} %get-tuple-element.44.taps, bf16[256,256]{1,0:T(8,128)(2,1)S(1)} %get-tuple-element.45.weights, f32[8,128]{1,0:T(8,128)S(1)} %collective-permute-done.8.across, ...), custom_call_target="tpu_custom_call" | custom-call | tf_op jit(solution)/shard_map/pallas_call | solution.py:494
  41.9 3.0 %collective-permute-start.13 = (f32[264,128]{1,0:T(8,128)S(1)}, f32[264,128]{1,0:T(8,128)S(1)}, u32[]{:S(2)}, u32[]{:S(2)}) collective-permute-start(f32[264,128]{1,0:T(8,128)S(1)} %get-tuple-element.74), channel_id=1, source_target_pairs={{0,7},{1,0},{2,1},{3,2},{4,3},{5,4},{6,5},{7,6},{8,15},{9,8},{10,9... | collective-permute-start | bytes 405512 | tf_op jit(solution)/shard_map/ppermute | solution.py:515
  44.9 0.0 collective-permute-start.12
  44.9 0.0 collective-permute-start.16
  44.9 2.6 %collective-permute-done.13.refs_1_ = f32[264,128]{1,0:T(8,128)S(1)} collective-permute-done((f32[264,128]{1,0:T(8,128)S(1)}, f32[264,128]{1,0:T(8,128)S(1)}, u32[]{:S(2)}, u32[]{:S(2)}) %collective-permute-start.13) | collective-permute-done | bytes 135200 | tf_op jit(solution)/shard_map/ppermute | solution.py:515
  47.5 0.0 collective-permute-start.15
  47.5 5.1 %collective-permute-done.12.refs_0_ = f32[264,128]{1,0:T(8,128)S(1)} collective-permute-done((f32[264,128]{1,0:T(8,128)S(1)}, f32[264,128]{1,0:T(8,128)S(1)}, u32[]{:S(2)}, u32[]{:S(2)}) %collective-permute-start.12) | collective-permute-done | bytes 135200 | tf_op jit(solution)/shard_map/ppermute | solution.py:515
  52.6 0.0 collective-permute-start.14
  52.6 0.0 collective-permute-done.17.refs_9_
  52.6 0.0 collective-permute-done.16.refs_8_
  52.6 0.0 collective-permute-done.15.refs_3_
  52.7 1.3 %collective-permute-done.14.refs_2_ = f32[264,128]{1,0:T(8,128)S(1)} collective-permute-done((f32[264,128]{1,0:T(8,128)S(1)}, f32[264,128]{1,0:T(8,128)S(1)}, u32[]{:S(2)}, u32[]{:S(2)}) %collective-permute-start.14) | collective-permute-done | bytes 135200 | tf_op jit(solution)/shard_map/ppermute | solution.py:515
  54.0 0.4 collective-permute-done.18.refs_10_
  54.4 3.0 %shard_map.110 = (f32[4,64,256]{2,1,0:T(8,128)S(1)}, f32[64,256]{1,0:T(8,128)S(1)}, f32[64,256]{1,0:T(8,128)S(1)}, f32[192,256]{1,0:T(8,128)S(1)}, f32[128,256]{1,0:T(8,128)S(1)}) custom-call(f32[8,128]{1,0:T(8,128)S(1)} %get-tuple-element.44.taps, bf16[256,256]{1,0:T(8,128)(2,1)S(1)} %get-tuple-element.45.weights, ...), custom_call_target="tpu_custom_call" | custom-call | tf_op jit(solution)/shard_map/pallas_call | solution.py:494
  57.4 2.0 %collective-permute-start.20 = (f32[192,256]{1,0:T(8,128)S(1)}, f32[192,256]{1,0:T(8,128)S(1)}, u32[]{:S(2)}, u32[]{:S(2)}) collective-permute-start(f32[192,256]{1,0:T(8,128)S(1)} %get-tuple-element.84), channel_id=1, source_target_pairs={{0,16},{1,17},{2,18},{3,19},{4,20},{5,21},{6,22},{7,23},{8,0},{9,1... | collective-permute-start | bytes 589832 | tf_op jit(solution)/shard_map/ppermute | solution.py:515
  59.4 0.2 collective-permute-start.21
  59.6 0.4 collective-permute-start.19
  60.1 0.9 %collective-permute-done.19.to_pair = f32[64,256]{1,0:T(8,128)S(1)} collective-permute-done((f32[64,256]{1,0:T(8,128)S(1)}, f32[64,256]{1,0:T(8,128)S(1)}, u32[]{:S(2)}, u32[]{:S(2)}) %collective-permute-start.19) | collective-permute-done | bytes 65568 | tf_op jit(solution)/shard_map/ppermute | solution.py:515
  61.0 4.7 %collective-permute-done.21.to_corner = f32[128,256]{1,0:T(8,128)S(1)} collective-permute-done((f32[128,256]{1,0:T(8,128)S(1)}, f32[128,256]{1,0:T(8,128)S(1)}, u32[]{:S(2)}, u32[]{:S(2)}) %collective-permute-start.21) | collective-permute-done | bytes 131104 | tf_op jit(solution)/shard_map/ppermute | solution.py:515
  65.7 0.0 collective-permute-done.20.to_across
  65.7 0.8 %shard_map.111 = (f32[1,4,64,256]{3,2,1,0:T(8,128)}, f32[4,16,256]{2,1,0:T(8,128)}) custom-call(f32[4,64,256]{2,1,0:T(8,128)S(1)} %get-tuple-element.81.handoff_in, f32[64,256]{1,0:T(8,128)S(1)} %get-tuple-element.82.share, f32[64,256]{1,0:T(8,128)S(1)} %collective-permute-done.19.to_pair, f32[192,256]{1,0:T(8,128)S(1)} %collective-permute-done.20.to_across, ...), custom_call_target="tpu_custom_call" | custom-call | tf_op jit(solution)/shard_map/pallas_call | solution.py:494
  (2 shorter events, 0.0 us)
Async XLA Ops:
  0.6 6.8 %collective-permute-start = (f32[4,64,256]{2,1,0:T(8,128)}, f32[4,64,256]{2,1,0:T(8,128)S(1)}, u32[]{:S(2)}, u32[]{:S(2)}) collective-permute-start(f32[4,64,256]{2,1,0:T(8,128)} %bitcast.2), channel_id=1, source_target_pairs={{0,8},{1,9},{2,10},{3,11},{4,12},{5,13},{6,14},{7,15},{8,24},{9,25... | collective-permute-start | bytes 786440 | tf_op jit(solution)/shard_map/ppermute | solution.py:515
  3.7 3.8 %collective-permute-start.1 = (f32[8,128]{1,0:T(8,128)S(1)}, f32[8,128]{1,0:T(8,128)S(1)}, u32[]{:S(2)}, u32[]{:S(2)}) collective-permute-start(f32[8,128]{1,0:T(8,128)S(1)} %pad.4), channel_id=1, source_target_pairs={{8,24},{9,25},{10,26},{11,27},{12,28},{13,29},{14,30},{15,31}} | collective-permute-start | bytes 12296 | tf_op jit(solution)/shard_map/ppermute | solution.py:515
  6.4 1.0 %copy-start = (f32[680,128]{1,0:T(8,128)S(1)}, f32[680,128]{1,0:T(8,128)}, u32[]{:S(2)}) copy-start(f32[680,128]{1,0:T(8,128)} %shard_map.104.bundle) | copy-start | bytes 1044484
  7.4 0.7 %collective-permute-start.2 = (f32[4,64,256]{2,1,0:T(8,128)S(1)}, f32[4,64,256]{2,1,0:T(8,128)S(1)}, u32[]{:S(2)}, u32[]{:S(2)}) collective-permute-start(f32[4,64,256]{2,1,0:T(8,128)S(1)} %collective-permute-done.moved), channel_id=1, source_target_pairs={{24,16},{25,17},{26,18},{27,19},{28,20},{29,21},{30,22},{31,23}} | collective-permute-start | bytes 786440 | tf_op jit(solution)/shard_map/ppermute | solution.py:515
  8.2 8.5 %collective-permute-start.3 = (f32[272,128]{1,0:T(8,128)S(1)}, f32[272,128]{1,0:T(8,128)S(1)}, u32[]{:S(2)}, u32[]{:S(2)}) collective-permute-start(f32[272,128]{1,0:T(8,128)S(1)} %get-tuple-element.51), channel_id=1, source_target_pairs={{0,7},{1,0},{2,1},{3,2},{4,3},{5,4},{6,5},{7,6},{8,15},{9,8},{10,9... | collective-permute-start | bytes 417800 | tf_op jit(solution)/shard_map/ppermute | solution.py:515
  13.6 8.5 %collective-permute-start.4 = (f32[272,128]{1,0:T(8,128)S(1)}, f32[272,128]{1,0:T(8,128)S(1)}, u32[]{:S(2)}, u32[]{:S(2)}) collective-permute-start(f32[272,128]{1,0:T(8,128)S(1)} %get-tuple-element.51), channel_id=1, source_target_pairs={{0,1},{1,2},{2,3},{3,4},{4,5},{5,6},{6,7},{7,0},{8,9},{9,10},{10,1... | collective-permute-start | bytes 417800 | tf_op jit(solution)/shard_map/ppermute | solution.py:515
  13.6 1.0 %copy-start.1 = (bf16[4,4,64,256]{3,2,1,0:T(8,128)(2,1)S(1)}, bf16[4,4,64,256]{3,2,1,0:T(8,128)(2,1)}, u32[]{:S(2)}) copy-start(bf16[4,4,64,256]{3,2,1,0:T(8,128)(2,1)} %backward) | copy-start | bytes 1572868
  22.2 1.5 %collective-permute-start.5 = (f32[272,128]{1,0:T(8,128)S(1)}, f32[272,128]{1,0:T(8,128)S(1)}, u32[]{:S(2)}, u32[]{:S(2)}) collective-permute-start(f32[272,128]{1,0:T(8,128)S(1)} %collective-permute-done.4.refs_0_), channel_id=1, source_target_pairs={{0,8},{1,9},{2,10},{3,11},{4,12},{5,13},{6,14},{7,15},{8,0},{9,1},... | collective-permute-start | bytes 417800 | tf_op jit(solution)/shard_map/ppermute | solution.py:515
  22.7 1.4 %collective-permute-start.6 = (f32[272,128]{1,0:T(8,128)S(1)}, f32[272,128]{1,0:T(8,128)S(1)}, u32[]{:S(2)}, u32[]{:S(2)}) collective-permute-start(f32[272,128]{1,0:T(8,128)S(1)} %collective-permute-done.3.refs_1_), channel_id=1, source_target_pairs={{0,8},{1,9},{2,10},{3,11},{4,12},{5,13},{6,14},{7,15},{8,0},{9,1},... | collective-permute-start | bytes 417800 | tf_op jit(solution)/shard_map/ppermute | solution.py:515
  27.4 8.3 %collective-permute-start.7 = (f32[264,128]{1,0:T(8,128)S(1)}, f32[264,128]{1,0:T(8,128)S(1)}, u32[]{:S(2)}, u32[]{:S(2)}) collective-permute-start(f32[264,128]{1,0:T(8,128)S(1)} %get-tuple-element.63), channel_id=1, source_target_pairs={{0,7},{1,0},{2,1},{3,2},{4,3},{5,4},{6,5},{7,6},{8,15},{9,8},{10,9... | collective-permute-start | bytes 405512 | tf_op jit(solution)/shard_map/ppermute | solution.py:515
  28.3 7.9 %collective-permute-start.9 = (f32[264,128]{1,0:T(8,128)S(1)}, f32[264,128]{1,0:T(8,128)S(1)}, u32[]{:S(2)}, u32[]{:S(2)}) collective-permute-start(f32[264,128]{1,0:T(8,128)S(1)} %get-tuple-element.63), channel_id=1, source_target_pairs={{0,1},{1,2},{2,3},{3,4},{4,5},{5,6},{6,7},{7,0},{8,9},{9,10},{10,1... | collective-permute-start | bytes 405512 | tf_op jit(solution)/shard_map/ppermute | solution.py:515
  29.5 6.2 %collective-permute-start.8 = (f32[8,128]{1,0:T(8,128)S(1)}, f32[8,128]{1,0:T(8,128)S(1)}, u32[]{:S(2)}, u32[]{:S(2)}) collective-permute-start(f32[8,128]{1,0:T(8,128)S(1)} %pad.4), channel_id=1, source_target_pairs={{16,0},{17,1},{18,2},{19,3},{20,4},{21,5},{22,6},{23,7}} | collective-permute-start | bytes 12296 | tf_op jit(solution)/shard_map/ppermute | solution.py:515
  36.2 1.8 %collective-permute-start.10 = (f32[264,128]{1,0:T(8,128)S(1)}, f32[264,128]{1,0:T(8,128)S(1)}, u32[]{:S(2)}, u32[]{:S(2)}) collective-permute-start(f32[264,128]{1,0:T(8,128)S(1)} %collective-permute-done.9.refs_0_), channel_id=1, source_target_pairs={{0,8},{1,9},{2,10},{3,11},{4,12},{5,13},{6,14},{7,15},{8,0},{9,1},... | collective-permute-start | bytes 405512 | tf_op jit(solution)/shard_map/ppermute | solution.py:515
  36.2 1.8 %collective-permute-start.11 = (f32[264,128]{1,0:T(8,128)S(1)}, f32[264,128]{1,0:T(8,128)S(1)}, u32[]{:S(2)}, u32[]{:S(2)}) collective-permute-start(f32[264,128]{1,0:T(8,128)S(1)} %collective-permute-done.7.refs_1_), channel_id=1, source_target_pairs={{0,8},{1,9},{2,10},{3,11},{4,12},{5,13},{6,14},{7,15},{8,0},{9,1},... | collective-permute-start | bytes 405512 | tf_op jit(solution)/shard_map/ppermute | solution.py:515
  36.7 15.9 %collective-permute-start.17 = (f32[2,4,128,128]{3,2,1,0:T(8,128)S(1)}, f32[2,4,128,128]{3,2,1,0:T(8,128)S(1)}, u32[]{:S(2)}, u32[]{:S(2)}) collective-permute-start(f32[2,4,128,128]{3,2,1,0:T(8,128)S(1)} %get-tuple-element.79.refs_4_.refs_5_.refs_11_), channel_id=1, source_target_pairs={{16,0},{17,1},{18,2},{19,3},{20,4},{21,5},{22,6},{23,7}} | collective-permute-start | bytes 1572872 | tf_op jit(solution)/shard_map/ppermute | solution.py:515
  38.0 16.4 %collective-permute-start.18 = (f32[2,4,128,128]{3,2,1,0:T(8,128)S(1)}, f32[2,4,128,128]{3,2,1,0:T(8,128)S(1)}, u32[]{:S(2)}, u32[]{:S(2)}) collective-permute-start(f32[2,4,128,128]{3,2,1,0:T(8,128)S(1)} %get-tuple-element.80.refs_5_.refs_6_.refs_12_), channel_id=1, source_target_pairs={{16,0},{17,1},{18,2},{19,3},{20,4},{21,5},{22,6},{23,7}} | collective-permute-start | bytes 1572872 | tf_op jit(solution)/shard_map/ppermute | solution.py:515
  41.9 5.6 %collective-permute-start.13 = (f32[264,128]{1,0:T(8,128)S(1)}, f32[264,128]{1,0:T(8,128)S(1)}, u32[]{:S(2)}, u32[]{:S(2)}) collective-permute-start(f32[264,128]{1,0:T(8,128)S(1)} %get-tuple-element.74), channel_id=1, source_target_pairs={{0,7},{1,0},{2,1},{3,2},{4,3},{5,4},{6,5},{7,6},{8,15},{9,8},{10,9... | collective-permute-start | bytes 405512 | tf_op jit(solution)/shard_map/ppermute | solution.py:515
  44.9 7.7 %collective-permute-start.12 = (f32[264,128]{1,0:T(8,128)S(1)}, f32[264,128]{1,0:T(8,128)S(1)}, u32[]{:S(2)}, u32[]{:S(2)}) collective-permute-start(f32[264,128]{1,0:T(8,128)S(1)} %get-tuple-element.74), channel_id=1, source_target_pairs={{0,1},{1,2},{2,3},{3,4},{4,5},{5,6},{6,7},{7,0},{8,9},{9,10},{10,1... | collective-permute-start | bytes 405512 | tf_op jit(solution)/shard_map/ppermute | solution.py:515
  44.9 7.7 %collective-permute-start.16 = (f32[4,128,128]{2,1,0:T(8,128)S(1)}, f32[4,128,128]{2,1,0:T(8,128)S(1)}, u32[]{:S(2)}, u32[]{:S(2)}) collective-permute-start(f32[4,128,128]{2,1,0:T(8,128)S(1)} %get-tuple-element.78), channel_id=1, source_target_pairs={{0,8},{1,9},{2,10},{3,11},{4,12},{5,13},{6,14},{7,15},{8,0},{9,1},... | collective-permute-start | bytes 786440 | tf_op jit(solution)/shard_map/ppermute | solution.py:515
  47.5 5.2 %collective-permute-start.15 = (f32[264,128]{1,0:T(8,128)S(1)}, f32[264,128]{1,0:T(8,128)S(1)}, u32[]{:S(2)}, u32[]{:S(2)}) collective-permute-start(f32[264,128]{1,0:T(8,128)S(1)} %collective-permute-done.13.refs_1_), channel_id=1, source_target_pairs={{0,8},{1,9},{2,10},{3,11},{4,12},{5,13},{6,14},{7,15},{8,0},{9,1},... | collective-permute-start | bytes 405512 | tf_op jit(solution)/shard_map/ppermute | solution.py:515
  52.6 1.4 %collective-permute-start.14 = (f32[264,128]{1,0:T(8,128)S(1)}, f32[264,128]{1,0:T(8,128)S(1)}, u32[]{:S(2)}, u32[]{:S(2)}) collective-permute-start(f32[264,128]{1,0:T(8,128)S(1)} %collective-permute-done.12.refs_0_), channel_id=1, source_target_pairs={{0,8},{1,9},{2,10},{3,11},{4,12},{5,13},{6,14},{7,15},{8,0},{9,1},... | collective-permute-start | bytes 405512 | tf_op jit(solution)/shard_map/ppermute | solution.py:515
  57.4 8.3 %collective-permute-start.20 = (f32[192,256]{1,0:T(8,128)S(1)}, f32[192,256]{1,0:T(8,128)S(1)}, u32[]{:S(2)}, u32[]{:S(2)}) collective-permute-start(f32[192,256]{1,0:T(8,128)S(1)} %get-tuple-element.84), channel_id=1, source_target_pairs={{0,16},{1,17},{2,18},{3,19},{4,20},{5,21},{6,22},{7,23},{8,0},{9,1... | collective-permute-start | bytes 589832 | tf_op jit(solution)/shard_map/ppermute | solution.py:515
  59.4 6.3 %collective-permute-start.21 = (f32[128,256]{1,0:T(8,128)S(1)}, f32[128,256]{1,0:T(8,128)S(1)}, u32[]{:S(2)}, u32[]{:S(2)}) collective-permute-start(f32[128,256]{1,0:T(8,128)S(1)} %get-tuple-element.85), channel_id=1, source_target_pairs={{0,24},{1,25},{2,26},{3,27},{4,28},{5,29},{6,30},{7,31},{8,16},{9,... | collective-permute-start | bytes 393224 | tf_op jit(solution)/shard_map/ppermute | solution.py:515
  59.6 1.3 %collective-permute-start.19 = (f32[64,256]{1,0:T(8,128)S(1)}, f32[64,256]{1,0:T(8,128)S(1)}, u32[]{:S(2)}, u32[]{:S(2)}) collective-permute-start(f32[64,256]{1,0:T(8,128)S(1)} %get-tuple-element.83), channel_id=1, source_target_pairs={{0,8},{1,9},{2,10},{3,11},{4,12},{5,13},{6,14},{7,15},{8,0},{9,1},... | collective-permute-start | bytes 196616 | tf_op jit(solution)/shard_map/ppermute | solution.py:515

commit v13 on v10

--- a/solution.py
+++ b/solution.py
@@ -12,7 +12,7 @@
 GROUP = 6
 FIELD_ROWS = 32
 TAP_ROWS = 8
-OWN_KINDS, FIRST_KINDS, ACROSS_KINDS = 24, 25, 26
+OWN_KINDS, FIRST_KINDS = 24, 25
 LEAD = 1
 VMEM_BYTES = 16 * 2**20
 WHOLE_VMEM_BYTES = 62 * 2**20
@@ -216,13 +216,14 @@
         for i in range(planes):
             here = (step * planes + i) * orients
             lead[here : here + orients] = stored[step, i].astype(jnp.float32)
+    lead[lead.shape[0] - 8 :] = jnp.broadcast_to(jnp.concatenate([types, types], axis=1), (8, lead.shape[1]))
 
 
 def launch(incoming, backward, fields, kinds, axial, lateral, depth, diagonal, coupling):
     planes, orients, cells = backward.shape[1:]
     rows = 2 * orients
     operands = [incoming, backward, fields, kinds, axial, lateral, depth, diagonal.reshape(1, -1), coupling]
-    shapes = [(LEAD * planes * orients, cells), (TAP_ROWS + rows + FIELD_ROWS + planes * rows, rows)]
+    shapes = [(LEAD * planes * orients + 8, cells), (TAP_ROWS + rows + FIELD_ROWS + planes * rows, rows)]
     taken = [(LEAD,) + each.shape[1:] if i == 1 else each.shape for i, each in enumerate(operands)]
     return pl.pallas_call(
         launch_kernel,
@@ -236,8 +237,9 @@
     )(*operands)
 
 
-def turn_kernel(backward, lead, early, late, out, scratch):
+def turn_kernel(backward, lead, early, late, out, across, scratch):
     orients = scratch.shape[0] // 2
+    across[...] = lead[lead.shape[0] - 8 :, : scratch.shape[1]]
     for target, begin in ((early, 0), (late, LEAD)):
         for step in range(target.shape[0]):
             for i in range(target.shape[1]):
@@ -271,7 +273,6 @@
     out[at + FIRST_KINDS : at + FIRST_KINDS + 1] = jnp.where(
         sec == 0, base[at + OWN_KINDS : at + OWN_KINDS + 1], types[:1]
     )
-    out[at + ACROSS_KINDS : at + ACROSS_KINDS + 1] = types[:1]
 
     @pl.when(sec == 0)
     def _():
@@ -352,7 +353,7 @@
                 factor[kind, start + i] = jnp.take_along_axis(columns, right + at, axis=1, mode="promise_in_bounds")
 
 
-def early_kernel(taps, weights, *refs):
+def early_kernel(taps, weights, across, *refs):
     pieces, stored, (middle, half_out, kept, total, factor) = refs[:5], refs[5:7], refs[7:12]
     slab, other, first, second, scratch = refs[12:]
     sec, odd = position()
@@ -366,13 +367,11 @@
             slab[start + i] = piece[i * rows : (i + 1) * rows]
     at = planes * rows
     steps = LEAD + stored[1].shape[0]
-    own_kinds, first_kinds, across_kinds = (
-        pieces[0][at + row : at + row + 1] for row in (OWN_KINDS, FIRST_KINDS, ACROSS_KINDS)
-    )
+    own_kinds, first_kinds = (pieces[0][at + row : at + row + 1] for row in (OWN_KINDS, FIRST_KINDS))
     beside_kinds, beside_first = (pieces[3][at + row : at + row + 1] for row in (OWN_KINDS, FIRST_KINDS))
     kinds = scalars_of(jnp.where((sec == 1) | (sec == 2), beside_first, first_kinds), steps)
     kinds += scalars_of(jnp.where((sec == 1) | (sec == 2), own_kinds, beside_kinds), steps)
-    last_kinds = jnp.where(sec == 0, across_kinds, own_kinds)
+    last_kinds = jnp.where(sec == 0, across[:1], own_kinds)
     half_out[pair * rows :] = jnp.broadcast_to(last_kinds, (8, rows))
     width = 2 * planes * factor.shape[0]
     lines = [piece[at : at + width] for piece in pieces]
@@ -512,7 +511,7 @@
         incoming, backward, fields, block_types, axial_taps, lateral_taps, depth_taps, bend_diagonal, bend_coupling
     )
     types = jnp.pad(block_types.astype(jnp.float32), ((0, 7), (0, lanes - steps)))
-    types = send(types, {1: 3, 2: 0})
+    types = send(types, {1: 3})
     lead = send(lead, {2: 0})
     size = planes * rows + FIELD_ROWS
     base, taps, weights = call(
@@ -532,9 +531,9 @@
     (piece,) = call(pack_kernel, [(size, lanes)], [tile], [base, moved, passed, types])
     own = [send(piece, same, shift, 2 * shift) for shift in near]
     backward, _ = lax.optimization_barrier((backward, piece))
-    *stored, lead = call(
+    *stored, lead, across = call(
         turn_kernel,
-        [(count, planes, rows, lanes) for count in (LEAD, steps - LEAD, LEAD)],
+        [(count, planes, rows, lanes) for count in (LEAD, steps - LEAD, LEAD)] + [(8, lanes)],
         [tile],
         [backward, lead],
     )
@@ -547,7 +546,7 @@
         [(planes, rows, lanes), (pair * rows + 8, lanes), (planes, rows, lanes), (planes, rows, lanes)]
         + [(fields.shape[0], planes + 2 * reach[0], rows, lanes)],
         work(reach[0]),
-        [taps, weights, piece, *own, *swapped, *stored],
+        [taps, weights, across, piece, *own, *swapped, *stored],
     )
     own = [send(piece, same, shift, shift) for shift in near]
     beside_total = send(total, beside)

time: 60.3 us -> 58.6 us (0.972)
  starting transfers between devices: 21.1 us -> 19.9 us
  waiting for transfers between devices: 21.4 us -> 20.7 us
    ppermute x17, starting transfers between devices: 21.1 us -> 19.9 us  [send(): return lax.ppermute(array, ('sec', 'gx'), pairs)]
    ppermute x17, waiting for transfers between devices: 21.4 us -> 20.7 us  [send(): return lax.ppermute(array, ('sec', 'gx'), pairs)]
  transfers between devices with their start and end apart: 17 -> 17, of which waited for: 9 -> 10; matrix products, arithmetic and copies ran while one was open for 1% -> 1% of each run, Pallas kernels for 17% -> 18%
where the time goes in v13:
time: 58.6 us; the launch traced here: 58.3 us
  waiting for transfers between devices  20.7 us (35%)
  starting transfers between devices  19.9 us (34%)
  Pallas kernels  14.2 us (24%)
  local copies, waits for them, and re-layouts  2.02 us (3%)
  between operations  0.77 us (1%)
  other arithmetic  0.66 us (1%)
    ppermute x17, waiting for transfers between devices, send(): return lax.ppermute(array, ('sec', 'gx'), pairs)  20.7 us
    ppermute x17, starting transfers between devices, send(): return lax.ppermute(array, ('sec', 'gx'), pairs)  19.9 us
    pallas_call x6, Pallas kernels, call(): pl.pallas_call(kernel, in_specs=[IN_VMEM] * len(operands), out_specs=[IN_...  11.9 us
    pallas_call x1, Pallas kernels, launch(): pl.pallas_call(launch_kernel, in_specs=[pl.BlockSpec(memory_space=pltpu.H...  2.26 us
    unnamed x4, local copies, waits for them, and re-layouts  2.01 us
  transfers between devices with their start and end apart: 17, of which 10 were waited for; matrix products, arithmetic and copies ran while one was open for 1% of the time, Pallas kernels for 18%

profile of v13, /device:TPU:0, one launch (start us, length us, event | category | flops | bytes accessed | tf_op | source)
XLA Modules:
  0.0 58.3 jit_solution(11806334410641100458)
XLA Ops:
  0.6 2.4 %collective-permute-start = (f32[4,64,256]{2,1,0:T(8,128)}, f32[4,64,256]{2,1,0:T(8,128)S(1)}, u32[]{:S(2)}, u32[]{:S(2)}) collective-permute-start(f32[4,64,256]{2,1,0:T(8,128)} %bitcast.2), channel_id=1, source_target_pairs={{0,8},{1,9},{2,10},{3,11},{4,12},{5,13},{6,14},{7,15},{8,24},{9,25... | collective-permute-start | bytes 786440 | tf_op jit(solution)/shard_map/ppermute | solution.py:506
  3.0 0.7 %convert_element_type.5 = f32[1,4]{1,0:T(1,128)S(1)} convert(s32[1,4]{1,0:T(1,128)} %refs_3_.1) | non-fusion elementwise | flops 4 | bytes 32 | tf_op jit(solution)/shard_map/convert_element_type | solution.py:513
  3.7 0.6 %collective-permute-start.1 = (f32[8,128]{1,0:T(8,128)S(1)}, f32[8,128]{1,0:T(8,128)S(1)}, u32[]{:S(2)}, u32[]{:S(2)}) collective-permute-start(f32[8,128]{1,0:T(8,128)S(1)} %pad.4), channel_id=1, source_target_pairs={{8,24},{9,25},{10,26},{11,27},{12,28},{13,29},{14,30},{15,31}} | collective-permute-start | bytes 12296 | tf_op jit(solution)/shard_map/ppermute | solution.py:506
  4.3 2.3 %shard_map.104 = (f32[264,256]{1,0:T(8,128)}, f32[680,128]{1,0:T(8,128)}) custom-call(f32[1,4,64,256]{3,2,1,0:T(8,128)} %refs_0_.1, bf16[4,4,64,256]{3,2,1,0:T(8,128)(2,1)} %backward, f32[3,4,256]{2,1,0:T(4,128)} %refs_2_.1, s32[1,4]{1,0:T(1,128)} %refs_3_.1, f32[3,64]{1,0:T(4,128)} %refs_4_.1, f32[3,64]{1,0:T(4,128)} %refs_5_.1, f32[3,64]{1,0:T(4,128)} %refs_6_.1, ...), custom_call_target="tpu_custom_call" | custom-call | tf_op jit(solution)/shard_map/pallas_call | solution.py:228
  6.6 0.0 copy-start.1
  6.6 1.0 %copy-done.1 = f32[680,128]{1,0:T(8,128)S(1)} copy-done((f32[680,128]{1,0:T(8,128)S(1)}, f32[680,128]{1,0:T(8,128)}, u32[]{:S(2)}) %copy-start.1) | copy-done | bytes 348184
  7.6 0.0 collective-permute-done.1.types
  7.6 0.0 collective-permute-done.moved
  7.6 0.7 %collective-permute-start.2 = (f32[4,64,256]{2,1,0:T(8,128)S(1)}, f32[4,64,256]{2,1,0:T(8,128)S(1)}, u32[]{:S(2)}, u32[]{:S(2)}) collective-permute-start(f32[4,64,256]{2,1,0:T(8,128)S(1)} %collective-permute-done.moved), channel_id=1, source_target_pairs={{24,16},{25,17},{26,18},{27,19},{28,20},{29,21},{30,22},{31,23}} | collective-permute-start | bytes 786440 | tf_op jit(solution)/shard_map/ppermute | solution.py:506
  8.3 0.0 collective-permute-done.2.passed
  8.4 5.4 %collective-permute-start.5 = (f32[544,128]{1,0:T(8,128)S(1)}, f32[544,128]{1,0:T(8,128)S(1)}, u32[]{:S(2)}, u32[]{:S(2)}) collective-permute-start(f32[544,128]{1,0:T(8,128)S(1)} %shard_map.106.refs_0_), channel_id=1, source_target_pairs={{0,7},{1,0},{2,1},{3,2},{4,3},{5,4},{6,5},{7,6},{8,14},{9,15},{10,... | collective-permute-start | bytes 835592 | tf_op jit(solution)/shard_map/ppermute | solution.py:506
  13.8 0.0 collective-permute-start.4
  13.8 1.3 %collective-permute-start.3 = (f32[264,256]{1,0:T(8,128)}, f32[264,256]{1,0:T(8,128)S(1)}, u32[]{:S(2)}, u32[]{:S(2)}) collective-permute-start(f32[264,256]{1,0:T(8,128)} %get-tuple-element.39), channel_id=1, source_target_pairs={{16,0},{17,1},{18,2},{19,3},{20,4},{21,5},{22,6},{23,7}} | collective-permute-start | bytes 811016 | tf_op jit(solution)/shard_map/ppermute | solution.py:506
  15.1 8.7 %collective-permute-done.3.lead = f32[264,256]{1,0:T(8,128)S(1)} collective-permute-done((f32[264,256]{1,0:T(8,128)}, f32[264,256]{1,0:T(8,128)S(1)}, u32[]{:S(2)}, u32[]{:S(2)}) %collective-permute-start.3) | collective-permute-done | bytes 270368 | tf_op jit(solution)/shard_map/ppermute | solution.py:506
  23.8 0.0 copy-start
  23.8 1.0 %copy-done = bf16[4,4,64,256]{3,2,1,0:T(8,128)(2,1)S(1)} copy-done((bf16[4,4,64,256]{3,2,1,0:T(8,128)(2,1)S(1)}, bf16[4,4,64,256]{3,2,1,0:T(8,128)(2,1)}, u32[]{:S(2)}) %copy-start) | copy-done | bytes 524312
  24.8 0.4 shard_map.107
  25.2 0.0 collective-permute-done.5.refs_2_
  25.2 0.1 collective-permute-start.7
  25.3 0.5 collective-permute-done.4.refs_1_
  25.9 0.0 collective-permute-start.6
  25.9 1.0 %collective-permute-done.7.refs_4_ = f32[544,128]{1,0:T(8,128)S(1)} collective-permute-done((f32[544,128]{1,0:T(8,128)S(1)}, f32[544,128]{1,0:T(8,128)S(1)}, u32[]{:S(2)}, u32[]{:S(2)}) %collective-permute-start.7) | collective-permute-done | bytes 278560 | tf_op jit(solution)/shard_map/ppermute | solution.py:506
  26.9 0.6 collective-permute-done.6.refs_3_
  27.4 1.3 %collective-permute-start.13 = (f32[3,4,128,128]{3,2,1,0:T(8,128)S(1)}, f32[3,4,128,128]{3,2,1,0:T(8,128)S(1)}, u32[]{:S(2)}, u32[]{:S(2)}) collective-permute-start(f32[3,4,128,128]{3,2,1,0:T(8,128)S(1)} %get-tuple-element.54.refs_6_.refs_11_), channel_id=1, source_target_pairs={{16,0},{17,1},{18,2},{19,3},{20,4},{21,5},{22,6},{23,7}} | collective-permute-start | bytes 2359304 | tf_op jit(solution)/shard_map/ppermute | solution.py:506
  28.7 7.8 %shard_map.108 = (f32[4,128,128]{2,1,0:T(8,128)S(1)}, f32[264,128]{1,0:T(8,128)S(1)}, f32[4,128,128]{2,1,0:T(8,128)S(1)}, f32[4,128,128]{2,1,0:T(8,128)S(1)}, f32[3,20,128,128]{3,2,1,0:T(8,128)S(1)}) custom-call(f32[8,128]{1,0:T(8,128)S(1)} %get-tuple-element.32.taps, bf16[256,256]{1,0:T(8,128)(2,1)S(1)} %get-tuple-element.33.weights, ...), custom_call_target="tpu_custom_call" | custom-call | tf_op jit(solution)/shard_map/pallas_call | solution.py:481
  36.5 0.1 collective-permute-start.8
  36.6 4.7 %collective-permute-start.9 = (f32[264,128]{1,0:T(8,128)S(1)}, f32[264,128]{1,0:T(8,128)S(1)}, u32[]{:S(2)}, u32[]{:S(2)}) collective-permute-start(f32[264,128]{1,0:T(8,128)S(1)} %get-tuple-element.49), channel_id=1, source_target_pairs={{0,7},{1,0},{2,1},{3,2},{4,3},{5,4},{6,5},{7,6},{8,15},{9,8},{10,9... | collective-permute-start | bytes 405512 | tf_op jit(solution)/shard_map/ppermute | solution.py:506
  41.3 0.0 collective-permute-start.12
  41.3 3.2 %collective-permute-done.8.refs_0_ = f32[264,128]{1,0:T(8,128)S(1)} collective-permute-done((f32[264,128]{1,0:T(8,128)S(1)}, f32[264,128]{1,0:T(8,128)S(1)}, u32[]{:S(2)}, u32[]{:S(2)}) %collective-permute-start.8) | collective-permute-done | bytes 135200 | tf_op jit(solution)/shard_map/ppermute | solution.py:506
  44.5 0.0 collective-permute-start.10
  44.5 0.1 collective-permute-done.9.refs_1_
  44.5 0.5 collective-permute-start.11
  45.0 0.0 collective-permute-done.12.refs_7_
  45.0 0.8 %collective-permute-done.10.refs_2_ = f32[264,128]{1,0:T(8,128)S(1)} collective-permute-done((f32[264,128]{1,0:T(8,128)S(1)}, f32[264,128]{1,0:T(8,128)S(1)}, u32[]{:S(2)}, u32[]{:S(2)}) %collective-permute-start.10) | collective-permute-done | bytes 135200 | tf_op jit(solution)/shard_map/ppermute | solution.py:506
  45.8 0.2 collective-permute-done.11.refs_3_
  46.0 0.0 collective-permute-done.13.refs_9_
  46.0 2.9 %shard_map.109 = (f32[4,64,256]{2,1,0:T(8,128)S(1)}, f32[64,256]{1,0:T(8,128)S(1)}, f32[64,256]{1,0:T(8,128)S(1)}, f32[192,256]{1,0:T(8,128)S(1)}, f32[128,256]{1,0:T(8,128)S(1)}) custom-call(f32[8,128]{1,0:T(8,128)S(1)} %get-tuple-element.32.taps, bf16[256,256]{1,0:T(8,128)(2,1)S(1)} %get-tuple-element.33.weights, ...), custom_call_target="tpu_custom_call" | custom-call | tf_op jit(solution)/shard_map/pallas_call | solution.py:481
  49.0 2.2 %collective-permute-start.15 = (f32[192,256]{1,0:T(8,128)S(1)}, f32[192,256]{1,0:T(8,128)S(1)}, u32[]{:S(2)}, u32[]{:S(2)}) collective-permute-start(f32[192,256]{1,0:T(8,128)S(1)} %get-tuple-element.58), channel_id=1, source_target_pairs={{0,16},{1,17},{2,18},{3,19},{4,20},{5,21},{6,22},{7,23},{8,0},{9,1... | collective-permute-start | bytes 589832 | tf_op jit(solution)/shard_map/ppermute | solution.py:506
  51.2 0.2 collective-permute-start.16
  51.4 0.4 collective-permute-start.14
  51.9 0.9 %collective-permute-done.14.to_pair = f32[64,256]{1,0:T(8,128)S(1)} collective-permute-done((f32[64,256]{1,0:T(8,128)S(1)}, f32[64,256]{1,0:T(8,128)S(1)}, u32[]{:S(2)}, u32[]{:S(2)}) %collective-permute-start.14) | collective-permute-done | bytes 65568 | tf_op jit(solution)/shard_map/ppermute | solution.py:506
  52.8 4.7 %collective-permute-done.16.to_corner = f32[128,256]{1,0:T(8,128)S(1)} collective-permute-done((f32[128,256]{1,0:T(8,128)S(1)}, f32[128,256]{1,0:T(8,128)S(1)}, u32[]{:S(2)}, u32[]{:S(2)}) %collective-permute-start.16) | collective-permute-done | bytes 131104 | tf_op jit(solution)/shard_map/ppermute | solution.py:506
  57.5 0.0 collective-permute-done.15.to_across
  57.5 0.8 %shard_map.110 = (f32[1,4,64,256]{3,2,1,0:T(8,128)}, f32[4,16,256]{2,1,0:T(8,128)}) custom-call(f32[4,64,256]{2,1,0:T(8,128)S(1)} %get-tuple-element.55.handoff_in, f32[64,256]{1,0:T(8,128)S(1)} %get-tuple-element.56.share, f32[64,256]{1,0:T(8,128)S(1)} %collective-permute-done.14.to_pair, f32[192,256]{1,0:T(8,128)S(1)} %collective-permute-done.15.to_across, ...), custom_call_target="tpu_custom_call" | custom-call | tf_op jit(solution)/shard_map/pallas_call | solution.py:481
  (3 shorter events, 0.1 us)
Async XLA Ops:
  0.6 7.0 %collective-permute-start = (f32[4,64,256]{2,1,0:T(8,128)}, f32[4,64,256]{2,1,0:T(8,128)S(1)}, u32[]{:S(2)}, u32[]{:S(2)}) collective-permute-start(f32[4,64,256]{2,1,0:T(8,128)} %bitcast.2), channel_id=1, source_target_pairs={{0,8},{1,9},{2,10},{3,11},{4,12},{5,13},{6,14},{7,15},{8,24},{9,25... | collective-permute-start | bytes 786440 | tf_op jit(solution)/shard_map/ppermute | solution.py:506
  3.7 3.9 %collective-permute-start.1 = (f32[8,128]{1,0:T(8,128)S(1)}, f32[8,128]{1,0:T(8,128)S(1)}, u32[]{:S(2)}, u32[]{:S(2)}) collective-permute-start(f32[8,128]{1,0:T(8,128)S(1)} %pad.4), channel_id=1, source_target_pairs={{8,24},{9,25},{10,26},{11,27},{12,28},{13,29},{14,30},{15,31}} | collective-permute-start | bytes 12296 | tf_op jit(solution)/shard_map/ppermute | solution.py:506
  6.6 1.0 %copy-start.1 = (f32[680,128]{1,0:T(8,128)S(1)}, f32[680,128]{1,0:T(8,128)}, u32[]{:S(2)}) copy-start(f32[680,128]{1,0:T(8,128)} %get-tuple-element.31.bundle) | copy-start | bytes 1044484
  7.6 0.7 %collective-permute-start.2 = (f32[4,64,256]{2,1,0:T(8,128)S(1)}, f32[4,64,256]{2,1,0:T(8,128)S(1)}, u32[]{:S(2)}, u32[]{:S(2)}) collective-permute-start(f32[4,64,256]{2,1,0:T(8,128)S(1)} %collective-permute-done.moved), channel_id=1, source_target_pairs={{24,16},{25,17},{26,18},{27,19},{28,20},{29,21},{30,22},{31,23}} | collective-permute-start | bytes 786440 | tf_op jit(solution)/shard_map/ppermute | solution.py:506
  8.4 16.8 %collective-permute-start.5 = (f32[544,128]{1,0:T(8,128)S(1)}, f32[544,128]{1,0:T(8,128)S(1)}, u32[]{:S(2)}, u32[]{:S(2)}) collective-permute-start(f32[544,128]{1,0:T(8,128)S(1)} %shard_map.106.refs_0_), channel_id=1, source_target_pairs={{0,7},{1,0},{2,1},{3,2},{4,3},{5,4},{6,5},{7,6},{8,14},{9,15},{10,... | collective-permute-start | bytes 835592 | tf_op jit(solution)/shard_map/ppermute | solution.py:506
  13.8 12.1 %collective-permute-start.4 = (f32[544,128]{1,0:T(8,128)S(1)}, f32[544,128]{1,0:T(8,128)S(1)}, u32[]{:S(2)}, u32[]{:S(2)}) collective-permute-start(f32[544,128]{1,0:T(8,128)S(1)} %shard_map.106.refs_0_), channel_id=1, source_target_pairs={{0,1},{1,2},{2,3},{3,4},{4,5},{5,6},{6,7},{7,0},{8,10},{9,11},{10,... | collective-permute-start | bytes 835592 | tf_op jit(solution)/shard_map/ppermute | solution.py:506
  13.8 10.0 %collective-permute-start.3 = (f32[264,256]{1,0:T(8,128)}, f32[264,256]{1,0:T(8,128)S(1)}, u32[]{:S(2)}, u32[]{:S(2)}) collective-permute-start(f32[264,256]{1,0:T(8,128)} %get-tuple-element.39), channel_id=1, source_target_pairs={{16,0},{17,1},{18,2},{19,3},{20,4},{21,5},{22,6},{23,7}} | collective-permute-start | bytes 811016 | tf_op jit(solution)/shard_map/ppermute | solution.py:506
  23.8 1.0 %copy-start = (bf16[4,4,64,256]{3,2,1,0:T(8,128)(2,1)S(1)}, bf16[4,4,64,256]{3,2,1,0:T(8,128)(2,1)}, u32[]{:S(2)}) copy-start(bf16[4,4,64,256]{3,2,1,0:T(8,128)(2,1)} %backward) | copy-start | bytes 1572868
  25.2 1.6 %collective-permute-start.7 = (f32[544,128]{1,0:T(8,128)S(1)}, f32[544,128]{1,0:T(8,128)S(1)}, u32[]{:S(2)}, u32[]{:S(2)}) collective-permute-start(f32[544,128]{1,0:T(8,128)S(1)} %collective-permute-done.5.refs_2_), channel_id=1, source_target_pairs={{0,8},{1,9},{2,10},{3,11},{4,12},{5,13},{6,14},{7,15},{8,0},{9,1},... | collective-permute-start | bytes 835592 | tf_op jit(solution)/shard_map/ppermute | solution.py:506
  25.9 1.6 %collective-permute-start.6 = (f32[544,128]{1,0:T(8,128)S(1)}, f32[544,128]{1,0:T(8,128)S(1)}, u32[]{:S(2)}, u32[]{:S(2)}) collective-permute-start(f32[544,128]{1,0:T(8,128)S(1)} %collective-permute-done.4.refs_1_), channel_id=1, source_target_pairs={{0,8},{1,9},{2,10},{3,11},{4,12},{5,13},{6,14},{7,15},{8,0},{9,1},... | collective-permute-start | bytes 835592 | tf_op jit(solution)/shard_map/ppermute | solution.py:506
  27.4 18.6 %collective-permute-start.13 = (f32[3,4,128,128]{3,2,1,0:T(8,128)S(1)}, f32[3,4,128,128]{3,2,1,0:T(8,128)S(1)}, u32[]{:S(2)}, u32[]{:S(2)}) collective-permute-start(f32[3,4,128,128]{3,2,1,0:T(8,128)S(1)} %get-tuple-element.54.refs_6_.refs_11_), channel_id=1, source_target_pairs={{16,0},{17,1},{18,2},{19,3},{20,4},{21,5},{22,6},{23,7}} | collective-permute-start | bytes 2359304 | tf_op jit(solution)/shard_map/ppermute | solution.py:506
  36.5 8.0 %collective-permute-start.8 = (f32[264,128]{1,0:T(8,128)S(1)}, f32[264,128]{1,0:T(8,128)S(1)}, u32[]{:S(2)}, u32[]{:S(2)}) collective-permute-start(f32[264,128]{1,0:T(8,128)S(1)} %get-tuple-element.49), channel_id=1, source_target_pairs={{0,1},{1,2},{2,3},{3,4},{4,5},{5,6},{6,7},{7,0},{8,9},{9,10},{10,1... | collective-permute-start | bytes 405512 | tf_op jit(solution)/shard_map/ppermute | solution.py:506
  36.6 8.0 %collective-permute-start.9 = (f32[264,128]{1,0:T(8,128)S(1)}, f32[264,128]{1,0:T(8,128)S(1)}, u32[]{:S(2)}, u32[]{:S(2)}) collective-permute-start(f32[264,128]{1,0:T(8,128)S(1)} %get-tuple-element.49), channel_id=1, source_target_pairs={{0,7},{1,0},{2,1},{3,2},{4,3},{5,4},{6,5},{7,6},{8,15},{9,8},{10,9... | collective-permute-start | bytes 405512 | tf_op jit(solution)/shard_map/ppermute | solution.py:506
  41.3 3.7 %collective-permute-start.12 = (f32[4,128,128]{2,1,0:T(8,128)S(1)}, f32[4,128,128]{2,1,0:T(8,128)S(1)}, u32[]{:S(2)}, u32[]{:S(2)}) collective-permute-start(f32[4,128,128]{2,1,0:T(8,128)S(1)} %get-tuple-element.52.refs_6_), channel_id=1, source_target_pairs={{0,8},{1,9},{2,10},{3,11},{4,12},{5,13},{6,14},{7,15},{8,0},{9,1},... | collective-permute-start | bytes 786440 | tf_op jit(solution)/shard_map/ppermute | solution.py:506
  44.5 1.4 %collective-permute-start.10 = (f32[264,128]{1,0:T(8,128)S(1)}, f32[264,128]{1,0:T(8,128)S(1)}, u32[]{:S(2)}, u32[]{:S(2)}) collective-permute-start(f32[264,128]{1,0:T(8,128)S(1)} %collective-permute-done.8.refs_0_), channel_id=1, source_target_pairs={{0,8},{1,9},{2,10},{3,11},{4,12},{5,13},{6,14},{7,15},{8,0},{9,1},... | collective-permute-start | bytes 405512 | tf_op jit(solution)/shard_map/ppermute | solution.py:506
  44.5 1.5 %collective-permute-start.11 = (f32[264,128]{1,0:T(8,128)S(1)}, f32[264,128]{1,0:T(8,128)S(1)}, u32[]{:S(2)}, u32[]{:S(2)}) collective-permute-start(f32[264,128]{1,0:T(8,128)S(1)} %collective-permute-done.9.refs_1_), channel_id=1, source_target_pairs={{0,8},{1,9},{2,10},{3,11},{4,12},{5,13},{6,14},{7,15},{8,0},{9,1},... | collective-permute-start | bytes 405512 | tf_op jit(solution)/shard_map/ppermute | solution.py:506
  49.0 8.6 %collective-permute-start.15 = (f32[192,256]{1,0:T(8,128)S(1)}, f32[192,256]{1,0:T(8,128)S(1)}, u32[]{:S(2)}, u32[]{:S(2)}) collective-permute-start(f32[192,256]{1,0:T(8,128)S(1)} %get-tuple-element.58), channel_id=1, source_target_pairs={{0,16},{1,17},{2,18},{3,19},{4,20},{5,21},{6,22},{7,23},{8,0},{9,1... | collective-permute-start | bytes 589832 | tf_op jit(solution)/shard_map/ppermute | solution.py:506
  51.2 6.3 %collective-permute-start.16 = (f32[128,256]{1,0:T(8,128)S(1)}, f32[128,256]{1,0:T(8,128)S(1)}, u32[]{:S(2)}, u32[]{:S(2)}) collective-permute-start(f32[128,256]{1,0:T(8,128)S(1)} %get-tuple-element.59), channel_id=1, source_target_pairs={{0,24},{1,25},{2,26},{3,27},{4,28},{5,29},{6,30},{7,31},{8,16},{9,... | collective-permute-start | bytes 393224 | tf_op jit(solution)/shard_map/ppermute | solution.py:506
  51.4 1.3 %collective-permute-start.14 = (f32[64,256]{1,0:T(8,128)S(1)}, f32[64,256]{1,0:T(8,128)S(1)}, u32[]{:S(2)}, u32[]{:S(2)}) collective-permute-start(f32[64,256]{1,0:T(8,128)S(1)} %get-tuple-element.57), channel_id=1, source_target_pairs={{0,8},{1,9},{2,10},{3,11},{4,12},{5,13},{6,14},{7,15},{8,0},{9,1},... | collective-permute-start | bytes 196616 | tf_op jit(solution)/shard_map/ppermute | solution.py:506

commit v14 on v13

--- a/solution.py
+++ b/solution.py
@@ -344,7 +344,7 @@
 
 def spread_factor(columns, factor, starts, width):
     rows, lanes = factor.shape[2:]
-    pair = factor.shape[1] // len(starts)
+    pair = width // (2 * factor.shape[0])
     right = (lax.broadcasted_iota(jnp.int32, (rows, lanes), 1) >= lanes // 2).astype(jnp.int32)
     for piece, start in enumerate(starts):
         for kind in range(factor.shape[0]):
@@ -353,15 +353,36 @@
                 factor[kind, start + i] = jnp.take_along_axis(columns, right + at, axis=1, mode="promise_in_bounds")
 
 
+def slab_starts(planes, reach):
+    odd = position()[1]
+    mine, others = (planes * (1 + core) for core in (odd, 1 - odd))
+    return [reach, reach - mine, reach + mine, reach - others, reach + others]
+
+
+def fill_factor(pieces, starts, factor, scratch):
+    rows = scratch.shape[0]
+    planes = (pieces[0].shape[0] - FIELD_ROWS) // rows
+    width = 2 * planes * factor.shape[0]
+    lines = [piece[planes * rows : planes * rows + width] for piece in pieces]
+    lines.append(jnp.zeros((rows - width * len(pieces), rows), jnp.float32))
+    scratch[...] = jnp.exp(-jnp.concatenate(lines, axis=0)).T
+    spread_factor(reorder(scratch), factor, starts, width)
+
+
+def factor_kernel(*refs):
+    pieces, factor, scratch = refs[:3], refs[3], refs[4]
+    planes = (pieces[0].shape[0] - FIELD_ROWS) // scratch.shape[0]
+    fill_factor(pieces, slab_starts(planes, (factor.shape[1] - planes) // 2)[:3], factor, scratch)
+
+
 def early_kernel(taps, weights, across, *refs):
-    pieces, stored, (middle, half_out, kept, total, factor) = refs[:5], refs[5:7], refs[7:12]
-    slab, other, first, second, scratch = refs[12:]
+    pieces, stored, (middle, half_out, kept, total, factor) = refs[:5], refs[5:7], refs[8:13]
+    slab, other, first, second, scratch = refs[13:]
     sec, odd = position()
     planes, rows = middle.shape[:2]
     pair = planes // 2
     reach = (slab.shape[0] - planes) // 2
-    mine, others = (planes * (1 + core) for core in (odd, 1 - odd))
-    starts = [reach, reach - mine, reach + mine, reach - others, reach + others]
+    starts = slab_starts(planes, reach)
     for piece, start in zip(pieces, starts):
         for i in range(planes):
             slab[start + i] = piece[i * rows : (i + 1) * rows]
@@ -373,11 +394,7 @@
     kinds += scalars_of(jnp.where((sec == 1) | (sec == 2), own_kinds, beside_kinds), steps)
     last_kinds = jnp.where(sec == 0, across[:1], own_kinds)
     half_out[pair * rows :] = jnp.broadcast_to(last_kinds, (8, rows))
-    width = 2 * planes * factor.shape[0]
-    lines = [piece[at : at + width] for piece in pieces]
-    lines.append(jnp.zeros((rows - width * len(pieces), rows), jnp.float32))
-    scratch[...] = jnp.exp(-jnp.concatenate(lines, axis=0)).T
-    spread_factor(reorder(scratch), factor, starts, width)
+    fill_factor(pieces[3:], starts[3:], factor, scratch)
     total[...] = jnp.zeros(total.shape, jnp.float32)
     kept[...] = jnp.zeros(kept.shape, jnp.float32)
 
@@ -477,13 +494,15 @@
             handoff[0, pair + i] = to_corner[i * orients : (i + 1) * orients]
 
 
-def call(kernel, out_shape, scratch, operands, dtypes=None):
+def call(kernel, out_shape, scratch, operands, dtypes=None, aliases=None, cost=None):
     return pl.pallas_call(
         kernel,
         in_specs=[IN_VMEM] * len(operands),
         out_specs=[IN_VMEM] * len(out_shape),
         out_shape=[jax.ShapeDtypeStruct(shape, (dtypes or {}).get(i, jnp.float32)) for i, shape in enumerate(out_shape)],
         scratch_shapes=scratch,
+        input_output_aliases=aliases or {},
+        cost_estimate=cost,
         compiler_params=pltpu.CompilerParams(vmem_limit_bytes=VMEM_BYTES),
     )(*operands)
 
@@ -539,14 +558,18 @@
     )
     own[-1], *stored = lax.optimization_barrier((own[-1], *stored))
     swapped = [send(each, beside) for each in own]
-    late_stored, *swapped = lax.optimization_barrier((stored[1], *swapped))
+    table = (fields.shape[0], planes + 2 * reach[0], rows, lanes)
+    known, swapped[1] = lax.optimization_barrier((piece, swapped[1]))
+    (factor,) = call(factor_kernel, [table], [tile], [known, *own])
+    late_stored, factor, *swapped = lax.optimization_barrier((stored[1], factor, *swapped))
     late_last = send(late_stored, {2: 0})
     middle, piece, kept, total, factor = call(
         early_kernel,
         [(planes, rows, lanes), (pair * rows + 8, lanes), (planes, rows, lanes), (planes, rows, lanes)]
-        + [(fields.shape[0], planes + 2 * reach[0], rows, lanes)],
+        + [table],
         work(reach[0]),
-        [taps, weights, across, piece, *own, *swapped, *stored],
+        [taps, weights, across, piece, *own, *swapped, *stored, factor],
+        aliases={10: 4},
     )
     own = [send(piece, same, shift, shift) for shift in near]
     beside_total = send(total, beside)

time: 58.6 us -> 62.6 us (1.068)
  waiting for transfers between devices: 20.7 us -> 24.9 us
    ppermute x17, waiting for transfers between devices: 20.7 us -> 24.9 us  [send(): return lax.ppermute(array, ('sec', 'gx'), pairs)]
    pallas_call x6 -> x7, Pallas kernels: 11.9 us -> 12.2 us  [call(): pl.pallas_call(kernel, in_specs=[IN_VMEM] * len(operands), out_specs=[IN_...]
  transfers between devices with their start and end apart: 17 -> 17, of which waited for: 10 -> 8; matrix products, arithmetic and copies ran while one was open for 1% -> 1% of each run, Pallas kernels for 18% -> 17%
where the time goes in v14:
time: 62.6 us; the launch traced here: 62.3 us
  waiting for transfers between devices  24.9 us (40%)
  starting transfers between devices  19.5 us (31%)
  Pallas kernels  14.4 us (23%)
  local copies, waits for them, and re-layouts  2.02 us (3%)
  between operations  0.78 us (1%)
  other arithmetic  0.66 us (1%)
    ppermute x17, waiting for transfers between devices, send(): return lax.ppermute(array, ('sec', 'gx'), pairs)  24.9 us
    ppermute x17, starting transfers between devices, send(): return lax.ppermute(array, ('sec', 'gx'), pairs)  19.5 us
    pallas_call x7, Pallas kernels, call(): pl.pallas_call(kernel, in_specs=[IN_VMEM] * len(operands), out_specs=[IN_...  12.2 us
    pallas_call x1, Pallas kernels, launch(): pl.pallas_call(launch_kernel, in_specs=[pl.BlockSpec(memory_space=pltpu.H...  2.26 us
    unnamed x4, local copies, waits for them, and re-layouts  2.01 us
  transfers between devices with their start and end apart: 17, of which 8 were waited for; matrix products, arithmetic and copies ran while one was open for 1% of the time, Pallas kernels for 17%

profile of v14, /device:TPU:0, one launch (start us, length us, event | category | flops | bytes accessed | tf_op | source)
XLA Modules:
  0.0 62.3 jit_solution(10696482514281302664)
XLA Ops:
  0.6 2.4 %collective-permute-start = (f32[4,64,256]{2,1,0:T(8,128)}, f32[4,64,256]{2,1,0:T(8,128)S(1)}, u32[]{:S(2)}, u32[]{:S(2)}) collective-permute-start(f32[4,64,256]{2,1,0:T(8,128)} %bitcast.2), channel_id=1, source_target_pairs={{0,8},{1,9},{2,10},{3,11},{4,12},{5,13},{6,14},{7,15},{8,24},{9,25... | collective-permute-start | bytes 786440 | tf_op jit(solution)/shard_map/ppermute | solution.py:525
  3.0 0.7 %convert_element_type.5 = f32[1,4]{1,0:T(1,128)S(1)} convert(s32[1,4]{1,0:T(1,128)} %refs_3_.1) | non-fusion elementwise | flops 4 | bytes 32 | tf_op jit(solution)/shard_map/convert_element_type | solution.py:532
  3.7 0.6 %collective-permute-start.1 = (f32[8,128]{1,0:T(8,128)S(1)}, f32[8,128]{1,0:T(8,128)S(1)}, u32[]{:S(2)}, u32[]{:S(2)}) collective-permute-start(f32[8,128]{1,0:T(8,128)S(1)} %pad.4), channel_id=1, source_target_pairs={{8,24},{9,25},{10,26},{11,27},{12,28},{13,29},{14,30},{15,31}} | collective-permute-start | bytes 12296 | tf_op jit(solution)/shard_map/ppermute | solution.py:525
  4.3 2.3 %shard_map.104 = (f32[264,256]{1,0:T(8,128)}, f32[680,128]{1,0:T(8,128)}) custom-call(f32[1,4,64,256]{3,2,1,0:T(8,128)} %refs_0_.1, bf16[4,4,64,256]{3,2,1,0:T(8,128)(2,1)} %backward, f32[3,4,256]{2,1,0:T(4,128)} %refs_2_.1, s32[1,4]{1,0:T(1,128)} %refs_3_.1, f32[3,64]{1,0:T(4,128)} %refs_4_.1, f32[3,64]{1,0:T(4,128)} %refs_5_.1, f32[3,64]{1,0:T(4,128)} %refs_6_.1, ...), custom_call_target="tpu_custom_call" | custom-call | tf_op jit(solution)/shard_map/pallas_call | solution.py:228
  6.6 0.0 copy-start.1
  6.6 1.0 %copy-done.1 = f32[680,128]{1,0:T(8,128)S(1)} copy-done((f32[680,128]{1,0:T(8,128)S(1)}, f32[680,128]{1,0:T(8,128)}, u32[]{:S(2)}) %copy-start.1) | copy-done | bytes 348184
  7.6 0.0 collective-permute-done.1.types
  7.6 0.0 collective-permute-done.moved
  7.6 0.7 %collective-permute-start.2 = (f32[4,64,256]{2,1,0:T(8,128)S(1)}, f32[4,64,256]{2,1,0:T(8,128)S(1)}, u32[]{:S(2)}, u32[]{:S(2)}) collective-permute-start(f32[4,64,256]{2,1,0:T(8,128)S(1)} %collective-permute-done.moved), channel_id=1, source_target_pairs={{24,16},{25,17},{26,18},{27,19},{28,20},{29,21},{30,22},{31,23}} | collective-permute-start | bytes 786440 | tf_op jit(solution)/shard_map/ppermute | solution.py:525
  8.3 0.0 collective-permute-done.2.passed
  8.4 5.4 %collective-permute-start.5 = (f32[544,128]{1,0:T(8,128)S(1)}, f32[544,128]{1,0:T(8,128)S(1)}, u32[]{:S(2)}, u32[]{:S(2)}) collective-permute-start(f32[544,128]{1,0:T(8,128)S(1)} %shard_map.106.refs_0_), channel_id=1, source_target_pairs={{0,7},{1,0},{2,1},{3,2},{4,3},{5,4},{6,5},{7,6},{8,14},{9,15},{10,... | collective-permute-start | bytes 835592 | tf_op jit(solution)/shard_map/ppermute | solution.py:525
  13.8 0.0 collective-permute-start.4
  13.8 1.3 %collective-permute-start.3 = (f32[264,256]{1,0:T(8,128)}, f32[264,256]{1,0:T(8,128)S(1)}, u32[]{:S(2)}, u32[]{:S(2)}) collective-permute-start(f32[264,256]{1,0:T(8,128)} %get-tuple-element.42), channel_id=1, source_target_pairs={{16,0},{17,1},{18,2},{19,3},{20,4},{21,5},{22,6},{23,7}} | collective-permute-start | bytes 811016 | tf_op jit(solution)/shard_map/ppermute | solution.py:525
  15.1 8.7 %collective-permute-done.3.lead = f32[264,256]{1,0:T(8,128)S(1)} collective-permute-done((f32[264,256]{1,0:T(8,128)}, f32[264,256]{1,0:T(8,128)S(1)}, u32[]{:S(2)}, u32[]{:S(2)}) %collective-permute-start.3) | collective-permute-done | bytes 270368 | tf_op jit(solution)/shard_map/ppermute | solution.py:525
  23.8 0.0 copy-start
  23.8 1.0 %copy-done = bf16[4,4,64,256]{3,2,1,0:T(8,128)(2,1)S(1)} copy-done((bf16[4,4,64,256]{3,2,1,0:T(8,128)(2,1)S(1)}, bf16[4,4,64,256]{3,2,1,0:T(8,128)(2,1)}, u32[]{:S(2)}) %copy-start) | copy-done | bytes 524312
  24.8 0.4 shard_map.107
  25.2 0.0 collective-permute-done.5.refs_2_
  25.2 0.1 collective-permute-start.6
  25.3 0.5 collective-permute-done.4.refs_1_
  25.9 0.0 collective-permute-start.7
  25.9 1.0 %collective-permute-done.6.refs_4_ = f32[544,128]{1,0:T(8,128)S(1)} collective-permute-done((f32[544,128]{1,0:T(8,128)S(1)}, f32[544,128]{1,0:T(8,128)S(1)}, u32[]{:S(2)}, u32[]{:S(2)}) %collective-permute-start.6) | collective-permute-done | bytes 278560 | tf_op jit(solution)/shard_map/ppermute | solution.py:525
  26.9 0.9 %shard_map.108.refs_7_ = f32[3,20,128,128]{3,2,1,0:T(8,128)S(1)} custom-call(f32[544,128]{1,0:T(8,128)S(1)} %shard_map.106.refs_0_, f32[544,128]{1,0:T(8,128)S(1)} %collective-permute-done.4.refs_1_, f32[544,128]{1,0:T(8,128)S(1)} %collective-permute-done.5.refs_2_), custom_call_target="tpu_custom_call" | custom-call | tf_op jit(solution)/shard_map/pallas_call | solution.py:498
  27.8 0.0 collective-permute-done.7.refs_3_
  27.8 1.3 %collective-permute-start.13 = (f32[3,4,128,128]{3,2,1,0:T(8,128)S(1)}, f32[3,4,128,128]{3,2,1,0:T(8,128)S(1)}, u32[]{:S(2)}, u32[]{:S(2)}) collective-permute-start(f32[3,4,128,128]{3,2,1,0:T(8,128)S(1)} %get-tuple-element.60.refs_6_.refs_11_), channel_id=1, source_target_pairs={{16,0},{17,1},{18,2},{19,3},{20,4},{21,5},{22,6},{23,7}} | collective-permute-start | bytes 2359304 | tf_op jit(solution)/shard_map/ppermute | solution.py:525
  29.1 7.1 %shard_map.109 = (f32[4,128,128]{2,1,0:T(8,128)S(1)}, f32[264,128]{1,0:T(8,128)S(1)}, f32[4,128,128]{2,1,0:T(8,128)S(1)}, f32[4,128,128]{2,1,0:T(8,128)S(1)}, f32[3,20,128,128]{3,2,1,0:T(8,128)S(1)}) custom-call(f32[8,128]{1,0:T(8,128)S(1)} %get-tuple-element.35.taps, ...), custom_call_target="tpu_custom_call", output_to_operand_aliasing={{4}: (10, {})} | custom-call | tf_op jit(solution)/shard_map/pallas_call | solution.py:498
  36.2 4.8 %collective-permute-start.9 = (f32[264,128]{1,0:T(8,128)S(1)}, f32[264,128]{1,0:T(8,128)S(1)}, u32[]{:S(2)}, u32[]{:S(2)}) collective-permute-start(f32[264,128]{1,0:T(8,128)S(1)} %get-tuple-element.55), channel_id=1, source_target_pairs={{0,7},{1,0},{2,1},{3,2},{4,3},{5,4},{6,5},{7,6},{8,15},{9,8},{10,9... | collective-permute-start | bytes 405512 | tf_op jit(solution)/shard_map/ppermute | solution.py:525
  41.0 0.0 collective-permute-start.8
  41.0 0.0 collective-permute-start.12
  41.0 2.6 %collective-permute-done.9.refs_1_ = f32[264,128]{1,0:T(8,128)S(1)} collective-permute-done((f32[264,128]{1,0:T(8,128)S(1)}, f32[264,128]{1,0:T(8,128)S(1)}, u32[]{:S(2)}, u32[]{:S(2)}) %collective-permute-start.9) | collective-permute-done | bytes 135200 | tf_op jit(solution)/shard_map/ppermute | solution.py:525
  43.6 0.0 collective-permute-start.11
  43.6 5.1 %collective-permute-done.8.refs_0_ = f32[264,128]{1,0:T(8,128)S(1)} collective-permute-done((f32[264,128]{1,0:T(8,128)S(1)}, f32[264,128]{1,0:T(8,128)S(1)}, u32[]{:S(2)}, u32[]{:S(2)}) %collective-permute-start.8) | collective-permute-done | bytes 135200 | tf_op jit(solution)/shard_map/ppermute | solution.py:525
  48.7 0.0 collective-permute-start.10
  48.7 0.0 collective-permute-done.12.refs_7_
  48.7 0.0 collective-permute-done.11.refs_3_
  48.7 1.3 %collective-permute-done.10.refs_2_ = f32[264,128]{1,0:T(8,128)S(1)} collective-permute-done((f32[264,128]{1,0:T(8,128)S(1)}, f32[264,128]{1,0:T(8,128)S(1)}, u32[]{:S(2)}, u32[]{:S(2)}) %collective-permute-start.10) | collective-permute-done | bytes 135200 | tf_op jit(solution)/shard_map/ppermute | solution.py:525
  50.1 0.0 collective-permute-done.13.refs_9_
  50.1 2.9 %shard_map.110 = (f32[4,64,256]{2,1,0:T(8,128)S(1)}, f32[64,256]{1,0:T(8,128)S(1)}, f32[64,256]{1,0:T(8,128)S(1)}, f32[192,256]{1,0:T(8,128)S(1)}, f32[128,256]{1,0:T(8,128)S(1)}) custom-call(f32[8,128]{1,0:T(8,128)S(1)} %get-tuple-element.35.taps, bf16[256,256]{1,0:T(8,128)(2,1)S(1)} %get-tuple-element.36.weights, ...), custom_call_target="tpu_custom_call" | custom-call | tf_op jit(solution)/shard_map/pallas_call | solution.py:498
  52.9 2.5 %collective-permute-start.15 = (f32[192,256]{1,0:T(8,128)S(1)}, f32[192,256]{1,0:T(8,128)S(1)}, u32[]{:S(2)}, u32[]{:S(2)}) collective-permute-start(f32[192,256]{1,0:T(8,128)S(1)} %get-tuple-element.64), channel_id=1, source_target_pairs={{0,16},{1,17},{2,18},{3,19},{4,20},{5,21},{6,22},{7,23},{8,0},{9,1... | collective-permute-start | bytes 589832 | tf_op jit(solution)/shard_map/ppermute | solution.py:525
  55.4 0.1 collective-permute-start.16
  55.5 0.4 collective-permute-start.14
  55.9 0.9 %collective-permute-done.14.to_pair = f32[64,256]{1,0:T(8,128)S(1)} collective-permute-done((f32[64,256]{1,0:T(8,128)S(1)}, f32[64,256]{1,0:T(8,128)S(1)}, u32[]{:S(2)}, u32[]{:S(2)}) %collective-permute-start.14) | collective-permute-done | bytes 65568 | tf_op jit(solution)/shard_map/ppermute | solution.py:525
  56.8 4.7 %collective-permute-done.16.to_corner = f32[128,256]{1,0:T(8,128)S(1)} collective-permute-done((f32[128,256]{1,0:T(8,128)S(1)}, f32[128,256]{1,0:T(8,128)S(1)}, u32[]{:S(2)}, u32[]{:S(2)}) %collective-permute-start.16) | collective-permute-done | bytes 131104 | tf_op jit(solution)/shard_map/ppermute | solution.py:525
  61.6 0.0 collective-permute-done.15.to_across
  61.6 0.8 %shard_map.111 = (f32[1,4,64,256]{3,2,1,0:T(8,128)}, f32[4,16,256]{2,1,0:T(8,128)}) custom-call(f32[4,64,256]{2,1,0:T(8,128)S(1)} %get-tuple-element.61.handoff_in, f32[64,256]{1,0:T(8,128)S(1)} %get-tuple-element.62.share, f32[64,256]{1,0:T(8,128)S(1)} %collective-permute-done.14.to_pair, f32[192,256]{1,0:T(8,128)S(1)} %collective-permute-done.15.to_across, ...), custom_call_target="tpu_custom_call" | custom-call | tf_op jit(solution)/shard_map/pallas_call | solution.py:498
  (3 shorter events, 0.1 us)
Async XLA Ops:
  0.6 7.0 %collective-permute-start = (f32[4,64,256]{2,1,0:T(8,128)}, f32[4,64,256]{2,1,0:T(8,128)S(1)}, u32[]{:S(2)}, u32[]{:S(2)}) collective-permute-start(f32[4,64,256]{2,1,0:T(8,128)} %bitcast.2), channel_id=1, source_target_pairs={{0,8},{1,9},{2,10},{3,11},{4,12},{5,13},{6,14},{7,15},{8,24},{9,25... | collective-permute-start | bytes 786440 | tf_op jit(solution)/shard_map/ppermute | solution.py:525
  3.7 3.9 %collective-permute-start.1 = (f32[8,128]{1,0:T(8,128)S(1)}, f32[8,128]{1,0:T(8,128)S(1)}, u32[]{:S(2)}, u32[]{:S(2)}) collective-permute-start(f32[8,128]{1,0:T(8,128)S(1)} %pad.4), channel_id=1, source_target_pairs={{8,24},{9,25},{10,26},{11,27},{12,28},{13,29},{14,30},{15,31}} | collective-permute-start | bytes 12296 | tf_op jit(solution)/shard_map/ppermute | solution.py:525
  6.6 1.0 %copy-start.1 = (f32[680,128]{1,0:T(8,128)S(1)}, f32[680,128]{1,0:T(8,128)}, u32[]{:S(2)}) copy-start(f32[680,128]{1,0:T(8,128)} %get-tuple-element.34.bundle) | copy-start | bytes 1044484
  7.6 0.7 %collective-permute-start.2 = (f32[4,64,256]{2,1,0:T(8,128)S(1)}, f32[4,64,256]{2,1,0:T(8,128)S(1)}, u32[]{:S(2)}, u32[]{:S(2)}) collective-permute-start(f32[4,64,256]{2,1,0:T(8,128)S(1)} %collective-permute-done.moved), channel_id=1, source_target_pairs={{24,16},{25,17},{26,18},{27,19},{28,20},{29,21},{30,22},{31,23}} | collective-permute-start | bytes 786440 | tf_op jit(solution)/shard_map/ppermute | solution.py:525
  8.4 16.8 %collective-permute-start.5 = (f32[544,128]{1,0:T(8,128)S(1)}, f32[544,128]{1,0:T(8,128)S(1)}, u32[]{:S(2)}, u32[]{:S(2)}) collective-permute-start(f32[544,128]{1,0:T(8,128)S(1)} %shard_map.106.refs_0_), channel_id=1, source_target_pairs={{0,7},{1,0},{2,1},{3,2},{4,3},{5,4},{6,5},{7,6},{8,14},{9,15},{10,... | collective-permute-start | bytes 835592 | tf_op jit(solution)/shard_map/ppermute | solution.py:525
  13.8 12.1 %collective-permute-start.4 = (f32[544,128]{1,0:T(8,128)S(1)}, f32[544,128]{1,0:T(8,128)S(1)}, u32[]{:S(2)}, u32[]{:S(2)}) collective-permute-start(f32[544,128]{1,0:T(8,128)S(1)} %shard_map.106.refs_0_), channel_id=1, source_target_pairs={{0,1},{1,2},{2,3},{3,4},{4,5},{5,6},{6,7},{7,0},{8,10},{9,11},{10,... | collective-permute-start | bytes 835592 | tf_op jit(solution)/shard_map/ppermute | solution.py:525
  13.8 10.0 %collective-permute-start.3 = (f32[264,256]{1,0:T(8,128)}, f32[264,256]{1,0:T(8,128)S(1)}, u32[]{:S(2)}, u32[]{:S(2)}) collective-permute-start(f32[264,256]{1,0:T(8,128)} %get-tuple-element.42), channel_id=1, source_target_pairs={{16,0},{17,1},{18,2},{19,3},{20,4},{21,5},{22,6},{23,7}} | collective-permute-start | bytes 811016 | tf_op jit(solution)/shard_map/ppermute | solution.py:525
  23.8 1.0 %copy-start = (bf16[4,4,64,256]{3,2,1,0:T(8,128)(2,1)S(1)}, bf16[4,4,64,256]{3,2,1,0:T(8,128)(2,1)}, u32[]{:S(2)}) copy-start(bf16[4,4,64,256]{3,2,1,0:T(8,128)(2,1)} %backward) | copy-start | bytes 1572868
  25.2 1.6 %collective-permute-start.6 = (f32[544,128]{1,0:T(8,128)S(1)}, f32[544,128]{1,0:T(8,128)S(1)}, u32[]{:S(2)}, u32[]{:S(2)}) collective-permute-start(f32[544,128]{1,0:T(8,128)S(1)} %collective-permute-done.5.refs_2_), channel_id=1, source_target_pairs={{0,8},{1,9},{2,10},{3,11},{4,12},{5,13},{6,14},{7,15},{8,0},{9,1},... | collective-permute-start | bytes 835592 | tf_op jit(solution)/shard_map/ppermute | solution.py:525
  25.9 1.9 %collective-permute-start.7 = (f32[544,128]{1,0:T(8,128)S(1)}, f32[544,128]{1,0:T(8,128)S(1)}, u32[]{:S(2)}, u32[]{:S(2)}) collective-permute-start(f32[544,128]{1,0:T(8,128)S(1)} %collective-permute-done.4.refs_1_), channel_id=1, source_target_pairs={{0,8},{1,9},{2,10},{3,11},{4,12},{5,13},{6,14},{7,15},{8,0},{9,1},... | collective-permute-start | bytes 835592 | tf_op jit(solution)/shard_map/ppermute | solution.py:525
  27.8 22.3 %collective-permute-start.13 = (f32[3,4,128,128]{3,2,1,0:T(8,128)S(1)}, f32[3,4,128,128]{3,2,1,0:T(8,128)S(1)}, u32[]{:S(2)}, u32[]{:S(2)}) collective-permute-start(f32[3,4,128,128]{3,2,1,0:T(8,128)S(1)} %get-tuple-element.60.refs_6_.refs_11_), channel_id=1, source_target_pairs={{16,0},{17,1},{18,2},{19,3},{20,4},{21,5},{22,6},{23,7}} | collective-permute-start | bytes 2359304 | tf_op jit(solution)/shard_map/ppermute | solution.py:525
  36.2 7.3 %collective-permute-start.9 = (f32[264,128]{1,0:T(8,128)S(1)}, f32[264,128]{1,0:T(8,128)S(1)}, u32[]{:S(2)}, u32[]{:S(2)}) collective-permute-start(f32[264,128]{1,0:T(8,128)S(1)} %get-tuple-element.55), channel_id=1, source_target_pairs={{0,7},{1,0},{2,1},{3,2},{4,3},{5,4},{6,5},{7,6},{8,15},{9,8},{10,9... | collective-permute-start | bytes 405512 | tf_op jit(solution)/shard_map/ppermute | solution.py:525
  41.0 7.7 %collective-permute-start.8 = (f32[264,128]{1,0:T(8,128)S(1)}, f32[264,128]{1,0:T(8,128)S(1)}, u32[]{:S(2)}, u32[]{:S(2)}) collective-permute-start(f32[264,128]{1,0:T(8,128)S(1)} %get-tuple-element.55), channel_id=1, source_target_pairs={{0,1},{1,2},{2,3},{3,4},{4,5},{5,6},{6,7},{7,0},{8,9},{9,10},{10,1... | collective-permute-start | bytes 405512 | tf_op jit(solution)/shard_map/ppermute | solution.py:525
  41.0 7.7 %collective-permute-start.12 = (f32[4,128,128]{2,1,0:T(8,128)S(1)}, f32[4,128,128]{2,1,0:T(8,128)S(1)}, u32[]{:S(2)}, u32[]{:S(2)}) collective-permute-start(f32[4,128,128]{2,1,0:T(8,128)S(1)} %get-tuple-element.58.refs_6_), channel_id=1, source_target_pairs={{0,8},{1,9},{2,10},{3,11},{4,12},{5,13},{6,14},{7,15},{8,0},{9,1},... | collective-permute-start | bytes 786440 | tf_op jit(solution)/shard_map/ppermute | solution.py:525
  43.6 5.2 %collective-permute-start.11 = (f32[264,128]{1,0:T(8,128)S(1)}, f32[264,128]{1,0:T(8,128)S(1)}, u32[]{:S(2)}, u32[]{:S(2)}) collective-permute-start(f32[264,128]{1,0:T(8,128)S(1)} %collective-permute-done.9.refs_1_), channel_id=1, source_target_pairs={{0,8},{1,9},{2,10},{3,11},{4,12},{5,13},{6,14},{7,15},{8,0},{9,1},... | collective-permute-start | bytes 405512 | tf_op jit(solution)/shard_map/ppermute | solution.py:525
  48.7 1.4 %collective-permute-start.10 = (f32[264,128]{1,0:T(8,128)S(1)}, f32[264,128]{1,0:T(8,128)S(1)}, u32[]{:S(2)}, u32[]{:S(2)}) collective-permute-start(f32[264,128]{1,0:T(8,128)S(1)} %collective-permute-done.8.refs_0_), channel_id=1, source_target_pairs={{0,8},{1,9},{2,10},{3,11},{4,12},{5,13},{6,14},{7,15},{8,0},{9,1},... | collective-permute-start | bytes 405512 | tf_op jit(solution)/shard_map/ppermute | solution.py:525
  52.9 8.6 %collective-permute-start.15 = (f32[192,256]{1,0:T(8,128)S(1)}, f32[192,256]{1,0:T(8,128)S(1)}, u32[]{:S(2)}, u32[]{:S(2)}) collective-permute-start(f32[192,256]{1,0:T(8,128)S(1)} %get-tuple-element.64), channel_id=1, source_target_pairs={{0,16},{1,17},{2,18},{3,19},{4,20},{5,21},{6,22},{7,23},{8,0},{9,1... | collective-permute-start | bytes 589832 | tf_op jit(solution)/shard_map/ppermute | solution.py:525
  55.4 6.2 %collective-permute-start.16 = (f32[128,256]{1,0:T(8,128)S(1)}, f32[128,256]{1,0:T(8,128)S(1)}, u32[]{:S(2)}, u32[]{:S(2)}) collective-permute-start(f32[128,256]{1,0:T(8,128)S(1)} %get-tuple-element.65), channel_id=1, source_target_pairs={{0,24},{1,25},{2,26},{3,27},{4,28},{5,29},{6,30},{7,31},{8,16},{9,... | collective-permute-start | bytes 393224 | tf_op jit(solution)/shard_map/ppermute | solution.py:525
  55.5 1.3 %collective-permute-start.14 = (f32[64,256]{1,0:T(8,128)S(1)}, f32[64,256]{1,0:T(8,128)S(1)}, u32[]{:S(2)}, u32[]{:S(2)}) collective-permute-start(f32[64,256]{1,0:T(8,128)S(1)} %get-tuple-element.63), channel_id=1, source_target_pairs={{0,8},{1,9},{2,10},{3,11},{4,12},{5,13},{6,14},{7,15},{8,0},{9,1},... | collective-permute-start | bytes 196616 | tf_op jit(solution)/shard_map/ppermute | solution.py:525

commit v15 on v14

--- a/solution.py
+++ b/solution.py
@@ -356,7 +356,7 @@
 def slab_starts(planes, reach):
     odd = position()[1]
     mine, others = (planes * (1 + core) for core in (odd, 1 - odd))
-    return [reach, reach - mine, reach + mine, reach - others, reach + others]
+    return [reach, reach + mine, reach - mine, reach + others, reach - others]
 
 
 def fill_factor(pieces, starts, factor, scratch):
@@ -512,7 +512,7 @@
     steps, planes, orients, cells = backward.shape
     pair = planes // 2
     reach = (TICKS - 1) * steps, steps
-    near = (1, -1)
+    near = (-1, 1)
     rows = 2 * orients
     lanes = cells // 2
     last = n_sec - 1

time: 62.6 us -> 58.4 us (0.933)
  waiting for transfers between devices: 24.9 us -> 19.8 us
  starting transfers between devices: 19.5 us -> 20.5 us
    ppermute x17, waiting for transfers between devices: 24.9 us -> 19.8 us  [send(): return lax.ppermute(array, ('sec', 'gx'), pairs)]
    ppermute x17, starting transfers between devices: 19.5 us -> 20.5 us  [send(): return lax.ppermute(array, ('sec', 'gx'), pairs)]
  transfers between devices with their start and end apart: 17 -> 17, of which waited for: 8 -> 8; matrix products, arithmetic and copies ran while one was open for 1% -> 1% of each run, Pallas kernels for 17% -> 18%
where the time goes in v15:
time: 58.4 us; the launch traced here: 58.1 us
  starting transfers between devices  20.5 us (35%)
  waiting for transfers between devices  19.8 us (34%)
  Pallas kernels  14.3 us (24%)
  local copies, waits for them, and re-layouts  2.02 us (3%)
  between operations  0.79 us (1%)
  other arithmetic  0.66 us (1%)
    ppermute x17, starting transfers between devices, send(): return lax.ppermute(array, ('sec', 'gx'), pairs)  20.5 us
    ppermute x17, waiting for transfers between devices, send(): return lax.ppermute(array, ('sec', 'gx'), pairs)  19.8 us
    pallas_call x7, Pallas kernels, call(): pl.pallas_call(kernel, in_specs=[IN_VMEM] * len(operands), out_specs=[IN_...  12.1 us
    pallas_call x1, Pallas kernels, launch(): pl.pallas_call(launch_kernel, in_specs=[pl.BlockSpec(memory_space=pltpu.H...  2.26 us
    unnamed x4, local copies, waits for them, and re-layouts  2.01 us
  transfers between devices with their start and end apart: 17, of which 8 were waited for; matrix products, arithmetic and copies ran while one was open for 1% of the time, Pallas kernels for 18%

profile of v15, /device:TPU:0, one launch (start us, length us, event | category | flops | bytes accessed | tf_op | source)
XLA Modules:
  0.0 58.1 jit_solution(15655537071656303619)
XLA Ops:
  0.6 2.4 %collective-permute-start = (f32[4,64,256]{2,1,0:T(8,128)}, f32[4,64,256]{2,1,0:T(8,128)S(1)}, u32[]{:S(2)}, u32[]{:S(2)}) collective-permute-start(f32[4,64,256]{2,1,0:T(8,128)} %bitcast.2), channel_id=1, source_target_pairs={{0,8},{1,9},{2,10},{3,11},{4,12},{5,13},{6,14},{7,15},{8,24},{9,25... | collective-permute-start | bytes 786440 | tf_op jit(solution)/shard_map/ppermute | solution.py:525
  3.0 0.7 %convert_element_type.5 = f32[1,4]{1,0:T(1,128)S(1)} convert(s32[1,4]{1,0:T(1,128)} %refs_3_.1) | non-fusion elementwise | flops 4 | bytes 32 | tf_op jit(solution)/shard_map/convert_element_type | solution.py:532
  3.7 0.6 %collective-permute-start.1 = (f32[8,128]{1,0:T(8,128)S(1)}, f32[8,128]{1,0:T(8,128)S(1)}, u32[]{:S(2)}, u32[]{:S(2)}) collective-permute-start(f32[8,128]{1,0:T(8,128)S(1)} %pad.4), channel_id=1, source_target_pairs={{8,24},{9,25},{10,26},{11,27},{12,28},{13,29},{14,30},{15,31}} | collective-permute-start | bytes 12296 | tf_op jit(solution)/shard_map/ppermute | solution.py:525
  4.3 2.3 %shard_map.104 = (f32[264,256]{1,0:T(8,128)}, f32[680,128]{1,0:T(8,128)}) custom-call(f32[1,4,64,256]{3,2,1,0:T(8,128)} %refs_0_.1, bf16[4,4,64,256]{3,2,1,0:T(8,128)(2,1)} %backward, f32[3,4,256]{2,1,0:T(4,128)} %refs_2_.1, s32[1,4]{1,0:T(1,128)} %refs_3_.1, f32[3,64]{1,0:T(4,128)} %refs_4_.1, f32[3,64]{1,0:T(4,128)} %refs_5_.1, f32[3,64]{1,0:T(4,128)} %refs_6_.1, ...), custom_call_target="tpu_custom_call" | custom-call | tf_op jit(solution)/shard_map/pallas_call | solution.py:228
  6.6 0.0 copy-start.1
  6.6 1.0 %copy-done.1 = f32[680,128]{1,0:T(8,128)S(1)} copy-done((f32[680,128]{1,0:T(8,128)S(1)}, f32[680,128]{1,0:T(8,128)}, u32[]{:S(2)}) %copy-start.1) | copy-done | bytes 348184
  7.6 0.0 collective-permute-done.1.types
  7.6 0.0 collective-permute-done.moved
  7.6 0.7 %collective-permute-start.2 = (f32[4,64,256]{2,1,0:T(8,128)S(1)}, f32[4,64,256]{2,1,0:T(8,128)S(1)}, u32[]{:S(2)}, u32[]{:S(2)}) collective-permute-start(f32[4,64,256]{2,1,0:T(8,128)S(1)} %collective-permute-done.moved), channel_id=1, source_target_pairs={{24,16},{25,17},{26,18},{27,19},{28,20},{29,21},{30,22},{31,23}} | collective-permute-start | bytes 786440 | tf_op jit(solution)/shard_map/ppermute | solution.py:525
  8.3 0.0 collective-permute-done.2.passed
  8.4 2.4 %collective-permute-start.5 = (f32[544,128]{1,0:T(8,128)S(1)}, f32[544,128]{1,0:T(8,128)S(1)}, u32[]{:S(2)}, u32[]{:S(2)}) collective-permute-start(f32[544,128]{1,0:T(8,128)S(1)} %shard_map.106.refs_0_), channel_id=1, source_target_pairs={{0,1},{1,2},{2,3},{3,4},{4,5},{5,6},{6,7},{7,0},{8,10},{9,11},{10,... | collective-permute-start | bytes 835592 | tf_op jit(solution)/shard_map/ppermute | solution.py:525
  10.8 3.1 %collective-permute-start.4 = (f32[544,128]{1,0:T(8,128)S(1)}, f32[544,128]{1,0:T(8,128)S(1)}, u32[]{:S(2)}, u32[]{:S(2)}) collective-permute-start(f32[544,128]{1,0:T(8,128)S(1)} %shard_map.106.refs_0_), channel_id=1, source_target_pairs={{0,7},{1,0},{2,1},{3,2},{4,3},{5,4},{6,5},{7,6},{8,14},{9,15},{10,... | collective-permute-start | bytes 835592 | tf_op jit(solution)/shard_map/ppermute | solution.py:525
  13.9 1.3 %collective-permute-start.3 = (f32[264,256]{1,0:T(8,128)}, f32[264,256]{1,0:T(8,128)S(1)}, u32[]{:S(2)}, u32[]{:S(2)}) collective-permute-start(f32[264,256]{1,0:T(8,128)} %get-tuple-element.42), channel_id=1, source_target_pairs={{16,0},{17,1},{18,2},{19,3},{20,4},{21,5},{22,6},{23,7}} | collective-permute-start | bytes 811016 | tf_op jit(solution)/shard_map/ppermute | solution.py:525
  15.2 8.8 %collective-permute-done.3.lead = f32[264,256]{1,0:T(8,128)S(1)} collective-permute-done((f32[264,256]{1,0:T(8,128)}, f32[264,256]{1,0:T(8,128)S(1)}, u32[]{:S(2)}, u32[]{:S(2)}) %collective-permute-start.3) | collective-permute-done | bytes 270368 | tf_op jit(solution)/shard_map/ppermute | solution.py:525
  24.0 0.0 copy-start
  24.0 1.0 %copy-done = bf16[4,4,64,256]{3,2,1,0:T(8,128)(2,1)S(1)} copy-done((bf16[4,4,64,256]{3,2,1,0:T(8,128)(2,1)S(1)}, bf16[4,4,64,256]{3,2,1,0:T(8,128)(2,1)}, u32[]{:S(2)}) %copy-start) | copy-done | bytes 524312
  25.0 0.4 shard_map.107
  25.4 0.0 collective-permute-done.5.refs_2_
  25.4 0.1 collective-permute-start.6
  25.5 0.0 collective-permute-done.4.refs_1_
  25.5 0.5 collective-permute-start.7
  26.0 1.0 %collective-permute-done.6.refs_4_ = f32[544,128]{1,0:T(8,128)S(1)} collective-permute-done((f32[544,128]{1,0:T(8,128)S(1)}, f32[544,128]{1,0:T(8,128)S(1)}, u32[]{:S(2)}, u32[]{:S(2)}) %collective-permute-start.6) | collective-permute-done | bytes 278560 | tf_op jit(solution)/shard_map/ppermute | solution.py:525
  27.1 0.9 %shard_map.108.refs_7_ = f32[3,20,128,128]{3,2,1,0:T(8,128)S(1)} custom-call(f32[544,128]{1,0:T(8,128)S(1)} %shard_map.106.refs_0_, f32[544,128]{1,0:T(8,128)S(1)} %collective-permute-done.4.refs_1_, f32[544,128]{1,0:T(8,128)S(1)} %collective-permute-done.5.refs_2_), custom_call_target="tpu_custom_call" | custom-call | tf_op jit(solution)/shard_map/pallas_call | solution.py:498
  28.0 0.0 collective-permute-done.7.refs_3_
  28.0 1.3 %collective-permute-start.13 = (f32[3,4,128,128]{3,2,1,0:T(8,128)S(1)}, f32[3,4,128,128]{3,2,1,0:T(8,128)S(1)}, u32[]{:S(2)}, u32[]{:S(2)}) collective-permute-start(f32[3,4,128,128]{3,2,1,0:T(8,128)S(1)} %get-tuple-element.60.refs_6_.refs_11_), channel_id=1, source_target_pairs={{16,0},{17,1},{18,2},{19,3},{20,4},{21,5},{22,6},{23,7}} | collective-permute-start | bytes 2359304 | tf_op jit(solution)/shard_map/ppermute | solution.py:525
  29.3 7.0 %shard_map.109 = (f32[4,128,128]{2,1,0:T(8,128)S(1)}, f32[264,128]{1,0:T(8,128)S(1)}, f32[4,128,128]{2,1,0:T(8,128)S(1)}, f32[4,128,128]{2,1,0:T(8,128)S(1)}, f32[3,20,128,128]{3,2,1,0:T(8,128)S(1)}) custom-call(f32[8,128]{1,0:T(8,128)S(1)} %get-tuple-element.35.taps, ...), custom_call_target="tpu_custom_call", output_to_operand_aliasing={{4}: (10, {})} | custom-call | tf_op jit(solution)/shard_map/pallas_call | solution.py:498
  36.3 0.1 collective-permute-start.9
  36.4 4.7 %collective-permute-start.8 = (f32[264,128]{1,0:T(8,128)S(1)}, f32[264,128]{1,0:T(8,128)S(1)}, u32[]{:S(2)}, u32[]{:S(2)}) collective-permute-start(f32[264,128]{1,0:T(8,128)S(1)} %get-tuple-element.55), channel_id=1, source_target_pairs={{0,7},{1,0},{2,1},{3,2},{4,3},{5,4},{6,5},{7,6},{8,15},{9,8},{10,9... | collective-permute-start | bytes 405512 | tf_op jit(solution)/shard_map/ppermute | solution.py:525
  41.1 0.0 collective-permute-start.12
  41.1 3.1 %collective-permute-done.9.refs_1_ = f32[264,128]{1,0:T(8,128)S(1)} collective-permute-done((f32[264,128]{1,0:T(8,128)S(1)}, f32[264,128]{1,0:T(8,128)S(1)}, u32[]{:S(2)}, u32[]{:S(2)}) %collective-permute-start.9) | collective-permute-done | bytes 135200 | tf_op jit(solution)/shard_map/ppermute | solution.py:525
  44.2 0.0 collective-permute-start.11
  44.2 0.2 collective-permute-done.8.refs_0_
  44.4 0.4 collective-permute-start.10
  44.7 0.0 collective-permute-done.12.refs_7_
  44.8 0.8 %collective-permute-done.11.refs_3_ = f32[264,128]{1,0:T(8,128)S(1)} collective-permute-done((f32[264,128]{1,0:T(8,128)S(1)}, f32[264,128]{1,0:T(8,128)S(1)}, u32[]{:S(2)}, u32[]{:S(2)}) %collective-permute-start.11) | collective-permute-done | bytes 135200 | tf_op jit(solution)/shard_map/ppermute | solution.py:525
  45.6 0.2 collective-permute-done.10.refs_2_
  45.8 0.0 collective-permute-done.13.refs_9_
  45.8 2.9 %shard_map.110 = (f32[4,64,256]{2,1,0:T(8,128)S(1)}, f32[64,256]{1,0:T(8,128)S(1)}, f32[64,256]{1,0:T(8,128)S(1)}, f32[192,256]{1,0:T(8,128)S(1)}, f32[128,256]{1,0:T(8,128)S(1)}) custom-call(f32[8,128]{1,0:T(8,128)S(1)} %get-tuple-element.35.taps, bf16[256,256]{1,0:T(8,128)(2,1)S(1)} %get-tuple-element.36.weights, ...), custom_call_target="tpu_custom_call" | custom-call | tf_op jit(solution)/shard_map/pallas_call | solution.py:498
  48.7 2.3 %collective-permute-start.15 = (f32[192,256]{1,0:T(8,128)S(1)}, f32[192,256]{1,0:T(8,128)S(1)}, u32[]{:S(2)}, u32[]{:S(2)}) collective-permute-start(f32[192,256]{1,0:T(8,128)S(1)} %get-tuple-element.64), channel_id=1, source_target_pairs={{0,16},{1,17},{2,18},{3,19},{4,20},{5,21},{6,22},{7,23},{8,0},{9,1... | collective-permute-start | bytes 589832 | tf_op jit(solution)/shard_map/ppermute | solution.py:525
  51.0 0.3 collective-permute-start.16
  51.2 0.4 collective-permute-start.14
  51.7 0.9 %collective-permute-done.14.to_pair = f32[64,256]{1,0:T(8,128)S(1)} collective-permute-done((f32[64,256]{1,0:T(8,128)S(1)}, f32[64,256]{1,0:T(8,128)S(1)}, u32[]{:S(2)}, u32[]{:S(2)}) %collective-permute-start.14) | collective-permute-done | bytes 65568 | tf_op jit(solution)/shard_map/ppermute | solution.py:525
  52.6 4.7 %collective-permute-done.16.to_corner = f32[128,256]{1,0:T(8,128)S(1)} collective-permute-done((f32[128,256]{1,0:T(8,128)S(1)}, f32[128,256]{1,0:T(8,128)S(1)}, u32[]{:S(2)}, u32[]{:S(2)}) %collective-permute-start.16) | collective-permute-done | bytes 131104 | tf_op jit(solution)/shard_map/ppermute | solution.py:525
  57.3 0.0 collective-permute-done.15.to_across
  57.3 0.8 %shard_map.111 = (f32[1,4,64,256]{3,2,1,0:T(8,128)}, f32[4,16,256]{2,1,0:T(8,128)}) custom-call(f32[4,64,256]{2,1,0:T(8,128)S(1)} %get-tuple-element.61.handoff_in, f32[64,256]{1,0:T(8,128)S(1)} %get-tuple-element.62.share, f32[64,256]{1,0:T(8,128)S(1)} %collective-permute-done.14.to_pair, f32[192,256]{1,0:T(8,128)S(1)} %collective-permute-done.15.to_across, ...), custom_call_target="tpu_custom_call" | custom-call | tf_op jit(solution)/shard_map/pallas_call | solution.py:498
  (3 shorter events, 0.1 us)
Async XLA Ops:
  0.6 7.0 %collective-permute-start = (f32[4,64,256]{2,1,0:T(8,128)}, f32[4,64,256]{2,1,0:T(8,128)S(1)}, u32[]{:S(2)}, u32[]{:S(2)}) collective-permute-start(f32[4,64,256]{2,1,0:T(8,128)} %bitcast.2), channel_id=1, source_target_pairs={{0,8},{1,9},{2,10},{3,11},{4,12},{5,13},{6,14},{7,15},{8,24},{9,25... | collective-permute-start | bytes 786440 | tf_op jit(solution)/shard_map/ppermute | solution.py:525
  3.7 3.9 %collective-permute-start.1 = (f32[8,128]{1,0:T(8,128)S(1)}, f32[8,128]{1,0:T(8,128)S(1)}, u32[]{:S(2)}, u32[]{:S(2)}) collective-permute-start(f32[8,128]{1,0:T(8,128)S(1)} %pad.4), channel_id=1, source_target_pairs={{8,24},{9,25},{10,26},{11,27},{12,28},{13,29},{14,30},{15,31}} | collective-permute-start | bytes 12296 | tf_op jit(solution)/shard_map/ppermute | solution.py:525
  6.6 1.0 %copy-start.1 = (f32[680,128]{1,0:T(8,128)S(1)}, f32[680,128]{1,0:T(8,128)}, u32[]{:S(2)}) copy-start(f32[680,128]{1,0:T(8,128)} %get-tuple-element.34.bundle) | copy-start | bytes 1044484
  7.6 0.7 %collective-permute-start.2 = (f32[4,64,256]{2,1,0:T(8,128)S(1)}, f32[4,64,256]{2,1,0:T(8,128)S(1)}, u32[]{:S(2)}, u32[]{:S(2)}) collective-permute-start(f32[4,64,256]{2,1,0:T(8,128)S(1)} %collective-permute-done.moved), channel_id=1, source_target_pairs={{24,16},{25,17},{26,18},{27,19},{28,20},{29,21},{30,22},{31,23}} | collective-permute-start | bytes 786440 | tf_op jit(solution)/shard_map/ppermute | solution.py:525
  8.4 17.0 %collective-permute-start.5 = (f32[544,128]{1,0:T(8,128)S(1)}, f32[544,128]{1,0:T(8,128)S(1)}, u32[]{:S(2)}, u32[]{:S(2)}) collective-permute-start(f32[544,128]{1,0:T(8,128)S(1)} %shard_map.106.refs_0_), channel_id=1, source_target_pairs={{0,1},{1,2},{2,3},{3,4},{4,5},{5,6},{6,7},{7,0},{8,10},{9,11},{10,... | collective-permute-start | bytes 835592 | tf_op jit(solution)/shard_map/ppermute | solution.py:525
  10.8 14.8 %collective-permute-start.4 = (f32[544,128]{1,0:T(8,128)S(1)}, f32[544,128]{1,0:T(8,128)S(1)}, u32[]{:S(2)}, u32[]{:S(2)}) collective-permute-start(f32[544,128]{1,0:T(8,128)S(1)} %shard_map.106.refs_0_), channel_id=1, source_target_pairs={{0,7},{1,0},{2,1},{3,2},{4,3},{5,4},{6,5},{7,6},{8,14},{9,15},{10,... | collective-permute-start | bytes 835592 | tf_op jit(solution)/shard_map/ppermute | solution.py:525
  13.9 10.1 %collective-permute-start.3 = (f32[264,256]{1,0:T(8,128)}, f32[264,256]{1,0:T(8,128)S(1)}, u32[]{:S(2)}, u32[]{:S(2)}) collective-permute-start(f32[264,256]{1,0:T(8,128)} %get-tuple-element.42), channel_id=1, source_target_pairs={{16,0},{17,1},{18,2},{19,3},{20,4},{21,5},{22,6},{23,7}} | collective-permute-start | bytes 811016 | tf_op jit(solution)/shard_map/ppermute | solution.py:525
  24.0 1.0 %copy-start = (bf16[4,4,64,256]{3,2,1,0:T(8,128)(2,1)S(1)}, bf16[4,4,64,256]{3,2,1,0:T(8,128)(2,1)}, u32[]{:S(2)}) copy-start(bf16[4,4,64,256]{3,2,1,0:T(8,128)(2,1)} %backward) | copy-start | bytes 1572868
  25.4 1.6 %collective-permute-start.6 = (f32[544,128]{1,0:T(8,128)S(1)}, f32[544,128]{1,0:T(8,128)S(1)}, u32[]{:S(2)}, u32[]{:S(2)}) collective-permute-start(f32[544,128]{1,0:T(8,128)S(1)} %collective-permute-done.5.refs_2_), channel_id=1, source_target_pairs={{0,8},{1,9},{2,10},{3,11},{4,12},{5,13},{6,14},{7,15},{8,0},{9,1},... | collective-permute-start | bytes 835592 | tf_op jit(solution)/shard_map/ppermute | solution.py:525
  25.5 2.5 %collective-permute-start.7 = (f32[544,128]{1,0:T(8,128)S(1)}, f32[544,128]{1,0:T(8,128)S(1)}, u32[]{:S(2)}, u32[]{:S(2)}) collective-permute-start(f32[544,128]{1,0:T(8,128)S(1)} %collective-permute-done.4.refs_1_), channel_id=1, source_target_pairs={{0,8},{1,9},{2,10},{3,11},{4,12},{5,13},{6,14},{7,15},{8,0},{9,1},... | collective-permute-start | bytes 835592 | tf_op jit(solution)/shard_map/ppermute | solution.py:525
  28.0 17.8 %collective-permute-start.13 = (f32[3,4,128,128]{3,2,1,0:T(8,128)S(1)}, f32[3,4,128,128]{3,2,1,0:T(8,128)S(1)}, u32[]{:S(2)}, u32[]{:S(2)}) collective-permute-start(f32[3,4,128,128]{3,2,1,0:T(8,128)S(1)} %get-tuple-element.60.refs_6_.refs_11_), channel_id=1, source_target_pairs={{16,0},{17,1},{18,2},{19,3},{20,4},{21,5},{22,6},{23,7}} | collective-permute-start | bytes 2359304 | tf_op jit(solution)/shard_map/ppermute | solution.py:525
  36.3 7.9 %collective-permute-start.9 = (f32[264,128]{1,0:T(8,128)S(1)}, f32[264,128]{1,0:T(8,128)S(1)}, u32[]{:S(2)}, u32[]{:S(2)}) collective-permute-start(f32[264,128]{1,0:T(8,128)S(1)} %get-tuple-element.55), channel_id=1, source_target_pairs={{0,1},{1,2},{2,3},{3,4},{4,5},{5,6},{6,7},{7,0},{8,9},{9,10},{10,1... | collective-permute-start | bytes 405512 | tf_op jit(solution)/shard_map/ppermute | solution.py:525
  36.4 8.0 %collective-permute-start.8 = (f32[264,128]{1,0:T(8,128)S(1)}, f32[264,128]{1,0:T(8,128)S(1)}, u32[]{:S(2)}, u32[]{:S(2)}) collective-permute-start(f32[264,128]{1,0:T(8,128)S(1)} %get-tuple-element.55), channel_id=1, source_target_pairs={{0,7},{1,0},{2,1},{3,2},{4,3},{5,4},{6,5},{7,6},{8,15},{9,8},{10,9... | collective-permute-start | bytes 405512 | tf_op jit(solution)/shard_map/ppermute | solution.py:525
  41.1 3.6 %collective-permute-start.12 = (f32[4,128,128]{2,1,0:T(8,128)S(1)}, f32[4,128,128]{2,1,0:T(8,128)S(1)}, u32[]{:S(2)}, u32[]{:S(2)}) collective-permute-start(f32[4,128,128]{2,1,0:T(8,128)S(1)} %get-tuple-element.58.refs_6_), channel_id=1, source_target_pairs={{0,8},{1,9},{2,10},{3,11},{4,12},{5,13},{6,14},{7,15},{8,0},{9,1},... | collective-permute-start | bytes 786440 | tf_op jit(solution)/shard_map/ppermute | solution.py:525
  44.2 1.4 %collective-permute-start.11 = (f32[264,128]{1,0:T(8,128)S(1)}, f32[264,128]{1,0:T(8,128)S(1)}, u32[]{:S(2)}, u32[]{:S(2)}) collective-permute-start(f32[264,128]{1,0:T(8,128)S(1)} %collective-permute-done.9.refs_1_), channel_id=1, source_target_pairs={{0,8},{1,9},{2,10},{3,11},{4,12},{5,13},{6,14},{7,15},{8,0},{9,1},... | collective-permute-start | bytes 405512 | tf_op jit(solution)/shard_map/ppermute | solution.py:525
  44.4 1.4 %collective-permute-start.10 = (f32[264,128]{1,0:T(8,128)S(1)}, f32[264,128]{1,0:T(8,128)S(1)}, u32[]{:S(2)}, u32[]{:S(2)}) collective-permute-start(f32[264,128]{1,0:T(8,128)S(1)} %collective-permute-done.8.refs_0_), channel_id=1, source_target_pairs={{0,8},{1,9},{2,10},{3,11},{4,12},{5,13},{6,14},{7,15},{8,0},{9,1},... | collective-permute-start | bytes 405512 | tf_op jit(solution)/shard_map/ppermute | solution.py:525
  48.7 8.7 %collective-permute-start.15 = (f32[192,256]{1,0:T(8,128)S(1)}, f32[192,256]{1,0:T(8,128)S(1)}, u32[]{:S(2)}, u32[]{:S(2)}) collective-permute-start(f32[192,256]{1,0:T(8,128)S(1)} %get-tuple-element.64), channel_id=1, source_target_pairs={{0,16},{1,17},{2,18},{3,19},{4,20},{5,21},{6,22},{7,23},{8,0},{9,1... | collective-permute-start | bytes 589832 | tf_op jit(solution)/shard_map/ppermute | solution.py:525
  51.0 6.3 %collective-permute-start.16 = (f32[128,256]{1,0:T(8,128)S(1)}, f32[128,256]{1,0:T(8,128)S(1)}, u32[]{:S(2)}, u32[]{:S(2)}) collective-permute-start(f32[128,256]{1,0:T(8,128)S(1)} %get-tuple-element.65), channel_id=1, source_target_pairs={{0,24},{1,25},{2,26},{3,27},{4,28},{5,29},{6,30},{7,31},{8,16},{9,... | collective-permute-start | bytes 393224 | tf_op jit(solution)/shard_map/ppermute | solution.py:525
  51.2 1.3 %collective-permute-start.14 = (f32[64,256]{1,0:T(8,128)S(1)}, f32[64,256]{1,0:T(8,128)S(1)}, u32[]{:S(2)}, u32[]{:S(2)}) collective-permute-start(f32[64,256]{1,0:T(8,128)S(1)} %get-tuple-element.63), channel_id=1, source_target_pairs={{0,8},{1,9},{2,10},{3,11},{4,12},{5,13},{6,14},{7,15},{8,0},{9,1},... | collective-permute-start | bytes 196616 | tf_op jit(solution)/shard_map/ppermute | solution.py:525

commit v16 on v15

--- a/solution.py
+++ b/solution.py
@@ -13,7 +13,6 @@
 FIELD_ROWS = 32
 TAP_ROWS = 8
 OWN_KINDS, FIRST_KINDS = 24, 25
-LEAD = 1
 VMEM_BYTES = 16 * 2**20
 WHOLE_VMEM_BYTES = 62 * 2**20
 IN_VMEM = pl.BlockSpec(memory_space=pltpu.VMEM)
@@ -172,16 +171,12 @@
 
 
 def launch_kernel(*refs):
-    sources, (lead, bundle) = refs[:9], refs[9:11]
-    scratch, copies, sems = refs[11], refs[12:21], refs[21]
-    moves = [
-        pltpu.make_async_copy(source.at[pl.ds(0, copy.shape[0])], copy, sems.at[i])
-        for i, (source, copy) in enumerate(zip(sources, copies))
-    ]
+    sources, bundle, scratch, copies, sems = refs[:8], refs[8], refs[9], refs[10:18], refs[18]
+    moves = [pltpu.make_async_copy(s, c, sems.at[i]) for i, (s, c) in enumerate(zip(sources, copies))]
     for move in moves:
         move.start()
-    incoming, stored, fields, kinds, axial, lateral, depth, diagonal, coupling = copies
-    for move in moves[2:]:
+    incoming, fields, kinds, axial, lateral, depth, diagonal, coupling = copies
+    for move in moves[1:]:
         move.wait()
     rows = scratch.shape[0]
     orients = rows // 2
@@ -211,43 +206,28 @@
     for i in range(planes):
         here = at + FIELD_ROWS + i * rows
         bundle[here : here + rows] = to_tile(incoming[0, i], scratch)
-    moves[1].wait()
-    for step in range(LEAD):
-        for i in range(planes):
-            here = (step * planes + i) * orients
-            lead[here : here + orients] = stored[step, i].astype(jnp.float32)
-    lead[lead.shape[0] - 8 :] = jnp.broadcast_to(jnp.concatenate([types, types], axis=1), (8, lead.shape[1]))
-
-
-def launch(incoming, backward, fields, kinds, axial, lateral, depth, diagonal, coupling):
-    planes, orients, cells = backward.shape[1:]
+
+
+def launch(incoming, fields, kinds, axial, lateral, depth, diagonal, coupling):
+    planes, orients, cells = incoming.shape[1:]
     rows = 2 * orients
-    operands = [incoming, backward, fields, kinds, axial, lateral, depth, diagonal.reshape(1, -1), coupling]
-    shapes = [(LEAD * planes * orients + 8, cells), (TAP_ROWS + rows + FIELD_ROWS + planes * rows, rows)]
-    taken = [(LEAD,) + each.shape[1:] if i == 1 else each.shape for i, each in enumerate(operands)]
+    operands = [incoming, fields, kinds, axial, lateral, depth, diagonal.reshape(1, -1), coupling]
     return pl.pallas_call(
         launch_kernel,
         in_specs=[pl.BlockSpec(memory_space=pltpu.HBM)] * len(operands),
-        out_specs=[IN_VMEM] * len(shapes),
-        out_shape=[jax.ShapeDtypeStruct(shape, jnp.float32) for shape in shapes],
+        out_specs=IN_VMEM,
+        out_shape=jax.ShapeDtypeStruct((TAP_ROWS + rows + FIELD_ROWS + planes * rows, rows), jnp.float32),
         scratch_shapes=[pltpu.VMEM((rows, rows), jnp.float32)]
-        + [pltpu.VMEM(shape, each.dtype) for shape, each in zip(taken, operands)]
+        + [pltpu.VMEM(each.shape, each.dtype) for each in operands]
         + [pltpu.SemaphoreType.DMA((len(operands),))],
         compiler_params=pltpu.CompilerParams(vmem_limit_bytes=WHOLE_VMEM_BYTES),
     )(*operands)
 
 
-def turn_kernel(backward, lead, early, late, out, across, scratch):
-    orients = scratch.shape[0] // 2
-    across[...] = lead[lead.shape[0] - 8 :, : scratch.shape[1]]
-    for target, begin in ((early, 0), (late, LEAD)):
-        for step in range(target.shape[0]):
-            for i in range(target.shape[1]):
-                target[step, i] = to_tile(backward[begin + step, i].astype(jnp.float32), scratch)
+def turn_kernel(backward, out, scratch):
     for step in range(out.shape[0]):
         for i in range(out.shape[1]):
-            here = (step * out.shape[1] + i) * orients
-            out[step, i] = to_tile(lead[here : here + orients], scratch)
+            out[step, i] = to_tile(backward[step, i].astype(jnp.float32), scratch)
 
 
 def unpack_kernel(bundle, out, taps, weights):
@@ -376,8 +356,8 @@
 
 
 def early_kernel(taps, weights, across, *refs):
-    pieces, stored, (middle, half_out, kept, total, factor) = refs[:5], refs[5:7], refs[8:13]
-    slab, other, first, second, scratch = refs[13:]
+    pieces, stored, (middle, half_out, kept, total, factor) = refs[:5], refs[5], refs[7:12]
+    slab, other, first, second, scratch = refs[12:]
     sec, odd = position()
     planes, rows = middle.shape[:2]
     pair = planes // 2
@@ -387,7 +367,7 @@
         for i in range(planes):
             slab[start + i] = piece[i * rows : (i + 1) * rows]
     at = planes * rows
-    steps = LEAD + stored[1].shape[0]
+    steps = stored.shape[0]
     own_kinds, first_kinds = (pieces[0][at + row : at + row + 1] for row in (OWN_KINDS, FIRST_KINDS))
     beside_kinds, beside_first = (pieces[3][at + row : at + row + 1] for row in (OWN_KINDS, FIRST_KINDS))
     kinds = scalars_of(jnp.where((sec == 1) | (sec == 2), beside_first, first_kinds), steps)
@@ -401,10 +381,8 @@
     def after(step, state):
         @pl.when(sec == step // steps)
         def _():
-            j = step % steps
-            source = stored[0][j] if j < LEAD else stored[1][j - LEAD]
-            total[...] += state[reach : reach + planes] * source
-            if j + 1 == steps:
+            total[...] += state[reach : reach + planes] * stored[step % steps]
+            if (step + 1) % steps == 0:
                 kept[...] = state[reach : reach + planes]
 
     run_steps(kinds, taps, weights, reach, slab, other, first, second, factor, 0, after)
@@ -416,9 +394,9 @@
 
 def late_kernel(blocks, last, taps, weights, middle, *refs):
     pieces, refs = refs[: 2 * len(blocks)], refs[2 * len(blocks) :]
-    factor, kept, total_in, total_beside, series, stored = refs[0], refs[1], refs[2], refs[3], refs[4:6], refs[6:8]
-    handoff, share, to_pair, to_across, to_corner = refs[8:13]
-    slab, other, first, second, scratch, total, saved, whole = refs[13:]
+    factor, kept, total_in, total_beside, series, stored = refs[:6]
+    handoff, share, to_pair, to_across, to_corner = refs[6:11]
+    slab, other, first, second, scratch, total, saved, whole = refs[11:]
     sec, odd = position()
     planes, rows = middle.shape[:2]
     pair = planes // 2
@@ -443,8 +421,7 @@
 
             @pl.when(where)
             def _(source=source):
-                part = source[0][step] if step < LEAD else source[1][step - LEAD]
-                total[...] += state[reach : reach + planes] * part
+                total[...] += state[reach : reach + planes] * source[step]
 
     run_steps(kinds, taps, weights, reach, slab, other, first, second, factor, begun - reach, after)
     state = (slab, other)[reach % 2]
@@ -526,12 +503,11 @@
 
     same, beside = (0, 1, 2, 3), (1, 0, 3, 2)
     moved = send(incoming[0], {0: 1, 1: 3})
-    lead, bundle = launch(
-        incoming, backward, fields, block_types, axial_taps, lateral_taps, depth_taps, bend_diagonal, bend_coupling
-    )
-    types = jnp.pad(block_types.astype(jnp.float32), ((0, 7), (0, lanes - steps)))
-    types = send(types, {1: 3})
-    lead = send(lead, {2: 0})
+    bundle = launch(
+        incoming, fields, block_types, axial_taps, lateral_taps, depth_taps, bend_diagonal, bend_coupling
+    )
+    own_types = jnp.pad(block_types.astype(jnp.float32), ((0, 7), (0, lanes - steps)))
+    types = send(own_types, {1: 3})
     size = planes * rows + FIELD_ROWS
     base, taps, weights = call(
         unpack_kernel, [(size, lanes), (TAP_ROWS, lanes), (2 * rows, 2 * lanes)], [], [bundle], {2: jnp.bfloat16}
@@ -549,27 +525,23 @@
 
     (piece,) = call(pack_kernel, [(size, lanes)], [tile], [base, moved, passed, types])
     own = [send(piece, same, shift, 2 * shift) for shift in near]
-    backward, _ = lax.optimization_barrier((backward, piece))
-    *stored, lead, across = call(
-        turn_kernel,
-        [(count, planes, rows, lanes) for count in (LEAD, steps - LEAD, LEAD)] + [(8, lanes)],
-        [tile],
-        [backward, lead],
-    )
-    own[-1], *stored = lax.optimization_barrier((own[-1], *stored))
+    backward, own_types, _ = lax.optimization_barrier((backward, own_types, piece))
+    across_types = send(own_types, {2: 0})
+    (stored,) = call(turn_kernel, [(steps, planes, rows, lanes)], [tile], [backward])
+    own[-1], stored, across_types = lax.optimization_barrier((own[-1], stored, across_types))
     swapped = [send(each, beside) for each in own]
     table = (fields.shape[0], planes + 2 * reach[0], rows, lanes)
     known, swapped[1] = lax.optimization_barrier((piece, swapped[1]))
     (factor,) = call(factor_kernel, [table], [tile], [known, *own])
-    late_stored, factor, *swapped = lax.optimization_barrier((stored[1], factor, *swapped))
+    late_stored, factor, *swapped = lax.optimization_barrier((stored, factor, *swapped))
     late_last = send(late_stored, {2: 0})
     middle, piece, kept, total, factor = call(
         early_kernel,
         [(planes, rows, lanes), (pair * rows + 8, lanes), (planes, rows, lanes), (planes, rows, lanes)]
         + [table],
         work(reach[0]),
-        [taps, weights, across, piece, *own, *swapped, *stored, factor],
-        aliases={10: 4},
+        [taps, weights, across_types, piece, *own, *swapped, stored, factor],
+        aliases={9: 4},
     )
     own = [send(piece, same, shift, shift) for shift in near]
     beside_total = send(total, beside)
@@ -582,7 +554,7 @@
         + [(held + pair * orients, cells), (pair * orients, cells)],
         work(reach[1]) + [inner, inner, pltpu.VMEM((orients, cells), jnp.float32)],
         [taps, weights, middle, *own, *swapped, factor, kept, total, beside_total]
-        + [lead, late_last, *stored],
+        + [late_last, stored],
     )
     to_pair = send(to_pair, beside)
     to_across = send(to_across, (2, 0, 3, 1))

time: 58.4 us -> 56.9 us (0.974)
  waiting for transfers between devices: 19.8 us -> 16.9 us
  starting transfers between devices: 20.5 us -> 22 us
    ppermute x17, waiting for transfers between devices: 19.8 us -> 16.9 us  [send(): return lax.ppermute(array, ('sec', 'gx'), pairs)]
    ppermute x17, starting transfers between devices: 20.5 us -> 22 us  [send(): return lax.ppermute(array, ('sec', 'gx'), pairs)]
  transfers between devices with their start and end apart: 17 -> 17, of which waited for: 8 -> 7; matrix products, arithmetic and copies ran while one was open for 1% -> 1% of each run, Pallas kernels for 18% -> 18%
where the time goes in v16:
time: 56.9 us; the launch traced here: 56.6 us
  starting transfers between devices  22 us (39%)
  waiting for transfers between devices  16.9 us (30%)
  Pallas kernels  14.2 us (25%)
  local copies, waits for them, and re-layouts  2.02 us (4%)
  between operations  0.77 us (1%)
  other arithmetic  0.66 us (1%)
    ppermute x17, starting transfers between devices, send(): return lax.ppermute(array, ('sec', 'gx'), pairs)  22 us
    ppermute x17, waiting for transfers between devices, send(): return lax.ppermute(array, ('sec', 'gx'), pairs)  16.9 us
    pallas_call x7, Pallas kernels, call(): pl.pallas_call(kernel, in_specs=[IN_VMEM] * len(operands), out_specs=[IN_...  12.1 us
    pallas_call x1, Pallas kernels, launch(): pl.pallas_call(launch_kernel, in_specs=[pl.BlockSpec(memory_space=pltpu.H...  2.07 us
    unnamed x4, local copies, waits for them, and re-layouts  2.01 us
  transfers between devices with their start and end apart: 17, of which 7 were waited for; matrix products, arithmetic and copies ran while one was open for 1% of the time, Pallas kernels for 18%

profile of v16, /device:TPU:0, one launch (start us, length us, event | category | flops | bytes accessed | tf_op | source)
XLA Modules:
  0.0 56.6 jit_solution(13450091654327113653)
XLA Ops:
  0.6 2.4 %collective-permute-start = (f32[4,64,256]{2,1,0:T(8,128)}, f32[4,64,256]{2,1,0:T(8,128)S(1)}, u32[]{:S(2)}, u32[]{:S(2)}) collective-permute-start(f32[4,64,256]{2,1,0:T(8,128)} %bitcast.2), channel_id=1, source_target_pairs={{0,8},{1,9},{2,10},{3,11},{4,12},{5,13},{6,14},{7,15},{8,24},{9,25... | collective-permute-start | bytes 786440 | tf_op jit(solution)/shard_map/ppermute | solution.py:502
  3.0 0.7 %convert_element_type.5 = f32[1,4]{1,0:T(1,128)S(1)} convert(s32[1,4]{1,0:T(1,128)} %refs_2_.1) | non-fusion elementwise | flops 4 | bytes 32 | tf_op jit(solution)/shard_map/convert_element_type | solution.py:509
  3.7 0.6 %collective-permute-start.1 = (f32[8,128]{1,0:T(8,128)S(1)}, f32[8,128]{1,0:T(8,128)S(1)}, u32[]{:S(2)}, u32[]{:S(2)}) collective-permute-start(f32[8,128]{1,0:T(8,128)S(1)} %pad.4), channel_id=1, source_target_pairs={{8,24},{9,25},{10,26},{11,27},{12,28},{13,29},{14,30},{15,31}} | collective-permute-start | bytes 12296 | tf_op jit(solution)/shard_map/ppermute | solution.py:502
  4.3 2.1 %shard_map.104.bundle = f32[680,128]{1,0:T(8,128)} custom-call(f32[1,4,64,256]{3,2,1,0:T(8,128)} %refs_0_.1, f32[3,4,256]{2,1,0:T(4,128)} %refs_1_.1, s32[1,4]{1,0:T(1,128)} %refs_2_.1, f32[3,64]{1,0:T(4,128)} %refs_3_.1, f32[3,64]{1,0:T(4,128)} %refs_4_.1, f32[3,64]{1,0:T(4,128)} %refs_5_.1, f32[1,64]{1,0:T(1,128)} %bitcast.3, f32[64,64]{1,0:T(8,128)} %refs_7_.1), custom_call_target="tpu_custom_call" | custom-call | tf_op jit(solution)/shard_map/pallas_call | solution.py:215
  6.4 0.0 copy-start
  6.4 1.0 %copy-done = f32[680,128]{1,0:T(8,128)S(1)} copy-done((f32[680,128]{1,0:T(8,128)S(1)}, f32[680,128]{1,0:T(8,128)}, u32[]{:S(2)}) %copy-start) | copy-done | bytes 348184
  7.4 0.0 collective-permute-done.1.types
  7.4 0.0 collective-permute-done.moved
  7.5 0.7 %collective-permute-start.2 = (f32[4,64,256]{2,1,0:T(8,128)S(1)}, f32[4,64,256]{2,1,0:T(8,128)S(1)}, u32[]{:S(2)}, u32[]{:S(2)}) collective-permute-start(f32[4,64,256]{2,1,0:T(8,128)S(1)} %collective-permute-done.moved), channel_id=1, source_target_pairs={{24,16},{25,17},{26,18},{27,19},{28,20},{29,21},{30,22},{31,23}} | collective-permute-start | bytes 786440 | tf_op jit(solution)/shard_map/ppermute | solution.py:502
  8.1 0.0 collective-permute-done.2.passed
  8.2 2.4 %collective-permute-start.3 = (f32[544,128]{1,0:T(8,128)S(1)}, f32[544,128]{1,0:T(8,128)S(1)}, u32[]{:S(2)}, u32[]{:S(2)}) collective-permute-start(f32[544,128]{1,0:T(8,128)S(1)} %shard_map.106.refs_0_), channel_id=1, source_target_pairs={{0,1},{1,2},{2,3},{3,4},{4,5},{5,6},{6,7},{7,0},{8,10},{9,11},{10,... | collective-permute-start | bytes 835592 | tf_op jit(solution)/shard_map/ppermute | solution.py:502
  10.6 3.1 %collective-permute-start.5 = (f32[544,128]{1,0:T(8,128)S(1)}, f32[544,128]{1,0:T(8,128)S(1)}, u32[]{:S(2)}, u32[]{:S(2)}) collective-permute-start(f32[544,128]{1,0:T(8,128)S(1)} %shard_map.106.refs_0_), channel_id=1, source_target_pairs={{0,7},{1,0},{2,1},{3,2},{4,3},{5,4},{6,5},{7,6},{8,14},{9,15},{10,... | collective-permute-start | bytes 835592 | tf_op jit(solution)/shard_map/ppermute | solution.py:502
  13.7 1.3 %collective-permute-start.4 = (f32[8,128]{1,0:T(8,128)S(1)}, f32[8,128]{1,0:T(8,128)S(1)}, u32[]{:S(2)}, u32[]{:S(2)}) collective-permute-start(f32[8,128]{1,0:T(8,128)S(1)} %pad.4), channel_id=1, source_target_pairs={{16,0},{17,1},{18,2},{19,3},{20,4},{21,5},{22,6},{23,7}} | collective-permute-start | bytes 12296 | tf_op jit(solution)/shard_map/ppermute | solution.py:502
  15.0 0.0 copy-start.1
  15.0 1.0 %copy-done.1 = bf16[4,4,64,256]{3,2,1,0:T(8,128)(2,1)S(1)} copy-done((bf16[4,4,64,256]{3,2,1,0:T(8,128)(2,1)S(1)}, bf16[4,4,64,256]{3,2,1,0:T(8,128)(2,1)}, u32[]{:S(2)}) %copy-start.1) | copy-done | bytes 524312
  16.0 0.3 shard_map.107.refs_5_.refs_9_
  16.4 4.5 %collective-permute-done.4.across = f32[8,128]{1,0:T(8,128)S(1)} collective-permute-done((f32[8,128]{1,0:T(8,128)S(1)}, f32[8,128]{1,0:T(8,128)S(1)}, u32[]{:S(2)}, u32[]{:S(2)}) %collective-permute-start.4) | collective-permute-done | bytes 4128 | tf_op jit(solution)/shard_map/ppermute | solution.py:502
  20.9 0.0 collective-permute-done.3.refs_2_
  20.9 0.0 collective-permute-start.6
  20.9 0.0 collective-permute-done.5.refs_1_
  20.9 2.7 %collective-permute-start.7 = (f32[544,128]{1,0:T(8,128)S(1)}, f32[544,128]{1,0:T(8,128)S(1)}, u32[]{:S(2)}, u32[]{:S(2)}) collective-permute-start(f32[544,128]{1,0:T(8,128)S(1)} %collective-permute-done.5.refs_1_), channel_id=1, source_target_pairs={{0,8},{1,9},{2,10},{3,11},{4,12},{5,13},{6,14},{7,15},{8,0},{9,1},... | collective-permute-start | bytes 835592 | tf_op jit(solution)/shard_map/ppermute | solution.py:502
  23.6 0.0 collective-permute-done.6.refs_4_
  23.6 0.9 %shard_map.108.refs_6_ = f32[3,20,128,128]{3,2,1,0:T(8,128)S(1)} custom-call(f32[544,128]{1,0:T(8,128)S(1)} %shard_map.106.refs_0_, f32[544,128]{1,0:T(8,128)S(1)} %collective-permute-done.5.refs_1_, f32[544,128]{1,0:T(8,128)S(1)} %collective-permute-done.3.refs_2_), custom_call_target="tpu_custom_call" | custom-call | tf_op jit(solution)/shard_map/pallas_call | solution.py:475
  24.5 0.3 collective-permute-done.7.refs_3_
  24.8 1.3 %collective-permute-start.13 = (f32[4,4,128,128]{3,2,1,0:T(8,128)S(1)}, f32[4,4,128,128]{3,2,1,0:T(8,128)S(1)}, u32[]{:S(2)}, u32[]{:S(2)}) collective-permute-start(f32[4,4,128,128]{3,2,1,0:T(8,128)S(1)} %shard_map.107.refs_5_.refs_9_), channel_id=1, source_target_pairs={{16,0},{17,1},{18,2},{19,3},{20,4},{21,5},{22,6},{23,7}} | collective-permute-start | bytes 3145736 | tf_op jit(solution)/shard_map/ppermute | solution.py:502
  26.1 7.1 %shard_map.109 = (f32[4,128,128]{2,1,0:T(8,128)S(1)}, f32[264,128]{1,0:T(8,128)S(1)}, f32[4,128,128]{2,1,0:T(8,128)S(1)}, f32[4,128,128]{2,1,0:T(8,128)S(1)}, f32[3,20,128,128]{3,2,1,0:T(8,128)S(1)}) custom-call(f32[8,128]{1,0:T(8,128)S(1)} %get-tuple-element.29.taps, ...), custom_call_target="tpu_custom_call", output_to_operand_aliasing={{4}: (9, {})} | custom-call | tf_op jit(solution)/shard_map/pallas_call | solution.py:475
  33.1 2.2 %collective-permute-start.9 = (f32[264,128]{1,0:T(8,128)S(1)}, f32[264,128]{1,0:T(8,128)S(1)}, u32[]{:S(2)}, u32[]{:S(2)}) collective-permute-start(f32[264,128]{1,0:T(8,128)S(1)} %get-tuple-element.46), channel_id=1, source_target_pairs={{0,1},{1,2},{2,3},{3,4},{4,5},{5,6},{6,7},{7,0},{8,9},{9,10},{10,1... | collective-permute-start | bytes 405512 | tf_op jit(solution)/shard_map/ppermute | solution.py:502
  35.4 2.5 %collective-permute-start.8 = (f32[264,128]{1,0:T(8,128)S(1)}, f32[264,128]{1,0:T(8,128)S(1)}, u32[]{:S(2)}, u32[]{:S(2)}) collective-permute-start(f32[264,128]{1,0:T(8,128)S(1)} %get-tuple-element.46), channel_id=1, source_target_pairs={{0,7},{1,0},{2,1},{3,2},{4,3},{5,4},{6,5},{7,6},{8,15},{9,8},{10,9... | collective-permute-start | bytes 405512 | tf_op jit(solution)/shard_map/ppermute | solution.py:502
  37.9 0.0 collective-permute-start.12
  37.9 3.3 %collective-permute-done.9.refs_1_ = f32[264,128]{1,0:T(8,128)S(1)} collective-permute-done((f32[264,128]{1,0:T(8,128)S(1)}, f32[264,128]{1,0:T(8,128)S(1)}, u32[]{:S(2)}, u32[]{:S(2)}) %collective-permute-start.9) | collective-permute-done | bytes 135200 | tf_op jit(solution)/shard_map/ppermute | solution.py:502
  41.3 0.0 collective-permute-start.11
  41.3 1.8 %collective-permute-done.8.refs_0_ = f32[264,128]{1,0:T(8,128)S(1)} collective-permute-done((f32[264,128]{1,0:T(8,128)S(1)}, f32[264,128]{1,0:T(8,128)S(1)}, u32[]{:S(2)}, u32[]{:S(2)}) %collective-permute-start.8) | collective-permute-done | bytes 135200 | tf_op jit(solution)/shard_map/ppermute | solution.py:502
  43.0 0.0 collective-permute-start.10
  43.0 0.0 collective-permute-done.12.refs_7_
  43.0 0.0 collective-permute-done.11.refs_3_
  43.0 1.3 %collective-permute-done.10.refs_2_ = f32[264,128]{1,0:T(8,128)S(1)} collective-permute-done((f32[264,128]{1,0:T(8,128)S(1)}, f32[264,128]{1,0:T(8,128)S(1)}, u32[]{:S(2)}, u32[]{:S(2)}) %collective-permute-start.10) | collective-permute-done | bytes 135200 | tf_op jit(solution)/shard_map/ppermute | solution.py:502
  44.4 0.0 collective-permute-done.13.refs_8_
  44.4 2.9 %shard_map.110 = (f32[4,64,256]{2,1,0:T(8,128)S(1)}, f32[64,256]{1,0:T(8,128)S(1)}, f32[64,256]{1,0:T(8,128)S(1)}, f32[192,256]{1,0:T(8,128)S(1)}, f32[128,256]{1,0:T(8,128)S(1)}) custom-call(f32[8,128]{1,0:T(8,128)S(1)} %get-tuple-element.29.taps, bf16[256,256]{1,0:T(8,128)(2,1)S(1)} %get-tuple-element.30.weights, ...), custom_call_target="tpu_custom_call" | custom-call | tf_op jit(solution)/shard_map/pallas_call | solution.py:475
  47.3 2.3 %collective-permute-start.15 = (f32[192,256]{1,0:T(8,128)S(1)}, f32[192,256]{1,0:T(8,128)S(1)}, u32[]{:S(2)}, u32[]{:S(2)}) collective-permute-start(f32[192,256]{1,0:T(8,128)S(1)} %get-tuple-element.54), channel_id=1, source_target_pairs={{0,16},{1,17},{2,18},{3,19},{4,20},{5,21},{6,22},{7,23},{8,0},{9,1... | collective-permute-start | bytes 589832 | tf_op jit(solution)/shard_map/ppermute | solution.py:502
  49.7 0.1 collective-permute-start.16
  49.7 0.4 collective-permute-start.14
  50.2 0.9 %collective-permute-done.14.to_pair = f32[64,256]{1,0:T(8,128)S(1)} collective-permute-done((f32[64,256]{1,0:T(8,128)S(1)}, f32[64,256]{1,0:T(8,128)S(1)}, u32[]{:S(2)}, u32[]{:S(2)}) %collective-permute-start.14) | collective-permute-done | bytes 65568 | tf_op jit(solution)/shard_map/ppermute | solution.py:502
  51.1 4.7 %collective-permute-done.16.to_corner = f32[128,256]{1,0:T(8,128)S(1)} collective-permute-done((f32[128,256]{1,0:T(8,128)S(1)}, f32[128,256]{1,0:T(8,128)S(1)}, u32[]{:S(2)}, u32[]{:S(2)}) %collective-permute-start.16) | collective-permute-done | bytes 131104 | tf_op jit(solution)/shard_map/ppermute | solution.py:502
  55.8 0.0 collective-permute-done.15.to_across
  55.8 0.8 %shard_map.111 = (f32[1,4,64,256]{3,2,1,0:T(8,128)}, f32[4,16,256]{2,1,0:T(8,128)}) custom-call(f32[4,64,256]{2,1,0:T(8,128)S(1)} %get-tuple-element.51.handoff_in, f32[64,256]{1,0:T(8,128)S(1)} %get-tuple-element.52.share, f32[64,256]{1,0:T(8,128)S(1)} %collective-permute-done.14.to_pair, f32[192,256]{1,0:T(8,128)S(1)} %collective-permute-done.15.to_across, ...), custom_call_target="tpu_custom_call" | custom-call | tf_op jit(solution)/shard_map/pallas_call | solution.py:475
  (3 shorter events, 0.1 us)
Async XLA Ops:
  0.6 6.8 %collective-permute-start = (f32[4,64,256]{2,1,0:T(8,128)}, f32[4,64,256]{2,1,0:T(8,128)S(1)}, u32[]{:S(2)}, u32[]{:S(2)}) collective-permute-start(f32[4,64,256]{2,1,0:T(8,128)} %bitcast.2), channel_id=1, source_target_pairs={{0,8},{1,9},{2,10},{3,11},{4,12},{5,13},{6,14},{7,15},{8,24},{9,25... | collective-permute-start | bytes 786440 | tf_op jit(solution)/shard_map/ppermute | solution.py:502
  3.7 3.8 %collective-permute-start.1 = (f32[8,128]{1,0:T(8,128)S(1)}, f32[8,128]{1,0:T(8,128)S(1)}, u32[]{:S(2)}, u32[]{:S(2)}) collective-permute-start(f32[8,128]{1,0:T(8,128)S(1)} %pad.4), channel_id=1, source_target_pairs={{8,24},{9,25},{10,26},{11,27},{12,28},{13,29},{14,30},{15,31}} | collective-permute-start | bytes 12296 | tf_op jit(solution)/shard_map/ppermute | solution.py:502
  6.4 1.0 %copy-start = (f32[680,128]{1,0:T(8,128)S(1)}, f32[680,128]{1,0:T(8,128)}, u32[]{:S(2)}) copy-start(f32[680,128]{1,0:T(8,128)} %shard_map.104.bundle) | copy-start | bytes 1044484
  7.5 0.7 %collective-permute-start.2 = (f32[4,64,256]{2,1,0:T(8,128)S(1)}, f32[4,64,256]{2,1,0:T(8,128)S(1)}, u32[]{:S(2)}, u32[]{:S(2)}) collective-permute-start(f32[4,64,256]{2,1,0:T(8,128)S(1)} %collective-permute-done.moved), channel_id=1, source_target_pairs={{24,16},{25,17},{26,18},{27,19},{28,20},{29,21},{30,22},{31,23}} | collective-permute-start | bytes 786440 | tf_op jit(solution)/shard_map/ppermute | solution.py:502
  8.2 12.7 %collective-permute-start.3 = (f32[544,128]{1,0:T(8,128)S(1)}, f32[544,128]{1,0:T(8,128)S(1)}, u32[]{:S(2)}, u32[]{:S(2)}) collective-permute-start(f32[544,128]{1,0:T(8,128)S(1)} %shard_map.106.refs_0_), channel_id=1, source_target_pairs={{0,1},{1,2},{2,3},{3,4},{4,5},{5,6},{6,7},{7,0},{8,10},{9,11},{10,... | collective-permute-start | bytes 835592 | tf_op jit(solution)/shard_map/ppermute | solution.py:502
  10.6 10.3 %collective-permute-start.5 = (f32[544,128]{1,0:T(8,128)S(1)}, f32[544,128]{1,0:T(8,128)S(1)}, u32[]{:S(2)}, u32[]{:S(2)}) collective-permute-start(f32[544,128]{1,0:T(8,128)S(1)} %shard_map.106.refs_0_), channel_id=1, source_target_pairs={{0,7},{1,0},{2,1},{3,2},{4,3},{5,4},{6,5},{7,6},{8,14},{9,15},{10,... | collective-permute-start | bytes 835592 | tf_op jit(solution)/shard_map/ppermute | solution.py:502
  13.7 7.2 %collective-permute-start.4 = (f32[8,128]{1,0:T(8,128)S(1)}, f32[8,128]{1,0:T(8,128)S(1)}, u32[]{:S(2)}, u32[]{:S(2)}) collective-permute-start(f32[8,128]{1,0:T(8,128)S(1)} %pad.4), channel_id=1, source_target_pairs={{16,0},{17,1},{18,2},{19,3},{20,4},{21,5},{22,6},{23,7}} | collective-permute-start | bytes 12296 | tf_op jit(solution)/shard_map/ppermute | solution.py:502
  15.0 1.0 %copy-start.1 = (bf16[4,4,64,256]{3,2,1,0:T(8,128)(2,1)S(1)}, bf16[4,4,64,256]{3,2,1,0:T(8,128)(2,1)}, u32[]{:S(2)}) copy-start(bf16[4,4,64,256]{3,2,1,0:T(8,128)(2,1)} %backward) | copy-start | bytes 1572868
  20.9 2.7 %collective-permute-start.6 = (f32[544,128]{1,0:T(8,128)S(1)}, f32[544,128]{1,0:T(8,128)S(1)}, u32[]{:S(2)}, u32[]{:S(2)}) collective-permute-start(f32[544,128]{1,0:T(8,128)S(1)} %collective-permute-done.3.refs_2_), channel_id=1, source_target_pairs={{0,8},{1,9},{2,10},{3,11},{4,12},{5,13},{6,14},{7,15},{8,0},{9,1},... | collective-permute-start | bytes 835592 | tf_op jit(solution)/shard_map/ppermute | solution.py:502
  20.9 3.9 %collective-permute-start.7 = (f32[544,128]{1,0:T(8,128)S(1)}, f32[544,128]{1,0:T(8,128)S(1)}, u32[]{:S(2)}, u32[]{:S(2)}) collective-permute-start(f32[544,128]{1,0:T(8,128)S(1)} %collective-permute-done.5.refs_1_), channel_id=1, source_target_pairs={{0,8},{1,9},{2,10},{3,11},{4,12},{5,13},{6,14},{7,15},{8,0},{9,1},... | collective-permute-start | bytes 835592 | tf_op jit(solution)/shard_map/ppermute | solution.py:502
  24.8 19.6 %collective-permute-start.13 = (f32[4,4,128,128]{3,2,1,0:T(8,128)S(1)}, f32[4,4,128,128]{3,2,1,0:T(8,128)S(1)}, u32[]{:S(2)}, u32[]{:S(2)}) collective-permute-start(f32[4,4,128,128]{3,2,1,0:T(8,128)S(1)} %shard_map.107.refs_5_.refs_9_), channel_id=1, source_target_pairs={{16,0},{17,1},{18,2},{19,3},{20,4},{21,5},{22,6},{23,7}} | collective-permute-start | bytes 3145736 | tf_op jit(solution)/shard_map/ppermute | solution.py:502
  33.1 8.1 %collective-permute-start.9 = (f32[264,128]{1,0:T(8,128)S(1)}, f32[264,128]{1,0:T(8,128)S(1)}, u32[]{:S(2)}, u32[]{:S(2)}) collective-permute-start(f32[264,128]{1,0:T(8,128)S(1)} %get-tuple-element.46), channel_id=1, source_target_pairs={{0,1},{1,2},{2,3},{3,4},{4,5},{5,6},{6,7},{7,0},{8,9},{9,10},{10,1... | collective-permute-start | bytes 405512 | tf_op jit(solution)/shard_map/ppermute | solution.py:502
  35.4 7.6 %collective-permute-start.8 = (f32[264,128]{1,0:T(8,128)S(1)}, f32[264,128]{1,0:T(8,128)S(1)}, u32[]{:S(2)}, u32[]{:S(2)}) collective-permute-start(f32[264,128]{1,0:T(8,128)S(1)} %get-tuple-element.46), channel_id=1, source_target_pairs={{0,7},{1,0},{2,1},{3,2},{4,3},{5,4},{6,5},{7,6},{8,15},{9,8},{10,9... | collective-permute-start | bytes 405512 | tf_op jit(solution)/shard_map/ppermute | solution.py:502
  37.9 5.1 %collective-permute-start.12 = (f32[4,128,128]{2,1,0:T(8,128)S(1)}, f32[4,128,128]{2,1,0:T(8,128)S(1)}, u32[]{:S(2)}, u32[]{:S(2)}) collective-permute-start(f32[4,128,128]{2,1,0:T(8,128)S(1)} %get-tuple-element.49.refs_6_), channel_id=1, source_target_pairs={{0,8},{1,9},{2,10},{3,11},{4,12},{5,13},{6,14},{7,15},{8,0},{9,1},... | collective-permute-start | bytes 786440 | tf_op jit(solution)/shard_map/ppermute | solution.py:502
  41.3 1.8 %collective-permute-start.11 = (f32[264,128]{1,0:T(8,128)S(1)}, f32[264,128]{1,0:T(8,128)S(1)}, u32[]{:S(2)}, u32[]{:S(2)}) collective-permute-start(f32[264,128]{1,0:T(8,128)S(1)} %collective-permute-done.9.refs_1_), channel_id=1, source_target_pairs={{0,8},{1,9},{2,10},{3,11},{4,12},{5,13},{6,14},{7,15},{8,0},{9,1},... | collective-permute-start | bytes 405512 | tf_op jit(solution)/shard_map/ppermute | solution.py:502
  43.0 1.4 %collective-permute-start.10 = (f32[264,128]{1,0:T(8,128)S(1)}, f32[264,128]{1,0:T(8,128)S(1)}, u32[]{:S(2)}, u32[]{:S(2)}) collective-permute-start(f32[264,128]{1,0:T(8,128)S(1)} %collective-permute-done.8.refs_0_), channel_id=1, source_target_pairs={{0,8},{1,9},{2,10},{3,11},{4,12},{5,13},{6,14},{7,15},{8,0},{9,1},... | collective-permute-start | bytes 405512 | tf_op jit(solution)/shard_map/ppermute | solution.py:502
  47.3 8.5 %collective-permute-start.15 = (f32[192,256]{1,0:T(8,128)S(1)}, f32[192,256]{1,0:T(8,128)S(1)}, u32[]{:S(2)}, u32[]{:S(2)}) collective-permute-start(f32[192,256]{1,0:T(8,128)S(1)} %get-tuple-element.54), channel_id=1, source_target_pairs={{0,16},{1,17},{2,18},{3,19},{4,20},{5,21},{6,22},{7,23},{8,0},{9,1... | collective-permute-start | bytes 589832 | tf_op jit(solution)/shard_map/ppermute | solution.py:502
  49.7 6.2 %collective-permute-start.16 = (f32[128,256]{1,0:T(8,128)S(1)}, f32[128,256]{1,0:T(8,128)S(1)}, u32[]{:S(2)}, u32[]{:S(2)}) collective-permute-start(f32[128,256]{1,0:T(8,128)S(1)} %get-tuple-element.55), channel_id=1, source_target_pairs={{0,24},{1,25},{2,26},{3,27},{4,28},{5,29},{6,30},{7,31},{8,16},{9,... | collective-permute-start | bytes 393224 | tf_op jit(solution)/shard_map/ppermute | solution.py:502
  49.7 1.3 %collective-permute-start.14 = (f32[64,256]{1,0:T(8,128)S(1)}, f32[64,256]{1,0:T(8,128)S(1)}, u32[]{:S(2)}, u32[]{:S(2)}) collective-permute-start(f32[64,256]{1,0:T(8,128)S(1)} %get-tuple-element.53), channel_id=1, source_target_pairs={{0,8},{1,9},{2,10},{3,11},{4,12},{5,13},{6,14},{7,15},{8,0},{9,1},... | collective-permute-start | bytes 196616 | tf_op jit(solution)/shard_map/ppermute | solution.py:502

commit v17 on v16

--- a/solution.py
+++ b/solution.py
@@ -444,12 +444,14 @@
             (to_corner, last - sec),
         ):
             piece[i * count : (i + 1) * count] = whole[pl.ds(pl.multiple_of(who * count, count), count)]
-    for i in range(pair):
-        to_across[held + i * orients : held + (i + 1) * orients] = from_tile(state[reach + pair * odd + i], scratch)
+    few = planes // 4
+    for i in range(few):
+        to_across[held + i * orients : held + (i + 1) * orients] = from_tile(state[reach + i], scratch)
 
     @pl.when(sec == 1)
     def _():
-        to_corner[...] = to_across[held:]
+        for i in range(few, planes):
+            to_corner[(i - few) * orients : (i - few + 1) * orients] = from_tile(state[reach + i], scratch)
 
 
 def finish_kernel(contour, handoff_in, share, to_pair, to_across, to_corner, handoff, density):
@@ -465,10 +467,11 @@
     @pl.when(sec == 2)
     def _():
         orients = handoff.shape[2]
-        pair = planes // 2
-        for i in range(pair):
+        few = planes // 4
+        for i in range(few):
             handoff[0, i] = to_across[held + i * orients : held + (i + 1) * orients]
-            handoff[0, pair + i] = to_corner[i * orients : (i + 1) * orients]
+        for i in range(few, planes):
+            handoff[0, i] = to_corner[(i - few) * orients : (i - few + 1) * orients]
 
 
 def call(kernel, out_shape, scratch, operands, dtypes=None, aliases=None, cost=None):
@@ -551,7 +554,7 @@
         functools.partial(late_kernel, tuple(-shift for shift in near), last),
         [(planes, orients, cells)]
         + [(held, cells)] * 2
-        + [(held + pair * orients, cells), (pair * orients, cells)],
+        + [(held + planes // 4 * orients, cells), ((planes - planes // 4) * orients, cells)],
         work(reach[1]) + [inner, inner, pltpu.VMEM((orients, cells), jnp.float32)],
         [taps, weights, middle, *own, *swapped, factor, kept, total, beside_total]
         + [late_last, stored],
@@ -572,7 +575,7 @@
     return (
         n_sec == TICKS + 1 == 4
         and planes == steps
-        and planes % 2 == 0
+        and planes % 4 == 0
         and 2 * orients == 2 * CZ == cells // 2 == 128
         and 2 * kinds * planes <= OWN_KINDS and 10 * kinds * planes <= 2 * orients
         and GROUP < 2 * planes

time: 56.9 us -> 57 us (level)
  no operation moved by 1% of the time
where the time goes in v17:
time: 57 us; the launch traced here: 56.6 us
  starting transfers between devices  22.1 us (39%)
  waiting for transfers between devices  16.8 us (29%)
  Pallas kernels  14.2 us (25%)
  local copies, waits for them, and re-layouts  2.02 us (4%)
  between operations  0.77 us (1%)
  other arithmetic  0.66 us (1%)
    ppermute x17, starting transfers between devices, send(): return lax.ppermute(array, ('sec', 'gx'), pairs)  22.1 us
    ppermute x17, waiting for transfers between devices, send(): return lax.ppermute(array, ('sec', 'gx'), pairs)  16.8 us
    pallas_call x7, Pallas kernels, call(): pl.pallas_call(kernel, in_specs=[IN_VMEM] * len(operands), out_specs=[IN_...  12.1 us
    pallas_call x1, Pallas kernels, launch(): pl.pallas_call(launch_kernel, in_specs=[pl.BlockSpec(memory_space=pltpu.H...  2.07 us
    unnamed x4, local copies, waits for them, and re-layouts  2.01 us
  transfers between devices with their start and end apart: 17, of which 7 were waited for; matrix products, arithmetic and copies ran while one was open for 1% of the time, Pallas kernels for 18%

profile of v17, /device:TPU:0, one launch (start us, length us, event | category | flops | bytes accessed | tf_op | source)
XLA Modules:
  0.0 56.6 jit_solution(8722371979616629285)
XLA Ops:
  0.6 2.4 %collective-permute-start = (f32[4,64,256]{2,1,0:T(8,128)}, f32[4,64,256]{2,1,0:T(8,128)S(1)}, u32[]{:S(2)}, u32[]{:S(2)}) collective-permute-start(f32[4,64,256]{2,1,0:T(8,128)} %bitcast.2), channel_id=1, source_target_pairs={{0,8},{1,9},{2,10},{3,11},{4,12},{5,13},{6,14},{7,15},{8,24},{9,25... | collective-permute-start | bytes 786440 | tf_op jit(solution)/shard_map/ppermute | solution.py:505
  3.0 0.7 %convert_element_type.5 = f32[1,4]{1,0:T(1,128)S(1)} convert(s32[1,4]{1,0:T(1,128)} %refs_2_.1) | non-fusion elementwise | flops 4 | bytes 32 | tf_op jit(solution)/shard_map/convert_element_type | solution.py:512
  3.7 0.6 %collective-permute-start.1 = (f32[8,128]{1,0:T(8,128)S(1)}, f32[8,128]{1,0:T(8,128)S(1)}, u32[]{:S(2)}, u32[]{:S(2)}) collective-permute-start(f32[8,128]{1,0:T(8,128)S(1)} %pad.4), channel_id=1, source_target_pairs={{8,24},{9,25},{10,26},{11,27},{12,28},{13,29},{14,30},{15,31}} | collective-permute-start | bytes 12296 | tf_op jit(solution)/shard_map/ppermute | solution.py:505
  4.3 2.1 %shard_map.104.bundle = f32[680,128]{1,0:T(8,128)} custom-call(f32[1,4,64,256]{3,2,1,0:T(8,128)} %refs_0_.1, f32[3,4,256]{2,1,0:T(4,128)} %refs_1_.1, s32[1,4]{1,0:T(1,128)} %refs_2_.1, f32[3,64]{1,0:T(4,128)} %refs_3_.1, f32[3,64]{1,0:T(4,128)} %refs_4_.1, f32[3,64]{1,0:T(4,128)} %refs_5_.1, f32[1,64]{1,0:T(1,128)} %bitcast.3, f32[64,64]{1,0:T(8,128)} %refs_7_.1), custom_call_target="tpu_custom_call" | custom-call | tf_op jit(solution)/shard_map/pallas_call | solution.py:215
  6.4 0.0 copy-start
  6.4 1.0 %copy-done = f32[680,128]{1,0:T(8,128)S(1)} copy-done((f32[680,128]{1,0:T(8,128)S(1)}, f32[680,128]{1,0:T(8,128)}, u32[]{:S(2)}) %copy-start) | copy-done | bytes 348184
  7.4 0.0 collective-permute-done.1.types
  7.4 0.0 collective-permute-done.moved
  7.5 0.7 %collective-permute-start.2 = (f32[4,64,256]{2,1,0:T(8,128)S(1)}, f32[4,64,256]{2,1,0:T(8,128)S(1)}, u32[]{:S(2)}, u32[]{:S(2)}) collective-permute-start(f32[4,64,256]{2,1,0:T(8,128)S(1)} %collective-permute-done.moved), channel_id=1, source_target_pairs={{24,16},{25,17},{26,18},{27,19},{28,20},{29,21},{30,22},{31,23}} | collective-permute-start | bytes 786440 | tf_op jit(solution)/shard_map/ppermute | solution.py:505
  8.1 0.0 collective-permute-done.2.passed
  8.2 2.4 %collective-permute-start.3 = (f32[544,128]{1,0:T(8,128)S(1)}, f32[544,128]{1,0:T(8,128)S(1)}, u32[]{:S(2)}, u32[]{:S(2)}) collective-permute-start(f32[544,128]{1,0:T(8,128)S(1)} %shard_map.106.refs_0_), channel_id=1, source_target_pairs={{0,1},{1,2},{2,3},{3,4},{4,5},{5,6},{6,7},{7,0},{8,10},{9,11},{10,... | collective-permute-start | bytes 835592 | tf_op jit(solution)/shard_map/ppermute | solution.py:505
  10.6 3.1 %collective-permute-start.5 = (f32[544,128]{1,0:T(8,128)S(1)}, f32[544,128]{1,0:T(8,128)S(1)}, u32[]{:S(2)}, u32[]{:S(2)}) collective-permute-start(f32[544,128]{1,0:T(8,128)S(1)} %shard_map.106.refs_0_), channel_id=1, source_target_pairs={{0,7},{1,0},{2,1},{3,2},{4,3},{5,4},{6,5},{7,6},{8,14},{9,15},{10,... | collective-permute-start | bytes 835592 | tf_op jit(solution)/shard_map/ppermute | solution.py:505
  13.7 1.3 %collective-permute-start.4 = (f32[8,128]{1,0:T(8,128)S(1)}, f32[8,128]{1,0:T(8,128)S(1)}, u32[]{:S(2)}, u32[]{:S(2)}) collective-permute-start(f32[8,128]{1,0:T(8,128)S(1)} %pad.4), channel_id=1, source_target_pairs={{16,0},{17,1},{18,2},{19,3},{20,4},{21,5},{22,6},{23,7}} | collective-permute-start | bytes 12296 | tf_op jit(solution)/shard_map/ppermute | solution.py:505
  15.0 0.0 copy-start.1
  15.0 1.0 %copy-done.1 = bf16[4,4,64,256]{3,2,1,0:T(8,128)(2,1)S(1)} copy-done((bf16[4,4,64,256]{3,2,1,0:T(8,128)(2,1)S(1)}, bf16[4,4,64,256]{3,2,1,0:T(8,128)(2,1)}, u32[]{:S(2)}) %copy-start.1) | copy-done | bytes 524312
  16.0 0.3 shard_map.107.refs_5_.refs_9_
  16.4 4.5 %collective-permute-done.4.across = f32[8,128]{1,0:T(8,128)S(1)} collective-permute-done((f32[8,128]{1,0:T(8,128)S(1)}, f32[8,128]{1,0:T(8,128)S(1)}, u32[]{:S(2)}, u32[]{:S(2)}) %collective-permute-start.4) | collective-permute-done | bytes 4128 | tf_op jit(solution)/shard_map/ppermute | solution.py:505
  20.9 0.0 collective-permute-done.3.refs_2_
  20.9 0.0 collective-permute-start.6
  20.9 0.0 collective-permute-done.5.refs_1_
  20.9 2.7 %collective-permute-start.7 = (f32[544,128]{1,0:T(8,128)S(1)}, f32[544,128]{1,0:T(8,128)S(1)}, u32[]{:S(2)}, u32[]{:S(2)}) collective-permute-start(f32[544,128]{1,0:T(8,128)S(1)} %collective-permute-done.5.refs_1_), channel_id=1, source_target_pairs={{0,8},{1,9},{2,10},{3,11},{4,12},{5,13},{6,14},{7,15},{8,0},{9,1},... | collective-permute-start | bytes 835592 | tf_op jit(solution)/shard_map/ppermute | solution.py:505
  23.6 0.0 collective-permute-done.6.refs_4_
  23.6 0.9 %shard_map.108.refs_6_ = f32[3,20,128,128]{3,2,1,0:T(8,128)S(1)} custom-call(f32[544,128]{1,0:T(8,128)S(1)} %shard_map.106.refs_0_, f32[544,128]{1,0:T(8,128)S(1)} %collective-permute-done.5.refs_1_, f32[544,128]{1,0:T(8,128)S(1)} %collective-permute-done.3.refs_2_), custom_call_target="tpu_custom_call" | custom-call | tf_op jit(solution)/shard_map/pallas_call | solution.py:478
  24.5 0.3 collective-permute-done.7.refs_3_
  24.8 1.3 %collective-permute-start.13 = (f32[4,4,128,128]{3,2,1,0:T(8,128)S(1)}, f32[4,4,128,128]{3,2,1,0:T(8,128)S(1)}, u32[]{:S(2)}, u32[]{:S(2)}) collective-permute-start(f32[4,4,128,128]{3,2,1,0:T(8,128)S(1)} %shard_map.107.refs_5_.refs_9_), channel_id=1, source_target_pairs={{16,0},{17,1},{18,2},{19,3},{20,4},{21,5},{22,6},{23,7}} | collective-permute-start | bytes 3145736 | tf_op jit(solution)/shard_map/ppermute | solution.py:505
  26.1 7.1 %shard_map.109 = (f32[4,128,128]{2,1,0:T(8,128)S(1)}, f32[264,128]{1,0:T(8,128)S(1)}, f32[4,128,128]{2,1,0:T(8,128)S(1)}, f32[4,128,128]{2,1,0:T(8,128)S(1)}, f32[3,20,128,128]{3,2,1,0:T(8,128)S(1)}) custom-call(f32[8,128]{1,0:T(8,128)S(1)} %get-tuple-element.29.taps, ...), custom_call_target="tpu_custom_call", output_to_operand_aliasing={{4}: (9, {})} | custom-call | tf_op jit(solution)/shard_map/pallas_call | solution.py:478
  33.1 2.2 %collective-permute-start.9 = (f32[264,128]{1,0:T(8,128)S(1)}, f32[264,128]{1,0:T(8,128)S(1)}, u32[]{:S(2)}, u32[]{:S(2)}) collective-permute-start(f32[264,128]{1,0:T(8,128)S(1)} %get-tuple-element.46), channel_id=1, source_target_pairs={{0,1},{1,2},{2,3},{3,4},{4,5},{5,6},{6,7},{7,0},{8,9},{9,10},{10,1... | collective-permute-start | bytes 405512 | tf_op jit(solution)/shard_map/ppermute | solution.py:505
  35.4 2.5 %collective-permute-start.8 = (f32[264,128]{1,0:T(8,128)S(1)}, f32[264,128]{1,0:T(8,128)S(1)}, u32[]{:S(2)}, u32[]{:S(2)}) collective-permute-start(f32[264,128]{1,0:T(8,128)S(1)} %get-tuple-element.46), channel_id=1, source_target_pairs={{0,7},{1,0},{2,1},{3,2},{4,3},{5,4},{6,5},{7,6},{8,15},{9,8},{10,9... | collective-permute-start | bytes 405512 | tf_op jit(solution)/shard_map/ppermute | solution.py:505
  37.9 0.0 collective-permute-start.12
  37.9 3.3 %collective-permute-done.9.refs_1_ = f32[264,128]{1,0:T(8,128)S(1)} collective-permute-done((f32[264,128]{1,0:T(8,128)S(1)}, f32[264,128]{1,0:T(8,128)S(1)}, u32[]{:S(2)}, u32[]{:S(2)}) %collective-permute-start.9) | collective-permute-done | bytes 135200 | tf_op jit(solution)/shard_map/ppermute | solution.py:505
  41.3 0.0 collective-permute-start.11
  41.3 1.8 %collective-permute-done.8.refs_0_ = f32[264,128]{1,0:T(8,128)S(1)} collective-permute-done((f32[264,128]{1,0:T(8,128)S(1)}, f32[264,128]{1,0:T(8,128)S(1)}, u32[]{:S(2)}, u32[]{:S(2)}) %collective-permute-start.8) | collective-permute-done | bytes 135200 | tf_op jit(solution)/shard_map/ppermute | solution.py:505
  43.0 0.0 collective-permute-start.10
  43.0 0.0 collective-permute-done.12.refs_7_
  43.0 0.0 collective-permute-done.11.refs_3_
  43.0 1.3 %collective-permute-done.10.refs_2_ = f32[264,128]{1,0:T(8,128)S(1)} collective-permute-done((f32[264,128]{1,0:T(8,128)S(1)}, f32[264,128]{1,0:T(8,128)S(1)}, u32[]{:S(2)}, u32[]{:S(2)}) %collective-permute-start.10) | collective-permute-done | bytes 135200 | tf_op jit(solution)/shard_map/ppermute | solution.py:505
  44.4 0.0 collective-permute-done.13.refs_8_
  44.4 2.9 %shard_map.110 = (f32[4,64,256]{2,1,0:T(8,128)S(1)}, f32[64,256]{1,0:T(8,128)S(1)}, f32[64,256]{1,0:T(8,128)S(1)}, f32[128,256]{1,0:T(8,128)S(1)}, f32[192,256]{1,0:T(8,128)S(1)}) custom-call(f32[8,128]{1,0:T(8,128)S(1)} %get-tuple-element.29.taps, bf16[256,256]{1,0:T(8,128)(2,1)S(1)} %get-tuple-element.30.weights, ...), custom_call_target="tpu_custom_call" | custom-call | tf_op jit(solution)/shard_map/pallas_call | solution.py:478
  47.3 2.4 %collective-permute-start.16 = (f32[192,256]{1,0:T(8,128)S(1)}, f32[192,256]{1,0:T(8,128)S(1)}, u32[]{:S(2)}, u32[]{:S(2)}) collective-permute-start(f32[192,256]{1,0:T(8,128)S(1)} %get-tuple-element.55), channel_id=1, source_target_pairs={{0,24},{1,25},{2,26},{3,27},{4,28},{5,29},{6,30},{7,31},{8,16},{9,... | collective-permute-start | bytes 589832 | tf_op jit(solution)/shard_map/ppermute | solution.py:505
  49.7 0.0 collective-permute-start.15
  49.8 0.5 collective-permute-start.14
  50.2 0.9 %collective-permute-done.14.to_pair = f32[64,256]{1,0:T(8,128)S(1)} collective-permute-done((f32[64,256]{1,0:T(8,128)S(1)}, f32[64,256]{1,0:T(8,128)S(1)}, u32[]{:S(2)}, u32[]{:S(2)}) %collective-permute-start.14) | collective-permute-done | bytes 65568 | tf_op jit(solution)/shard_map/ppermute | solution.py:505
  51.2 4.6 %collective-permute-done.15.to_across = f32[128,256]{1,0:T(8,128)S(1)} collective-permute-done((f32[128,256]{1,0:T(8,128)S(1)}, f32[128,256]{1,0:T(8,128)S(1)}, u32[]{:S(2)}, u32[]{:S(2)}) %collective-permute-start.15) | collective-permute-done | bytes 131104 | tf_op jit(solution)/shard_map/ppermute | solution.py:505
  55.8 0.0 collective-permute-done.16.to_corner
  55.8 0.8 %shard_map.111 = (f32[1,4,64,256]{3,2,1,0:T(8,128)}, f32[4,16,256]{2,1,0:T(8,128)}) custom-call(f32[4,64,256]{2,1,0:T(8,128)S(1)} %get-tuple-element.51.handoff_in, f32[64,256]{1,0:T(8,128)S(1)} %get-tuple-element.52.share, f32[64,256]{1,0:T(8,128)S(1)} %collective-permute-done.14.to_pair, f32[128,256]{1,0:T(8,128)S(1)} %collective-permute-done.15.to_across, ...), custom_call_target="tpu_custom_call" | custom-call | tf_op jit(solution)/shard_map/pallas_call | solution.py:478
  (3 shorter events, 0.1 us)
Async XLA Ops:
  0.6 6.8 %collective-permute-start = (f32[4,64,256]{2,1,0:T(8,128)}, f32[4,64,256]{2,1,0:T(8,128)S(1)}, u32[]{:S(2)}, u32[]{:S(2)}) collective-permute-start(f32[4,64,256]{2,1,0:T(8,128)} %bitcast.2), channel_id=1, source_target_pairs={{0,8},{1,9},{2,10},{3,11},{4,12},{5,13},{6,14},{7,15},{8,24},{9,25... | collective-permute-start | bytes 786440 | tf_op jit(solution)/shard_map/ppermute | solution.py:505
  3.7 3.8 %collective-permute-start.1 = (f32[8,128]{1,0:T(8,128)S(1)}, f32[8,128]{1,0:T(8,128)S(1)}, u32[]{:S(2)}, u32[]{:S(2)}) collective-permute-start(f32[8,128]{1,0:T(8,128)S(1)} %pad.4), channel_id=1, source_target_pairs={{8,24},{9,25},{10,26},{11,27},{12,28},{13,29},{14,30},{15,31}} | collective-permute-start | bytes 12296 | tf_op jit(solution)/shard_map/ppermute | solution.py:505
  6.4 1.0 %copy-start = (f32[680,128]{1,0:T(8,128)S(1)}, f32[680,128]{1,0:T(8,128)}, u32[]{:S(2)}) copy-start(f32[680,128]{1,0:T(8,128)} %shard_map.104.bundle) | copy-start | bytes 1044484
  7.5 0.7 %collective-permute-start.2 = (f32[4,64,256]{2,1,0:T(8,128)S(1)}, f32[4,64,256]{2,1,0:T(8,128)S(1)}, u32[]{:S(2)}, u32[]{:S(2)}) collective-permute-start(f32[4,64,256]{2,1,0:T(8,128)S(1)} %collective-permute-done.moved), channel_id=1, source_target_pairs={{24,16},{25,17},{26,18},{27,19},{28,20},{29,21},{30,22},{31,23}} | collective-permute-start | bytes 786440 | tf_op jit(solution)/shard_map/ppermute | solution.py:505
  8.2 12.7 %collective-permute-start.3 = (f32[544,128]{1,0:T(8,128)S(1)}, f32[544,128]{1,0:T(8,128)S(1)}, u32[]{:S(2)}, u32[]{:S(2)}) collective-permute-start(f32[544,128]{1,0:T(8,128)S(1)} %shard_map.106.refs_0_), channel_id=1, source_target_pairs={{0,1},{1,2},{2,3},{3,4},{4,5},{5,6},{6,7},{7,0},{8,10},{9,11},{10,... | collective-permute-start | bytes 835592 | tf_op jit(solution)/shard_map/ppermute | solution.py:505
  10.6 10.3 %collective-permute-start.5 = (f32[544,128]{1,0:T(8,128)S(1)}, f32[544,128]{1,0:T(8,128)S(1)}, u32[]{:S(2)}, u32[]{:S(2)}) collective-permute-start(f32[544,128]{1,0:T(8,128)S(1)} %shard_map.106.refs_0_), channel_id=1, source_target_pairs={{0,7},{1,0},{2,1},{3,2},{4,3},{5,4},{6,5},{7,6},{8,14},{9,15},{10,... | collective-permute-start | bytes 835592 | tf_op jit(solution)/shard_map/ppermute | solution.py:505
  13.7 7.2 %collective-permute-start.4 = (f32[8,128]{1,0:T(8,128)S(1)}, f32[8,128]{1,0:T(8,128)S(1)}, u32[]{:S(2)}, u32[]{:S(2)}) collective-permute-start(f32[8,128]{1,0:T(8,128)S(1)} %pad.4), channel_id=1, source_target_pairs={{16,0},{17,1},{18,2},{19,3},{20,4},{21,5},{22,6},{23,7}} | collective-permute-start | bytes 12296 | tf_op jit(solution)/shard_map/ppermute | solution.py:505
  15.0 1.0 %copy-start.1 = (bf16[4,4,64,256]{3,2,1,0:T(8,128)(2,1)S(1)}, bf16[4,4,64,256]{3,2,1,0:T(8,128)(2,1)}, u32[]{:S(2)}) copy-start(bf16[4,4,64,256]{3,2,1,0:T(8,128)(2,1)} %backward) | copy-start | bytes 1572868
  20.9 2.7 %collective-permute-start.6 = (f32[544,128]{1,0:T(8,128)S(1)}, f32[544,128]{1,0:T(8,128)S(1)}, u32[]{:S(2)}, u32[]{:S(2)}) collective-permute-start(f32[544,128]{1,0:T(8,128)S(1)} %collective-permute-done.3.refs_2_), channel_id=1, source_target_pairs={{0,8},{1,9},{2,10},{3,11},{4,12},{5,13},{6,14},{7,15},{8,0},{9,1},... | collective-permute-start | bytes 835592 | tf_op jit(solution)/shard_map/ppermute | solution.py:505
  20.9 3.9 %collective-permute-start.7 = (f32[544,128]{1,0:T(8,128)S(1)}, f32[544,128]{1,0:T(8,128)S(1)}, u32[]{:S(2)}, u32[]{:S(2)}) collective-permute-start(f32[544,128]{1,0:T(8,128)S(1)} %collective-permute-done.5.refs_1_), channel_id=1, source_target_pairs={{0,8},{1,9},{2,10},{3,11},{4,12},{5,13},{6,14},{7,15},{8,0},{9,1},... | collective-permute-start | bytes 835592 | tf_op jit(solution)/shard_map/ppermute | solution.py:505
  24.8 19.6 %collective-permute-start.13 = (f32[4,4,128,128]{3,2,1,0:T(8,128)S(1)}, f32[4,4,128,128]{3,2,1,0:T(8,128)S(1)}, u32[]{:S(2)}, u32[]{:S(2)}) collective-permute-start(f32[4,4,128,128]{3,2,1,0:T(8,128)S(1)} %shard_map.107.refs_5_.refs_9_), channel_id=1, source_target_pairs={{16,0},{17,1},{18,2},{19,3},{20,4},{21,5},{22,6},{23,7}} | collective-permute-start | bytes 3145736 | tf_op jit(solution)/shard_map/ppermute | solution.py:505
  33.1 8.1 %collective-permute-start.9 = (f32[264,128]{1,0:T(8,128)S(1)}, f32[264,128]{1,0:T(8,128)S(1)}, u32[]{:S(2)}, u32[]{:S(2)}) collective-permute-start(f32[264,128]{1,0:T(8,128)S(1)} %get-tuple-element.46), channel_id=1, source_target_pairs={{0,1},{1,2},{2,3},{3,4},{4,5},{5,6},{6,7},{7,0},{8,9},{9,10},{10,1... | collective-permute-start | bytes 405512 | tf_op jit(solution)/shard_map/ppermute | solution.py:505
  35.4 7.6 %collective-permute-start.8 = (f32[264,128]{1,0:T(8,128)S(1)}, f32[264,128]{1,0:T(8,128)S(1)}, u32[]{:S(2)}, u32[]{:S(2)}) collective-permute-start(f32[264,128]{1,0:T(8,128)S(1)} %get-tuple-element.46), channel_id=1, source_target_pairs={{0,7},{1,0},{2,1},{3,2},{4,3},{5,4},{6,5},{7,6},{8,15},{9,8},{10,9... | collective-permute-start | bytes 405512 | tf_op jit(solution)/shard_map/ppermute | solution.py:505
  37.9 5.1 %collective-permute-start.12 = (f32[4,128,128]{2,1,0:T(8,128)S(1)}, f32[4,128,128]{2,1,0:T(8,128)S(1)}, u32[]{:S(2)}, u32[]{:S(2)}) collective-permute-start(f32[4,128,128]{2,1,0:T(8,128)S(1)} %get-tuple-element.49.refs_6_), channel_id=1, source_target_pairs={{0,8},{1,9},{2,10},{3,11},{4,12},{5,13},{6,14},{7,15},{8,0},{9,1},... | collective-permute-start | bytes 786440 | tf_op jit(solution)/shard_map/ppermute | solution.py:505
  41.3 1.8 %collective-permute-start.11 = (f32[264,128]{1,0:T(8,128)S(1)}, f32[264,128]{1,0:T(8,128)S(1)}, u32[]{:S(2)}, u32[]{:S(2)}) collective-permute-start(f32[264,128]{1,0:T(8,128)S(1)} %collective-permute-done.9.refs_1_), channel_id=1, source_target_pairs={{0,8},{1,9},{2,10},{3,11},{4,12},{5,13},{6,14},{7,15},{8,0},{9,1},... | collective-permute-start | bytes 405512 | tf_op jit(solution)/shard_map/ppermute | solution.py:505
  43.0 1.4 %collective-permute-start.10 = (f32[264,128]{1,0:T(8,128)S(1)}, f32[264,128]{1,0:T(8,128)S(1)}, u32[]{:S(2)}, u32[]{:S(2)}) collective-permute-start(f32[264,128]{1,0:T(8,128)S(1)} %collective-permute-done.8.refs_0_), channel_id=1, source_target_pairs={{0,8},{1,9},{2,10},{3,11},{4,12},{5,13},{6,14},{7,15},{8,0},{9,1},... | collective-permute-start | bytes 405512 | tf_op jit(solution)/shard_map/ppermute | solution.py:505
  47.3 8.5 %collective-permute-start.16 = (f32[192,256]{1,0:T(8,128)S(1)}, f32[192,256]{1,0:T(8,128)S(1)}, u32[]{:S(2)}, u32[]{:S(2)}) collective-permute-start(f32[192,256]{1,0:T(8,128)S(1)} %get-tuple-element.55), channel_id=1, source_target_pairs={{0,24},{1,25},{2,26},{3,27},{4,28},{5,29},{6,30},{7,31},{8,16},{9,... | collective-permute-start | bytes 589832 | tf_op jit(solution)/shard_map/ppermute | solution.py:505
  49.7 6.1 %collective-permute-start.15 = (f32[128,256]{1,0:T(8,128)S(1)}, f32[128,256]{1,0:T(8,128)S(1)}, u32[]{:S(2)}, u32[]{:S(2)}) collective-permute-start(f32[128,256]{1,0:T(8,128)S(1)} %get-tuple-element.54), channel_id=1, source_target_pairs={{0,16},{1,17},{2,18},{3,19},{4,20},{5,21},{6,22},{7,23},{8,0},{9,1... | collective-permute-start | bytes 393224 | tf_op jit(solution)/shard_map/ppermute | solution.py:505
  49.8 1.4 %collective-permute-start.14 = (f32[64,256]{1,0:T(8,128)S(1)}, f32[64,256]{1,0:T(8,128)S(1)}, u32[]{:S(2)}, u32[]{:S(2)}) collective-permute-start(f32[64,256]{1,0:T(8,128)S(1)} %get-tuple-element.53), channel_id=1, source_target_pairs={{0,8},{1,9},{2,10},{3,11},{4,12},{5,13},{6,14},{7,15},{8,0},{9,1},... | collective-permute-start | bytes 196616 | tf_op jit(solution)/shard_map/ppermute | solution.py:505

commit v18 on v16

--- a/solution.py
+++ b/solution.py
@@ -531,8 +531,7 @@
     own[-1], stored, across_types = lax.optimization_barrier((own[-1], stored, across_types))
     swapped = [send(each, beside) for each in own]
     table = (fields.shape[0], planes + 2 * reach[0], rows, lanes)
-    known, swapped[1] = lax.optimization_barrier((piece, swapped[1]))
-    (factor,) = call(factor_kernel, [table], [tile], [known, *own])
+    (factor,) = call(factor_kernel, [table], [tile], [piece, *own])
     late_stored, factor, *swapped = lax.optimization_barrier((stored, factor, *swapped))
     late_last = send(late_stored, {2: 0})
     middle, piece, kept, total, factor = call(

time: 56.9 us -> 57 us (level)
  transfers between devices with their start and end apart: 17 -> 17, of which waited for: 7 -> 8; matrix products, arithmetic and copies ran while one was open for 1% -> 1% of each run, Pallas kernels for 18% -> 18%
where the time goes in v18:
time: 57 us; the launch traced here: 56.7 us
  starting transfers between devices  21.8 us (38%)
  waiting for transfers between devices  17.3 us (30%)
  Pallas kernels  14.2 us (25%)
  local copies, waits for them, and re-layouts  2.02 us (4%)
  between operations  0.77 us (1%)
  other arithmetic  0.66 us (1%)
    ppermute x17, starting transfers between devices, send(): return lax.ppermute(array, ('sec', 'gx'), pairs)  21.8 us
    ppermute x17, waiting for transfers between devices, send(): return lax.ppermute(array, ('sec', 'gx'), pairs)  17.3 us
    pallas_call x7, Pallas kernels, call(): pl.pallas_call(kernel, in_specs=[IN_VMEM] * len(operands), out_specs=[IN_...  12.1 us
    pallas_call x1, Pallas kernels, launch(): pl.pallas_call(launch_kernel, in_specs=[pl.BlockSpec(memory_space=pltpu.H...  2.07 us
    unnamed x4, local copies, waits for them, and re-layouts  2.01 us
  transfers between devices with their start and end apart: 17, of which 8 were waited for; matrix products, arithmetic and copies ran while one was open for 1% of the time, Pallas kernels for 18%

profile of v18, /device:TPU:0, one launch (start us, length us, event | category | flops | bytes accessed | tf_op | source)
XLA Modules:
  0.0 56.7 jit_solution(13336566118292398882)
XLA Ops:
  0.6 2.4 %collective-permute-start = (f32[4,64,256]{2,1,0:T(8,128)}, f32[4,64,256]{2,1,0:T(8,128)S(1)}, u32[]{:S(2)}, u32[]{:S(2)}) collective-permute-start(f32[4,64,256]{2,1,0:T(8,128)} %bitcast.2), channel_id=1, source_target_pairs={{0,8},{1,9},{2,10},{3,11},{4,12},{5,13},{6,14},{7,15},{8,24},{9,25... | collective-permute-start | bytes 786440 | tf_op jit(solution)/shard_map/ppermute | solution.py:502
  3.0 0.7 %convert_element_type.5 = f32[1,4]{1,0:T(1,128)S(1)} convert(s32[1,4]{1,0:T(1,128)} %refs_2_.1) | non-fusion elementwise | flops 4 | bytes 32 | tf_op jit(solution)/shard_map/convert_element_type | solution.py:509
  3.7 0.6 %collective-permute-start.1 = (f32[8,128]{1,0:T(8,128)S(1)}, f32[8,128]{1,0:T(8,128)S(1)}, u32[]{:S(2)}, u32[]{:S(2)}) collective-permute-start(f32[8,128]{1,0:T(8,128)S(1)} %pad.4), channel_id=1, source_target_pairs={{8,24},{9,25},{10,26},{11,27},{12,28},{13,29},{14,30},{15,31}} | collective-permute-start | bytes 12296 | tf_op jit(solution)/shard_map/ppermute | solution.py:502
  4.3 2.1 %shard_map.104.bundle = f32[680,128]{1,0:T(8,128)} custom-call(f32[1,4,64,256]{3,2,1,0:T(8,128)} %refs_0_.1, f32[3,4,256]{2,1,0:T(4,128)} %refs_1_.1, s32[1,4]{1,0:T(1,128)} %refs_2_.1, f32[3,64]{1,0:T(4,128)} %refs_3_.1, f32[3,64]{1,0:T(4,128)} %refs_4_.1, f32[3,64]{1,0:T(4,128)} %refs_5_.1, f32[1,64]{1,0:T(1,128)} %bitcast.3, f32[64,64]{1,0:T(8,128)} %refs_7_.1), custom_call_target="tpu_custom_call" | custom-call | tf_op jit(solution)/shard_map/pallas_call | solution.py:215
  6.4 0.0 copy-start
  6.4 1.0 %copy-done = f32[680,128]{1,0:T(8,128)S(1)} copy-done((f32[680,128]{1,0:T(8,128)S(1)}, f32[680,128]{1,0:T(8,128)}, u32[]{:S(2)}) %copy-start) | copy-done | bytes 348184
  7.4 0.0 collective-permute-done.1.types
  7.4 0.0 collective-permute-done.moved
  7.5 0.7 %collective-permute-start.2 = (f32[4,64,256]{2,1,0:T(8,128)S(1)}, f32[4,64,256]{2,1,0:T(8,128)S(1)}, u32[]{:S(2)}, u32[]{:S(2)}) collective-permute-start(f32[4,64,256]{2,1,0:T(8,128)S(1)} %collective-permute-done.moved), channel_id=1, source_target_pairs={{24,16},{25,17},{26,18},{27,19},{28,20},{29,21},{30,22},{31,23}} | collective-permute-start | bytes 786440 | tf_op jit(solution)/shard_map/ppermute | solution.py:502
  8.1 0.0 collective-permute-done.2.passed
  8.2 2.4 %collective-permute-start.3 = (f32[544,128]{1,0:T(8,128)S(1)}, f32[544,128]{1,0:T(8,128)S(1)}, u32[]{:S(2)}, u32[]{:S(2)}) collective-permute-start(f32[544,128]{1,0:T(8,128)S(1)} %shard_map.106.refs_0_), channel_id=1, source_target_pairs={{0,1},{1,2},{2,3},{3,4},{4,5},{5,6},{6,7},{7,0},{8,10},{9,11},{10,... | collective-permute-start | bytes 835592 | tf_op jit(solution)/shard_map/ppermute | solution.py:502
  10.6 3.1 %collective-permute-start.5 = (f32[544,128]{1,0:T(8,128)S(1)}, f32[544,128]{1,0:T(8,128)S(1)}, u32[]{:S(2)}, u32[]{:S(2)}) collective-permute-start(f32[544,128]{1,0:T(8,128)S(1)} %shard_map.106.refs_0_), channel_id=1, source_target_pairs={{0,7},{1,0},{2,1},{3,2},{4,3},{5,4},{6,5},{7,6},{8,14},{9,15},{10,... | collective-permute-start | bytes 835592 | tf_op jit(solution)/shard_map/ppermute | solution.py:502
  13.7 1.3 %collective-permute-start.4 = (f32[8,128]{1,0:T(8,128)S(1)}, f32[8,128]{1,0:T(8,128)S(1)}, u32[]{:S(2)}, u32[]{:S(2)}) collective-permute-start(f32[8,128]{1,0:T(8,128)S(1)} %pad.4), channel_id=1, source_target_pairs={{16,0},{17,1},{18,2},{19,3},{20,4},{21,5},{22,6},{23,7}} | collective-permute-start | bytes 12296 | tf_op jit(solution)/shard_map/ppermute | solution.py:502
  15.0 0.0 copy-start.1
  15.0 1.0 %copy-done.1 = bf16[4,4,64,256]{3,2,1,0:T(8,128)(2,1)S(1)} copy-done((bf16[4,4,64,256]{3,2,1,0:T(8,128)(2,1)S(1)}, bf16[4,4,64,256]{3,2,1,0:T(8,128)(2,1)}, u32[]{:S(2)}) %copy-start.1) | copy-done | bytes 524312
  16.0 0.3 shard_map.107.refs_5_.refs_9_
  16.4 4.5 %collective-permute-done.4.across = f32[8,128]{1,0:T(8,128)S(1)} collective-permute-done((f32[8,128]{1,0:T(8,128)S(1)}, f32[8,128]{1,0:T(8,128)S(1)}, u32[]{:S(2)}, u32[]{:S(2)}) %collective-permute-start.4) | collective-permute-done | bytes 4128 | tf_op jit(solution)/shard_map/ppermute | solution.py:502
  20.9 0.0 collective-permute-done.3.refs_2_
  20.9 0.0 collective-permute-done.5.refs_1_
  20.9 2.7 %collective-permute-start.6 = (f32[544,128]{1,0:T(8,128)S(1)}, f32[544,128]{1,0:T(8,128)S(1)}, u32[]{:S(2)}, u32[]{:S(2)}) collective-permute-start(f32[544,128]{1,0:T(8,128)S(1)} %collective-permute-done.5.refs_1_), channel_id=1, source_target_pairs={{0,8},{1,9},{2,10},{3,11},{4,12},{5,13},{6,14},{7,15},{8,0},{9,1},... | collective-permute-start | bytes 835592 | tf_op jit(solution)/shard_map/ppermute | solution.py:502
  23.6 0.0 collective-permute-start.7
  23.6 0.9 %shard_map.108.refs_6_ = f32[3,20,128,128]{3,2,1,0:T(8,128)S(1)} custom-call(f32[544,128]{1,0:T(8,128)S(1)} %shard_map.106.refs_0_, f32[544,128]{1,0:T(8,128)S(1)} %collective-permute-done.5.refs_1_, f32[544,128]{1,0:T(8,128)S(1)} %collective-permute-done.3.refs_2_), custom_call_target="tpu_custom_call" | custom-call | tf_op jit(solution)/shard_map/pallas_call | solution.py:475
  24.5 0.3 collective-permute-done.6.refs_3_
  24.8 0.4 collective-permute-done.7.refs_4_
  25.2 1.3 %collective-permute-start.13 = (f32[4,4,128,128]{3,2,1,0:T(8,128)S(1)}, f32[4,4,128,128]{3,2,1,0:T(8,128)S(1)}, u32[]{:S(2)}, u32[]{:S(2)}) collective-permute-start(f32[4,4,128,128]{3,2,1,0:T(8,128)S(1)} %shard_map.107.refs_5_.refs_9_), channel_id=1, source_target_pairs={{16,0},{17,1},{18,2},{19,3},{20,4},{21,5},{22,6},{23,7}} | collective-permute-start | bytes 3145736 | tf_op jit(solution)/shard_map/ppermute | solution.py:502
  26.5 7.1 %shard_map.109 = (f32[4,128,128]{2,1,0:T(8,128)S(1)}, f32[264,128]{1,0:T(8,128)S(1)}, f32[4,128,128]{2,1,0:T(8,128)S(1)}, f32[4,128,128]{2,1,0:T(8,128)S(1)}, f32[3,20,128,128]{3,2,1,0:T(8,128)S(1)}) custom-call(f32[8,128]{1,0:T(8,128)S(1)} %get-tuple-element.27.taps, ...), custom_call_target="tpu_custom_call", output_to_operand_aliasing={{4}: (9, {})} | custom-call | tf_op jit(solution)/shard_map/pallas_call | solution.py:475
  33.5 2.2 %collective-permute-start.9 = (f32[264,128]{1,0:T(8,128)S(1)}, f32[264,128]{1,0:T(8,128)S(1)}, u32[]{:S(2)}, u32[]{:S(2)}) collective-permute-start(f32[264,128]{1,0:T(8,128)S(1)} %get-tuple-element.42), channel_id=1, source_target_pairs={{0,1},{1,2},{2,3},{3,4},{4,5},{5,6},{6,7},{7,0},{8,9},{9,10},{10,1... | collective-permute-start | bytes 405512 | tf_op jit(solution)/shard_map/ppermute | solution.py:502
  35.8 2.5 %collective-permute-start.8 = (f32[264,128]{1,0:T(8,128)S(1)}, f32[264,128]{1,0:T(8,128)S(1)}, u32[]{:S(2)}, u32[]{:S(2)}) collective-permute-start(f32[264,128]{1,0:T(8,128)S(1)} %get-tuple-element.42), channel_id=1, source_target_pairs={{0,7},{1,0},{2,1},{3,2},{4,3},{5,4},{6,5},{7,6},{8,15},{9,8},{10,9... | collective-permute-start | bytes 405512 | tf_op jit(solution)/shard_map/ppermute | solution.py:502
  38.3 0.0 collective-permute-start.12
  38.3 3.3 %collective-permute-done.9.refs_1_ = f32[264,128]{1,0:T(8,128)S(1)} collective-permute-done((f32[264,128]{1,0:T(8,128)S(1)}, f32[264,128]{1,0:T(8,128)S(1)}, u32[]{:S(2)}, u32[]{:S(2)}) %collective-permute-start.9) | collective-permute-done | bytes 135200 | tf_op jit(solution)/shard_map/ppermute | solution.py:502
  41.7 0.0 collective-permute-start.11
  41.7 1.7 %collective-permute-done.8.refs_0_ = f32[264,128]{1,0:T(8,128)S(1)} collective-permute-done((f32[264,128]{1,0:T(8,128)S(1)}, f32[264,128]{1,0:T(8,128)S(1)}, u32[]{:S(2)}, u32[]{:S(2)}) %collective-permute-start.8) | collective-permute-done | bytes 135200 | tf_op jit(solution)/shard_map/ppermute | solution.py:502
  43.4 0.0 collective-permute-start.10
  43.4 0.0 collective-permute-done.12.refs_7_
  43.4 0.0 collective-permute-done.11.refs_3_
  43.4 1.3 %collective-permute-done.10.refs_2_ = f32[264,128]{1,0:T(8,128)S(1)} collective-permute-done((f32[264,128]{1,0:T(8,128)S(1)}, f32[264,128]{1,0:T(8,128)S(1)}, u32[]{:S(2)}, u32[]{:S(2)}) %collective-permute-start.10) | collective-permute-done | bytes 135200 | tf_op jit(solution)/shard_map/ppermute | solution.py:502
  44.8 0.0 collective-permute-done.13.refs_8_
  44.8 2.9 %shard_map.110 = (f32[4,64,256]{2,1,0:T(8,128)S(1)}, f32[64,256]{1,0:T(8,128)S(1)}, f32[64,256]{1,0:T(8,128)S(1)}, f32[192,256]{1,0:T(8,128)S(1)}, f32[128,256]{1,0:T(8,128)S(1)}) custom-call(f32[8,128]{1,0:T(8,128)S(1)} %get-tuple-element.27.taps, bf16[256,256]{1,0:T(8,128)(2,1)S(1)} %get-tuple-element.28.weights, ...), custom_call_target="tpu_custom_call" | custom-call | tf_op jit(solution)/shard_map/pallas_call | solution.py:475
  47.7 2.1 %collective-permute-start.15 = (f32[192,256]{1,0:T(8,128)S(1)}, f32[192,256]{1,0:T(8,128)S(1)}, u32[]{:S(2)}, u32[]{:S(2)}) collective-permute-start(f32[192,256]{1,0:T(8,128)S(1)} %get-tuple-element.50), channel_id=1, source_target_pairs={{0,16},{1,17},{2,18},{3,19},{4,20},{5,21},{6,22},{7,23},{8,0},{9,1... | collective-permute-start | bytes 589832 | tf_op jit(solution)/shard_map/ppermute | solution.py:502
  49.8 0.1 collective-permute-start.16
  49.9 0.4 collective-permute-start.14
  50.3 0.9 %collective-permute-done.14.to_pair = f32[64,256]{1,0:T(8,128)S(1)} collective-permute-done((f32[64,256]{1,0:T(8,128)S(1)}, f32[64,256]{1,0:T(8,128)S(1)}, u32[]{:S(2)}, u32[]{:S(2)}) %collective-permute-start.14) | collective-permute-done | bytes 65568 | tf_op jit(solution)/shard_map/ppermute | solution.py:502
  51.2 4.7 %collective-permute-done.16.to_corner = f32[128,256]{1,0:T(8,128)S(1)} collective-permute-done((f32[128,256]{1,0:T(8,128)S(1)}, f32[128,256]{1,0:T(8,128)S(1)}, u32[]{:S(2)}, u32[]{:S(2)}) %collective-permute-start.16) | collective-permute-done | bytes 131104 | tf_op jit(solution)/shard_map/ppermute | solution.py:502
  56.0 0.0 collective-permute-done.15.to_across
  56.0 0.8 %shard_map.111 = (f32[1,4,64,256]{3,2,1,0:T(8,128)}, f32[4,16,256]{2,1,0:T(8,128)}) custom-call(f32[4,64,256]{2,1,0:T(8,128)S(1)} %get-tuple-element.47.handoff_in, f32[64,256]{1,0:T(8,128)S(1)} %get-tuple-element.48.share, f32[64,256]{1,0:T(8,128)S(1)} %collective-permute-done.14.to_pair, f32[192,256]{1,0:T(8,128)S(1)} %collective-permute-done.15.to_across, ...), custom_call_target="tpu_custom_call" | custom-call | tf_op jit(solution)/shard_map/pallas_call | solution.py:475
  (3 shorter events, 0.1 us)
Async XLA Ops:
  0.6 6.8 %collective-permute-start = (f32[4,64,256]{2,1,0:T(8,128)}, f32[4,64,256]{2,1,0:T(8,128)S(1)}, u32[]{:S(2)}, u32[]{:S(2)}) collective-permute-start(f32[4,64,256]{2,1,0:T(8,128)} %bitcast.2), channel_id=1, source_target_pairs={{0,8},{1,9},{2,10},{3,11},{4,12},{5,13},{6,14},{7,15},{8,24},{9,25... | collective-permute-start | bytes 786440 | tf_op jit(solution)/shard_map/ppermute | solution.py:502
  3.7 3.8 %collective-permute-start.1 = (f32[8,128]{1,0:T(8,128)S(1)}, f32[8,128]{1,0:T(8,128)S(1)}, u32[]{:S(2)}, u32[]{:S(2)}) collective-permute-start(f32[8,128]{1,0:T(8,128)S(1)} %pad.4), channel_id=1, source_target_pairs={{8,24},{9,25},{10,26},{11,27},{12,28},{13,29},{14,30},{15,31}} | collective-permute-start | bytes 12296 | tf_op jit(solution)/shard_map/ppermute | solution.py:502
  6.4 1.0 %copy-start = (f32[680,128]{1,0:T(8,128)S(1)}, f32[680,128]{1,0:T(8,128)}, u32[]{:S(2)}) copy-start(f32[680,128]{1,0:T(8,128)} %shard_map.104.bundle) | copy-start | bytes 1044484
  7.5 0.7 %collective-permute-start.2 = (f32[4,64,256]{2,1,0:T(8,128)S(1)}, f32[4,64,256]{2,1,0:T(8,128)S(1)}, u32[]{:S(2)}, u32[]{:S(2)}) collective-permute-start(f32[4,64,256]{2,1,0:T(8,128)S(1)} %collective-permute-done.moved), channel_id=1, source_target_pairs={{24,16},{25,17},{26,18},{27,19},{28,20},{29,21},{30,22},{31,23}} | collective-permute-start | bytes 786440 | tf_op jit(solution)/shard_map/ppermute | solution.py:502
  8.2 12.7 %collective-permute-start.3 = (f32[544,128]{1,0:T(8,128)S(1)}, f32[544,128]{1,0:T(8,128)S(1)}, u32[]{:S(2)}, u32[]{:S(2)}) collective-permute-start(f32[544,128]{1,0:T(8,128)S(1)} %shard_map.106.refs_0_), channel_id=1, source_target_pairs={{0,1},{1,2},{2,3},{3,4},{4,5},{5,6},{6,7},{7,0},{8,10},{9,11},{10,... | collective-permute-start | bytes 835592 | tf_op jit(solution)/shard_map/ppermute | solution.py:502
  10.6 10.3 %collective-permute-start.5 = (f32[544,128]{1,0:T(8,128)S(1)}, f32[544,128]{1,0:T(8,128)S(1)}, u32[]{:S(2)}, u32[]{:S(2)}) collective-permute-start(f32[544,128]{1,0:T(8,128)S(1)} %shard_map.106.refs_0_), channel_id=1, source_target_pairs={{0,7},{1,0},{2,1},{3,2},{4,3},{5,4},{6,5},{7,6},{8,14},{9,15},{10,... | collective-permute-start | bytes 835592 | tf_op jit(solution)/shard_map/ppermute | solution.py:502
  13.7 7.2 %collective-permute-start.4 = (f32[8,128]{1,0:T(8,128)S(1)}, f32[8,128]{1,0:T(8,128)S(1)}, u32[]{:S(2)}, u32[]{:S(2)}) collective-permute-start(f32[8,128]{1,0:T(8,128)S(1)} %pad.4), channel_id=1, source_target_pairs={{16,0},{17,1},{18,2},{19,3},{20,4},{21,5},{22,6},{23,7}} | collective-permute-start | bytes 12296 | tf_op jit(solution)/shard_map/ppermute | solution.py:502
  15.0 1.0 %copy-start.1 = (bf16[4,4,64,256]{3,2,1,0:T(8,128)(2,1)S(1)}, bf16[4,4,64,256]{3,2,1,0:T(8,128)(2,1)}, u32[]{:S(2)}) copy-start(bf16[4,4,64,256]{3,2,1,0:T(8,128)(2,1)} %backward) | copy-start | bytes 1572868
  20.9 3.9 %collective-permute-start.6 = (f32[544,128]{1,0:T(8,128)S(1)}, f32[544,128]{1,0:T(8,128)S(1)}, u32[]{:S(2)}, u32[]{:S(2)}) collective-permute-start(f32[544,128]{1,0:T(8,128)S(1)} %collective-permute-done.5.refs_1_), channel_id=1, source_target_pairs={{0,8},{1,9},{2,10},{3,11},{4,12},{5,13},{6,14},{7,15},{8,0},{9,1},... | collective-permute-start | bytes 835592 | tf_op jit(solution)/shard_map/ppermute | solution.py:502
  23.6 1.6 %collective-permute-start.7 = (f32[544,128]{1,0:T(8,128)S(1)}, f32[544,128]{1,0:T(8,128)S(1)}, u32[]{:S(2)}, u32[]{:S(2)}) collective-permute-start(f32[544,128]{1,0:T(8,128)S(1)} %collective-permute-done.3.refs_2_), channel_id=1, source_target_pairs={{0,8},{1,9},{2,10},{3,11},{4,12},{5,13},{6,14},{7,15},{8,0},{9,1},... | collective-permute-start | bytes 835592 | tf_op jit(solution)/shard_map/ppermute | solution.py:502
  25.2 19.6 %collective-permute-start.13 = (f32[4,4,128,128]{3,2,1,0:T(8,128)S(1)}, f32[4,4,128,128]{3,2,1,0:T(8,128)S(1)}, u32[]{:S(2)}, u32[]{:S(2)}) collective-permute-start(f32[4,4,128,128]{3,2,1,0:T(8,128)S(1)} %shard_map.107.refs_5_.refs_9_), channel_id=1, source_target_pairs={{16,0},{17,1},{18,2},{19,3},{20,4},{21,5},{22,6},{23,7}} | collective-permute-start | bytes 3145736 | tf_op jit(solution)/shard_map/ppermute | solution.py:502
  33.5 8.1 %collective-permute-start.9 = (f32[264,128]{1,0:T(8,128)S(1)}, f32[264,128]{1,0:T(8,128)S(1)}, u32[]{:S(2)}, u32[]{:S(2)}) collective-permute-start(f32[264,128]{1,0:T(8,128)S(1)} %get-tuple-element.42), channel_id=1, source_target_pairs={{0,1},{1,2},{2,3},{3,4},{4,5},{5,6},{6,7},{7,0},{8,9},{9,10},{10,1... | collective-permute-start | bytes 405512 | tf_op jit(solution)/shard_map/ppermute | solution.py:502
  35.8 7.6 %collective-permute-start.8 = (f32[264,128]{1,0:T(8,128)S(1)}, f32[264,128]{1,0:T(8,128)S(1)}, u32[]{:S(2)}, u32[]{:S(2)}) collective-permute-start(f32[264,128]{1,0:T(8,128)S(1)} %get-tuple-element.42), channel_id=1, source_target_pairs={{0,7},{1,0},{2,1},{3,2},{4,3},{5,4},{6,5},{7,6},{8,15},{9,8},{10,9... | collective-permute-start | bytes 405512 | tf_op jit(solution)/shard_map/ppermute | solution.py:502
  38.3 5.1 %collective-permute-start.12 = (f32[4,128,128]{2,1,0:T(8,128)S(1)}, f32[4,128,128]{2,1,0:T(8,128)S(1)}, u32[]{:S(2)}, u32[]{:S(2)}) collective-permute-start(f32[4,128,128]{2,1,0:T(8,128)S(1)} %get-tuple-element.45.refs_6_), channel_id=1, source_target_pairs={{0,8},{1,9},{2,10},{3,11},{4,12},{5,13},{6,14},{7,15},{8,0},{9,1},... | collective-permute-start | bytes 786440 | tf_op jit(solution)/shard_map/ppermute | solution.py:502
  41.7 1.8 %collective-permute-start.11 = (f32[264,128]{1,0:T(8,128)S(1)}, f32[264,128]{1,0:T(8,128)S(1)}, u32[]{:S(2)}, u32[]{:S(2)}) collective-permute-start(f32[264,128]{1,0:T(8,128)S(1)} %collective-permute-done.9.refs_1_), channel_id=1, source_target_pairs={{0,8},{1,9},{2,10},{3,11},{4,12},{5,13},{6,14},{7,15},{8,0},{9,1},... | collective-permute-start | bytes 405512 | tf_op jit(solution)/shard_map/ppermute | solution.py:502
  43.4 1.4 %collective-permute-start.10 = (f32[264,128]{1,0:T(8,128)S(1)}, f32[264,128]{1,0:T(8,128)S(1)}, u32[]{:S(2)}, u32[]{:S(2)}) collective-permute-start(f32[264,128]{1,0:T(8,128)S(1)} %collective-permute-done.8.refs_0_), channel_id=1, source_target_pairs={{0,8},{1,9},{2,10},{3,11},{4,12},{5,13},{6,14},{7,15},{8,0},{9,1},... | collective-permute-start | bytes 405512 | tf_op jit(solution)/shard_map/ppermute | solution.py:502
  47.7 8.3 %collective-permute-start.15 = (f32[192,256]{1,0:T(8,128)S(1)}, f32[192,256]{1,0:T(8,128)S(1)}, u32[]{:S(2)}, u32[]{:S(2)}) collective-permute-start(f32[192,256]{1,0:T(8,128)S(1)} %get-tuple-element.50), channel_id=1, source_target_pairs={{0,16},{1,17},{2,18},{3,19},{4,20},{5,21},{6,22},{7,23},{8,0},{9,1... | collective-permute-start | bytes 589832 | tf_op jit(solution)/shard_map/ppermute | solution.py:502
  49.8 6.2 %collective-permute-start.16 = (f32[128,256]{1,0:T(8,128)S(1)}, f32[128,256]{1,0:T(8,128)S(1)}, u32[]{:S(2)}, u32[]{:S(2)}) collective-permute-start(f32[128,256]{1,0:T(8,128)S(1)} %get-tuple-element.51), channel_id=1, source_target_pairs={{0,24},{1,25},{2,26},{3,27},{4,28},{5,29},{6,30},{7,31},{8,16},{9,... | collective-permute-start | bytes 393224 | tf_op jit(solution)/shard_map/ppermute | solution.py:502
  49.9 1.3 %collective-permute-start.14 = (f32[64,256]{1,0:T(8,128)S(1)}, f32[64,256]{1,0:T(8,128)S(1)}, u32[]{:S(2)}, u32[]{:S(2)}) collective-permute-start(f32[64,256]{1,0:T(8,128)S(1)} %get-tuple-element.49), channel_id=1, source_target_pairs={{0,8},{1,9},{2,10},{3,11},{4,12},{5,13},{6,14},{7,15},{8,0},{9,1},... | collective-permute-start | bytes 196616 | tf_op jit(solution)/shard_map/ppermute | solution.py:502
